TPU v7x, 32 devices: a whole 2x2x4 slice. The times are simulated.
32 devices in a mesh: gx: 4 (over x, core), gy: 8 (over z, y).
Axes of the slice: x: 2, y: 2, z: 4, core: 2. Of those that a mesh axis runs over, the one named last changes fastest.
Arguments:
- source: bfloat16 [16, 512, 256], P(None, ('gx', 'gy')), may hold values from -6 to 6
- leaf_flux: bfloat16 [32768, 256], P(('gx', 'gy')), may hold values from -0.375 to 0.375
- leaf_particular: bfloat16 [131072, 256], P(('gx', 'gy')), may hold values from -0.375 to 0.375
- leaf_lift: bfloat16 [32768, 256], P(('gx', 'gy')), may hold values from -0.75 to 0.75
- box_up: bfloat16 [20480, 1024], P(('gx', 'gy')), may hold values from -0.1875 to 0.1875
- box_down: bfloat16 [32768, 640], P(('gx', 'gy')), may hold values from -0.25 to 0.25
- up_one: bfloat16 [8192, 768], P(('gx', 'gy')), may hold values from -0.1875 to 0.1875
- down_one: bfloat16 [8192, 768], P(('gx', 'gy')), may hold values from -0.21875 to 0.21875
- up_two: bfloat16 [4096, 1536], P(('gx', 'gy')), may hold values from -0.125 to 0.125
- down_two: bfloat16 [4096, 1536], P(('gx', 'gy')), may hold values from -0.15625 to 0.15625
- up_root: bfloat16 [2048, 256], P(('gx', 'gy')), may hold values from -0.125 to 0.125
- down_root: bfloat16 [2048, 256], P(('gx', 'gy')), may hold values from -0.375 to 0.375
Outputs:
- solution: float32 [16, 512, 256], P(None, ('gx', 'gy'))
All inputs are finite; a program needn't handle non-finite values.
Results may differ from a plain program's by a relative error of at most 0.014.
Values may be sent and summed in bfloat16 or wider, within the bound.
No kernel may reach another device: no remote copies, remote signals or barrier semaphores. Data moves between devices by JAX's collectives and lax.ppermute only.
A program may use at most 64 MiB of HBM per device.

v0:
```python
import jax
import jax.numpy as jnp
from jax import lax
from jax.sharding import PartitionSpec as P

AXES = ("gx", "gy")


def contract(left, right):
    return lax.dot_general(
        left, right, (((1,), (1,)), ((), ())), preferred_element_type=jnp.float32
    )


def product(left, right):
    return jnp.dot(left, right, preferred_element_type=jnp.float32)


def rounded(value):
    return value.astype(jnp.bfloat16)


def swap(value, mask):
    count = lax.axis_size(AXES)
    return lax.ppermute(value, AXES, [(i, i ^ mask) for i in range(count)])


def partner_sum(total, mask):
    return total + swap(rounded(total), mask).astype(jnp.float32)


def bits_of(first, last):
    bits = []
    while first < last:
        bits.append(first)
        first *= 2
    return bits


def placed(pieces, place, axis):
    bit = len(pieces) // 2
    if bit == 0:
        return pieces[0]
    low, high = placed(pieces[:bit], place, axis), placed(pieces[bit:], place, axis)
    upper = place & bit != 0
    return jnp.concatenate(
        [jnp.where(upper, high, low), jnp.where(upper, low, high)], axis=axis
    )


def joined_pair(joined, other, upper, axis):
    return jnp.stack(
        [jnp.where(upper, other, joined), jnp.where(upper, joined, other)], axis=axis
    )


def tie(*values):
    return lax.optimization_barrier(values)


def quad_order(halves, width, place):
    own, other = halves
    upper = place & 1 != 0
    blocks = []
    for start in range(0, own.shape[1], width):
        left, right = own[:, start : start + width], other[:, start : start + width]
        blocks += [jnp.where(upper, right, left), jnp.where(upper, left, right)]
    return jnp.concatenate(blocks, axis=1)


def per_device(
    source,
    leaf_flux,
    leaf_particular,
    leaf_lift,
    box_up,
    box_down,
    up_one,
    down_one,
    up_two,
    down_two,
    up_root,
    down_root,
):
    rhs_count, leaves, points = source.shape
    edge_count = leaf_flux.shape[0] // leaves
    count = lax.axis_size(AXES)
    place = lax.axis_index(AXES)
    k_zero = up_one.shape[0]
    inner_dev = box_up.shape[0] - k_zero
    k_one = up_one.shape[1] - k_zero
    width = up_two.shape[0]
    quad = k_one // width
    family = (up_two.shape[1] - k_one) // up_root.shape[0]
    near = quad // 2
    pair = family // 2
    root_points = up_root.shape[1]

    far = pair // 2

    roots = jnp.concatenate([up_root, down_root], axis=1)
    roots_far = swap(roots, far)
    up_two_near = swap(up_two, near)

    flux = jnp.einsum(
        "rlq,leq->rle",
        source,
        leaf_flux.reshape(leaves, edge_count, points),
        preferred_element_type=jnp.float32,
    )
    flux = rounded(flux).reshape(rhs_count, leaves * edge_count)
    box_state = rounded(contract(flux, box_up))
    first_sum = product(box_state[:, inner_dev:], up_one)

    first_sum, roots_far = tie(first_sum, roots_far)
    roots = joined_pair(roots, roots_far, place & far != 0, 0)
    roots_near = swap(roots, near)
    first_sum = partner_sum(first_sum, 1)

    first_sum, roots_near = tie(first_sum, roots_near)
    roots = joined_pair(roots, roots_near, place & near != 0, 1)
    roots_one = swap(roots, 1)
    first_sum = partner_sum(first_sum, near)
    first_state = rounded(first_sum)

    def piece(mask):
        start = k_zero + (place ^ mask) % quad * width
        return lax.dynamic_slice_in_dim(first_state, start, width, 1)

    second_sum = product(piece(0), up_two) + product(piece(near), up_two_near)
    second_sum, roots_one = tie(second_sum, roots_one)
    roots = joined_pair(roots, roots_one, place & 1 != 0, 2)
    roots_pair = swap(roots, pair)
    down_two_near = swap(down_two, near)
    second_sum = partner_sum(second_sum, far)

    second_sum, roots_pair = tie(second_sum, roots_pair)
    roots = joined_pair(roots, roots_pair, place & pair != 0, 0)
    roots = roots.reshape(-1, roots.shape[-1])
    second_sum = partner_sum(second_sum, 1)
    second_sum = partner_sum(second_sum, pair)
    second_state = rounded(second_sum)

    root_sum = product(second_state[:, k_one:], roots[:, :root_points])
    root_sum, down_two_near = tie(root_sum, down_two_near)
    for bit in bits_of(family, count):
        root_sum = partner_sum(root_sum, bit)
    root_state = rounded(root_sum)

    top_bound = rounded(contract(root_state, roots[:, root_points:]))
    second_input = jnp.concatenate([second_state[:, :k_one], top_bound], axis=1)
    own_mid = rounded(contract(second_input, down_two))
    near_mid = rounded(contract(second_input, down_two_near))
    mid_bound = placed([own_mid, near_mid], place // near, 1)
    other_mid = swap(mid_bound, 1)
    mid_bound = quad_order((mid_bound, other_mid), width, place)
    first_input = jnp.concatenate([first_state[:, :k_zero], mid_bound], axis=1)

    box_bound = rounded(contract(first_input, down_one))
    box_input = jnp.concatenate([box_state[:, :inner_dev], box_bound], axis=1)
    leaf_bound = rounded(contract(box_input, box_down)).reshape(rhs_count, leaves, edge_count)
    lifted = jnp.einsum(
        "rle,leq->rlq",
        leaf_bound,
        leaf_lift.reshape(leaves, edge_count, points),
        preferred_element_type=jnp.float32,
    )
    particular = jnp.einsum(
        "rlq,lqp->rlp",
        source,
        leaf_particular.reshape(leaves, points, points),
        preferred_element_type=jnp.float32,
    )
    return lifted + particular


def solution(mesh):
    return jax.shard_map(
        per_device,
        mesh=mesh,
        in_specs=(P(None, AXES, None),) + (P(AXES, None),) * 11,
        out_specs=P(None, AXES, None),
        check_vma=False,
    )
```

profile of v0, /device:TPU:0, one launch (start us, length us, event | category | flops | bytes accessed | tf_op | source)
XLA Modules:
  0.0 55.8 jit_solution(11138169161072589938)
XLA Ops:
  0.0 0.0 copy-start
  0.0 0.0 copy-start.4
  0.0 0.9 %constant_dynamic-update-slice_fusion.1 = bf16[64,512]{1,0:T(8,128)(2,1)S(1)} fusion(bf16[64,256]{1,0:T(8,128)(2,1)} %param.22), kind=kLoop, calls=%fused_computation.42 | loop fusion | bytes 65536
  0.9 0.8 %constant_dynamic-update-slice_fusion = bf16[64,512]{1,0:T(8,128)(2,1)S(1)} fusion(bf16[64,512]{1,0:T(8,128)(2,1)S(1)} %constant_dynamic-update-slice_fusion.1, bf16[64,256]{1,0:T(8,128)(2,1)} %param.23), kind=kLoop, calls=%fused_computation.41 | loop fusion | bytes 65536 | tf_op jit(solution)/shard_map/concatenate | solution.py:101
  1.7 4.0 %collective-permute-start = (bf16[64,512]{1,0:T(8,128)(2,1)S(1)}, bf16[64,512]{1,0:T(8,128)(2,1)S(1)}, u32[]{:S(2)}, u32[]{:S(2)}) collective-permute-start(bf16[64,512]{1,0:T(8,128)(2,1)S(1)} %constant_dynamic-update-slice_fusion), channel_id=1, source_target_pairs={{0,4},{1,5},{2,6},{3,7},{4,0},{5,1},{6,2},{7,3},{8,12},{9,13},{10,... | collective-permute-start | bytes 196616 | tf_op jit(solution)/shard_map/ppermute | solution.py:25
  5.7 1.6 %collective-permute-start.4 = (bf16[128,1536]{1,0:T(8,128)(2,1)}, bf16[128,1536]{1,0:T(8,128)(2,1)S(1)}, u32[]{:S(2)}, u32[]{:S(2)}) collective-permute-start(bf16[128,1536]{1,0:T(8,128)(2,1)} %param.20), channel_id=1, source_target_pairs={{0,2},{1,3},{2,0},{3,1},{4,6},{5,7},{6,4},{7,5},{8,10},{9,11},{10,... | collective-permute-start | bytes 1179656 | tf_op jit(solution)/shard_map/ppermute | solution.py:25
  7.3 1.3 %fusion.1 = bf16[16,16,64]{2,0,1:T(8,128)(2,1)S(1)} fusion(bf16[16,64,256]{2,1,0:T(8,128)(2,1)} %bitcast.48, bf16[16,16,256]{2,1,0:T(8,128)(2,1)} %param.12), kind=kOutput, calls=%fused_computation.5 | convolution fusion | flops 8404992 | bytes 688128 | tf_op jit(solution)/shard_map/rlq,leq->rle/dot_general | solution.py:105
  8.6 0.1 reshape.19
  8.7 1.8 %convolution_convert_fusion.3 = bf16[16,640]{1,0:T(8,128)(2,1)S(1)} fusion(bf16[16,1024]{1,0:T(8,128)(2,1)S(1)} %reshape.19, bf16[640,1024]{1,0:T(8,128)(2,1)} %param.16), kind=kOutput, calls=%fused_computation.8 | convolution fusion | flops 20981760 | bytes 1363968 | tf_op jit(solution)/shard_map/dot_general | solution.py:10
  10.5 0.0 copy-done.4
  10.5 0.0 copy-start.6
  10.5 0.2 fusion.13
  10.7 0.0 copy-start.5
  10.7 0.0 collective-permute-done
  10.8 1.6 %collective-permute-start.1 = (bf16[16,768]{1,0:T(8,128)(2,1)S(1)}, bf16[16,768]{1,0:T(8,128)(2,1)S(1)}, u32[]{:S(2)}, u32[]{:S(2)}) collective-permute-start(bf16[16,768]{1,0:T(8,128)(2,1)S(1)} %convert_element_type.72), channel_id=1, source_target_pairs={{0,1},{1,0},{2,3},{3,2},{4,5},{5,4},{6,7},{7,6},{8,9},{9,8},{10,11... | collective-permute-start | bytes 73736 | tf_op jit(solution)/shard_map/ppermute | solution.py:25
  12.4 0.5 collective-permute-start.2
  12.9 1.8 %collective-permute-done.1 = bf16[16,768]{1,0:T(8,128)(2,1)S(1)} collective-permute-done((bf16[16,768]{1,0:T(8,128)(2,1)S(1)}, bf16[16,768]{1,0:T(8,128)(2,1)S(1)}, u32[]{:S(2)}, u32[]{:S(2)}) %collective-permute-start.1) | collective-permute-done | bytes 24608 | tf_op jit(solution)/shard_map/ppermute | solution.py:25
  14.7 5.0 %collective-permute-done.2 = bf16[2,64,512]{2,1,0:T(8,128)(2,1)S(1)} collective-permute-done((bf16[2,64,512]{2,1,0:T(8,128)(2,1)S(1)}, bf16[2,64,512]{2,1,0:T(8,128)(2,1)S(1)}, u32[]{:S(2)}, u32[]{:S(2)}) %collective-permute-start.2) | collective-permute-done | bytes 131104 | tf_op jit(solution)/shard_map/ppermute | solution.py:25
  19.7 1.5 %collective-permute-start.3 = (bf16[16,768]{1,0:T(8,128)(2,1)S(1)}, bf16[16,768]{1,0:T(8,128)(2,1)S(1)}, u32[]{:S(2)}, u32[]{:S(2)}) collective-permute-start(bf16[16,768]{1,0:T(8,128)(2,1)S(1)} %convert_element_type.74), channel_id=1, source_target_pairs={{0,2},{1,3},{2,0},{3,1},{4,6},{5,7},{6,4},{7,5},{8,10},{9,11},{10,... | collective-permute-start | bytes 73736 | tf_op jit(solution)/shard_map/ppermute | solution.py:25
  21.3 1.6 %collective-permute-start.5 = (bf16[2,2,64,512]{3,2,1,0:T(8,128)(2,1)S(1)}, bf16[2,2,64,512]{3,2,1,0:T(8,128)(2,1)S(1)}, u32[]{:S(2)}, u32[]{:S(2)}) collective-permute-start(bf16[2,2,64,512]{3,2,1,0:T(8,128)(2,1)S(1)} %pad_maximum_fusion.2), channel_id=1, source_target_pairs={{0,1},{1,0},{2,3},{3,2},{4,5},{5,4},{6,7},{7,6},{8,9},{9,8},{10,11... | collective-permute-start | bytes 786440 | tf_op jit(solution)/shard_map/ppermute | solution.py:25
  22.9 0.7 %collective-permute-done.3 = bf16[16,768]{1,0:T(8,128)(2,1)S(1)} collective-permute-done((bf16[16,768]{1,0:T(8,128)(2,1)S(1)}, bf16[16,768]{1,0:T(8,128)(2,1)S(1)}, u32[]{:S(2)}, u32[]{:S(2)}) %collective-permute-start.3) | collective-permute-done | bytes 24608 | tf_op jit(solution)/shard_map/ppermute | solution.py:25
  23.5 0.0 collective-permute-done.4
  23.6 0.2 fusion.15
  23.7 0.0 copy-done.5
  23.7 0.2 convolution_add_fusion
  23.9 4.4 %collective-permute-done.5 = bf16[2,2,64,512]{3,2,1,0:T(8,128)(2,1)S(1)} collective-permute-done((bf16[2,2,64,512]{3,2,1,0:T(8,128)(2,1)S(1)}, bf16[2,2,64,512]{3,2,1,0:T(8,128)(2,1)S(1)}, u32[]{:S(2)}, u32[]{:S(2)}) %collective-permute-start.5) | collective-permute-done | bytes 262176 | tf_op jit(solution)/shard_map/ppermute | solution.py:25
  28.3 0.8 %pad_maximum_fusion.1 = bf16[2,2,2,64,512]{4,3,2,1,0:T(8,128)(2,1)} fusion(bf16[2,2,1,64,512]{4,3,2,1,0:T(8,128)(2,1)S(1)} %get-tuple-element.28, bf16[2,2,1,64,512]{4,3,2,1,0:T(8,128)(2,1)S(1)} %get-tuple-element.27), kind=kLoop, calls=%fused_computation.16 | loop fusion | flops 262144 | bytes 1048576 | tf_op jit(solution)/shard_map/stack | solution.py:52
  29.1 0.0 collective-permute-start.7
  29.2 1.2 %collective-permute-start.6 = (bf16[16,1536]{1,0:T(8,128)(2,1)S(1)}, bf16[16,1536]{1,0:T(8,128)(2,1)S(1)}, u32[]{:S(2)}, u32[]{:S(2)}) collective-permute-start(bf16[16,1536]{1,0:T(8,128)(2,1)S(1)} %convert_element_type.77), channel_id=1, source_target_pairs={{0,4},{1,5},{2,6},{3,7},{4,0},{5,1},{6,2},{7,3},{8,12},{9,13},{10,... | collective-permute-start | bytes 147464 | tf_op jit(solution)/shard_map/ppermute | solution.py:25
  30.4 0.3 collective-permute-start.10
  30.7 4.7 %collective-permute-done.6 = bf16[16,1536]{1,0:T(8,128)(2,1)S(1)} collective-permute-done((bf16[16,1536]{1,0:T(8,128)(2,1)S(1)}, bf16[16,1536]{1,0:T(8,128)(2,1)S(1)}, u32[]{:S(2)}, u32[]{:S(2)}) %collective-permute-start.6) | collective-permute-done | bytes 49184 | tf_op jit(solution)/shard_map/ppermute | solution.py:25
  35.4 0.0 collective-permute-done.7
  35.4 1.6 %collective-permute-start.8 = (bf16[16,1536]{1,0:T(8,128)(2,1)S(1)}, bf16[16,1536]{1,0:T(8,128)(2,1)S(1)}, u32[]{:S(2)}, u32[]{:S(2)}) collective-permute-start(bf16[16,1536]{1,0:T(8,128)(2,1)S(1)} %convert_element_type.79), channel_id=1, source_target_pairs={{0,1},{1,0},{2,3},{3,2},{4,5},{5,4},{6,7},{7,6},{8,9},{9,8},{10,11... | collective-permute-start | bytes 147464 | tf_op jit(solution)/shard_map/ppermute | solution.py:25
  37.1 0.1 select_bitcast_fusion.1
  37.1 2.5 %collective-permute-done.8 = bf16[16,1536]{1,0:T(8,128)(2,1)S(1)} collective-permute-done((bf16[16,1536]{1,0:T(8,128)(2,1)S(1)}, bf16[16,1536]{1,0:T(8,128)(2,1)S(1)}, u32[]{:S(2)}, u32[]{:S(2)}) %collective-permute-start.8) | collective-permute-done | bytes 49184 | tf_op jit(solution)/shard_map/ppermute | solution.py:25
  39.6 0.1 collective-permute-start.9
  39.7 0.0 copy-start.3
  39.7 0.1 pad_maximum_fusion
  39.8 1.1 %collective-permute-done.9 = bf16[16,1536]{1,0:T(8,128)(2,1)S(1)} collective-permute-done((bf16[16,1536]{1,0:T(8,128)(2,1)S(1)}, bf16[16,1536]{1,0:T(8,128)(2,1)S(1)}, u32[]{:S(2)}, u32[]{:S(2)}) %collective-permute-start.9) | collective-permute-done | bytes 49184 | tf_op jit(solution)/shard_map/ppermute | solution.py:25
  40.9 0.2 fusion.3
  41.1 1.7 %collective-permute-done.10 = bf16[128,1536]{1,0:T(8,128)(2,1)} collective-permute-done((bf16[128,1536]{1,0:T(8,128)(2,1)}, bf16[128,1536]{1,0:T(8,128)(2,1)}, u32[]{:S(2)}, u32[]{:S(2)}) %collective-permute-start.10) | collective-permute-done | bytes 393248 | tf_op jit(solution)/shard_map/ppermute | solution.py:25
  42.8 1.5 %collective-permute-start.11 = (bf16[16,256]{1,0:T(8,128)(2,1)S(1)}, bf16[16,256]{1,0:T(8,128)(2,1)S(1)}, u32[]{:S(2)}, u32[]{:S(2)}) collective-permute-start(bf16[16,256]{1,0:T(8,128)(2,1)S(1)} %convert_element_type.84), channel_id=1, source_target_pairs={{0,16},{1,17},{2,18},{3,19},{4,20},{5,21},{6,22},{7,23},{8,24},{9,... | collective-permute-start | bytes 24584 | tf_op jit(solution)/shard_map/ppermute | solution.py:25
  44.3 0.0 copy-done
  44.3 0.0 copy-done.3
  44.3 0.4 convolution_bitcast_fusion.1
  44.7 0.0 copy-done.6
  44.7 0.0 slice-start
  44.7 0.0 copy-start.1
  44.7 1.7 %collective-permute-done.11 = bf16[16,256]{1,0:T(8,128)(2,1)S(1)} collective-permute-done((bf16[16,256]{1,0:T(8,128)(2,1)S(1)}, bf16[16,256]{1,0:T(8,128)(2,1)S(1)}, u32[]{:S(2)}, u32[]{:S(2)}) %collective-permute-start.11) | collective-permute-done | bytes 8224 | tf_op jit(solution)/shard_map/ppermute | solution.py:25
  46.5 0.2 convolution_convert_fusion.2
  46.7 1.2 %convolution_convert_fusion.6 = bf16[16,128]{1,0:T(8,128)(2,1)S(1)} fusion(bf16[128,1536]{1,0:T(8,128)(2,1)} %collective-permute-done.10, bf16[16,1024]{1,0:T(8,128)(2,1)S(1)} %convolution_convert_fusion.2, bf16[16,512]{1,0:T(8,128)(2,1)S(1)} %slice.39), kind=kOutput, calls=%fused_computation.11 | convolution fusion | flops 6391808 | bytes 446464 | tf_op jit(solution)/shard_map/dot_general | solution.py:10
  47.9 0.0 copy-start.2
  47.9 1.3 %broadcast_select_fusion = (bf16[16,128]{1,0:T(8,128)(2,1)S(1)}, bf16[16,128]{1,0:T(8,128)(2,1)S(1)}) fusion(bf16[16,128]{1,0:T(8,128)(2,1)S(1)} %convolution_convert_fusion.6, pred[]{:T(512)S(6)} %ne.38, bf16[128,1536]{1,0:T(8,128)(2,1)} %param.21, bf16[16,1024]{1,0:T(8,128)(2,1)S(1)} %convolution_convert_fusion.2, bf16[16,512]{1,0:T(8,128)(2,1)S(1)} %slice.39), kind=kOutput, calls=%fused_computation.55 | convolution fusion | flops 6395904 | bytes 454657 | tf_op jit(solution)/shard_map/dot_general | solution.py:10
  49.2 1.6 %collective-permute-start.12 = (bf16[16,256]{1,0:T(8,128)(2,1)S(1)}, bf16[16,256]{1,0:T(8,128)(2,1)S(1)}, u32[]{:S(2)}, u32[]{:S(2)}) collective-permute-start(bf16[16,256]{1,0:T(8,128)(2,1)S(1)} %pad_maximum_fusion.7), channel_id=1, source_target_pairs={{0,1},{1,0},{2,3},{3,2},{4,5},{5,4},{6,7},{7,6},{8,9},{9,8},{10,11... | collective-permute-start | bytes 24584 | tf_op jit(solution)/shard_map/ppermute | solution.py:25
  50.7 2.1 %collective-permute-done.12 = bf16[16,256]{1,0:T(8,128)(2,1)S(1)} collective-permute-done((bf16[16,256]{1,0:T(8,128)(2,1)S(1)}, bf16[16,256]{1,0:T(8,128)(2,1)S(1)}, u32[]{:S(2)}, u32[]{:S(2)}) %collective-permute-start.12) | collective-permute-done | bytes 8224 | tf_op jit(solution)/shard_map/ppermute | solution.py:25
  52.9 1.2 %convolution_convert_fusion.4 = bf16[16,256]{1,0:T(8,128)(2,1)S(1)} fusion(bf16[16,768]{1,0:T(8,128)(2,1)S(1)} %constant_dynamic-update-slice_fusion.2, bf16[256,768]{1,0:T(8,128)(2,1)} %param.19), kind=kOutput, calls=%fused_computation.9 | convolution fusion | flops 6295552 | bytes 425984 | tf_op jit(solution)/shard_map/dot_general | solution.py:10
  54.1 0.0 slice-done
  54.1 0.0 copy-done.1
  54.2 0.4 convolution_convert_fusion.1
  54.6 0.1 reshape.21
  54.7 0.0 copy-done.2
  54.8 0.2 fusion
  54.9 0.9 %copy.23 = f32[16,16,256]{2,1,0:T(8,128)} copy(f32[16,16,256]{2,0,1:T(8,128)S(1)} %fusion) | data formatting | bytes 524288 | tf_op jit(solution)/shard_map/add | solution.py:174
  (23 shorter events, 0.3 us)
Async XLA Ops:
  0.0 44.3 %copy-start = (bf16[4096,256]{1,0:T(8,128)(2,1)S(1)}, bf16[4096,256]{1,0:T(8,128)(2,1)}, u32[]{:S(2)}) copy-start(bf16[4096,256]{1,0:T(8,128)(2,1)} %param.14) | copy-start | bytes 6291460
  0.0 10.5 %copy-start.4 = (bf16[256,768]{1,0:T(8,128)(2,1)S(1)}, bf16[256,768]{1,0:T(8,128)(2,1)}, u32[]{:S(2)}) copy-start(bf16[256,768]{1,0:T(8,128)(2,1)} %param.18) | copy-start | bytes 1179652
  1.7 9.1 %collective-permute-start = (bf16[64,512]{1,0:T(8,128)(2,1)S(1)}, bf16[64,512]{1,0:T(8,128)(2,1)S(1)}, u32[]{:S(2)}, u32[]{:S(2)}) collective-permute-start(bf16[64,512]{1,0:T(8,128)(2,1)S(1)} %constant_dynamic-update-slice_fusion), channel_id=1, source_target_pairs={{0,4},{1,5},{2,6},{3,7},{4,0},{5,1},{6,2},{7,3},{8,12},{9,13},{10,... | collective-permute-start | bytes 196616 | tf_op jit(solution)/shard_map/ppermute | solution.py:25
  5.7 17.8 %collective-permute-start.4 = (bf16[128,1536]{1,0:T(8,128)(2,1)}, bf16[128,1536]{1,0:T(8,128)(2,1)S(1)}, u32[]{:S(2)}, u32[]{:S(2)}) collective-permute-start(bf16[128,1536]{1,0:T(8,128)(2,1)} %param.20), channel_id=1, source_target_pairs={{0,2},{1,3},{2,0},{3,1},{4,6},{5,7},{6,4},{7,5},{8,10},{9,11},{10,... | collective-permute-start | bytes 1179656 | tf_op jit(solution)/shard_map/ppermute | solution.py:25
  10.5 34.2 %copy-start.6 = (bf16[16,640]{1,0:T(8,128)(2,1)}, bf16[16,640]{1,0:T(8,128)(2,1)S(1)}, u32[]{:S(2)}) copy-start(bf16[16,640]{1,0:T(8,128)(2,1)S(1)} %convolution_convert_fusion.3) | copy-start | bytes 61444
  10.7 13.0 %copy-start.5 = (bf16[128,1536]{1,0:T(8,128)(2,1)S(1)}, bf16[128,1536]{1,0:T(8,128)(2,1)}, u32[]{:S(2)}) copy-start(bf16[128,1536]{1,0:T(8,128)(2,1)} %param.20) | copy-start | bytes 1179652
  10.8 3.9 %collective-permute-start.1 = (bf16[16,768]{1,0:T(8,128)(2,1)S(1)}, bf16[16,768]{1,0:T(8,128)(2,1)S(1)}, u32[]{:S(2)}, u32[]{:S(2)}) collective-permute-start(bf16[16,768]{1,0:T(8,128)(2,1)S(1)} %convert_element_type.72), channel_id=1, source_target_pairs={{0,1},{1,0},{2,3},{3,2},{4,5},{5,4},{6,7},{7,6},{8,9},{9,8},{10,11... | collective-permute-start | bytes 73736 | tf_op jit(solution)/shard_map/ppermute | solution.py:25
  12.4 7.3 %collective-permute-start.2 = (bf16[2,64,512]{2,1,0:T(8,128)(2,1)S(1)}, bf16[2,64,512]{2,1,0:T(8,128)(2,1)S(1)}, u32[]{:S(2)}, u32[]{:S(2)}) collective-permute-start(bf16[2,64,512]{2,1,0:T(8,128)(2,1)S(1)} %pad_maximum_fusion.3), channel_id=1, source_target_pairs={{0,2},{1,3},{2,0},{3,1},{4,6},{5,7},{6,4},{7,5},{8,10},{9,11},{10,... | collective-permute-start | bytes 393224 | tf_op jit(solution)/shard_map/ppermute | solution.py:25
  19.7 3.8 %collective-permute-start.3 = (bf16[16,768]{1,0:T(8,128)(2,1)S(1)}, bf16[16,768]{1,0:T(8,128)(2,1)S(1)}, u32[]{:S(2)}, u32[]{:S(2)}) collective-permute-start(bf16[16,768]{1,0:T(8,128)(2,1)S(1)} %convert_element_type.74), channel_id=1, source_target_pairs={{0,2},{1,3},{2,0},{3,1},{4,6},{5,7},{6,4},{7,5},{8,10},{9,11},{10,... | collective-permute-start | bytes 73736 | tf_op jit(solution)/shard_map/ppermute | solution.py:25
  21.3 7.0 %collective-permute-start.5 = (bf16[2,2,64,512]{3,2,1,0:T(8,128)(2,1)S(1)}, bf16[2,2,64,512]{3,2,1,0:T(8,128)(2,1)S(1)}, u32[]{:S(2)}, u32[]{:S(2)}) collective-permute-start(bf16[2,2,64,512]{3,2,1,0:T(8,128)(2,1)S(1)} %pad_maximum_fusion.2), channel_id=1, source_target_pairs={{0,1},{1,0},{2,3},{3,2},{4,5},{5,4},{6,7},{7,6},{8,9},{9,8},{10,11... | collective-permute-start | bytes 786440 | tf_op jit(solution)/shard_map/ppermute | solution.py:25
  29.1 6.3 %collective-permute-start.7 = (bf16[2,2,2,64,512]{4,3,2,1,0:T(8,128)(2,1)}, bf16[2,2,2,64,512]{4,3,2,1,0:T(8,128)(2,1)S(1)}, u32[]{:S(2)}, u32[]{:S(2)}) collective-permute-start(bf16[2,2,2,64,512]{4,3,2,1,0:T(8,128)(2,1)} %pad_maximum_fusion.1), channel_id=1, source_target_pairs={{0,8},{1,9},{2,10},{3,11},{4,12},{5,13},{6,14},{7,15},{8,0},{9,1},... | collective-permute-start | bytes 1572872 | tf_op jit(solution)/shard_map/ppermute | solution.py:25
  29.2 6.2 %collective-permute-start.6 = (bf16[16,1536]{1,0:T(8,128)(2,1)S(1)}, bf16[16,1536]{1,0:T(8,128)(2,1)S(1)}, u32[]{:S(2)}, u32[]{:S(2)}) collective-permute-start(bf16[16,1536]{1,0:T(8,128)(2,1)S(1)} %convert_element_type.77), channel_id=1, source_target_pairs={{0,4},{1,5},{2,6},{3,7},{4,0},{5,1},{6,2},{7,3},{8,12},{9,13},{10,... | collective-permute-start | bytes 147464 | tf_op jit(solution)/shard_map/ppermute | solution.py:25
  30.4 12.4 %collective-permute-start.10 = (bf16[128,1536]{1,0:T(8,128)(2,1)}, bf16[128,1536]{1,0:T(8,128)(2,1)}, u32[]{:S(2)}, u32[]{:S(2)}) collective-permute-start(bf16[128,1536]{1,0:T(8,128)(2,1)} %param.21), channel_id=1, source_target_pairs={{0,2},{1,3},{2,0},{3,1},{4,6},{5,7},{6,4},{7,5},{8,10},{9,11},{10,... | collective-permute-start | bytes 1179656 | tf_op jit(solution)/shard_map/ppermute | solution.py:25
  35.4 4.2 %collective-permute-start.8 = (bf16[16,1536]{1,0:T(8,128)(2,1)S(1)}, bf16[16,1536]{1,0:T(8,128)(2,1)S(1)}, u32[]{:S(2)}, u32[]{:S(2)}) collective-permute-start(bf16[16,1536]{1,0:T(8,128)(2,1)S(1)} %convert_element_type.79), channel_id=1, source_target_pairs={{0,1},{1,0},{2,3},{3,2},{4,5},{5,4},{6,7},{7,6},{8,9},{9,8},{10,11... | collective-permute-start | bytes 147464 | tf_op jit(solution)/shard_map/ppermute | solution.py:25
  39.6 1.3 %collective-permute-start.9 = (bf16[16,1536]{1,0:T(8,128)(2,1)S(1)}, bf16[16,1536]{1,0:T(8,128)(2,1)S(1)}, u32[]{:S(2)}, u32[]{:S(2)}) collective-permute-start(bf16[16,1536]{1,0:T(8,128)(2,1)S(1)} %fusion.7), channel_id=1, source_target_pairs={{0,8},{1,9},{2,10},{3,11},{4,12},{5,13},{6,14},{7,15},{8,0},{9,1},... | collective-permute-start | bytes 147464 | tf_op jit(solution)/shard_map/ppermute | solution.py:25
  39.7 4.6 %copy-start.3 = (bf16[16,16,256]{2,1,0:T(8,128)(2,1)S(1)}, bf16[16,16,256]{2,1,0:T(8,128)(2,1)}, u32[]{:S(2)}) copy-start(bf16[16,16,256]{2,1,0:T(8,128)(2,1)} %param.12) | copy-start | bytes 393220
  42.8 3.7 %collective-permute-start.11 = (bf16[16,256]{1,0:T(8,128)(2,1)S(1)}, bf16[16,256]{1,0:T(8,128)(2,1)S(1)}, u32[]{:S(2)}, u32[]{:S(2)}) collective-permute-start(bf16[16,256]{1,0:T(8,128)(2,1)S(1)} %convert_element_type.84), channel_id=1, source_target_pairs={{0,16},{1,17},{2,18},{3,19},{4,20},{5,21},{6,22},{7,23},{8,24},{9,... | collective-permute-start | bytes 24584 | tf_op jit(solution)/shard_map/ppermute | solution.py:25
  44.7 9.4 %slice-start = ((bf16[16,640]{1,0:T(8,128)(2,1)}), bf16[16,384]{1,0:T(8,128)(2,1)S(1)}, s32[]{:S(2)}) async-start(bf16[16,640]{1,0:T(8,128)(2,1)} %copy-done.6), calls=%async_computation | async-start | bytes 24576 | tf_op jit(solution)/shard_map/slice | solution.py:160
  44.7 9.4 %copy-start.1 = (bf16[1024,640]{1,0:T(8,128)(2,1)S(1)}, bf16[1024,640]{1,0:T(8,128)(2,1)}, u32[]{:S(2)}) copy-start(bf16[1024,640]{1,0:T(8,128)(2,1)} %param.17) | copy-start | bytes 3932164
  47.9 6.8 %copy-start.2 = (bf16[1024,256]{1,0:T(8,128)(2,1)S(1)}, bf16[1024,256]{1,0:T(8,128)(2,1)}, u32[]{:S(2)}) copy-start(bf16[1024,256]{1,0:T(8,128)(2,1)} %param.15) | copy-start | bytes 1572868
  49.2 3.7 %collective-permute-start.12 = (bf16[16,256]{1,0:T(8,128)(2,1)S(1)}, bf16[16,256]{1,0:T(8,128)(2,1)S(1)}, u32[]{:S(2)}, u32[]{:S(2)}) collective-permute-start(bf16[16,256]{1,0:T(8,128)(2,1)S(1)} %pad_maximum_fusion.7), channel_id=1, source_target_pairs={{0,1},{1,0},{2,3},{3,2},{4,5},{5,4},{6,7},{7,6},{8,9},{9,8},{10,11... | collective-permute-start | bytes 24584 | tf_op jit(solution)/shard_map/ppermute | solution.py:25
where the time goes:
time: 56.1 us; the launch traced here: 55.8 us
  waiting for transfers between devices  25.7 us (46%)
  starting transfers between devices  17.1 us (30%)
  matrix products  8.64 us (15%)
  local copies, waits for them, and re-layouts  2.87 us (5%)
  other arithmetic  1.27 us (2%)
    ppermute x13, waiting for transfers between devices, swap(): return lax.ppermute(value, AXES, [(i, i ^ mask) for i in range(count)])  25.7 us
    ppermute x13, starting transfers between devices, swap(): return lax.ppermute(value, AXES, [(i, i ^ mask) for i in range(count)])  17.1 us
    dot_general x6, matrix products, contract(): lax.dot_general(left, right, (((1,), (1,)), ((), ())), preferred_element_...  6.08 us
    dot_general x1, matrix products, per_device(): jnp.einsum('rlq,leq->rle', source, leaf_flux.reshape(leaves, edge_count,...  1.29 us
    another operation x8, other arithmetic, joined_pair(): jnp.stack([jnp.where(upper, other, joined), jnp.where(upper, joined, othe...  1.14 us
  transfers between devices with their start and end apart: 13, of which 10 were waited for; matrix products, arithmetic and copies ran while one was open for 8% of the time, Pallas kernels for 0%

commit v1 on v0

--- a/solution.py
+++ b/solution.py
@@ -58,16 +58,6 @@
     return lax.optimization_barrier(values)
 
 
-def quad_order(halves, width, place):
-    own, other = halves
-    upper = place & 1 != 0
-    blocks = []
-    for start in range(0, own.shape[1], width):
-        left, right = own[:, start : start + width], other[:, start : start + width]
-        blocks += [jnp.where(upper, right, left), jnp.where(upper, left, right)]
-    return jnp.concatenate(blocks, axis=1)
-
-
 def per_device(
     source,
     leaf_flux,
@@ -98,10 +88,6 @@
 
     far = pair // 2
 
-    roots = jnp.concatenate([up_root, down_root], axis=1)
-    roots_far = swap(roots, far)
-    up_two_near = swap(up_two, near)
-
     flux = jnp.einsum(
         "rlq,leq->rle",
         source,
@@ -112,48 +98,43 @@
     box_state = rounded(contract(flux, box_up))
     first_sum = product(box_state[:, inner_dev:], up_one)
 
+    roots = jnp.concatenate([up_root, down_root], axis=1)
+    roots_far = swap(roots, far)
+    first_sum = partner_sum(first_sum, 1)
+
     first_sum, roots_far = tie(first_sum, roots_far)
     roots = joined_pair(roots, roots_far, place & far != 0, 0)
-    roots_near = swap(roots, near)
-    first_sum = partner_sum(first_sum, 1)
-
-    first_sum, roots_near = tie(first_sum, roots_near)
-    roots = joined_pair(roots, roots_near, place & near != 0, 1)
     roots_one = swap(roots, 1)
     first_sum = partner_sum(first_sum, near)
     first_state = rounded(first_sum)
 
-    def piece(mask):
-        start = k_zero + (place ^ mask) % quad * width
-        return lax.dynamic_slice_in_dim(first_state, start, width, 1)
+    piece = lax.dynamic_slice_in_dim(first_state, k_zero + place % quad * width, width, 1)
+    second_sum = product(piece, up_two)
+    second_sum, roots_one = tie(second_sum, roots_one)
+    roots = joined_pair(roots, roots_one, place & 1 != 0, 1)
+    roots_near = swap(roots, near)
+    second_sum = partner_sum(second_sum, far | pair)
 
-    second_sum = product(piece(0), up_two) + product(piece(near), up_two_near)
-    second_sum, roots_one = tie(second_sum, roots_one)
-    roots = joined_pair(roots, roots_one, place & 1 != 0, 2)
+    second_sum = partner_sum(second_sum, 1 | pair)
+    second_sum, roots_near = tie(second_sum, roots_near)
+    roots = joined_pair(roots, roots_near, place & near != 0, 1)
     roots_pair = swap(roots, pair)
-    down_two_near = swap(down_two, near)
-    second_sum = partner_sum(second_sum, far)
-
-    second_sum, roots_pair = tie(second_sum, roots_pair)
+    second_sum = partner_sum(second_sum, near | pair)
+    second_sum = partner_sum(second_sum, pair)
+    second_state = rounded(second_sum)
     roots = joined_pair(roots, roots_pair, place & pair != 0, 0)
     roots = roots.reshape(-1, roots.shape[-1])
-    second_sum = partner_sum(second_sum, 1)
-    second_sum = partner_sum(second_sum, pair)
-    second_state = rounded(second_sum)
 
     root_sum = product(second_state[:, k_one:], roots[:, :root_points])
-    root_sum, down_two_near = tie(root_sum, down_two_near)
     for bit in bits_of(family, count):
-        root_sum = partner_sum(root_sum, bit)
+        root_sum = partner_sum(root_sum, bit | pair)
     root_state = rounded(root_sum)
 
     top_bound = rounded(contract(root_state, roots[:, root_points:]))
     second_input = jnp.concatenate([second_state[:, :k_one], top_bound], axis=1)
-    own_mid = rounded(contract(second_input, down_two))
-    near_mid = rounded(contract(second_input, down_two_near))
-    mid_bound = placed([own_mid, near_mid], place // near, 1)
-    other_mid = swap(mid_bound, 1)
-    mid_bound = quad_order((mid_bound, other_mid), width, place)
+    mid_bound = rounded(contract(second_input, down_two))
+    mid_bound = placed([mid_bound, swap(mid_bound, 1)], place, 1)
+    mid_bound = placed([mid_bound, swap(mid_bound, near)], place // near, 1)
     first_input = jnp.concatenate([first_state[:, :k_zero], mid_bound], axis=1)
 
     box_bound = rounded(contract(first_input, down_one))

time: 56.1 us -> 54.1 us (0.964)
  waiting for transfers between devices: 25.7 us -> 31.6 us
  starting transfers between devices: 17.1 us -> 11.4 us
  local copies, waits for them, and re-layouts: 2.87 us -> 1.2 us
    ppermute x13, waiting for transfers between devices: 25.7 us -> 31.6 us  [swap(): return lax.ppermute(value, AXES, [(i, i ^ mask) for i in range(count)])]
    ppermute x13, starting transfers between devices: 17.1 us -> 11.4 us  [swap(): return lax.ppermute(value, AXES, [(i, i ^ mask) for i in range(count)])]
    dot_general x6 -> x5, matrix products: 6.08 us -> 3.93 us  [contract(): lax.dot_general(left, right, (((1,), (1,)), ((), ())), preferred_element_...]
    dot_general x1, matrix products: 0.19 us -> 1.29 us  [per_device(): jnp.einsum('rle,leq->rlq', leaf_bound, leaf_lift.reshape(leaves, edge_cou...]
    unnamed x16 -> x17, local copies, waits for them, and re-layouts: 0.96 us -> 0.04 us
    concatenate x1, local copies, waits for them, and re-layouts: 0.76 us -> 0.01 us  [per_device(): roots = jnp.concatenate([up_root, down_root], axis=1)]
    dot_general x1, matrix products: 0.38 us -> 1.09 us  [per_device(): jnp.einsum('rlq,lqp->rlp', source, leaf_particular.reshape(leaves, points...]
  transfers between devices with their start and end apart: 13 -> 13, of which waited for: 10 -> 11; matrix products, arithmetic and copies ran while one was open for 8% -> 4% of each run, Pallas kernels for 0% -> 0%
where the time goes in v1:
time: 54.1 us; the launch traced here: 54 us
  waiting for transfers between devices  31.6 us (58%)
  starting transfers between devices  11.4 us (21%)
  matrix products  8.29 us (15%)
  other arithmetic  1.27 us (2%)
  local copies, waits for them, and re-layouts  1.2 us (2%)
    ppermute x13, waiting for transfers between devices, swap(): return lax.ppermute(value, AXES, [(i, i ^ mask) for i in range(count)])  31.6 us
    ppermute x13, starting transfers between devices, swap(): return lax.ppermute(value, AXES, [(i, i ^ mask) for i in range(count)])  11.4 us
    dot_general x5, matrix products, contract(): lax.dot_general(left, right, (((1,), (1,)), ((), ())), preferred_element_...  3.93 us
    dot_general x1, matrix products, per_device(): jnp.einsum('rlq,leq->rle', source, leaf_flux.reshape(leaves, edge_count,...  1.44 us
    dot_general x1, matrix products, per_device(): jnp.einsum('rle,leq->rlq', leaf_bound, leaf_lift.reshape(leaves, edge_cou...  1.29 us
    another operation x8, other arithmetic, joined_pair(): jnp.stack([jnp.where(upper, other, joined), jnp.where(upper, joined, othe...  1.16 us
    dot_general x1, matrix products, per_device(): jnp.einsum('rlq,lqp->rlp', source, leaf_particular.reshape(leaves, points...  1.09 us
  transfers between devices with their start and end apart: 13, of which 11 were waited for; matrix products, arithmetic and copies ran while one was open for 4% of the time, Pallas kernels for 0%

profile of v1, /device:TPU:0, one launch (start us, length us, event | category | flops | bytes accessed | tf_op | source)
XLA Modules:
  0.0 54.0 jit_solution(11998995551076727167)
XLA Ops:
  0.0 0.0 copy-start
  0.0 0.0 copy-start.5
  0.0 0.0 copy-start.6
  0.0 0.0 copy-start.7
  0.0 1.4 %fusion.1 = bf16[16,16,64]{2,0,1:T(8,128)(2,1)S(1)} fusion(bf16[16,64,256]{2,1,0:T(8,128)(2,1)} %bitcast.45, bf16[16,16,256]{2,1,0:T(8,128)(2,1)} %param.12), kind=kOutput, calls=%fused_computation.4 | convolution fusion | flops 8404992 | bytes 688128 | tf_op jit(solution)/shard_map/rlq,leq->rle/dot_general | solution.py:91
  1.5 0.1 reshape.19
  1.6 0.0 copy-start.3
  1.6 1.8 %convolution_convert_fusion.3 = bf16[16,640]{1,0:T(8,128)(2,1)S(1)} fusion(bf16[16,1024]{1,0:T(8,128)(2,1)S(1)} %reshape.19, bf16[640,1024]{1,0:T(8,128)(2,1)} %param.16), kind=kOutput, calls=%fused_computation.7 | convolution fusion | flops 20981760 | bytes 1363968 | tf_op jit(solution)/shard_map/dot_general | solution.py:10
  3.4 0.0 copy-done.5
  3.4 0.2 fusion.30
  3.6 3.0 %collective-permute-start = (bf16[16,768]{1,0:T(8,128)(2,1)S(1)}, bf16[16,768]{1,0:T(8,128)(2,1)S(1)}, u32[]{:S(2)}, u32[]{:S(2)}) collective-permute-start(bf16[16,768]{1,0:T(8,128)(2,1)S(1)} %get-tuple-element.29), channel_id=1, source_target_pairs={{0,1},{1,0},{2,3},{3,2},{4,5},{5,4},{6,7},{7,6},{8,9},{9,8},{10,11... | collective-permute-start | bytes 73736 | tf_op jit(solution)/shard_map/ppermute | solution.py:25
  6.6 0.0 copy-done.6
  6.7 0.0 copy-done.7
  6.7 2.7 %collective-permute-start.1 = (bf16[64,512]{1,0:T(8,128)(2,1)S(1)}, bf16[64,512]{1,0:T(8,128)(2,1)S(1)}, u32[]{:S(2)}, u32[]{:S(2)}) collective-permute-start(bf16[64,512]{1,0:T(8,128)(2,1)S(1)} %constant_dynamic-update-slice_fusion), channel_id=1, source_target_pairs={{0,4},{1,5},{2,6},{3,7},{4,0},{5,1},{6,2},{7,3},{8,12},{9,13},{10,... | collective-permute-start | bytes 196616 | tf_op jit(solution)/shard_map/ppermute | solution.py:25
  9.3 0.0 collective-permute-done
  9.3 2.9 %collective-permute-done.1 = bf16[64,512]{1,0:T(8,128)(2,1)S(1)} collective-permute-done((bf16[64,512]{1,0:T(8,128)(2,1)S(1)}, bf16[64,512]{1,0:T(8,128)(2,1)S(1)}, u32[]{:S(2)}, u32[]{:S(2)}) %collective-permute-start.1) | collective-permute-done | bytes 65568 | tf_op jit(solution)/shard_map/ppermute | solution.py:25
  12.2 1.3 %collective-permute-start.2 = (bf16[16,768]{1,0:T(8,128)(2,1)S(1)}, bf16[16,768]{1,0:T(8,128)(2,1)S(1)}, u32[]{:S(2)}, u32[]{:S(2)}) collective-permute-start(bf16[16,768]{1,0:T(8,128)(2,1)S(1)} %convert_element_type.77), channel_id=1, source_target_pairs={{0,2},{1,3},{2,0},{3,1},{4,6},{5,7},{6,4},{7,5},{8,10},{9,11},{10,... | collective-permute-start | bytes 73736 | tf_op jit(solution)/shard_map/ppermute | solution.py:25
  13.5 0.6 %collective-permute-start.3 = (bf16[2,64,512]{2,1,0:T(8,128)(2,1)S(1)}, bf16[2,64,512]{2,1,0:T(8,128)(2,1)S(1)}, u32[]{:S(2)}, u32[]{:S(2)}) collective-permute-start(bf16[2,64,512]{2,1,0:T(8,128)(2,1)S(1)} %pad_maximum_fusion.3), channel_id=1, source_target_pairs={{0,1},{1,0},{2,3},{3,2},{4,5},{5,4},{6,7},{7,6},{8,9},{9,8},{10,11... | collective-permute-start | bytes 393224 | tf_op jit(solution)/shard_map/ppermute | solution.py:25
  14.1 1.9 %collective-permute-done.2 = bf16[16,768]{1,0:T(8,128)(2,1)S(1)} collective-permute-done((bf16[16,768]{1,0:T(8,128)(2,1)S(1)}, bf16[16,768]{1,0:T(8,128)(2,1)S(1)}, u32[]{:S(2)}, u32[]{:S(2)}) %collective-permute-start.2) | collective-permute-done | bytes 24608 | tf_op jit(solution)/shard_map/ppermute | solution.py:25
  16.0 0.0 copy-done.3
  16.1 0.2 fusion.24
  16.2 2.3 %collective-permute-done.3 = bf16[2,64,512]{2,1,0:T(8,128)(2,1)S(1)} collective-permute-done((bf16[2,64,512]{2,1,0:T(8,128)(2,1)S(1)}, bf16[2,64,512]{2,1,0:T(8,128)(2,1)S(1)}, u32[]{:S(2)}, u32[]{:S(2)}) %collective-permute-start.3) | collective-permute-done | bytes 131104 | tf_op jit(solution)/shard_map/ppermute | solution.py:25
  18.6 0.1 collective-permute-start.4
  18.7 5.7 %collective-permute-done.4 = bf16[16,1536]{1,0:T(8,128)(2,1)S(1)} collective-permute-done((bf16[16,1536]{1,0:T(8,128)(2,1)S(1)}, bf16[16,1536]{1,0:T(8,128)(2,1)S(1)}, u32[]{:S(2)}, u32[]{:S(2)}) %collective-permute-start.4) | collective-permute-done | bytes 49184 | tf_op jit(solution)/shard_map/ppermute | solution.py:25
  24.4 0.3 collective-permute-start.5
  24.7 0.1 collective-permute-start.6
  24.8 3.4 %collective-permute-done.5 = bf16[16,1536]{1,0:T(8,128)(2,1)S(1)} collective-permute-done((bf16[16,1536]{1,0:T(8,128)(2,1)S(1)}, bf16[16,1536]{1,0:T(8,128)(2,1)S(1)}, u32[]{:S(2)}, u32[]{:S(2)}) %collective-permute-start.5) | collective-permute-done | bytes 49184 | tf_op jit(solution)/shard_map/ppermute | solution.py:25
  28.2 5.2 %collective-permute-done.6 = bf16[2,2,64,512]{3,2,1,0:T(8,128)(2,1)S(1)} collective-permute-done((bf16[2,2,64,512]{3,2,1,0:T(8,128)(2,1)S(1)}, bf16[2,2,64,512]{3,2,1,0:T(8,128)(2,1)S(1)}, u32[]{:S(2)}, u32[]{:S(2)}) %collective-permute-start.6) | collective-permute-done | bytes 262176 | tf_op jit(solution)/shard_map/ppermute | solution.py:25
  33.4 0.1 collective-permute-start.7
  33.5 0.9 %pad_maximum_fusion.1 = bf16[2,2,2,64,512]{4,3,2,1,0:T(8,128)(2,1)} fusion(bf16[2,1,2,64,512]{4,3,2,1,0:T(8,128)(2,1)S(1)} %get-tuple-element.20, bf16[2,1,2,64,512]{4,3,2,1,0:T(8,128)(2,1)S(1)} %get-tuple-element.19), kind=kLoop, calls=%fused_computation.14 | loop fusion | flops 262144 | bytes 1048576 | tf_op jit(solution)/shard_map/stack | solution.py:52
  34.4 0.3 collective-permute-start.9
  34.7 2.6 %collective-permute-done.7 = bf16[16,1536]{1,0:T(8,128)(2,1)S(1)} collective-permute-done((bf16[16,1536]{1,0:T(8,128)(2,1)S(1)}, bf16[16,1536]{1,0:T(8,128)(2,1)S(1)}, u32[]{:S(2)}, u32[]{:S(2)}) %collective-permute-start.7) | collective-permute-done | bytes 49184 | tf_op jit(solution)/shard_map/ppermute | solution.py:25
  37.3 0.1 collective-permute-start.8
  37.4 1.2 %collective-permute-done.8 = bf16[16,1536]{1,0:T(8,128)(2,1)S(1)} collective-permute-done((bf16[16,1536]{1,0:T(8,128)(2,1)S(1)}, bf16[16,1536]{1,0:T(8,128)(2,1)S(1)}, u32[]{:S(2)}, u32[]{:S(2)}) %collective-permute-start.8) | collective-permute-done | bytes 49184 | tf_op jit(solution)/shard_map/ppermute | solution.py:25
  38.7 0.0 collective-permute-done.9
  38.7 0.1 select_bitcast_fusion.1
  38.8 0.0 copy-start.4
  38.8 0.1 pad_maximum_fusion
  38.9 0.0 copy-start.2
  38.9 0.2 fusion.31
  39.1 1.3 %collective-permute-start.10 = (bf16[16,256]{1,0:T(8,128)(2,1)S(1)}, bf16[16,256]{1,0:T(8,128)(2,1)S(1)}, u32[]{:S(2)}, u32[]{:S(2)}) collective-permute-start(bf16[16,256]{1,0:T(8,128)(2,1)S(1)} %get-tuple-element.31), channel_id=1, source_target_pairs={{0,24},{1,25},{2,26},{3,27},{4,28},{5,29},{6,30},{7,31},{8,16},{9,... | collective-permute-start | bytes 24584 | tf_op jit(solution)/shard_map/ppermute | solution.py:25
  40.3 1.8 %collective-permute-done.10 = bf16[16,256]{1,0:T(8,128)(2,1)S(1)} collective-permute-done((bf16[16,256]{1,0:T(8,128)(2,1)S(1)}, bf16[16,256]{1,0:T(8,128)(2,1)S(1)}, u32[]{:S(2)}, u32[]{:S(2)}) %collective-permute-start.10) | collective-permute-done | bytes 8224 | tf_op jit(solution)/shard_map/ppermute | solution.py:25
  42.1 0.2 convolution_convert_fusion.2
  42.4 0.0 copy-done.4
  42.4 0.2 convolution_convert_fusion.5
  42.6 1.6 %collective-permute-start.11 = (bf16[16,128]{1,0:T(8,128)(2,1)S(1)}, bf16[16,128]{1,0:T(8,128)(2,1)S(1)}, u32[]{:S(2)}, u32[]{:S(2)}) collective-permute-start(bf16[16,128]{1,0:T(8,128)(2,1)S(1)} %convolution_convert_fusion.5), channel_id=1, source_target_pairs={{0,1},{1,0},{2,3},{3,2},{4,5},{5,4},{6,7},{7,6},{8,9},{9,8},{10,11... | collective-permute-start | bytes 12296 | tf_op jit(solution)/shard_map/ppermute | solution.py:25
  44.1 2.1 %collective-permute-done.11 = bf16[16,128]{1,0:T(8,128)(2,1)S(1)} collective-permute-done((bf16[16,128]{1,0:T(8,128)(2,1)S(1)}, bf16[16,128]{1,0:T(8,128)(2,1)S(1)}, u32[]{:S(2)}, u32[]{:S(2)}) %collective-permute-start.11) | collective-permute-done | bytes 4128 | tf_op jit(solution)/shard_map/ppermute | solution.py:25
  46.2 0.2 collective-permute-start.12
  46.4 0.0 copy-done
  46.4 0.0 copy-done.2
  46.4 0.0 copy-start.1
  46.4 1.1 %convolution_bitcast_fusion.1 = f32[16,16,256]{2,0,1:T(8,128)} fusion(bf16[16,256,256]{2,1,0:T(8,128)(2,1)S(1)} %bitcast.42, bf16[16,16,256]{2,1,0:T(8,128)(2,1)S(1)} %copy-done.2), kind=kOutput, calls=%fused_computation.2 | convolution fusion | flops 33554432 | bytes 2490368 | tf_op jit(solution)/shard_map/rlq,lqp->rlp/dot_general | solution.py:149
  47.5 2.4 %collective-permute-done.12 = bf16[16,256]{1,0:T(8,128)(2,1)S(1)} collective-permute-done((bf16[16,256]{1,0:T(8,128)(2,1)S(1)}, bf16[16,256]{1,0:T(8,128)(2,1)S(1)}, u32[]{:S(2)}, u32[]{:S(2)}) %collective-permute-start.12) | collective-permute-done | bytes 8224 | tf_op jit(solution)/shard_map/ppermute | solution.py:25
  50.0 1.2 %convolution_convert_fusion.4 = bf16[16,256]{1,0:T(8,128)(2,1)S(1)} fusion(bf16[256,768]{1,0:T(8,128)(2,1)} %param.19, bf16[16,256]{1,0:T(8,128)(2,1)S(1)} %get-tuple-element.26, bf16[16,256]{1,0:T(8,128)(2,1)S(1)} %get-tuple-element.25, bf16[16,256]{1,0:T(8,128)(2,1)S(1)} %slice.30), kind=kOutput, calls=%fused_computation.8 | convolution fusion | flops 6369280 | bytes 425984 | tf_op jit(solution)/shard_map/dot_general | solution.py:10
  51.1 0.0 copy-done.1
  51.1 0.5 convolution_convert_fusion.1
  51.7 0.1 reshape.21
  51.8 1.3 %fusion = f32[16,16,256]{2,0,1:T(8,128)S(1)} fusion(f32[16,16,256]{2,0,1:T(8,128)} %convolution_bitcast_fusion.1, bf16[16,64,256]{2,1,0:T(8,128)(2,1)} %bitcast.46, bf16[16,16,64]{2,1,0:T(8,128)(2,1)S(1)} %reshape.21), kind=kOutput, calls=%fused_computation.1 | convolution fusion | flops 8454144 | bytes 1081344 | tf_op jit(solution)/shard_map/rle,leq->rlq/dot_general | solution.py:143
  53.1 0.9 %copy.23 = f32[16,16,256]{2,1,0:T(8,128)} copy(f32[16,16,256]{2,0,1:T(8,128)S(1)} %fusion) | data formatting | bytes 524288 | tf_op jit(solution)/shard_map/add | solution.py:155
  (23 shorter events, 0.3 us)
Async XLA Ops:
  0.0 46.4 %copy-start = (bf16[4096,256]{1,0:T(8,128)(2,1)S(1)}, bf16[4096,256]{1,0:T(8,128)(2,1)}, u32[]{:S(2)}) copy-start(bf16[4096,256]{1,0:T(8,128)(2,1)} %param.14) | copy-start | bytes 6291460
  0.0 3.4 %copy-start.5 = (bf16[256,768]{1,0:T(8,128)(2,1)S(1)}, bf16[256,768]{1,0:T(8,128)(2,1)}, u32[]{:S(2)}) copy-start(bf16[256,768]{1,0:T(8,128)(2,1)} %param.18) | copy-start | bytes 1179652
  0.0 6.6 %copy-start.6 = (bf16[64,256]{1,0:T(8,128)(2,1)S(1)}, bf16[64,256]{1,0:T(8,128)(2,1)}, u32[]{:S(2)}) copy-start(bf16[64,256]{1,0:T(8,128)(2,1)} %param.22) | copy-start | bytes 98308
  0.0 6.6 %copy-start.7 = (bf16[64,256]{1,0:T(8,128)(2,1)S(1)}, bf16[64,256]{1,0:T(8,128)(2,1)}, u32[]{:S(2)}) copy-start(bf16[64,256]{1,0:T(8,128)(2,1)} %param.23) | copy-start | bytes 98308
  1.6 14.4 %copy-start.3 = (bf16[128,1536]{1,0:T(8,128)(2,1)S(1)}, bf16[128,1536]{1,0:T(8,128)(2,1)}, u32[]{:S(2)}) copy-start(bf16[128,1536]{1,0:T(8,128)(2,1)} %param.20) | copy-start | bytes 1179652
  3.6 5.7 %collective-permute-start = (bf16[16,768]{1,0:T(8,128)(2,1)S(1)}, bf16[16,768]{1,0:T(8,128)(2,1)S(1)}, u32[]{:S(2)}, u32[]{:S(2)}) collective-permute-start(bf16[16,768]{1,0:T(8,128)(2,1)S(1)} %get-tuple-element.29), channel_id=1, source_target_pairs={{0,1},{1,0},{2,3},{3,2},{4,5},{5,4},{6,7},{7,6},{8,9},{9,8},{10,11... | collective-permute-start | bytes 73736 | tf_op jit(solution)/shard_map/ppermute | solution.py:25
  6.7 5.5 %collective-permute-start.1 = (bf16[64,512]{1,0:T(8,128)(2,1)S(1)}, bf16[64,512]{1,0:T(8,128)(2,1)S(1)}, u32[]{:S(2)}, u32[]{:S(2)}) collective-permute-start(bf16[64,512]{1,0:T(8,128)(2,1)S(1)} %constant_dynamic-update-slice_fusion), channel_id=1, source_target_pairs={{0,4},{1,5},{2,6},{3,7},{4,0},{5,1},{6,2},{7,3},{8,12},{9,13},{10,... | collective-permute-start | bytes 196616 | tf_op jit(solution)/shard_map/ppermute | solution.py:25
  12.2 3.8 %collective-permute-start.2 = (bf16[16,768]{1,0:T(8,128)(2,1)S(1)}, bf16[16,768]{1,0:T(8,128)(2,1)S(1)}, u32[]{:S(2)}, u32[]{:S(2)}) collective-permute-start(bf16[16,768]{1,0:T(8,128)(2,1)S(1)} %convert_element_type.77), channel_id=1, source_target_pairs={{0,2},{1,3},{2,0},{3,1},{4,6},{5,7},{6,4},{7,5},{8,10},{9,11},{10,... | collective-permute-start | bytes 73736 | tf_op jit(solution)/shard_map/ppermute | solution.py:25
  13.5 5.0 %collective-permute-start.3 = (bf16[2,64,512]{2,1,0:T(8,128)(2,1)S(1)}, bf16[2,64,512]{2,1,0:T(8,128)(2,1)S(1)}, u32[]{:S(2)}, u32[]{:S(2)}) collective-permute-start(bf16[2,64,512]{2,1,0:T(8,128)(2,1)S(1)} %pad_maximum_fusion.3), channel_id=1, source_target_pairs={{0,1},{1,0},{2,3},{3,2},{4,5},{5,4},{6,7},{7,6},{8,9},{9,8},{10,11... | collective-permute-start | bytes 393224 | tf_op jit(solution)/shard_map/ppermute | solution.py:25
  18.6 5.8 %collective-permute-start.4 = (bf16[16,1536]{1,0:T(8,128)(2,1)S(1)}, bf16[16,1536]{1,0:T(8,128)(2,1)S(1)}, u32[]{:S(2)}, u32[]{:S(2)}) collective-permute-start(bf16[16,1536]{1,0:T(8,128)(2,1)S(1)} %convert_element_type.80), channel_id=1, source_target_pairs={{0,12},{1,13},{2,14},{3,15},{4,8},{5,9},{6,10},{7,11},{8,4},{9,5},... | collective-permute-start | bytes 147464 | tf_op jit(solution)/shard_map/ppermute | solution.py:25
  24.4 3.8 %collective-permute-start.5 = (bf16[16,1536]{1,0:T(8,128)(2,1)S(1)}, bf16[16,1536]{1,0:T(8,128)(2,1)S(1)}, u32[]{:S(2)}, u32[]{:S(2)}) collective-permute-start(bf16[16,1536]{1,0:T(8,128)(2,1)S(1)} %fusion.7), channel_id=1, source_target_pairs={{0,9},{1,8},{2,11},{3,10},{4,13},{5,12},{6,15},{7,14},{8,1},{9,0},... | collective-permute-start | bytes 147464 | tf_op jit(solution)/shard_map/ppermute | solution.py:25
  24.7 8.7 %collective-permute-start.6 = (bf16[2,2,64,512]{3,2,1,0:T(8,128)(2,1)S(1)}, bf16[2,2,64,512]{3,2,1,0:T(8,128)(2,1)S(1)}, u32[]{:S(2)}, u32[]{:S(2)}) collective-permute-start(bf16[2,2,64,512]{3,2,1,0:T(8,128)(2,1)S(1)} %pad_maximum_fusion.2), channel_id=1, source_target_pairs={{0,2},{1,3},{2,0},{3,1},{4,6},{5,7},{6,4},{7,5},{8,10},{9,11},{10,... | collective-permute-start | bytes 786440 | tf_op jit(solution)/shard_map/ppermute | solution.py:25
  33.4 3.9 %collective-permute-start.7 = (bf16[16,1536]{1,0:T(8,128)(2,1)S(1)}, bf16[16,1536]{1,0:T(8,128)(2,1)S(1)}, u32[]{:S(2)}, u32[]{:S(2)}) collective-permute-start(bf16[16,1536]{1,0:T(8,128)(2,1)S(1)} %convert_element_type.84), channel_id=1, source_target_pairs={{0,10},{1,11},{2,8},{3,9},{4,14},{5,15},{6,12},{7,13},{8,2},{9,3},... | collective-permute-start | bytes 147464 | tf_op jit(solution)/shard_map/ppermute | solution.py:25
  34.4 4.3 %collective-permute-start.9 = (bf16[2,2,2,64,512]{4,3,2,1,0:T(8,128)(2,1)}, bf16[2,2,2,64,512]{4,3,2,1,0:T(8,128)(2,1)S(1)}, u32[]{:S(2)}, u32[]{:S(2)}) collective-permute-start(bf16[2,2,2,64,512]{4,3,2,1,0:T(8,128)(2,1)} %pad_maximum_fusion.1), channel_id=1, source_target_pairs={{0,8},{1,9},{2,10},{3,11},{4,12},{5,13},{6,14},{7,15},{8,0},{9,1},... | collective-permute-start | bytes 1572872 | tf_op jit(solution)/shard_map/ppermute | solution.py:25
  37.3 1.3 %collective-permute-start.8 = (bf16[16,1536]{1,0:T(8,128)(2,1)S(1)}, bf16[16,1536]{1,0:T(8,128)(2,1)S(1)}, u32[]{:S(2)}, u32[]{:S(2)}) collective-permute-start(bf16[16,1536]{1,0:T(8,128)(2,1)S(1)} %fusion.8), channel_id=1, source_target_pairs={{0,8},{1,9},{2,10},{3,11},{4,12},{5,13},{6,14},{7,15},{8,0},{9,1},... | collective-permute-start | bytes 147464 | tf_op jit(solution)/shard_map/ppermute | solution.py:25
  38.8 3.6 %copy-start.4 = (bf16[128,1536]{1,0:T(8,128)(2,1)S(1)}, bf16[128,1536]{1,0:T(8,128)(2,1)}, u32[]{:S(2)}) copy-start(bf16[128,1536]{1,0:T(8,128)(2,1)} %param.21) | copy-start | bytes 1179652
  38.9 7.5 %copy-start.2 = (bf16[16,16,256]{2,1,0:T(8,128)(2,1)S(1)}, bf16[16,16,256]{2,1,0:T(8,128)(2,1)}, u32[]{:S(2)}) copy-start(bf16[16,16,256]{2,1,0:T(8,128)(2,1)} %param.12) | copy-start | bytes 393220
  39.1 3.1 %collective-permute-start.10 = (bf16[16,256]{1,0:T(8,128)(2,1)S(1)}, bf16[16,256]{1,0:T(8,128)(2,1)S(1)}, u32[]{:S(2)}, u32[]{:S(2)}) collective-permute-start(bf16[16,256]{1,0:T(8,128)(2,1)S(1)} %get-tuple-element.31), channel_id=1, source_target_pairs={{0,24},{1,25},{2,26},{3,27},{4,28},{5,29},{6,30},{7,31},{8,16},{9,... | collective-permute-start | bytes 24584 | tf_op jit(solution)/shard_map/ppermute | solution.py:25
  42.6 3.6 %collective-permute-start.11 = (bf16[16,128]{1,0:T(8,128)(2,1)S(1)}, bf16[16,128]{1,0:T(8,128)(2,1)S(1)}, u32[]{:S(2)}, u32[]{:S(2)}) collective-permute-start(bf16[16,128]{1,0:T(8,128)(2,1)S(1)} %convolution_convert_fusion.5), channel_id=1, source_target_pairs={{0,1},{1,0},{2,3},{3,2},{4,5},{5,4},{6,7},{7,6},{8,9},{9,8},{10,11... | collective-permute-start | bytes 12296 | tf_op jit(solution)/shard_map/ppermute | solution.py:25
  46.2 3.7 %collective-permute-start.12 = (bf16[16,256]{1,0:T(8,128)(2,1)S(1)}, bf16[16,256]{1,0:T(8,128)(2,1)S(1)}, u32[]{:S(2)}, u32[]{:S(2)}) collective-permute-start(bf16[16,256]{1,0:T(8,128)(2,1)S(1)} %pad_maximum_fusion.4), channel_id=1, source_target_pairs={{0,2},{1,3},{2,0},{3,1},{4,6},{5,7},{6,4},{7,5},{8,10},{9,11},{10,... | collective-permute-start | bytes 24584 | tf_op jit(solution)/shard_map/ppermute | solution.py:25
  46.4 4.7 %copy-start.1 = (bf16[1024,640]{1,0:T(8,128)(2,1)S(1)}, bf16[1024,640]{1,0:T(8,128)(2,1)}, u32[]{:S(2)}) copy-start(bf16[1024,640]{1,0:T(8,128)(2,1)} %param.17) | copy-start | bytes 3932164

commit v2 on v1

--- a/solution.py
+++ b/solution.py
@@ -88,6 +88,17 @@
 
     far = pair // 2
 
+    roots = jnp.concatenate([up_root, down_root], axis=1)
+    roots = lax.all_to_all(
+        jnp.broadcast_to(roots, (pair,) + roots.shape),
+        AXES,
+        0,
+        0,
+        axis_index_groups=[list(range(i, i + pair)) for i in range(0, count, pair)],
+    )
+    roots = joined_pair(roots, swap(roots, pair), place & pair != 0, 0)
+    roots = roots.reshape(-1, roots.shape[-1])
+
     flux = jnp.einsum(
         "rlq,leq->rle",
         source,
@@ -98,32 +109,15 @@
     box_state = rounded(contract(flux, box_up))
     first_sum = product(box_state[:, inner_dev:], up_one)
 
-    roots = jnp.concatenate([up_root, down_root], axis=1)
-    roots_far = swap(roots, far)
-    first_sum = partner_sum(first_sum, 1)
-
-    first_sum, roots_far = tie(first_sum, roots_far)
-    roots = joined_pair(roots, roots_far, place & far != 0, 0)
-    roots_one = swap(roots, 1)
-    first_sum = partner_sum(first_sum, near)
+    for bit in bits_of(1, quad):
+        first_sum = partner_sum(first_sum, bit)
     first_state = rounded(first_sum)
 
     piece = lax.dynamic_slice_in_dim(first_state, k_zero + place % quad * width, width, 1)
     second_sum = product(piece, up_two)
-    second_sum, roots_one = tie(second_sum, roots_one)
-    roots = joined_pair(roots, roots_one, place & 1 != 0, 1)
-    roots_near = swap(roots, near)
-    second_sum = partner_sum(second_sum, far | pair)
-
-    second_sum = partner_sum(second_sum, 1 | pair)
-    second_sum, roots_near = tie(second_sum, roots_near)
-    roots = joined_pair(roots, roots_near, place & near != 0, 1)
-    roots_pair = swap(roots, pair)
-    second_sum = partner_sum(second_sum, near | pair)
-    second_sum = partner_sum(second_sum, pair)
+    for mask in (far | pair, 1 | pair, near | pair, pair):
+        second_sum = partner_sum(second_sum, mask)
     second_state = rounded(second_sum)
-    roots = joined_pair(roots, roots_pair, place & pair != 0, 0)
-    roots = roots.reshape(-1, roots.shape[-1])
 
     root_sum = product(second_state[:, k_one:], roots[:, :root_points])
     for bit in bits_of(family, count):

time: 54.1 us -> 54.7 us (1.011)
  waiting for transfers between devices: 31.6 us -> 21.9 us
  starting transfers between devices: 11.4 us -> 19.3 us
  local copies, waits for them, and re-layouts: 1.2 us -> 3.19 us
    ppermute x13 -> x10, waiting for transfers between devices: 31.6 us -> 14.9 us  [swap(): return lax.ppermute(value, AXES, [(i, i ^ mask) for i in range(count)])]
    all_to_all x0 -> x1, waiting for transfers between devices: none -> 7 us  [per_device(): lax.all_to_all(jnp.broadcast_to(roots, (pair,) + roots.shape), AXES, 0, 0...]
    all_to_all x0 -> x1, starting transfers between devices: none -> 6.12 us  [per_device(): lax.all_to_all(jnp.broadcast_to(roots, (pair,) + roots.shape), AXES, 0, 0...]
    ppermute x13 -> x10, starting transfers between devices: 11.4 us -> 13.2 us  [swap(): return lax.ppermute(value, AXES, [(i, i ^ mask) for i in range(count)])]
    another operation x8 -> x2, other arithmetic: 1.16 us -> 0.18 us  [joined_pair(): jnp.stack([jnp.where(upper, other, joined), jnp.where(upper, joined, othe...]
    broadcast_in_dim x0 -> x1, local copies, waits for them, and re-layouts: none -> 0.87 us  [per_device(): jnp.broadcast_to(roots, (pair,) + roots.shape)]
    select_n x2, other arithmetic: 0.01 us -> 0.72 us  [placed(): jnp.where(upper, high, low)]
    slice x1, local copies, waits for them, and re-layouts: 0.01 us -> 0.7 us  [per_device(): first_input = jnp.concatenate([first_state[:, :k_zero], mid_bound], axis=1)]
  transfers between devices with their start and end apart: 13 -> 11, of which waited for: 11 -> 8; matrix products, arithmetic and copies ran while one was open for 4% -> 5% of each run, Pallas kernels for 0% -> 0%
where the time goes in v2:
time: 54.7 us; the launch traced here: 54.4 us
  waiting for transfers between devices  21.9 us (40%)
  starting transfers between devices  19.3 us (35%)
  matrix products  8.18 us (15%)
  local copies, waits for them, and re-layouts  3.19 us (6%)
  other arithmetic  1.61 us (3%)
    ppermute x10, waiting for transfers between devices, swap(): return lax.ppermute(value, AXES, [(i, i ^ mask) for i in range(count)])  14.9 us
    ppermute x10, starting transfers between devices, swap(): return lax.ppermute(value, AXES, [(i, i ^ mask) for i in range(count)])  13.2 us
    all_to_all x1, waiting for transfers between devices, per_device(): lax.all_to_all(jnp.broadcast_to(roots, (pair,) + roots.shape), AXES, 0, 0...  7 us
    all_to_all x1, starting transfers between devices, per_device(): lax.all_to_all(jnp.broadcast_to(roots, (pair,) + roots.shape), AXES, 0, 0...  6.12 us
    dot_general x5, matrix products, contract(): lax.dot_general(left, right, (((1,), (1,)), ((), ())), preferred_element_...  3.82 us
    dot_general x1, matrix products, per_device(): jnp.einsum('rlq,leq->rle', source, leaf_flux.reshape(leaves, edge_count,...  1.44 us
    dot_general x1, matrix products, per_device(): jnp.einsum('rle,leq->rlq', leaf_bound, leaf_lift.reshape(leaves, edge_cou...  1.29 us
    dot_general x1, matrix products, per_device(): jnp.einsum('rlq,lqp->rlp', source, leaf_particular.reshape(leaves, points...  1.09 us
  transfers between devices with their start and end apart: 11, of which 8 were waited for; matrix products, arithmetic and copies ran while one was open for 5% of the time, Pallas kernels for 0%

profile of v2, /device:TPU:0, one launch (start us, length us, event | category | flops | bytes accessed | tf_op | source)
XLA Modules:
  0.0 54.4 jit_solution(8201370817056070904)
XLA Ops:
  0.0 0.0 copy-start
  0.0 0.0 copy-start.5
  0.0 1.4 %fusion.1 = bf16[16,16,64]{2,0,1:T(8,128)(2,1)S(1)} fusion(bf16[16,64,256]{2,1,0:T(8,128)(2,1)} %bitcast.29, bf16[16,16,256]{2,1,0:T(8,128)(2,1)} %param.12), kind=kOutput, calls=%fused_computation.4 | convolution fusion | flops 8404992 | bytes 688128 | tf_op jit(solution)/shard_map/rlq,leq->rle/dot_general | solution.py:102
  1.5 0.0 copy-start.3
  1.5 0.1 reshape.19
  1.6 0.0 copy-start.9
  1.6 0.0 copy-start.10
  1.6 1.8 %convolution_convert_fusion.3 = bf16[16,640]{1,0:T(8,128)(2,1)S(1)} fusion(bf16[16,1024]{1,0:T(8,128)(2,1)S(1)} %reshape.19, bf16[640,1024]{1,0:T(8,128)(2,1)} %param.16), kind=kOutput, calls=%fused_computation.7 | convolution fusion | flops 20981760 | bytes 1363968 | tf_op jit(solution)/shard_map/dot_general | solution.py:10
  3.4 0.0 copy-done.5
  3.4 0.0 copy-start.6
  3.4 0.2 fusion.32
  3.6 3.0 %collective-permute-start = (bf16[16,768]{1,0:T(8,128)(2,1)S(1)}, bf16[16,768]{1,0:T(8,128)(2,1)S(1)}, u32[]{:S(2)}, u32[]{:S(2)}) collective-permute-start(bf16[16,768]{1,0:T(8,128)(2,1)S(1)} %get-tuple-element.11), channel_id=1, source_target_pairs={{0,1},{1,0},{2,3},{3,2},{4,5},{5,4},{6,7},{7,6},{8,9},{9,8},{10,11... | collective-permute-start | bytes 73736 | tf_op jit(solution)/shard_map/ppermute | solution.py:25
  6.6 1.8 %collective-permute-done = bf16[16,768]{1,0:T(8,128)(2,1)S(1)} collective-permute-done((bf16[16,768]{1,0:T(8,128)(2,1)S(1)}, bf16[16,768]{1,0:T(8,128)(2,1)S(1)}, u32[]{:S(2)}, u32[]{:S(2)}) %collective-permute-start) | collective-permute-done | bytes 24608 | tf_op jit(solution)/shard_map/ppermute | solution.py:25
  8.4 0.0 copy-done.6
  8.4 2.1 %collective-permute-start.1 = (bf16[16,768]{1,0:T(8,128)(2,1)S(1)}, bf16[16,768]{1,0:T(8,128)(2,1)S(1)}, u32[]{:S(2)}, u32[]{:S(2)}) collective-permute-start(bf16[16,768]{1,0:T(8,128)(2,1)S(1)} %fusion.13), channel_id=1, source_target_pairs={{0,2},{1,3},{2,0},{3,1},{4,6},{5,7},{6,4},{7,5},{8,10},{9,11},{10,... | collective-permute-start | bytes 73736 | tf_op jit(solution)/shard_map/ppermute | solution.py:25
  10.6 1.8 %collective-permute-done.1 = bf16[16,768]{1,0:T(8,128)(2,1)S(1)} collective-permute-done((bf16[16,768]{1,0:T(8,128)(2,1)S(1)}, bf16[16,768]{1,0:T(8,128)(2,1)S(1)}, u32[]{:S(2)}, u32[]{:S(2)}) %collective-permute-start.1) | collective-permute-done | bytes 24608 | tf_op jit(solution)/shard_map/ppermute | solution.py:25
  12.4 0.0 copy-done.3
  12.4 0.0 copy-start.7
  12.4 0.2 fusion.33
  12.6 0.4 copy-done.7
  13.0 0.2 collective-permute-start.2
  13.2 0.0 copy-done.9
  13.2 0.0 copy-done.10
  13.2 0.9 %broadcast_in_dim.3 = bf16[8,64,512]{2,1,0:T(8,128)(2,1)} broadcast(bf16[64,512]{1,0:T(8,128)(2,1)S(1)} %pad_maximum_fusion.1), dimensions={1,2} | broadcast | bytes 589824 | tf_op jit(solution)/shard_map/broadcast_in_dim | solution.py:93
  14.1 6.1 %all-to-all-start = ((bf16[8,64,512]{2,1,0:T(8,128)(2,1)}), bf16[8,64,512]{2,1,0:T(8,128)(2,1)S(1)}, u32[]{:S(2)}, u32[]{:S(2)}) async-start(bf16[8,64,512]{2,1,0:T(8,128)(2,1)} %broadcast_in_dim.3), calls=%async_computation | async-start | bytes 1048576 | tf_op jit(solution)/shard_map/all_to_all | solution.py:92
  20.2 0.0 collective-permute-done.2
  20.2 1.8 %collective-permute-start.3 = (bf16[16,1536]{1,0:T(8,128)(2,1)S(1)}, bf16[16,1536]{1,0:T(8,128)(2,1)S(1)}, u32[]{:S(2)}, u32[]{:S(2)}) collective-permute-start(bf16[16,1536]{1,0:T(8,128)(2,1)S(1)} %fusion.7), channel_id=1, source_target_pairs={{0,9},{1,8},{2,11},{3,10},{4,13},{5,12},{6,15},{7,14},{8,1},{9,0},... | collective-permute-start | bytes 147464 | tf_op jit(solution)/shard_map/ppermute | solution.py:25
  22.0 4.3 %collective-permute-done.3 = bf16[16,1536]{1,0:T(8,128)(2,1)S(1)} collective-permute-done((bf16[16,1536]{1,0:T(8,128)(2,1)S(1)}, bf16[16,1536]{1,0:T(8,128)(2,1)S(1)}, u32[]{:S(2)}, u32[]{:S(2)}) %collective-permute-start.3) | collective-permute-done | bytes 49184 | tf_op jit(solution)/shard_map/ppermute | solution.py:25
  26.4 2.1 %collective-permute-start.4 = (bf16[16,1536]{1,0:T(8,128)(2,1)S(1)}, bf16[16,1536]{1,0:T(8,128)(2,1)S(1)}, u32[]{:S(2)}, u32[]{:S(2)}) collective-permute-start(bf16[16,1536]{1,0:T(8,128)(2,1)S(1)} %fusion.31), channel_id=1, source_target_pairs={{0,10},{1,11},{2,8},{3,9},{4,14},{5,15},{6,12},{7,13},{8,2},{9,3},... | collective-permute-start | bytes 147464 | tf_op jit(solution)/shard_map/ppermute | solution.py:25
  28.5 7.0 %all-to-all-done = bf16[8,64,512]{2,1,0:T(8,128)(2,1)S(1)} async-done(((bf16[8,64,512]{2,1,0:T(8,128)(2,1)}), bf16[8,64,512]{2,1,0:T(8,128)(2,1)S(1)}, u32[]{:S(2)}, u32[]{:S(2)}) %all-to-all-start) | async-done | bytes 524320 | tf_op jit(solution)/shard_map/all_to_all | solution.py:92
  35.5 0.0 collective-permute-start.6
  35.5 0.0 collective-permute-done.4
  35.5 0.6 %collective-permute-start.5 = (bf16[16,1536]{1,0:T(8,128)(2,1)S(1)}, bf16[16,1536]{1,0:T(8,128)(2,1)S(1)}, u32[]{:S(2)}, u32[]{:S(2)}) collective-permute-start(bf16[16,1536]{1,0:T(8,128)(2,1)S(1)} %fusion.8), channel_id=1, source_target_pairs={{0,8},{1,9},{2,10},{3,11},{4,12},{5,13},{6,14},{7,15},{8,0},{9,1},... | collective-permute-start | bytes 147464 | tf_op jit(solution)/shard_map/ppermute | solution.py:25
  36.1 1.4 %collective-permute-done.5 = bf16[16,1536]{1,0:T(8,128)(2,1)S(1)} collective-permute-done((bf16[16,1536]{1,0:T(8,128)(2,1)S(1)}, bf16[16,1536]{1,0:T(8,128)(2,1)S(1)}, u32[]{:S(2)}, u32[]{:S(2)}) %collective-permute-start.5) | collective-permute-done | bytes 49184 | tf_op jit(solution)/shard_map/ppermute | solution.py:25
  37.5 0.0 collective-permute-done.6
  37.5 0.1 select_bitcast_fusion.1
  37.6 0.0 copy-start.4
  37.6 0.1 pad_maximum_fusion
  37.7 0.0 copy-start.2
  37.7 0.2 fusion.34
  37.9 1.2 %collective-permute-start.7 = (bf16[16,256]{1,0:T(8,128)(2,1)S(1)}, bf16[16,256]{1,0:T(8,128)(2,1)S(1)}, u32[]{:S(2)}, u32[]{:S(2)}) collective-permute-start(bf16[16,256]{1,0:T(8,128)(2,1)S(1)} %get-tuple-element.15), channel_id=1, source_target_pairs={{0,24},{1,25},{2,26},{3,27},{4,28},{5,29},{6,30},{7,31},{8,16},{9,... | collective-permute-start | bytes 24584 | tf_op jit(solution)/shard_map/ppermute | solution.py:25
  39.2 1.8 %collective-permute-done.7 = bf16[16,256]{1,0:T(8,128)(2,1)S(1)} collective-permute-done((bf16[16,256]{1,0:T(8,128)(2,1)S(1)}, bf16[16,256]{1,0:T(8,128)(2,1)S(1)}, u32[]{:S(2)}, u32[]{:S(2)}) %collective-permute-start.7) | collective-permute-done | bytes 8224 | tf_op jit(solution)/shard_map/ppermute | solution.py:25
  41.0 0.2 convolution_convert_fusion.2
  41.2 0.0 copy-done.4
  41.2 0.2 convolution_convert_fusion.5
  41.5 1.5 %collective-permute-start.8 = (bf16[16,128]{1,0:T(8,128)(2,1)S(1)}, bf16[16,128]{1,0:T(8,128)(2,1)S(1)}, u32[]{:S(2)}, u32[]{:S(2)}) collective-permute-start(bf16[16,128]{1,0:T(8,128)(2,1)S(1)} %convolution_convert_fusion.5), channel_id=1, source_target_pairs={{0,1},{1,0},{2,3},{3,2},{4,5},{5,4},{6,7},{7,6},{8,9},{9,8},{10,11... | collective-permute-start | bytes 12296 | tf_op jit(solution)/shard_map/ppermute | solution.py:25
  42.9 2.1 %collective-permute-done.8 = bf16[16,128]{1,0:T(8,128)(2,1)S(1)} collective-permute-done((bf16[16,128]{1,0:T(8,128)(2,1)S(1)}, bf16[16,128]{1,0:T(8,128)(2,1)S(1)}, u32[]{:S(2)}, u32[]{:S(2)}) %collective-permute-start.8) | collective-permute-done | bytes 4128 | tf_op jit(solution)/shard_map/ppermute | solution.py:25
  45.1 0.6 %pad_maximum_fusion.2 = bf16[16,256]{1,0:T(8,128)(2,1)} fusion(bf16[16,128]{1,0:T(8,128)(2,1)S(1)} %get-tuple-element.10, bf16[16,128]{1,0:T(8,128)(2,1)S(1)} %get-tuple-element.9), kind=kLoop, calls=%fused_computation.44 | loop fusion | flops 16384 | bytes 16384 | tf_op jit(solution)/shard_map/concatenate | solution.py:46
  45.7 0.6 %collective-permute-start.9 = (bf16[16,256]{1,0:T(8,128)(2,1)}, bf16[16,256]{1,0:T(8,128)(2,1)}, u32[]{:S(2)}, u32[]{:S(2)}) collective-permute-start(bf16[16,256]{1,0:T(8,128)(2,1)} %pad_maximum_fusion.2), channel_id=1, source_target_pairs={{0,2},{1,3},{2,0},{3,1},{4,6},{5,7},{6,4},{7,5},{8,10},{9,11},{10,... | collective-permute-start | bytes 24584 | tf_op jit(solution)/shard_map/ppermute | solution.py:25
  46.3 0.0 copy-done.8
  46.3 0.0 copy-done
  46.3 0.0 copy-done.2
  46.3 0.0 slice-start
  46.3 1.1 %convolution_bitcast_fusion.1 = f32[16,16,256]{2,0,1:T(8,128)} fusion(bf16[16,256,256]{2,1,0:T(8,128)(2,1)S(1)} %bitcast.26, bf16[16,16,256]{2,1,0:T(8,128)(2,1)S(1)} %copy-done.2), kind=kOutput, calls=%fused_computation.2 | convolution fusion | flops 33554432 | bytes 2490368 | tf_op jit(solution)/shard_map/rlq,lqp->rlp/dot_general | solution.py:143
  47.4 0.7 %slice.30 = bf16[16,256]{1,0:T(8,128)(2,1)S(1)} slice(bf16[16,768]{1,0:T(8,128)(2,1)} %copy-done.7), slice={[0:16], [0:256]} | slice | bytes 16384 | tf_op jit(solution)/shard_map/slice | solution.py:132
  48.1 1.5 %collective-permute-done.9 = bf16[16,256]{1,0:T(8,128)(2,1)} collective-permute-done((bf16[16,256]{1,0:T(8,128)(2,1)}, bf16[16,256]{1,0:T(8,128)(2,1)}, u32[]{:S(2)}, u32[]{:S(2)}) %collective-permute-start.9) | collective-permute-done | bytes 8224 | tf_op jit(solution)/shard_map/ppermute | solution.py:25
  49.7 0.7 %broadcast_select_fusion.1 = (bf16[16,256]{1,0:T(8,128)(2,1)S(1)}, bf16[16,256]{1,0:T(8,128)(2,1)S(1)}) fusion(bf16[16,256]{1,0:T(8,128)(2,1)} %collective-permute-done.9, pred[]{:T(512)S(6)} %ne.25, bf16[16,128]{1,0:T(8,128)(2,1)} %copy-done.8, bf16[16,128]{1,0:T(8,128)(2,1)S(1)} %get-tuple-element.9), kind=kLoop, calls=%fused_computation.46 | loop fusion | flops 24576 | bytes 32769 | tf_op jit(solution)/shard_map/jit(_where)/select_n | solution.py:47
  50.4 1.2 %convolution_convert_fusion.4 = bf16[16,256]{1,0:T(8,128)(2,1)S(1)} fusion(bf16[256,768]{1,0:T(8,128)(2,1)} %param.19, bf16[16,256]{1,0:T(8,128)(2,1)S(1)} %get-tuple-element.8, bf16[16,256]{1,0:T(8,128)(2,1)S(1)} %get-tuple-element.7, bf16[16,256]{1,0:T(8,128)(2,1)S(1)} %slice.30), kind=kOutput, calls=%fused_computation.8 | convolution fusion | flops 6369280 | bytes 425984 | tf_op jit(solution)/shard_map/dot_general | solution.py:10
  51.6 0.0 copy-done.1
  51.6 0.0 slice-done
  51.6 0.4 convolution_convert_fusion.1
  52.1 0.1 reshape.21
  52.2 1.3 %fusion = f32[16,16,256]{2,0,1:T(8,128)S(1)} fusion(f32[16,16,256]{2,0,1:T(8,128)} %convolution_bitcast_fusion.1, bf16[16,64,256]{2,1,0:T(8,128)(2,1)} %bitcast.30, bf16[16,16,64]{2,1,0:T(8,128)(2,1)S(1)} %reshape.21), kind=kOutput, calls=%fused_computation.1 | convolution fusion | flops 8454144 | bytes 1081344 | tf_op jit(solution)/shard_map/rle,leq->rlq/dot_general | solution.py:137
  53.5 0.9 %copy.21 = f32[16,16,256]{2,1,0:T(8,128)} copy(f32[16,16,256]{2,0,1:T(8,128)S(1)} %fusion) | data formatting | bytes 524288 | tf_op jit(solution)/shard_map/add | solution.py:149
  (12 shorter events, 0.2 us)
Async XLA Ops:
  0.0 46.3 %copy-start = (bf16[4096,256]{1,0:T(8,128)(2,1)S(1)}, bf16[4096,256]{1,0:T(8,128)(2,1)}, u32[]{:S(2)}) copy-start(bf16[4096,256]{1,0:T(8,128)(2,1)} %param.14) | copy-start | bytes 6291460
  0.0 3.4 %copy-start.5 = (bf16[256,768]{1,0:T(8,128)(2,1)S(1)}, bf16[256,768]{1,0:T(8,128)(2,1)}, u32[]{:S(2)}) copy-start(bf16[256,768]{1,0:T(8,128)(2,1)} %param.18) | copy-start | bytes 1179652
  1.5 10.9 %copy-start.3 = (bf16[128,1536]{1,0:T(8,128)(2,1)S(1)}, bf16[128,1536]{1,0:T(8,128)(2,1)}, u32[]{:S(2)}) copy-start(bf16[128,1536]{1,0:T(8,128)(2,1)} %param.20) | copy-start | bytes 1179652
  1.6 11.6 %copy-start.9 = (bf16[64,256]{1,0:T(8,128)(2,1)S(1)}, bf16[64,256]{1,0:T(8,128)(2,1)}, u32[]{:S(2)}) copy-start(bf16[64,256]{1,0:T(8,128)(2,1)} %param.23) | copy-start | bytes 98308
  1.6 11.6 %copy-start.10 = (bf16[64,256]{1,0:T(8,128)(2,1)S(1)}, bf16[64,256]{1,0:T(8,128)(2,1)}, u32[]{:S(2)}) copy-start(bf16[64,256]{1,0:T(8,128)(2,1)} %param.22) | copy-start | bytes 98308
  3.4 5.0 %copy-start.6 = (bf16[16,640]{1,0:T(8,128)(2,1)}, bf16[16,640]{1,0:T(8,128)(2,1)S(1)}, u32[]{:S(2)}) copy-start(bf16[16,640]{1,0:T(8,128)(2,1)S(1)} %convolution_convert_fusion.3) | copy-start | bytes 61444
  3.6 4.8 %collective-permute-start = (bf16[16,768]{1,0:T(8,128)(2,1)S(1)}, bf16[16,768]{1,0:T(8,128)(2,1)S(1)}, u32[]{:S(2)}, u32[]{:S(2)}) collective-permute-start(bf16[16,768]{1,0:T(8,128)(2,1)S(1)} %get-tuple-element.11), channel_id=1, source_target_pairs={{0,1},{1,0},{2,3},{3,2},{4,5},{5,4},{6,7},{7,6},{8,9},{9,8},{10,11... | collective-permute-start | bytes 73736 | tf_op jit(solution)/shard_map/ppermute | solution.py:25
  8.4 3.9 %collective-permute-start.1 = (bf16[16,768]{1,0:T(8,128)(2,1)S(1)}, bf16[16,768]{1,0:T(8,128)(2,1)S(1)}, u32[]{:S(2)}, u32[]{:S(2)}) collective-permute-start(bf16[16,768]{1,0:T(8,128)(2,1)S(1)} %fusion.13), channel_id=1, source_target_pairs={{0,2},{1,3},{2,0},{3,1},{4,6},{5,7},{6,4},{7,5},{8,10},{9,11},{10,... | collective-permute-start | bytes 73736 | tf_op jit(solution)/shard_map/ppermute | solution.py:25
  12.4 0.6 %copy-start.7 = (bf16[16,768]{1,0:T(8,128)(2,1)}, bf16[16,768]{1,0:T(8,128)(2,1)S(1)}, u32[]{:S(2)}) copy-start(bf16[16,768]{1,0:T(8,128)(2,1)S(1)} %add_convert_fusion.1) | copy-start | bytes 73732
  13.0 7.2 %collective-permute-start.2 = (bf16[16,1536]{1,0:T(8,128)(2,1)S(1)}, bf16[16,1536]{1,0:T(8,128)(2,1)S(1)}, u32[]{:S(2)}, u32[]{:S(2)}) collective-permute-start(bf16[16,1536]{1,0:T(8,128)(2,1)S(1)} %get-tuple-element.13), channel_id=1, source_target_pairs={{0,12},{1,13},{2,14},{3,15},{4,8},{5,9},{6,10},{7,11},{8,4},{9,5},... | collective-permute-start | bytes 147464 | tf_op jit(solution)/shard_map/ppermute | solution.py:25
  14.1 21.4 %all-to-all-start = ((bf16[8,64,512]{2,1,0:T(8,128)(2,1)}), bf16[8,64,512]{2,1,0:T(8,128)(2,1)S(1)}, u32[]{:S(2)}, u32[]{:S(2)}) async-start(bf16[8,64,512]{2,1,0:T(8,128)(2,1)} %broadcast_in_dim.3), calls=%async_computation | async-start | bytes 1048576 | tf_op jit(solution)/shard_map/all_to_all | solution.py:92
  20.2 6.1 %collective-permute-start.3 = (bf16[16,1536]{1,0:T(8,128)(2,1)S(1)}, bf16[16,1536]{1,0:T(8,128)(2,1)S(1)}, u32[]{:S(2)}, u32[]{:S(2)}) collective-permute-start(bf16[16,1536]{1,0:T(8,128)(2,1)S(1)} %fusion.7), channel_id=1, source_target_pairs={{0,9},{1,8},{2,11},{3,10},{4,13},{5,12},{6,15},{7,14},{8,1},{9,0},... | collective-permute-start | bytes 147464 | tf_op jit(solution)/shard_map/ppermute | solution.py:25
  26.4 9.1 %collective-permute-start.4 = (bf16[16,1536]{1,0:T(8,128)(2,1)S(1)}, bf16[16,1536]{1,0:T(8,128)(2,1)S(1)}, u32[]{:S(2)}, u32[]{:S(2)}) collective-permute-start(bf16[16,1536]{1,0:T(8,128)(2,1)S(1)} %fusion.31), channel_id=1, source_target_pairs={{0,10},{1,11},{2,8},{3,9},{4,14},{5,15},{6,12},{7,13},{8,2},{9,3},... | collective-permute-start | bytes 147464 | tf_op jit(solution)/shard_map/ppermute | solution.py:25
  35.5 2.0 %collective-permute-start.6 = (bf16[8,64,512]{2,1,0:T(8,128)(2,1)S(1)}, bf16[8,64,512]{2,1,0:T(8,128)(2,1)S(1)}, u32[]{:S(2)}, u32[]{:S(2)}) collective-permute-start(bf16[8,64,512]{2,1,0:T(8,128)(2,1)S(1)} %all-to-all-done), channel_id=1, source_target_pairs={{0,8},{1,9},{2,10},{3,11},{4,12},{5,13},{6,14},{7,15},{8,0},{9,1},... | collective-permute-start | bytes 1572872 | tf_op jit(solution)/shard_map/ppermute | solution.py:25
  35.5 1.9 %collective-permute-start.5 = (bf16[16,1536]{1,0:T(8,128)(2,1)S(1)}, bf16[16,1536]{1,0:T(8,128)(2,1)S(1)}, u32[]{:S(2)}, u32[]{:S(2)}) collective-permute-start(bf16[16,1536]{1,0:T(8,128)(2,1)S(1)} %fusion.8), channel_id=1, source_target_pairs={{0,8},{1,9},{2,10},{3,11},{4,12},{5,13},{6,14},{7,15},{8,0},{9,1},... | collective-permute-start | bytes 147464 | tf_op jit(solution)/shard_map/ppermute | solution.py:25
  37.6 3.6 %copy-start.4 = (bf16[128,1536]{1,0:T(8,128)(2,1)S(1)}, bf16[128,1536]{1,0:T(8,128)(2,1)}, u32[]{:S(2)}) copy-start(bf16[128,1536]{1,0:T(8,128)(2,1)} %param.21) | copy-start | bytes 1179652
  37.7 8.6 %copy-start.2 = (bf16[16,16,256]{2,1,0:T(8,128)(2,1)S(1)}, bf16[16,16,256]{2,1,0:T(8,128)(2,1)}, u32[]{:S(2)}) copy-start(bf16[16,16,256]{2,1,0:T(8,128)(2,1)} %param.12) | copy-start | bytes 393220
  37.9 3.1 %collective-permute-start.7 = (bf16[16,256]{1,0:T(8,128)(2,1)S(1)}, bf16[16,256]{1,0:T(8,128)(2,1)S(1)}, u32[]{:S(2)}, u32[]{:S(2)}) collective-permute-start(bf16[16,256]{1,0:T(8,128)(2,1)S(1)} %get-tuple-element.15), channel_id=1, source_target_pairs={{0,24},{1,25},{2,26},{3,27},{4,28},{5,29},{6,30},{7,31},{8,16},{9,... | collective-permute-start | bytes 24584 | tf_op jit(solution)/shard_map/ppermute | solution.py:25
  41.5 3.6 %collective-permute-start.8 = (bf16[16,128]{1,0:T(8,128)(2,1)S(1)}, bf16[16,128]{1,0:T(8,128)(2,1)S(1)}, u32[]{:S(2)}, u32[]{:S(2)}) collective-permute-start(bf16[16,128]{1,0:T(8,128)(2,1)S(1)} %convolution_convert_fusion.5), channel_id=1, source_target_pairs={{0,1},{1,0},{2,3},{3,2},{4,5},{5,4},{6,7},{7,6},{8,9},{9,8},{10,11... | collective-permute-start | bytes 12296 | tf_op jit(solution)/shard_map/ppermute | solution.py:25
  45.1 1.2 %copy-start.8 = (bf16[16,128]{1,0:T(8,128)(2,1)}, bf16[16,128]{1,0:T(8,128)(2,1)S(1)}, u32[]{:S(2)}) copy-start(bf16[16,128]{1,0:T(8,128)(2,1)S(1)} %get-tuple-element.10) | copy-start | bytes 12292
  45.7 4.0 %collective-permute-start.9 = (bf16[16,256]{1,0:T(8,128)(2,1)}, bf16[16,256]{1,0:T(8,128)(2,1)}, u32[]{:S(2)}, u32[]{:S(2)}) collective-permute-start(bf16[16,256]{1,0:T(8,128)(2,1)} %pad_maximum_fusion.2), channel_id=1, source_target_pairs={{0,2},{1,3},{2,0},{3,1},{4,6},{5,7},{6,4},{7,5},{8,10},{9,11},{10,... | collective-permute-start | bytes 24584 | tf_op jit(solution)/shard_map/ppermute | solution.py:25
  46.3 5.2 %copy-start.1 = (bf16[1024,640]{1,0:T(8,128)(2,1)S(1)}, bf16[1024,640]{1,0:T(8,128)(2,1)}, u32[]{:S(2)}) copy-start(bf16[1024,640]{1,0:T(8,128)(2,1)} %param.17) | copy-start | bytes 3932164
  46.3 5.2 %slice-start = ((bf16[16,640]{1,0:T(8,128)(2,1)}), bf16[16,384]{1,0:T(8,128)(2,1)S(1)}, s32[]{:S(2)}) async-start(bf16[16,640]{1,0:T(8,128)(2,1)} %copy-done.6), calls=%async_computation.1 | async-start | bytes 24576 | tf_op jit(solution)/shard_map/slice | solution.py:135

commit v3 on v1

--- a/solution.py
+++ b/solution.py
@@ -1,6 +1,8 @@
 import jax
 import jax.numpy as jnp
 from jax import lax
+from jax.experimental import pallas as pl
+from jax.experimental.pallas import tpu as pltpu
 from jax.sharding import PartitionSpec as P
 
 AXES = ("gx", "gy")
@@ -56,6 +58,111 @@
 
 def tie(*values):
     return lax.optimization_barrier(values)
+
+
+def fetch(sources, scratch, sems):
+    copies = [
+        pltpu.make_async_copy(source, space, sems.at[i])
+        for i, (source, space) in enumerate(zip(sources, scratch))
+    ]
+    for copy in copies:
+        copy.start()
+    return copies
+
+
+def head_kernel(source_hbm, flux_hbm, up_hbm, one_hbm, state_ref, term_ref, low_ref, *rest):
+    *scratch, sems = rest
+    source, leaf_flux, box_up, up_one = scratch
+    copies = fetch((source_hbm, flux_hbm, up_hbm, one_hbm), scratch, sems)
+    rhs_count, leaves, points = source.shape
+    edge_count = leaf_flux.shape[0] // leaves
+    copies[0].wait()
+    copies[1].wait()
+    rows = source[...].reshape(rhs_count * leaves, points)
+    every = contract(rows, leaf_flux[...]).reshape(rhs_count, leaves, leaves * edge_count)
+    leaf = lax.broadcasted_iota(jnp.int32, every.shape, 1)
+    column = lax.broadcasted_iota(jnp.int32, every.shape, 2)
+    own = (column >= leaf * edge_count) & (column < leaf * edge_count + edge_count)
+    flux = rounded(jnp.sum(jnp.where(own, every, 0.0), axis=1))
+    copies[2].wait()
+    state = rounded(contract(flux, box_up[...]))
+    state_ref[...] = state
+    copies[3].wait()
+    term = product(state[:, state.shape[1] - up_one.shape[0] :], up_one[...])
+    term_ref[...] = term
+    low_ref[...] = rounded(term)
+
+
+def head(source, leaf_flux, box_up, up_one):
+    operands = (source, leaf_flux, box_up, up_one)
+    rhs_count = source.shape[0]
+    term = (rhs_count, up_one.shape[1])
+    return pl.pallas_call(
+        head_kernel,
+        out_shape=(
+            jax.ShapeDtypeStruct((rhs_count, box_up.shape[0]), jnp.bfloat16),
+            jax.ShapeDtypeStruct(term, jnp.float32),
+            jax.ShapeDtypeStruct(term, jnp.bfloat16),
+        ),
+        in_specs=[pl.BlockSpec(memory_space=pl.ANY)] * 4,
+        scratch_shapes=[pltpu.VMEM(x.shape, x.dtype) for x in operands]
+        + [pltpu.SemaphoreType.DMA((4,))],
+        compiler_params=pltpu.CompilerParams(vmem_limit_bytes=2**24),
+        cost_estimate=pl.CostEstimate(
+            flops=2 * rhs_count * sum(x.size for x in operands[1:]),
+            bytes_accessed=2 * sum(x.size for x in operands),
+            transcendentals=0,
+        ),
+    )(*operands)
+
+
+def tail_kernel(
+    first_ref, mid_ref, box_ref, particular_ref, one_hbm, down_hbm, lift_hbm, out_ref, *rest
+):
+    *scratch, sems = rest
+    down_one, box_down, leaf_lift = scratch
+    copies = fetch((one_hbm, down_hbm, lift_hbm), scratch, sems)
+    leaves = out_ref.shape[1]
+    edge_count = leaf_lift.shape[0] // leaves
+    inner, inner_dev = first_ref.shape[1], box_ref.shape[1]
+    copies[0].wait()
+    bound = rounded(
+        contract(first_ref[...], down_one[:, :inner]) + contract(mid_ref[...], down_one[:, inner:])
+    )
+    copies[1].wait()
+    edges = rounded(
+        contract(box_ref[...], box_down[:, :inner_dev]) + contract(bound, box_down[:, inner_dev:])
+    )
+    copies[2].wait()
+    pair_count = 2 * edge_count
+    column = lax.broadcasted_iota(jnp.int32, (edges.shape[0], pair_count), 1)
+    for leaf in range(leaves):
+        start = leaf // 2 * pair_count
+        both = edges[:, start : start + pair_count].astype(jnp.float32)
+        mine = (column < edge_count) if leaf % 2 == 0 else (column >= edge_count)
+        part = rounded(jnp.where(mine, both, 0.0))
+        lifted = product(part, leaf_lift[start : start + pair_count, :])
+        out_ref[:, leaf, :] = lifted + particular_ref[leaf]
+
+
+def tail(first_inner, mid_bound, box_inner, particular, down_one, box_down, leaf_lift):
+    leaves, rhs_count, points = particular.shape
+    weights = (down_one, box_down, leaf_lift)
+    return pl.pallas_call(
+        tail_kernel,
+        out_shape=jax.ShapeDtypeStruct((rhs_count, leaves, points), jnp.float32),
+        in_specs=[pl.BlockSpec(memory_space=pltpu.VMEM)] * 4
+        + [pl.BlockSpec(memory_space=pl.ANY)] * 3,
+        out_specs=pl.BlockSpec(memory_space=pltpu.VMEM),
+        scratch_shapes=[pltpu.VMEM(x.shape, x.dtype) for x in weights]
+        + [pltpu.SemaphoreType.DMA((3,))],
+        compiler_params=pltpu.CompilerParams(vmem_limit_bytes=2**24),
+        cost_estimate=pl.CostEstimate(
+            flops=2 * rhs_count * sum(x.size for x in weights),
+            bytes_accessed=2 * sum(x.size for x in weights) + 8 * particular.size,
+            transcendentals=0,
+        ),
+    )(first_inner, mid_bound, box_inner, particular, *weights)
 
 
 def per_device(
@@ -73,7 +180,6 @@
     down_root,
 ):
     rhs_count, leaves, points = source.shape
-    edge_count = leaf_flux.shape[0] // leaves
     count = lax.axis_size(AXES)
     place = lax.axis_index(AXES)
     k_zero = up_one.shape[0]
@@ -88,19 +194,11 @@
 
     far = pair // 2
 
-    flux = jnp.einsum(
-        "rlq,leq->rle",
-        source,
-        leaf_flux.reshape(leaves, edge_count, points),
-        preferred_element_type=jnp.float32,
-    )
-    flux = rounded(flux).reshape(rhs_count, leaves * edge_count)
-    box_state = rounded(contract(flux, box_up))
-    first_sum = product(box_state[:, inner_dev:], up_one)
+    box_state, first_sum, first_low = head(source, leaf_flux, box_up, up_one)
 
     roots = jnp.concatenate([up_root, down_root], axis=1)
     roots_far = swap(roots, far)
-    first_sum = partner_sum(first_sum, 1)
+    first_sum = first_sum + swap(first_low, 1).astype(jnp.float32)
 
     first_sum, roots_far = tie(first_sum, roots_far)
     roots = joined_pair(roots, roots_far, place & far != 0, 0)
@@ -135,24 +233,21 @@
     mid_bound = rounded(contract(second_input, down_two))
     mid_bound = placed([mid_bound, swap(mid_bound, 1)], place, 1)
     mid_bound = placed([mid_bound, swap(mid_bound, near)], place // near, 1)
-    first_input = jnp.concatenate([first_state[:, :k_zero], mid_bound], axis=1)
-
-    box_bound = rounded(contract(first_input, down_one))
-    box_input = jnp.concatenate([box_state[:, :inner_dev], box_bound], axis=1)
-    leaf_bound = rounded(contract(box_input, box_down)).reshape(rhs_count, leaves, edge_count)
-    lifted = jnp.einsum(
-        "rle,leq->rlq",
-        leaf_bound,
-        leaf_lift.reshape(leaves, edge_count, points),
-        preferred_element_type=jnp.float32,
-    )
     particular = jnp.einsum(
-        "rlq,lqp->rlp",
+        "rlq,lqp->lrp",
         source,
         leaf_particular.reshape(leaves, points, points),
         preferred_element_type=jnp.float32,
     )
-    return lifted + particular
+    return tail(
+        first_state[:, :k_zero],
+        mid_bound,
+        box_state[:, :inner_dev],
+        particular,
+        down_one,
+        box_down,
+        leaf_lift,
+    )
 
 
 def solution(mesh):

time: 54.1 us -> 59.2 us (1.094)
  matrix products: 8.29 us -> 1.87 us
  local copies, waits for them, and re-layouts: 1.2 us -> 7.43 us
  Pallas kernels: 0 us -> 3.94 us
  waiting for transfers between devices: 31.6 us -> 32.3 us
    unnamed x17 -> x29, local copies, waits for them, and re-layouts: 0.04 us -> 7.42 us
    pallas_call x0 -> x2, Pallas kernels: none -> 3.94 us  [the longest x1 2.32 us: tail(): pl.pallas_call(tail_kernel, out_shape=jax.ShapeDtypeStruct((rhs_count, le...]
    dot_general x5 -> x2, matrix products: 3.93 us -> 0.44 us  [contract(): lax.dot_general(left, right, (((1,), (1,)), ((), ())), preferred_element_...]
    dot_general x3 -> x1, matrix products: 3.83 us -> 1.09 us  [per_device(): jnp.einsum('rlq,lqp->lrp', source, leaf_particular.reshape(leaves, points...]
    add x1 -> x0, local copies, waits for them, and re-layouts: 0.86 us -> none  [per_device(): return lifted + particular]
    ppermute x13, waiting for transfers between devices: 31.6 us -> 32.3 us  [swap(): return lax.ppermute(value, AXES, [(i, i ^ mask) for i in range(count)])]
  transfers between devices with their start and end apart: 13 -> 13, of which waited for: 11 -> 11; matrix products, arithmetic and copies ran while one was open for 4% -> 3% of each run, Pallas kernels for 0% -> 0%
where the time goes in v3:
time: 59.2 us; the launch traced here: 58.8 us
  waiting for transfers between devices  32.3 us (55%)
  starting transfers between devices  11.5 us (19%)
  local copies, waits for them, and re-layouts  7.43 us (13%)
  Pallas kernels  3.94 us (7%)
  matrix products  1.87 us (3%)
  other arithmetic  1.52 us (3%)
    ppermute x13, waiting for transfers between devices, swap(): return lax.ppermute(value, AXES, [(i, i ^ mask) for i in range(count)])  32.3 us
    ppermute x13, starting transfers between devices, swap(): return lax.ppermute(value, AXES, [(i, i ^ mask) for i in range(count)])  11.5 us
    unnamed x29, local copies, waits for them, and re-layouts  7.42 us
    pallas_call x1, Pallas kernels, tail(): pl.pallas_call(tail_kernel, out_shape=jax.ShapeDtypeStruct((rhs_count, le...  2.32 us
    pallas_call x1, Pallas kernels, head(): pl.pallas_call(head_kernel, out_shape=(jax.ShapeDtypeStruct((rhs_count, b...  1.63 us
    another operation x8, other arithmetic, joined_pair(): jnp.stack([jnp.where(upper, other, joined), jnp.where(upper, joined, othe...  1.4 us
  transfers between devices with their start and end apart: 13, of which 11 were waited for; matrix products, arithmetic and copies ran while one was open for 3% of the time, Pallas kernels for 0%

profile of v3, /device:TPU:0, one launch (start us, length us, event | category | flops | bytes accessed | tf_op | source)
XLA Modules:
  0.0 58.8 jit_solution(4620573534996639441)
XLA Ops:
  0.0 0.0 copy-start
  0.0 0.0 copy-start.1
  0.0 1.5 %copy-done.1 = bf16[640,1024]{1,0:T(8,128)(2,1)S(1)} copy-done((bf16[640,1024]{1,0:T(8,128)(2,1)S(1)}, bf16[640,1024]{1,0:T(8,128)(2,1)}, u32[]{:S(2)}) %copy-start.1) | copy-done | bytes 1310744
  1.5 0.0 copy-start.4
  1.5 0.9 %copy-done.4 = bf16[16,16,256]{2,1,0:T(8,128)(2,1)S(1)} copy-done((bf16[16,16,256]{2,1,0:T(8,128)(2,1)S(1)}, bf16[16,16,256]{2,1,0:T(8,128)(2,1)}, u32[]{:S(2)}) %copy-start.4) | copy-done | bytes 131096
  2.4 0.0 copy-start.6
  2.4 1.0 %copy-done.6 = bf16[1024,256]{1,0:T(8,128)(2,1)S(1)} copy-done((bf16[1024,256]{1,0:T(8,128)(2,1)S(1)}, bf16[1024,256]{1,0:T(8,128)(2,1)}, u32[]{:S(2)}) %copy-start.6) | copy-done | bytes 524312
  3.4 0.0 copy-start.8
  3.4 1.0 %copy-done.8 = bf16[256,768]{1,0:T(8,128)(2,1)S(1)} copy-done((bf16[256,768]{1,0:T(8,128)(2,1)S(1)}, bf16[256,768]{1,0:T(8,128)(2,1)}, u32[]{:S(2)}) %copy-start.8) | copy-done | bytes 393240
  4.4 0.0 copy-start.12
  4.4 0.0 copy-start.13
  4.4 0.0 copy-start.10
  4.4 1.6 %shard_map.118 = (bf16[16,640]{1,0:T(8,128)(2,1)S(1)}, f32[16,768]{1,0:T(8,128)S(1)}, bf16[16,768]{1,0:T(8,128)(2,1)S(1)}) custom-call(bf16[16,16,256]{2,1,0:T(8,128)(2,1)S(1)} %copy-done.4, bf16[1024,256]{1,0:T(8,128)(2,1)S(1)} %copy-done.6, bf16[640,1024]{1,0:T(8,128)(2,1)S(1)} %copy-done.1, bf16[256,768]{1,0:T(8,128)(2,1)S(1)} %copy-done.8), custom_call_target="tpu_custom_call" | custom-call | flops 35651584 | bytes 2359296 | tf_op jit(solution)/shard_map/pallas_call | solution.py:100
  6.1 3.0 %collective-permute-start = (bf16[16,768]{1,0:T(8,128)(2,1)S(1)}, bf16[16,768]{1,0:T(8,128)(2,1)S(1)}, u32[]{:S(2)}, u32[]{:S(2)}) collective-permute-start(bf16[16,768]{1,0:T(8,128)(2,1)S(1)} %get-tuple-element.15), channel_id=1, source_target_pairs={{0,1},{1,0},{2,3},{3,2},{4,5},{5,4},{6,7},{7,6},{8,9},{9,8},{10,11... | collective-permute-start | bytes 73736 | tf_op jit(solution)/shard_map/ppermute | solution.py:27
  9.1 0.0 copy-done.12
  9.1 0.0 copy-done.13
  9.1 2.7 %collective-permute-start.1 = (bf16[64,512]{1,0:T(8,128)(2,1)S(1)}, bf16[64,512]{1,0:T(8,128)(2,1)S(1)}, u32[]{:S(2)}, u32[]{:S(2)}) collective-permute-start(bf16[64,512]{1,0:T(8,128)(2,1)S(1)} %constant_dynamic-update-slice_fusion), channel_id=1, source_target_pairs={{0,4},{1,5},{2,6},{3,7},{4,0},{5,1},{6,2},{7,3},{8,12},{9,13},{10,... | collective-permute-start | bytes 196616 | tf_op jit(solution)/shard_map/ppermute | solution.py:27
  11.8 0.0 collective-permute-done
  11.8 2.9 %collective-permute-done.1 = bf16[64,512]{1,0:T(8,128)(2,1)S(1)} collective-permute-done((bf16[64,512]{1,0:T(8,128)(2,1)S(1)}, bf16[64,512]{1,0:T(8,128)(2,1)S(1)}, u32[]{:S(2)}, u32[]{:S(2)}) %collective-permute-start.1) | collective-permute-done | bytes 65568 | tf_op jit(solution)/shard_map/ppermute | solution.py:27
  14.6 1.3 %collective-permute-start.2 = (bf16[16,768]{1,0:T(8,128)(2,1)S(1)}, bf16[16,768]{1,0:T(8,128)(2,1)S(1)}, u32[]{:S(2)}, u32[]{:S(2)}) collective-permute-start(bf16[16,768]{1,0:T(8,128)(2,1)S(1)} %convert_element_type.55), channel_id=1, source_target_pairs={{0,2},{1,3},{2,0},{3,1},{4,6},{5,7},{6,4},{7,5},{8,10},{9,11},{10,... | collective-permute-start | bytes 73736 | tf_op jit(solution)/shard_map/ppermute | solution.py:27
  16.0 0.6 collective-permute-start.3
  16.5 1.9 %collective-permute-done.2 = bf16[16,768]{1,0:T(8,128)(2,1)S(1)} collective-permute-done((bf16[16,768]{1,0:T(8,128)(2,1)S(1)}, bf16[16,768]{1,0:T(8,128)(2,1)S(1)}, u32[]{:S(2)}, u32[]{:S(2)}) %collective-permute-start.2) | collective-permute-done | bytes 24608 | tf_op jit(solution)/shard_map/ppermute | solution.py:27
  18.5 0.0 copy-done.10
  18.5 0.2 fusion.11
  18.7 2.3 %collective-permute-done.3 = bf16[2,64,512]{2,1,0:T(8,128)(2,1)S(1)} collective-permute-done((bf16[2,64,512]{2,1,0:T(8,128)(2,1)S(1)}, bf16[2,64,512]{2,1,0:T(8,128)(2,1)S(1)}, u32[]{:S(2)}, u32[]{:S(2)}) %collective-permute-start.3) | collective-permute-done | bytes 131104 | tf_op jit(solution)/shard_map/ppermute | solution.py:27
  21.0 0.1 collective-permute-start.4
  21.1 5.7 %collective-permute-done.4 = bf16[16,1536]{1,0:T(8,128)(2,1)S(1)} collective-permute-done((bf16[16,1536]{1,0:T(8,128)(2,1)S(1)}, bf16[16,1536]{1,0:T(8,128)(2,1)S(1)}, u32[]{:S(2)}, u32[]{:S(2)}) %collective-permute-start.4) | collective-permute-done | bytes 49184 | tf_op jit(solution)/shard_map/ppermute | solution.py:27
  26.8 0.3 collective-permute-start.5
  27.1 0.1 collective-permute-start.6
  27.2 3.4 %collective-permute-done.5 = bf16[16,1536]{1,0:T(8,128)(2,1)S(1)} collective-permute-done((bf16[16,1536]{1,0:T(8,128)(2,1)S(1)}, bf16[16,1536]{1,0:T(8,128)(2,1)S(1)}, u32[]{:S(2)}, u32[]{:S(2)}) %collective-permute-start.5) | collective-permute-done | bytes 49184 | tf_op jit(solution)/shard_map/ppermute | solution.py:27
  30.6 5.2 %collective-permute-done.6 = bf16[2,2,64,512]{3,2,1,0:T(8,128)(2,1)S(1)} collective-permute-done((bf16[2,2,64,512]{3,2,1,0:T(8,128)(2,1)S(1)}, bf16[2,2,64,512]{3,2,1,0:T(8,128)(2,1)S(1)}, u32[]{:S(2)}, u32[]{:S(2)}) %collective-permute-start.6) | collective-permute-done | bytes 262176 | tf_op jit(solution)/shard_map/ppermute | solution.py:27
  35.8 0.1 collective-permute-start.7
  36.0 0.1 pad_maximum_fusion.1
  36.0 0.4 collective-permute-start.9
  36.4 3.3 %collective-permute-done.7 = bf16[16,1536]{1,0:T(8,128)(2,1)S(1)} collective-permute-done((bf16[16,1536]{1,0:T(8,128)(2,1)S(1)}, bf16[16,1536]{1,0:T(8,128)(2,1)S(1)}, u32[]{:S(2)}, u32[]{:S(2)}) %collective-permute-start.7) | collective-permute-done | bytes 49184 | tf_op jit(solution)/shard_map/ppermute | solution.py:27
  39.8 0.1 collective-permute-start.8
  39.9 1.2 %collective-permute-done.8 = bf16[16,1536]{1,0:T(8,128)(2,1)S(1)} collective-permute-done((bf16[16,1536]{1,0:T(8,128)(2,1)S(1)}, bf16[16,1536]{1,0:T(8,128)(2,1)S(1)}, u32[]{:S(2)}, u32[]{:S(2)}) %collective-permute-start.8) | collective-permute-done | bytes 49184 | tf_op jit(solution)/shard_map/ppermute | solution.py:27
  41.1 0.0 collective-permute-done.9
  41.1 1.1 %select_bitcast_fusion.1 = (bf16[1,2,2,2,64,512]{5,4,3,2,1,0:T(8,128)(2,1)S(1)}, bf16[1,2,2,2,64,512]{5,4,3,2,1,0:T(8,128)(2,1)S(1)}) fusion(bf16[2,2,2,64,512]{4,3,2,1,0:T(8,128)(2,1)} %collective-permute-done.9, pred[]{:T(512)S(6)} %ne.36, bf16[2,1,2,64,512]{4,3,2,1,0:T(8,128)(2,1)S(1)} %get-tuple-element.26, ...), kind=kLoop, calls=%fused_computation.8 | loop fusion | flops 786432 | bytes 2097153 | tf_op jit(solution)/shard_map/stack | solution.py:54
  42.2 0.0 copy-start.11
  42.2 0.0 copy-start.5
  42.2 0.1 pad_maximum_fusion
  42.4 0.0 copy-start.2
  42.4 0.2 fusion.15
  42.5 1.3 %collective-permute-start.10 = (bf16[16,256]{1,0:T(8,128)(2,1)S(1)}, bf16[16,256]{1,0:T(8,128)(2,1)S(1)}, u32[]{:S(2)}, u32[]{:S(2)}) collective-permute-start(bf16[16,256]{1,0:T(8,128)(2,1)S(1)} %get-tuple-element.35), channel_id=1, source_target_pairs={{0,24},{1,25},{2,26},{3,27},{4,28},{5,29},{6,30},{7,31},{8,16},{9,... | collective-permute-start | bytes 24584 | tf_op jit(solution)/shard_map/ppermute | solution.py:27
  43.8 1.8 %collective-permute-done.10 = bf16[16,256]{1,0:T(8,128)(2,1)S(1)} collective-permute-done((bf16[16,256]{1,0:T(8,128)(2,1)S(1)}, bf16[16,256]{1,0:T(8,128)(2,1)S(1)}, u32[]{:S(2)}, u32[]{:S(2)}) %collective-permute-start.10) | collective-permute-done | bytes 8224 | tf_op jit(solution)/shard_map/ppermute | solution.py:27
  45.6 0.2 convolution_convert_fusion
  45.9 0.0 copy-done.11
  45.9 0.2 convolution_convert_fusion.1
  46.1 1.6 %collective-permute-start.11 = (bf16[16,128]{1,0:T(8,128)(2,1)S(1)}, bf16[16,128]{1,0:T(8,128)(2,1)S(1)}, u32[]{:S(2)}, u32[]{:S(2)}) collective-permute-start(bf16[16,128]{1,0:T(8,128)(2,1)S(1)} %convolution_convert_fusion.1), channel_id=1, source_target_pairs={{0,1},{1,0},{2,3},{3,2},{4,5},{5,4},{6,7},{7,6},{8,9},{9,8},{10,11... | collective-permute-start | bytes 12296 | tf_op jit(solution)/shard_map/ppermute | solution.py:27
  47.6 2.1 %collective-permute-done.11 = bf16[16,128]{1,0:T(8,128)(2,1)S(1)} collective-permute-done((bf16[16,128]{1,0:T(8,128)(2,1)S(1)}, bf16[16,128]{1,0:T(8,128)(2,1)S(1)}, u32[]{:S(2)}, u32[]{:S(2)}) %collective-permute-start.11) | collective-permute-done | bytes 4128 | tf_op jit(solution)/shard_map/ppermute | solution.py:27
  49.7 0.2 collective-permute-start.12
  49.9 0.0 copy-done
  49.9 0.0 copy-done.5
  49.9 1.1 %fusion.3.particular_ref = f32[16,16,256]{2,1,0:T(8,128)} fusion(bf16[16,256,256]{2,1,0:T(8,128)(2,1)S(1)} %bitcast.25, bf16[16,16,256]{2,1,0:T(8,128)(2,1)S(1)} %copy-done.5), kind=kOutput, calls=%fused_computation.13 | convolution fusion | flops 33554432 | bytes 2490368 | tf_op jit(solution)/shard_map/rlq,lqp->lrp/dot_general | solution.py:236
  51.0 2.4 %collective-permute-done.12 = bf16[16,256]{1,0:T(8,128)(2,1)S(1)} collective-permute-done((bf16[16,256]{1,0:T(8,128)(2,1)S(1)}, bf16[16,256]{1,0:T(8,128)(2,1)S(1)}, u32[]{:S(2)}, u32[]{:S(2)}) %collective-permute-start.12) | collective-permute-done | bytes 8224 | tf_op jit(solution)/shard_map/ppermute | solution.py:27
  53.5 0.0 copy-done.2
  53.5 0.0 copy-start.3
  53.5 0.9 %copy-done.3 = f32[16,16,256]{2,1,0:T(8,128)S(1)} copy-done((f32[16,16,256]{2,1,0:T(8,128)S(1)}, f32[16,16,256]{2,1,0:T(8,128)}, u32[]{:S(2)}) %copy-start.3) | copy-done | bytes 262168
  54.4 0.0 copy-start.7
  54.4 1.0 %copy-done.7 = bf16[1024,256]{1,0:T(8,128)(2,1)S(1)} copy-done((bf16[1024,256]{1,0:T(8,128)(2,1)S(1)}, bf16[1024,256]{1,0:T(8,128)(2,1)}, u32[]{:S(2)}) %copy-start.7) | copy-done | bytes 524312
  55.5 0.0 copy-start.9
  55.5 1.0 %copy-done.9 = bf16[256,768]{1,0:T(8,128)(2,1)S(1)} copy-done((bf16[256,768]{1,0:T(8,128)(2,1)S(1)}, bf16[256,768]{1,0:T(8,128)(2,1)}, u32[]{:S(2)}) %copy-start.9) | copy-done | bytes 393240
  56.5 2.3 %shard_map.119 = f32[16,16,256]{2,1,0:T(8,128)} custom-call(bf16[16,256]{1,0:T(8,128)(2,1)S(1)} %slice.24.first_ref, bf16[16,512]{1,0:T(8,128)(2,1)S(1)} %pad_maximum_fusion.4.mid_ref, bf16[16,384]{1,0:T(8,128)(2,1)S(1)} %slice.23.box_ref, f32[16,16,256]{2,1,0:T(8,128)S(1)} %copy-done.3, bf16[256,768]{1,0:T(8,128)(2,1)S(1)} %copy-done.9, ...), custom_call_target="tpu_custom_call" | custom-call | flops 35651584 | bytes 2752512 | tf_op jit(solution)/shard_map/pallas_call | solution.py:151
  (23 shorter events, 0.3 us)
Async XLA Ops:
  0.0 49.9 %copy-start = (bf16[4096,256]{1,0:T(8,128)(2,1)S(1)}, bf16[4096,256]{1,0:T(8,128)(2,1)}, u32[]{:S(2)}) copy-start(bf16[4096,256]{1,0:T(8,128)(2,1)} %param.14) | copy-start | bytes 6291460
  0.0 1.5 %copy-start.1 = (bf16[640,1024]{1,0:T(8,128)(2,1)S(1)}, bf16[640,1024]{1,0:T(8,128)(2,1)}, u32[]{:S(2)}) copy-start(bf16[640,1024]{1,0:T(8,128)(2,1)} %up_hbm.1) | copy-start | bytes 3932164
  1.5 0.9 %copy-start.4 = (bf16[16,16,256]{2,1,0:T(8,128)(2,1)S(1)}, bf16[16,16,256]{2,1,0:T(8,128)(2,1)}, u32[]{:S(2)}) copy-start(bf16[16,16,256]{2,1,0:T(8,128)(2,1)} %source_hbm.1) | copy-start | bytes 393220
  2.4 1.0 %copy-start.6 = (bf16[1024,256]{1,0:T(8,128)(2,1)S(1)}, bf16[1024,256]{1,0:T(8,128)(2,1)}, u32[]{:S(2)}) copy-start(bf16[1024,256]{1,0:T(8,128)(2,1)} %flux_hbm.1) | copy-start | bytes 1572868
  3.4 1.0 %copy-start.8 = (bf16[256,768]{1,0:T(8,128)(2,1)S(1)}, bf16[256,768]{1,0:T(8,128)(2,1)}, u32[]{:S(2)}) copy-start(bf16[256,768]{1,0:T(8,128)(2,1)} %one_hbm.2) | copy-start | bytes 1179652
  4.4 4.7 %copy-start.12 = (bf16[64,256]{1,0:T(8,128)(2,1)S(1)}, bf16[64,256]{1,0:T(8,128)(2,1)}, u32[]{:S(2)}) copy-start(bf16[64,256]{1,0:T(8,128)(2,1)} %param.22) | copy-start | bytes 98308
  4.4 4.7 %copy-start.13 = (bf16[64,256]{1,0:T(8,128)(2,1)S(1)}, bf16[64,256]{1,0:T(8,128)(2,1)}, u32[]{:S(2)}) copy-start(bf16[64,256]{1,0:T(8,128)(2,1)} %param.23) | copy-start | bytes 98308
  4.4 14.1 %copy-start.10 = (bf16[128,1536]{1,0:T(8,128)(2,1)S(1)}, bf16[128,1536]{1,0:T(8,128)(2,1)}, u32[]{:S(2)}) copy-start(bf16[128,1536]{1,0:T(8,128)(2,1)} %param.20) | copy-start | bytes 1179652
  6.1 5.7 %collective-permute-start = (bf16[16,768]{1,0:T(8,128)(2,1)S(1)}, bf16[16,768]{1,0:T(8,128)(2,1)S(1)}, u32[]{:S(2)}, u32[]{:S(2)}) collective-permute-start(bf16[16,768]{1,0:T(8,128)(2,1)S(1)} %get-tuple-element.15), channel_id=1, source_target_pairs={{0,1},{1,0},{2,3},{3,2},{4,5},{5,4},{6,7},{7,6},{8,9},{9,8},{10,11... | collective-permute-start | bytes 73736 | tf_op jit(solution)/shard_map/ppermute | solution.py:27
  9.1 5.5 %collective-permute-start.1 = (bf16[64,512]{1,0:T(8,128)(2,1)S(1)}, bf16[64,512]{1,0:T(8,128)(2,1)S(1)}, u32[]{:S(2)}, u32[]{:S(2)}) collective-permute-start(bf16[64,512]{1,0:T(8,128)(2,1)S(1)} %constant_dynamic-update-slice_fusion), channel_id=1, source_target_pairs={{0,4},{1,5},{2,6},{3,7},{4,0},{5,1},{6,2},{7,3},{8,12},{9,13},{10,... | collective-permute-start | bytes 196616 | tf_op jit(solution)/shard_map/ppermute | solution.py:27
  14.6 3.8 %collective-permute-start.2 = (bf16[16,768]{1,0:T(8,128)(2,1)S(1)}, bf16[16,768]{1,0:T(8,128)(2,1)S(1)}, u32[]{:S(2)}, u32[]{:S(2)}) collective-permute-start(bf16[16,768]{1,0:T(8,128)(2,1)S(1)} %convert_element_type.55), channel_id=1, source_target_pairs={{0,2},{1,3},{2,0},{3,1},{4,6},{5,7},{6,4},{7,5},{8,10},{9,11},{10,... | collective-permute-start | bytes 73736 | tf_op jit(solution)/shard_map/ppermute | solution.py:27
  16.0 5.0 %collective-permute-start.3 = (bf16[2,64,512]{2,1,0:T(8,128)(2,1)S(1)}, bf16[2,64,512]{2,1,0:T(8,128)(2,1)S(1)}, u32[]{:S(2)}, u32[]{:S(2)}) collective-permute-start(bf16[2,64,512]{2,1,0:T(8,128)(2,1)S(1)} %pad_maximum_fusion.3), channel_id=1, source_target_pairs={{0,1},{1,0},{2,3},{3,2},{4,5},{5,4},{6,7},{7,6},{8,9},{9,8},{10,11... | collective-permute-start | bytes 393224 | tf_op jit(solution)/shard_map/ppermute | solution.py:27
  21.0 5.8 %collective-permute-start.4 = (bf16[16,1536]{1,0:T(8,128)(2,1)S(1)}, bf16[16,1536]{1,0:T(8,128)(2,1)S(1)}, u32[]{:S(2)}, u32[]{:S(2)}) collective-permute-start(bf16[16,1536]{1,0:T(8,128)(2,1)S(1)} %convert_element_type.58), channel_id=1, source_target_pairs={{0,12},{1,13},{2,14},{3,15},{4,8},{5,9},{6,10},{7,11},{8,4},{9,5},... | collective-permute-start | bytes 147464 | tf_op jit(solution)/shard_map/ppermute | solution.py:27
  26.8 3.8 %collective-permute-start.5 = (bf16[16,1536]{1,0:T(8,128)(2,1)S(1)}, bf16[16,1536]{1,0:T(8,128)(2,1)S(1)}, u32[]{:S(2)}, u32[]{:S(2)}) collective-permute-start(bf16[16,1536]{1,0:T(8,128)(2,1)S(1)} %fusion.5), channel_id=1, source_target_pairs={{0,9},{1,8},{2,11},{3,10},{4,13},{5,12},{6,15},{7,14},{8,1},{9,0},... | collective-permute-start | bytes 147464 | tf_op jit(solution)/shard_map/ppermute | solution.py:27
  27.1 8.7 %collective-permute-start.6 = (bf16[2,2,64,512]{3,2,1,0:T(8,128)(2,1)S(1)}, bf16[2,2,64,512]{3,2,1,0:T(8,128)(2,1)S(1)}, u32[]{:S(2)}, u32[]{:S(2)}) collective-permute-start(bf16[2,2,64,512]{3,2,1,0:T(8,128)(2,1)S(1)} %pad_maximum_fusion.2), channel_id=1, source_target_pairs={{0,2},{1,3},{2,0},{3,1},{4,6},{5,7},{6,4},{7,5},{8,10},{9,11},{10,... | collective-permute-start | bytes 786440 | tf_op jit(solution)/shard_map/ppermute | solution.py:27
  35.8 3.9 %collective-permute-start.7 = (bf16[16,1536]{1,0:T(8,128)(2,1)S(1)}, bf16[16,1536]{1,0:T(8,128)(2,1)S(1)}, u32[]{:S(2)}, u32[]{:S(2)}) collective-permute-start(bf16[16,1536]{1,0:T(8,128)(2,1)S(1)} %convert_element_type.62), channel_id=1, source_target_pairs={{0,10},{1,11},{2,8},{3,9},{4,14},{5,15},{6,12},{7,13},{8,2},{9,3},... | collective-permute-start | bytes 147464 | tf_op jit(solution)/shard_map/ppermute | solution.py:27
  36.0 5.1 %collective-permute-start.9 = (bf16[2,2,2,64,512]{4,3,2,1,0:T(8,128)(2,1)S(1)}, bf16[2,2,2,64,512]{4,3,2,1,0:T(8,128)(2,1)}, u32[]{:S(2)}, u32[]{:S(2)}) collective-permute-start(bf16[2,2,2,64,512]{4,3,2,1,0:T(8,128)(2,1)S(1)} %pad_maximum_fusion.1), channel_id=1, source_target_pairs={{0,8},{1,9},{2,10},{3,11},{4,12},{5,13},{6,14},{7,15},{8,0},{9,1},... | collective-permute-start | bytes 1572872 | tf_op jit(solution)/shard_map/ppermute | solution.py:27
  39.8 1.3 %collective-permute-start.8 = (bf16[16,1536]{1,0:T(8,128)(2,1)S(1)}, bf16[16,1536]{1,0:T(8,128)(2,1)S(1)}, u32[]{:S(2)}, u32[]{:S(2)}) collective-permute-start(bf16[16,1536]{1,0:T(8,128)(2,1)S(1)} %fusion.6), channel_id=1, source_target_pairs={{0,8},{1,9},{2,10},{3,11},{4,12},{5,13},{6,14},{7,15},{8,0},{9,1},... | collective-permute-start | bytes 147464 | tf_op jit(solution)/shard_map/ppermute | solution.py:27
  42.2 3.6 %copy-start.11 = (bf16[128,1536]{1,0:T(8,128)(2,1)S(1)}, bf16[128,1536]{1,0:T(8,128)(2,1)}, u32[]{:S(2)}) copy-start(bf16[128,1536]{1,0:T(8,128)(2,1)} %param.21) | copy-start | bytes 1179652
  42.2 7.7 %copy-start.5 = (bf16[16,16,256]{2,1,0:T(8,128)(2,1)S(1)}, bf16[16,16,256]{2,1,0:T(8,128)(2,1)}, u32[]{:S(2)}) copy-start(bf16[16,16,256]{2,1,0:T(8,128)(2,1)} %source_hbm.1) | copy-start | bytes 393220
  42.4 11.1 %copy-start.2 = (bf16[1024,640]{1,0:T(8,128)(2,1)S(1)}, bf16[1024,640]{1,0:T(8,128)(2,1)}, u32[]{:S(2)}) copy-start(bf16[1024,640]{1,0:T(8,128)(2,1)} %down_hbm.1) | copy-start | bytes 3932164
  42.5 3.1 %collective-permute-start.10 = (bf16[16,256]{1,0:T(8,128)(2,1)S(1)}, bf16[16,256]{1,0:T(8,128)(2,1)S(1)}, u32[]{:S(2)}, u32[]{:S(2)}) collective-permute-start(bf16[16,256]{1,0:T(8,128)(2,1)S(1)} %get-tuple-element.35), channel_id=1, source_target_pairs={{0,24},{1,25},{2,26},{3,27},{4,28},{5,29},{6,30},{7,31},{8,16},{9,... | collective-permute-start | bytes 24584 | tf_op jit(solution)/shard_map/ppermute | solution.py:27
  46.1 3.6 %collective-permute-start.11 = (bf16[16,128]{1,0:T(8,128)(2,1)S(1)}, bf16[16,128]{1,0:T(8,128)(2,1)S(1)}, u32[]{:S(2)}, u32[]{:S(2)}) collective-permute-start(bf16[16,128]{1,0:T(8,128)(2,1)S(1)} %convolution_convert_fusion.1), channel_id=1, source_target_pairs={{0,1},{1,0},{2,3},{3,2},{4,5},{5,4},{6,7},{7,6},{8,9},{9,8},{10,11... | collective-permute-start | bytes 12296 | tf_op jit(solution)/shard_map/ppermute | solution.py:27
  49.7 3.7 %collective-permute-start.12 = (bf16[16,256]{1,0:T(8,128)(2,1)S(1)}, bf16[16,256]{1,0:T(8,128)(2,1)S(1)}, u32[]{:S(2)}, u32[]{:S(2)}) collective-permute-start(bf16[16,256]{1,0:T(8,128)(2,1)S(1)} %pad_maximum_fusion.5), channel_id=1, source_target_pairs={{0,2},{1,3},{2,0},{3,1},{4,6},{5,7},{6,4},{7,5},{8,10},{9,11},{10,... | collective-permute-start | bytes 24584 | tf_op jit(solution)/shard_map/ppermute | solution.py:27
  53.5 1.0 %copy-start.3 = (f32[16,16,256]{2,1,0:T(8,128)S(1)}, f32[16,16,256]{2,1,0:T(8,128)}, u32[]{:S(2)}) copy-start(f32[16,16,256]{2,1,0:T(8,128)} %fusion.3.particular_ref) | copy-start | bytes 786436
  54.4 1.0 %copy-start.7 = (bf16[1024,256]{1,0:T(8,128)(2,1)S(1)}, bf16[1024,256]{1,0:T(8,128)(2,1)}, u32[]{:S(2)}) copy-start(bf16[1024,256]{1,0:T(8,128)(2,1)} %lift_hbm.1) | copy-start | bytes 1572868
  55.5 1.0 %copy-start.9 = (bf16[256,768]{1,0:T(8,128)(2,1)S(1)}, bf16[256,768]{1,0:T(8,128)(2,1)}, u32[]{:S(2)}) copy-start(bf16[256,768]{1,0:T(8,128)(2,1)} %one_hbm.3) | copy-start | bytes 1179652

commit v4 on v3

--- a/solution.py
+++ b/solution.py
@@ -107,7 +107,6 @@
         in_specs=[pl.BlockSpec(memory_space=pl.ANY)] * 4,
         scratch_shapes=[pltpu.VMEM(x.shape, x.dtype) for x in operands]
         + [pltpu.SemaphoreType.DMA((4,))],
-        compiler_params=pltpu.CompilerParams(vmem_limit_bytes=2**24),
         cost_estimate=pl.CostEstimate(
             flops=2 * rhs_count * sum(x.size for x in operands[1:]),
             bytes_accessed=2 * sum(x.size for x in operands),
@@ -117,11 +116,11 @@
 
 
 def tail_kernel(
-    first_ref, mid_ref, box_ref, particular_ref, one_hbm, down_hbm, lift_hbm, out_ref, *rest
+    first_ref, mid_ref, box_ref, one_hbm, down_hbm, lift_hbm, particular_hbm, out_ref, *rest
 ):
     *scratch, sems = rest
-    down_one, box_down, leaf_lift = scratch
-    copies = fetch((one_hbm, down_hbm, lift_hbm), scratch, sems)
+    down_one, box_down, leaf_lift, particular = scratch
+    copies = fetch((one_hbm, down_hbm, lift_hbm, particular_hbm), scratch, sems)
     leaves = out_ref.shape[1]
     edge_count = leaf_lift.shape[0] // leaves
     inner, inner_dev = first_ref.shape[1], box_ref.shape[1]
@@ -134,6 +133,7 @@
         contract(box_ref[...], box_down[:, :inner_dev]) + contract(bound, box_down[:, inner_dev:])
     )
     copies[2].wait()
+    copies[3].wait()
     pair_count = 2 * edge_count
     column = lax.broadcasted_iota(jnp.int32, (edges.shape[0], pair_count), 1)
     for leaf in range(leaves):
@@ -142,27 +142,27 @@
         mine = (column < edge_count) if leaf % 2 == 0 else (column >= edge_count)
         part = rounded(jnp.where(mine, both, 0.0))
         lifted = product(part, leaf_lift[start : start + pair_count, :])
-        out_ref[:, leaf, :] = lifted + particular_ref[leaf]
+        out_ref[:, leaf, :] = lifted + particular[leaf]
 
 
 def tail(first_inner, mid_bound, box_inner, particular, down_one, box_down, leaf_lift):
     leaves, rhs_count, points = particular.shape
     weights = (down_one, box_down, leaf_lift)
+    fetched = weights + (particular,)
     return pl.pallas_call(
         tail_kernel,
         out_shape=jax.ShapeDtypeStruct((rhs_count, leaves, points), jnp.float32),
-        in_specs=[pl.BlockSpec(memory_space=pltpu.VMEM)] * 4
-        + [pl.BlockSpec(memory_space=pl.ANY)] * 3,
+        in_specs=[pl.BlockSpec(memory_space=pltpu.VMEM)] * 3
+        + [pl.BlockSpec(memory_space=pl.ANY)] * 4,
         out_specs=pl.BlockSpec(memory_space=pltpu.VMEM),
-        scratch_shapes=[pltpu.VMEM(x.shape, x.dtype) for x in weights]
-        + [pltpu.SemaphoreType.DMA((3,))],
-        compiler_params=pltpu.CompilerParams(vmem_limit_bytes=2**24),
+        scratch_shapes=[pltpu.VMEM(x.shape, x.dtype) for x in fetched]
+        + [pltpu.SemaphoreType.DMA((4,))],
         cost_estimate=pl.CostEstimate(
             flops=2 * rhs_count * sum(x.size for x in weights),
             bytes_accessed=2 * sum(x.size for x in weights) + 8 * particular.size,
             transcendentals=0,
         ),
-    )(first_inner, mid_bound, box_inner, particular, *weights)
+    )(first_inner, mid_bound, box_inner, *fetched)
 
 
 def per_device(

time: 59.2 us -> 54.3 us (0.917)
  local copies, waits for them, and re-layouts: 7.43 us -> 1.22 us
  Pallas kernels: 3.94 us -> 6.97 us
  waiting for transfers between devices: 32.3 us -> 29.6 us
  other arithmetic: 1.52 us -> 2.68 us
    unnamed x29 -> x15, local copies, waits for them, and re-layouts: 7.42 us -> 0.04 us
    ppermute x13, waiting for transfers between devices: 32.3 us -> 29.6 us  [swap(): return lax.ppermute(value, AXES, [(i, i ^ mask) for i in range(count)])]
    pallas_call x1, Pallas kernels: 2.32 us -> 3.88 us  [tail(): pl.pallas_call(tail_kernel, out_shape=jax.ShapeDtypeStruct((rhs_count, le...]
    pallas_call x1, Pallas kernels: 1.63 us -> 3.09 us  [head(): pl.pallas_call(head_kernel, out_shape=(jax.ShapeDtypeStruct((rhs_count, b...]
    add x1, other arithmetic: 0.01 us -> 0.81 us  [per_device(): first_sum = first_sum + swap(first_low, 1).astype(jnp.float32)]
    slice x1, local copies, waits for them, and re-layouts: 0.01 us -> 0.6 us  [per_device(): box_state[:, :inner_dev]]
    concatenate x2, other arithmetic: 0.01 us -> 0.61 us  [placed(): jnp.concatenate([jnp.where(upper, high, low), jnp.where(upper, low, high)...]
  transfers between devices with their start and end apart: 13 -> 13, of which waited for: 11 -> 11; matrix products, arithmetic and copies ran while one was open for 3% -> 8% of each run, Pallas kernels for 0% -> 0%
where the time goes in v4:
time: 54.3 us; the launch traced here: 54 us
  waiting for transfers between devices  29.6 us (55%)
  starting transfers between devices  11.4 us (21%)
  Pallas kernels  6.97 us (13%)
  other arithmetic  2.68 us (5%)
  matrix products  1.87 us (3%)
  local copies, waits for them, and re-layouts  1.22 us (2%)
    ppermute x13, waiting for transfers between devices, swap(): return lax.ppermute(value, AXES, [(i, i ^ mask) for i in range(count)])  29.6 us
    ppermute x13, starting transfers between devices, swap(): return lax.ppermute(value, AXES, [(i, i ^ mask) for i in range(count)])  11.4 us
    pallas_call x1, Pallas kernels, tail(): pl.pallas_call(tail_kernel, out_shape=jax.ShapeDtypeStruct((rhs_count, le...  3.88 us
    pallas_call x1, Pallas kernels, head(): pl.pallas_call(head_kernel, out_shape=(jax.ShapeDtypeStruct((rhs_count, b...  3.09 us
    another operation x8, other arithmetic, joined_pair(): jnp.stack([jnp.where(upper, other, joined), jnp.where(upper, joined, othe...  1.17 us
    dot_general x1, matrix products, per_device(): jnp.einsum('rlq,lqp->lrp', source, leaf_particular.reshape(leaves, points...  1.09 us
  transfers between devices with their start and end apart: 13, of which 11 were waited for; matrix products, arithmetic and copies ran while one was open for 8% of the time, Pallas kernels for 0%

profile of v4, /device:TPU:0, one launch (start us, length us, event | category | flops | bytes accessed | tf_op | source)
XLA Modules:
  0.0 54.0 jit_solution(5655885071118849455)
XLA Ops:
  0.0 0.0 copy-start
  0.0 0.0 copy-start.4
  0.0 0.0 copy-start.5
  0.0 0.0 copy-start.2
  0.0 3.1 %shard_map.118 = (bf16[16,640]{1,0:T(8,128)(2,1)}, f32[16,768]{1,0:T(8,128)}, bf16[16,768]{1,0:T(8,128)(2,1)}) custom-call(bf16[16,16,256]{2,1,0:T(8,128)(2,1)} %source_hbm.1, bf16[1024,256]{1,0:T(8,128)(2,1)} %flux_hbm.1, bf16[640,1024]{1,0:T(8,128)(2,1)} %up_hbm.1, bf16[256,768]{1,0:T(8,128)(2,1)} %one_hbm.2), custom_call_target="tpu_custom_call" | custom-call | flops 35651584 | bytes 2359296 | tf_op jit(solution)/shard_map/pallas_call | solution.py:100
  3.1 3.0 %collective-permute-start = (bf16[16,768]{1,0:T(8,128)(2,1)}, bf16[16,768]{1,0:T(8,128)(2,1)S(1)}, u32[]{:S(2)}, u32[]{:S(2)}) collective-permute-start(bf16[16,768]{1,0:T(8,128)(2,1)} %get-tuple-element.15), channel_id=1, source_target_pairs={{0,1},{1,0},{2,3},{3,2},{4,5},{5,4},{6,7},{7,6},{8,9},{9,8},{10,11... | collective-permute-start | bytes 73736 | tf_op jit(solution)/shard_map/ppermute | solution.py:27
  6.2 0.0 copy-done.4
  6.2 0.0 copy-done.5
  6.2 2.7 %collective-permute-start.1 = (bf16[64,512]{1,0:T(8,128)(2,1)S(1)}, bf16[64,512]{1,0:T(8,128)(2,1)S(1)}, u32[]{:S(2)}, u32[]{:S(2)}) collective-permute-start(bf16[64,512]{1,0:T(8,128)(2,1)S(1)} %constant_dynamic-update-slice_fusion), channel_id=1, source_target_pairs={{0,4},{1,5},{2,6},{3,7},{4,0},{5,1},{6,2},{7,3},{8,12},{9,13},{10,... | collective-permute-start | bytes 196616 | tf_op jit(solution)/shard_map/ppermute | solution.py:27
  8.8 0.0 collective-permute-done
  8.8 0.8 %convert_add_fusion.3 = f32[16,768]{1,0:T(8,128)S(1)} fusion(f32[16,768]{1,0:T(8,128)} %get-tuple-element.14, bf16[16,768]{1,0:T(8,128)(2,1)S(1)} %collective-permute-done), kind=kLoop, calls=%fused_computation.29 | loop fusion | flops 24576 | bytes 122880 | tf_op jit(solution)/shard_map/add | solution.py:201
  9.6 2.1 %collective-permute-done.1 = bf16[64,512]{1,0:T(8,128)(2,1)S(1)} collective-permute-done((bf16[64,512]{1,0:T(8,128)(2,1)S(1)}, bf16[64,512]{1,0:T(8,128)(2,1)S(1)}, u32[]{:S(2)}, u32[]{:S(2)}) %collective-permute-start.1) | collective-permute-done | bytes 65568 | tf_op jit(solution)/shard_map/ppermute | solution.py:27
  11.7 1.3 %collective-permute-start.2 = (bf16[16,768]{1,0:T(8,128)(2,1)S(1)}, bf16[16,768]{1,0:T(8,128)(2,1)S(1)}, u32[]{:S(2)}, u32[]{:S(2)}) collective-permute-start(bf16[16,768]{1,0:T(8,128)(2,1)S(1)} %convert_element_type.55), channel_id=1, source_target_pairs={{0,2},{1,3},{2,0},{3,1},{4,6},{5,7},{6,4},{7,5},{8,10},{9,11},{10,... | collective-permute-start | bytes 73736 | tf_op jit(solution)/shard_map/ppermute | solution.py:27
  13.0 0.6 %collective-permute-start.3 = (bf16[2,64,512]{2,1,0:T(8,128)(2,1)S(1)}, bf16[2,64,512]{2,1,0:T(8,128)(2,1)S(1)}, u32[]{:S(2)}, u32[]{:S(2)}) collective-permute-start(bf16[2,64,512]{2,1,0:T(8,128)(2,1)S(1)} %pad_maximum_fusion.3), channel_id=1, source_target_pairs={{0,1},{1,0},{2,3},{3,2},{4,5},{5,4},{6,7},{7,6},{8,9},{9,8},{10,11... | collective-permute-start | bytes 393224 | tf_op jit(solution)/shard_map/ppermute | solution.py:27
  13.6 1.9 %collective-permute-done.2 = bf16[16,768]{1,0:T(8,128)(2,1)S(1)} collective-permute-done((bf16[16,768]{1,0:T(8,128)(2,1)S(1)}, bf16[16,768]{1,0:T(8,128)(2,1)S(1)}, u32[]{:S(2)}, u32[]{:S(2)}) %collective-permute-start.2) | collective-permute-done | bytes 24608 | tf_op jit(solution)/shard_map/ppermute | solution.py:27
  15.5 0.0 copy-done.2
  15.6 0.2 fusion.11
  15.7 2.3 %collective-permute-done.3 = bf16[2,64,512]{2,1,0:T(8,128)(2,1)S(1)} collective-permute-done((bf16[2,64,512]{2,1,0:T(8,128)(2,1)S(1)}, bf16[2,64,512]{2,1,0:T(8,128)(2,1)S(1)}, u32[]{:S(2)}, u32[]{:S(2)}) %collective-permute-start.3) | collective-permute-done | bytes 131104 | tf_op jit(solution)/shard_map/ppermute | solution.py:27
  18.1 0.1 collective-permute-start.4
  18.2 5.7 %collective-permute-done.4 = bf16[16,1536]{1,0:T(8,128)(2,1)S(1)} collective-permute-done((bf16[16,1536]{1,0:T(8,128)(2,1)S(1)}, bf16[16,1536]{1,0:T(8,128)(2,1)S(1)}, u32[]{:S(2)}, u32[]{:S(2)}) %collective-permute-start.4) | collective-permute-done | bytes 49184 | tf_op jit(solution)/shard_map/ppermute | solution.py:27
  23.9 0.3 collective-permute-start.5
  24.2 0.1 collective-permute-start.6
  24.3 3.4 %collective-permute-done.5 = bf16[16,1536]{1,0:T(8,128)(2,1)S(1)} collective-permute-done((bf16[16,1536]{1,0:T(8,128)(2,1)S(1)}, bf16[16,1536]{1,0:T(8,128)(2,1)S(1)}, u32[]{:S(2)}, u32[]{:S(2)}) %collective-permute-start.5) | collective-permute-done | bytes 49184 | tf_op jit(solution)/shard_map/ppermute | solution.py:27
  27.7 5.2 %collective-permute-done.6 = bf16[2,2,64,512]{3,2,1,0:T(8,128)(2,1)S(1)} collective-permute-done((bf16[2,2,64,512]{3,2,1,0:T(8,128)(2,1)S(1)}, bf16[2,2,64,512]{3,2,1,0:T(8,128)(2,1)S(1)}, u32[]{:S(2)}, u32[]{:S(2)}) %collective-permute-start.6) | collective-permute-done | bytes 262176 | tf_op jit(solution)/shard_map/ppermute | solution.py:27
  32.9 0.1 collective-permute-start.7
  33.0 0.9 %pad_maximum_fusion.1 = bf16[2,2,2,64,512]{4,3,2,1,0:T(8,128)(2,1)} fusion(bf16[2,1,2,64,512]{4,3,2,1,0:T(8,128)(2,1)S(1)} %get-tuple-element.26, bf16[2,1,2,64,512]{4,3,2,1,0:T(8,128)(2,1)S(1)} %get-tuple-element.25), kind=kLoop, calls=%fused_computation.6 | loop fusion | flops 262144 | bytes 1048576 | tf_op jit(solution)/shard_map/stack | solution.py:54
  33.9 0.3 collective-permute-start.9
  34.2 2.6 %collective-permute-done.7 = bf16[16,1536]{1,0:T(8,128)(2,1)S(1)} collective-permute-done((bf16[16,1536]{1,0:T(8,128)(2,1)S(1)}, bf16[16,1536]{1,0:T(8,128)(2,1)S(1)}, u32[]{:S(2)}, u32[]{:S(2)}) %collective-permute-start.7) | collective-permute-done | bytes 49184 | tf_op jit(solution)/shard_map/ppermute | solution.py:27
  36.8 0.1 collective-permute-start.8
  36.9 1.2 %collective-permute-done.8 = bf16[16,1536]{1,0:T(8,128)(2,1)S(1)} collective-permute-done((bf16[16,1536]{1,0:T(8,128)(2,1)S(1)}, bf16[16,1536]{1,0:T(8,128)(2,1)S(1)}, u32[]{:S(2)}, u32[]{:S(2)}) %collective-permute-start.8) | collective-permute-done | bytes 49184 | tf_op jit(solution)/shard_map/ppermute | solution.py:27
  38.2 0.0 collective-permute-done.9
  38.2 0.1 select_bitcast_fusion.1
  38.3 0.0 copy-start.3
  38.3 0.0 copy-start.1
  38.3 0.1 pad_maximum_fusion
  38.4 0.0 copy-start.6
  38.4 0.2 fusion.15
  38.6 1.3 %collective-permute-start.10 = (bf16[16,256]{1,0:T(8,128)(2,1)S(1)}, bf16[16,256]{1,0:T(8,128)(2,1)S(1)}, u32[]{:S(2)}, u32[]{:S(2)}) collective-permute-start(bf16[16,256]{1,0:T(8,128)(2,1)S(1)} %get-tuple-element.35), channel_id=1, source_target_pairs={{0,24},{1,25},{2,26},{3,27},{4,28},{5,29},{6,30},{7,31},{8,16},{9,... | collective-permute-start | bytes 24584 | tf_op jit(solution)/shard_map/ppermute | solution.py:27
  39.8 1.8 %collective-permute-done.10 = bf16[16,256]{1,0:T(8,128)(2,1)S(1)} collective-permute-done((bf16[16,256]{1,0:T(8,128)(2,1)S(1)}, bf16[16,256]{1,0:T(8,128)(2,1)S(1)}, u32[]{:S(2)}, u32[]{:S(2)}) %collective-permute-start.10) | collective-permute-done | bytes 8224 | tf_op jit(solution)/shard_map/ppermute | solution.py:27
  41.7 0.2 convolution_convert_fusion
  41.9 0.0 copy-done.3
  41.9 0.2 convolution_convert_fusion.1
  42.1 1.6 %collective-permute-start.11 = (bf16[16,128]{1,0:T(8,128)(2,1)S(1)}, bf16[16,128]{1,0:T(8,128)(2,1)S(1)}, u32[]{:S(2)}, u32[]{:S(2)}) collective-permute-start(bf16[16,128]{1,0:T(8,128)(2,1)S(1)} %convolution_convert_fusion.1), channel_id=1, source_target_pairs={{0,1},{1,0},{2,3},{3,2},{4,5},{5,4},{6,7},{7,6},{8,9},{9,8},{10,11... | collective-permute-start | bytes 12296 | tf_op jit(solution)/shard_map/ppermute | solution.py:27
  43.7 2.1 %collective-permute-done.11 = bf16[16,128]{1,0:T(8,128)(2,1)S(1)} collective-permute-done((bf16[16,128]{1,0:T(8,128)(2,1)S(1)}, bf16[16,128]{1,0:T(8,128)(2,1)S(1)}, u32[]{:S(2)}, u32[]{:S(2)}) %collective-permute-start.11) | collective-permute-done | bytes 4128 | tf_op jit(solution)/shard_map/ppermute | solution.py:27
  45.8 0.2 collective-permute-start.12
  45.9 0.0 copy-done
  45.9 0.0 copy-done.1
  45.9 1.1 %fusion.3.particular_hbm = f32[16,16,256]{2,1,0:T(8,128)} fusion(bf16[16,256,256]{2,1,0:T(8,128)(2,1)S(1)} %bitcast.25, bf16[16,16,256]{2,1,0:T(8,128)(2,1)S(1)} %copy-done.1), kind=kOutput, calls=%fused_computation.13 | convolution fusion | flops 33554432 | bytes 2490368 | tf_op jit(solution)/shard_map/rlq,lqp->lrp/dot_general | solution.py:236
  47.0 0.0 copy-done.6
  47.0 0.6 %slice.23.box_ref = bf16[16,384]{1,0:T(8,128)(2,1)} slice(bf16[16,640]{1,0:T(8,128)(2,1)S(1)} %copy-done.6), slice={[0:16], [0:384]} | slice | bytes 24576 | tf_op jit(solution)/shard_map/slice | solution.py:245
  47.6 0.6 %slice.24.first_ref = bf16[16,256]{1,0:T(8,128)(2,1)} slice(bf16[16,768]{1,0:T(8,128)(2,1)S(1)} %add_convert_fusion.1), slice={[0:16], [0:256]} | slice | bytes 16384 | tf_op jit(solution)/shard_map/slice | solution.py:243
  48.2 1.3 %collective-permute-done.12 = bf16[16,256]{1,0:T(8,128)(2,1)S(1)} collective-permute-done((bf16[16,256]{1,0:T(8,128)(2,1)S(1)}, bf16[16,256]{1,0:T(8,128)(2,1)S(1)}, u32[]{:S(2)}, u32[]{:S(2)}) %collective-permute-start.12) | collective-permute-done | bytes 8224 | tf_op jit(solution)/shard_map/ppermute | solution.py:27
  49.5 0.6 %pad_maximum_fusion.4.mid_ref = bf16[16,512]{1,0:T(8,128)(2,1)} fusion(bf16[16,256]{1,0:T(8,128)(2,1)S(1)} %get-tuple-element.32, bf16[16,256]{1,0:T(8,128)(2,1)S(1)} %get-tuple-element.31), kind=kLoop, calls=%fused_computation.31 | loop fusion | flops 32768 | bytes 32768 | tf_op jit(solution)/shard_map/concatenate | solution.py:48
  50.1 3.9 %shard_map.119 = f32[16,16,256]{2,1,0:T(8,128)} custom-call(bf16[16,256]{1,0:T(8,128)(2,1)} %slice.24.first_ref, bf16[16,512]{1,0:T(8,128)(2,1)} %pad_maximum_fusion.4.mid_ref, bf16[16,384]{1,0:T(8,128)(2,1)} %slice.23.box_ref, bf16[256,768]{1,0:T(8,128)(2,1)} %one_hbm.3, bf16[1024,640]{1,0:T(8,128)(2,1)} %down_hbm.1, bf16[1024,256]{1,0:T(8,128)(2,1)} %lift_hbm.1, ...), custom_call_target="tpu_custom_call" | custom-call | flops 35651584 | bytes 2752512 | tf_op jit(solution)/shard_map/pallas_call | solution.py:152
  (19 shorter events, 0.2 us)
Async XLA Ops:
  0.0 45.9 %copy-start = (bf16[4096,256]{1,0:T(8,128)(2,1)S(1)}, bf16[4096,256]{1,0:T(8,128)(2,1)}, u32[]{:S(2)}) copy-start(bf16[4096,256]{1,0:T(8,128)(2,1)} %param.14) | copy-start | bytes 6291460
  0.0 6.2 %copy-start.4 = (bf16[64,256]{1,0:T(8,128)(2,1)S(1)}, bf16[64,256]{1,0:T(8,128)(2,1)}, u32[]{:S(2)}) copy-start(bf16[64,256]{1,0:T(8,128)(2,1)} %param.22) | copy-start | bytes 98308
  0.0 6.2 %copy-start.5 = (bf16[64,256]{1,0:T(8,128)(2,1)S(1)}, bf16[64,256]{1,0:T(8,128)(2,1)}, u32[]{:S(2)}) copy-start(bf16[64,256]{1,0:T(8,128)(2,1)} %param.23) | copy-start | bytes 98308
  0.0 15.5 %copy-start.2 = (bf16[128,1536]{1,0:T(8,128)(2,1)S(1)}, bf16[128,1536]{1,0:T(8,128)(2,1)}, u32[]{:S(2)}) copy-start(bf16[128,1536]{1,0:T(8,128)(2,1)} %param.20) | copy-start | bytes 1179652
  3.1 5.7 %collective-permute-start = (bf16[16,768]{1,0:T(8,128)(2,1)}, bf16[16,768]{1,0:T(8,128)(2,1)S(1)}, u32[]{:S(2)}, u32[]{:S(2)}) collective-permute-start(bf16[16,768]{1,0:T(8,128)(2,1)} %get-tuple-element.15), channel_id=1, source_target_pairs={{0,1},{1,0},{2,3},{3,2},{4,5},{5,4},{6,7},{7,6},{8,9},{9,8},{10,11... | collective-permute-start | bytes 73736 | tf_op jit(solution)/shard_map/ppermute | solution.py:27
  6.2 5.5 %collective-permute-start.1 = (bf16[64,512]{1,0:T(8,128)(2,1)S(1)}, bf16[64,512]{1,0:T(8,128)(2,1)S(1)}, u32[]{:S(2)}, u32[]{:S(2)}) collective-permute-start(bf16[64,512]{1,0:T(8,128)(2,1)S(1)} %constant_dynamic-update-slice_fusion), channel_id=1, source_target_pairs={{0,4},{1,5},{2,6},{3,7},{4,0},{5,1},{6,2},{7,3},{8,12},{9,13},{10,... | collective-permute-start | bytes 196616 | tf_op jit(solution)/shard_map/ppermute | solution.py:27
  11.7 3.8 %collective-permute-start.2 = (bf16[16,768]{1,0:T(8,128)(2,1)S(1)}, bf16[16,768]{1,0:T(8,128)(2,1)S(1)}, u32[]{:S(2)}, u32[]{:S(2)}) collective-permute-start(bf16[16,768]{1,0:T(8,128)(2,1)S(1)} %convert_element_type.55), channel_id=1, source_target_pairs={{0,2},{1,3},{2,0},{3,1},{4,6},{5,7},{6,4},{7,5},{8,10},{9,11},{10,... | collective-permute-start | bytes 73736 | tf_op jit(solution)/shard_map/ppermute | solution.py:27
  13.0 5.0 %collective-permute-start.3 = (bf16[2,64,512]{2,1,0:T(8,128)(2,1)S(1)}, bf16[2,64,512]{2,1,0:T(8,128)(2,1)S(1)}, u32[]{:S(2)}, u32[]{:S(2)}) collective-permute-start(bf16[2,64,512]{2,1,0:T(8,128)(2,1)S(1)} %pad_maximum_fusion.3), channel_id=1, source_target_pairs={{0,1},{1,0},{2,3},{3,2},{4,5},{5,4},{6,7},{7,6},{8,9},{9,8},{10,11... | collective-permute-start | bytes 393224 | tf_op jit(solution)/shard_map/ppermute | solution.py:27
  18.1 5.8 %collective-permute-start.4 = (bf16[16,1536]{1,0:T(8,128)(2,1)S(1)}, bf16[16,1536]{1,0:T(8,128)(2,1)S(1)}, u32[]{:S(2)}, u32[]{:S(2)}) collective-permute-start(bf16[16,1536]{1,0:T(8,128)(2,1)S(1)} %convert_element_type.58), channel_id=1, source_target_pairs={{0,12},{1,13},{2,14},{3,15},{4,8},{5,9},{6,10},{7,11},{8,4},{9,5},... | collective-permute-start | bytes 147464 | tf_op jit(solution)/shard_map/ppermute | solution.py:27
  23.9 3.8 %collective-permute-start.5 = (bf16[16,1536]{1,0:T(8,128)(2,1)S(1)}, bf16[16,1536]{1,0:T(8,128)(2,1)S(1)}, u32[]{:S(2)}, u32[]{:S(2)}) collective-permute-start(bf16[16,1536]{1,0:T(8,128)(2,1)S(1)} %fusion.5), channel_id=1, source_target_pairs={{0,9},{1,8},{2,11},{3,10},{4,13},{5,12},{6,15},{7,14},{8,1},{9,0},... | collective-permute-start | bytes 147464 | tf_op jit(solution)/shard_map/ppermute | solution.py:27
  24.2 8.7 %collective-permute-start.6 = (bf16[2,2,64,512]{3,2,1,0:T(8,128)(2,1)S(1)}, bf16[2,2,64,512]{3,2,1,0:T(8,128)(2,1)S(1)}, u32[]{:S(2)}, u32[]{:S(2)}) collective-permute-start(bf16[2,2,64,512]{3,2,1,0:T(8,128)(2,1)S(1)} %pad_maximum_fusion.2), channel_id=1, source_target_pairs={{0,2},{1,3},{2,0},{3,1},{4,6},{5,7},{6,4},{7,5},{8,10},{9,11},{10,... | collective-permute-start | bytes 786440 | tf_op jit(solution)/shard_map/ppermute | solution.py:27
  32.9 3.9 %collective-permute-start.7 = (bf16[16,1536]{1,0:T(8,128)(2,1)S(1)}, bf16[16,1536]{1,0:T(8,128)(2,1)S(1)}, u32[]{:S(2)}, u32[]{:S(2)}) collective-permute-start(bf16[16,1536]{1,0:T(8,128)(2,1)S(1)} %convert_element_type.62), channel_id=1, source_target_pairs={{0,10},{1,11},{2,8},{3,9},{4,14},{5,15},{6,12},{7,13},{8,2},{9,3},... | collective-permute-start | bytes 147464 | tf_op jit(solution)/shard_map/ppermute | solution.py:27
  33.9 4.3 %collective-permute-start.9 = (bf16[2,2,2,64,512]{4,3,2,1,0:T(8,128)(2,1)}, bf16[2,2,2,64,512]{4,3,2,1,0:T(8,128)(2,1)S(1)}, u32[]{:S(2)}, u32[]{:S(2)}) collective-permute-start(bf16[2,2,2,64,512]{4,3,2,1,0:T(8,128)(2,1)} %pad_maximum_fusion.1), channel_id=1, source_target_pairs={{0,8},{1,9},{2,10},{3,11},{4,12},{5,13},{6,14},{7,15},{8,0},{9,1},... | collective-permute-start | bytes 1572872 | tf_op jit(solution)/shard_map/ppermute | solution.py:27
  36.8 1.3 %collective-permute-start.8 = (bf16[16,1536]{1,0:T(8,128)(2,1)S(1)}, bf16[16,1536]{1,0:T(8,128)(2,1)S(1)}, u32[]{:S(2)}, u32[]{:S(2)}) collective-permute-start(bf16[16,1536]{1,0:T(8,128)(2,1)S(1)} %fusion.6), channel_id=1, source_target_pairs={{0,8},{1,9},{2,10},{3,11},{4,12},{5,13},{6,14},{7,15},{8,0},{9,1},... | collective-permute-start | bytes 147464 | tf_op jit(solution)/shard_map/ppermute | solution.py:27
  38.3 3.6 %copy-start.3 = (bf16[128,1536]{1,0:T(8,128)(2,1)S(1)}, bf16[128,1536]{1,0:T(8,128)(2,1)}, u32[]{:S(2)}) copy-start(bf16[128,1536]{1,0:T(8,128)(2,1)} %param.21) | copy-start | bytes 1179652
  38.3 7.7 %copy-start.1 = (bf16[16,16,256]{2,1,0:T(8,128)(2,1)S(1)}, bf16[16,16,256]{2,1,0:T(8,128)(2,1)}, u32[]{:S(2)}) copy-start(bf16[16,16,256]{2,1,0:T(8,128)(2,1)} %source_hbm.1) | copy-start | bytes 393220
  38.4 8.6 %copy-start.6 = (bf16[16,640]{1,0:T(8,128)(2,1)S(1)}, bf16[16,640]{1,0:T(8,128)(2,1)}, u32[]{:S(2)}) copy-start(bf16[16,640]{1,0:T(8,128)(2,1)} %get-tuple-element.22) | copy-start | bytes 61444
  38.6 3.1 %collective-permute-start.10 = (bf16[16,256]{1,0:T(8,128)(2,1)S(1)}, bf16[16,256]{1,0:T(8,128)(2,1)S(1)}, u32[]{:S(2)}, u32[]{:S(2)}) collective-permute-start(bf16[16,256]{1,0:T(8,128)(2,1)S(1)} %get-tuple-element.35), channel_id=1, source_target_pairs={{0,24},{1,25},{2,26},{3,27},{4,28},{5,29},{6,30},{7,31},{8,16},{9,... | collective-permute-start | bytes 24584 | tf_op jit(solution)/shard_map/ppermute | solution.py:27
  42.1 3.6 %collective-permute-start.11 = (bf16[16,128]{1,0:T(8,128)(2,1)S(1)}, bf16[16,128]{1,0:T(8,128)(2,1)S(1)}, u32[]{:S(2)}, u32[]{:S(2)}) collective-permute-start(bf16[16,128]{1,0:T(8,128)(2,1)S(1)} %convolution_convert_fusion.1), channel_id=1, source_target_pairs={{0,1},{1,0},{2,3},{3,2},{4,5},{5,4},{6,7},{7,6},{8,9},{9,8},{10,11... | collective-permute-start | bytes 12296 | tf_op jit(solution)/shard_map/ppermute | solution.py:27
  45.8 3.7 %collective-permute-start.12 = (bf16[16,256]{1,0:T(8,128)(2,1)S(1)}, bf16[16,256]{1,0:T(8,128)(2,1)S(1)}, u32[]{:S(2)}, u32[]{:S(2)}) collective-permute-start(bf16[16,256]{1,0:T(8,128)(2,1)S(1)} %pad_maximum_fusion.5), channel_id=1, source_target_pairs={{0,2},{1,3},{2,0},{3,1},{4,6},{5,7},{6,4},{7,5},{8,10},{9,11},{10,... | collective-permute-start | bytes 24584 | tf_op jit(solution)/shard_map/ppermute | solution.py:27

commit v5 on v4

--- a/solution.py
+++ b/solution.py
@@ -54,10 +54,6 @@
     return jnp.stack(
         [jnp.where(upper, other, joined), jnp.where(upper, joined, other)], axis=axis
     )
-
-
-def tie(*values):
-    return lax.optimization_barrier(values)
 
 
 def fetch(sources, scratch, sems):
@@ -200,7 +196,6 @@
     roots_far = swap(roots, far)
     first_sum = first_sum + swap(first_low, 1).astype(jnp.float32)
 
-    first_sum, roots_far = tie(first_sum, roots_far)
     roots = joined_pair(roots, roots_far, place & far != 0, 0)
     roots_one = swap(roots, 1)
     first_sum = partner_sum(first_sum, near)
@@ -208,13 +203,11 @@
 
     piece = lax.dynamic_slice_in_dim(first_state, k_zero + place % quad * width, width, 1)
     second_sum = product(piece, up_two)
-    second_sum, roots_one = tie(second_sum, roots_one)
     roots = joined_pair(roots, roots_one, place & 1 != 0, 1)
     roots_near = swap(roots, near)
     second_sum = partner_sum(second_sum, far | pair)
 
     second_sum = partner_sum(second_sum, 1 | pair)
-    second_sum, roots_near = tie(second_sum, roots_near)
     roots = joined_pair(roots, roots_near, place & near != 0, 1)
     roots_pair = swap(roots, pair)
     second_sum = partner_sum(second_sum, near | pair)

time: 54.3 us -> 50 us (0.921)
  waiting for transfers between devices: 29.6 us -> 19.9 us
  starting transfers between devices: 11.4 us -> 16.1 us
  other arithmetic: 2.68 us -> 3.47 us
    ppermute x13, waiting for transfers between devices: 29.6 us -> 19.9 us  [swap(): return lax.ppermute(value, AXES, [(i, i ^ mask) for i in range(count)])]
    ppermute x13, starting transfers between devices: 11.4 us -> 16.1 us  [swap(): return lax.ppermute(value, AXES, [(i, i ^ mask) for i in range(count)])]
    convert_element_type x7 -> x6, other arithmetic: 0.07 us -> 1.71 us  [rounded(): return value.astype(jnp.bfloat16)]
    add x2 -> x0, other arithmetic: 0.82 us -> none  [the longest x1 0.81 us: per_device(): first_sum = first_sum + swap(first_low, 1).astype(jnp.float32)]
  transfers between devices with their start and end apart: 13 -> 13, of which waited for: 11 -> 11; matrix products, arithmetic and copies ran while one was open for 8% -> 9% of each run, Pallas kernels for 0% -> 0%
where the time goes in v5:
time: 50 us; the launch traced here: 49.7 us
  waiting for transfers between devices  19.9 us (40%)
  starting transfers between devices  16.1 us (32%)
  Pallas kernels  6.98 us (14%)
  other arithmetic  3.47 us (7%)
  matrix products  1.89 us (4%)
  local copies, waits for them, and re-layouts  1.24 us (2%)
    ppermute x13, waiting for transfers between devices, swap(): return lax.ppermute(value, AXES, [(i, i ^ mask) for i in range(count)])  19.9 us
    ppermute x13, starting transfers between devices, swap(): return lax.ppermute(value, AXES, [(i, i ^ mask) for i in range(count)])  16.1 us
    pallas_call x1, Pallas kernels, tail(): pl.pallas_call(tail_kernel, out_shape=jax.ShapeDtypeStruct((rhs_count, le...  3.88 us
    pallas_call x1, Pallas kernels, head(): pl.pallas_call(head_kernel, out_shape=(jax.ShapeDtypeStruct((rhs_count, b...  3.09 us
    convert_element_type x6, other arithmetic, rounded(): return value.astype(jnp.bfloat16)  1.71 us
    another operation x8, other arithmetic, joined_pair(): jnp.stack([jnp.where(upper, other, joined), jnp.where(upper, joined, othe...  1.15 us
    dot_general x1, matrix products, per_device(): jnp.einsum('rlq,lqp->lrp', source, leaf_particular.reshape(leaves, points...  1.1 us
  transfers between devices with their start and end apart: 13, of which 11 were waited for; matrix products, arithmetic and copies ran while one was open for 9% of the time, Pallas kernels for 0%

profile of v5, /device:TPU:0, one launch (start us, length us, event | category | flops | bytes accessed | tf_op | source)
XLA Modules:
  0.0 49.7 jit_solution(4215371201617532559)
XLA Ops:
  0.0 0.0 copy-start
  0.0 0.0 copy-start.4
  0.0 0.0 copy-start.5
  0.0 0.0 copy-start.2
  0.0 3.1 %shard_map.118 = (bf16[16,640]{1,0:T(8,128)(2,1)}, f32[16,768]{1,0:T(8,128)}, bf16[16,768]{1,0:T(8,128)(2,1)}) custom-call(bf16[16,16,256]{2,1,0:T(8,128)(2,1)} %source_hbm.1, bf16[1024,256]{1,0:T(8,128)(2,1)} %flux_hbm.1, bf16[640,1024]{1,0:T(8,128)(2,1)} %up_hbm.1, bf16[256,768]{1,0:T(8,128)(2,1)} %one_hbm.2), custom_call_target="tpu_custom_call" | custom-call | flops 35651584 | bytes 2359296 | tf_op jit(solution)/shard_map/pallas_call | solution.py:96
  3.1 3.0 %collective-permute-start = (bf16[16,768]{1,0:T(8,128)(2,1)}, bf16[16,768]{1,0:T(8,128)(2,1)S(1)}, u32[]{:S(2)}, u32[]{:S(2)}) collective-permute-start(bf16[16,768]{1,0:T(8,128)(2,1)} %get-tuple-element.9), channel_id=1, source_target_pairs={{0,1},{1,0},{2,3},{3,2},{4,5},{5,4},{6,7},{7,6},{8,9},{9,8},{10,11... | collective-permute-start | bytes 73736 | tf_op jit(solution)/shard_map/ppermute | solution.py:27
  6.2 0.0 copy-done.4
  6.2 2.0 %collective-permute-done = bf16[16,768]{1,0:T(8,128)(2,1)S(1)} collective-permute-done((bf16[16,768]{1,0:T(8,128)(2,1)}, bf16[16,768]{1,0:T(8,128)(2,1)S(1)}, u32[]{:S(2)}, u32[]{:S(2)}) %collective-permute-start) | collective-permute-done | bytes 24608 | tf_op jit(solution)/shard_map/ppermute | solution.py:27
  8.2 0.8 %fusion.10 = bf16[16,768]{1,0:T(8,128)(2,1)S(1)} fusion(f32[16,768]{1,0:T(8,128)} %get-tuple-element.8, bf16[16,768]{1,0:T(8,128)(2,1)S(1)} %collective-permute-done), kind=kLoop, calls=%fused_computation.30 | loop fusion | flops 36864 | bytes 98304 | tf_op jit(solution)/shard_map/convert_element_type | solution.py:22
  9.0 2.1 %collective-permute-start.1 = (bf16[16,768]{1,0:T(8,128)(2,1)S(1)}, bf16[16,768]{1,0:T(8,128)(2,1)S(1)}, u32[]{:S(2)}, u32[]{:S(2)}) collective-permute-start(bf16[16,768]{1,0:T(8,128)(2,1)S(1)} %fusion.10), channel_id=1, source_target_pairs={{0,2},{1,3},{2,0},{3,1},{4,6},{5,7},{6,4},{7,5},{8,10},{9,11},{10,... | collective-permute-start | bytes 73736 | tf_op jit(solution)/shard_map/ppermute | solution.py:27
  11.1 0.0 copy-done.5
  11.1 2.6 %collective-permute-start.6 = (bf16[64,512]{1,0:T(8,128)(2,1)S(1)}, bf16[64,512]{1,0:T(8,128)(2,1)S(1)}, u32[]{:S(2)}, u32[]{:S(2)}) collective-permute-start(bf16[64,512]{1,0:T(8,128)(2,1)S(1)} %constant_dynamic-update-slice_fusion), channel_id=1, source_target_pairs={{0,4},{1,5},{2,6},{3,7},{4,0},{5,1},{6,2},{7,3},{8,12},{9,13},{10,... | collective-permute-start | bytes 196616 | tf_op jit(solution)/shard_map/ppermute | solution.py:27
  13.6 0.0 collective-permute-done.1
  13.7 0.8 %add_convert_fusion.1 = bf16[16,768]{1,0:T(8,128)(2,1)S(1)} fusion(bf16[16,768]{1,0:T(8,128)(2,1)S(1)} %collective-permute-done.1, f32[16,768]{1,0:T(8,128)} %get-tuple-element.8, bf16[16,768]{1,0:T(8,128)(2,1)S(1)} %collective-permute-done), kind=kLoop, calls=%fused_computation.28 | loop fusion | flops 61440 | bytes 122880 | tf_op jit(solution)/shard_map/convert_element_type | solution.py:22
  14.5 0.0 copy-done.2
  14.5 0.2 fusion.17
  14.6 0.1 collective-permute-start.2
  14.7 2.0 %collective-permute-done.6 = bf16[64,512]{1,0:T(8,128)(2,1)S(1)} collective-permute-done((bf16[64,512]{1,0:T(8,128)(2,1)S(1)}, bf16[64,512]{1,0:T(8,128)(2,1)S(1)}, u32[]{:S(2)}, u32[]{:S(2)}) %collective-permute-start.6) | collective-permute-done | bytes 65568 | tf_op jit(solution)/shard_map/ppermute | solution.py:27
  16.8 1.7 %collective-permute-start.7 = (bf16[2,64,512]{2,1,0:T(8,128)(2,1)S(1)}, bf16[2,64,512]{2,1,0:T(8,128)(2,1)S(1)}, u32[]{:S(2)}, u32[]{:S(2)}) collective-permute-start(bf16[2,64,512]{2,1,0:T(8,128)(2,1)S(1)} %pad_maximum_fusion.3), channel_id=1, source_target_pairs={{0,1},{1,0},{2,3},{3,2},{4,5},{5,4},{6,7},{7,6},{8,9},{9,8},{10,11... | collective-permute-start | bytes 393224 | tf_op jit(solution)/shard_map/ppermute | solution.py:27
  18.4 1.1 %collective-permute-done.2 = bf16[16,1536]{1,0:T(8,128)(2,1)S(1)} collective-permute-done((bf16[16,1536]{1,0:T(8,128)(2,1)S(1)}, bf16[16,1536]{1,0:T(8,128)(2,1)S(1)}, u32[]{:S(2)}, u32[]{:S(2)}) %collective-permute-start.2) | collective-permute-done | bytes 49184 | tf_op jit(solution)/shard_map/ppermute | solution.py:27
  19.6 1.2 %collective-permute-start.3 = (bf16[16,1536]{1,0:T(8,128)(2,1)S(1)}, bf16[16,1536]{1,0:T(8,128)(2,1)S(1)}, u32[]{:S(2)}, u32[]{:S(2)}) collective-permute-start(bf16[16,1536]{1,0:T(8,128)(2,1)S(1)} %fusion.5), channel_id=1, source_target_pairs={{0,9},{1,8},{2,11},{3,10},{4,13},{5,12},{6,15},{7,14},{8,1},{9,0},... | collective-permute-start | bytes 147464 | tf_op jit(solution)/shard_map/ppermute | solution.py:27
  20.7 1.8 %collective-permute-done.7 = bf16[2,64,512]{2,1,0:T(8,128)(2,1)S(1)} collective-permute-done((bf16[2,64,512]{2,1,0:T(8,128)(2,1)S(1)}, bf16[2,64,512]{2,1,0:T(8,128)(2,1)S(1)}, u32[]{:S(2)}, u32[]{:S(2)}) %collective-permute-start.7) | collective-permute-done | bytes 131104 | tf_op jit(solution)/shard_map/ppermute | solution.py:27
  22.6 0.1 collective-permute-start.8
  22.7 0.8 %collective-permute-done.3 = bf16[16,1536]{1,0:T(8,128)(2,1)S(1)} collective-permute-done((bf16[16,1536]{1,0:T(8,128)(2,1)S(1)}, bf16[16,1536]{1,0:T(8,128)(2,1)S(1)}, u32[]{:S(2)}, u32[]{:S(2)}) %collective-permute-start.3) | collective-permute-done | bytes 49184 | tf_op jit(solution)/shard_map/ppermute | solution.py:27
  23.5 1.3 %collective-permute-start.4 = (bf16[16,1536]{1,0:T(8,128)(2,1)S(1)}, bf16[16,1536]{1,0:T(8,128)(2,1)S(1)}, u32[]{:S(2)}, u32[]{:S(2)}) collective-permute-start(bf16[16,1536]{1,0:T(8,128)(2,1)S(1)} %fusion.16), channel_id=1, source_target_pairs={{0,10},{1,11},{2,8},{3,9},{4,14},{5,15},{6,12},{7,13},{8,2},{9,3},... | collective-permute-start | bytes 147464 | tf_op jit(solution)/shard_map/ppermute | solution.py:27
  24.8 6.1 %collective-permute-done.8 = bf16[2,2,64,512]{3,2,1,0:T(8,128)(2,1)S(1)} collective-permute-done((bf16[2,2,64,512]{3,2,1,0:T(8,128)(2,1)S(1)}, bf16[2,2,64,512]{3,2,1,0:T(8,128)(2,1)S(1)}, u32[]{:S(2)}, u32[]{:S(2)}) %collective-permute-start.8) | collective-permute-done | bytes 262176 | tf_op jit(solution)/shard_map/ppermute | solution.py:27
  31.0 0.9 %pad_maximum_fusion.1 = bf16[2,2,2,64,512]{4,3,2,1,0:T(8,128)(2,1)} fusion(bf16[2,1,2,64,512]{4,3,2,1,0:T(8,128)(2,1)S(1)} %get-tuple-element.14, bf16[2,1,2,64,512]{4,3,2,1,0:T(8,128)(2,1)S(1)} %get-tuple-element.13), kind=kLoop, calls=%fused_computation.6 | loop fusion | flops 262144 | bytes 1048576 | tf_op jit(solution)/shard_map/stack | solution.py:54
  31.8 0.0 collective-permute-start.9
  31.8 0.0 collective-permute-done.4
  31.9 0.6 %collective-permute-start.5 = (bf16[16,1536]{1,0:T(8,128)(2,1)S(1)}, bf16[16,1536]{1,0:T(8,128)(2,1)S(1)}, u32[]{:S(2)}, u32[]{:S(2)}) collective-permute-start(bf16[16,1536]{1,0:T(8,128)(2,1)S(1)} %fusion.6), channel_id=1, source_target_pairs={{0,8},{1,9},{2,10},{3,11},{4,12},{5,13},{6,14},{7,15},{8,0},{9,1},... | collective-permute-start | bytes 147464 | tf_op jit(solution)/shard_map/ppermute | solution.py:27
  32.4 1.4 %collective-permute-done.5 = bf16[16,1536]{1,0:T(8,128)(2,1)S(1)} collective-permute-done((bf16[16,1536]{1,0:T(8,128)(2,1)S(1)}, bf16[16,1536]{1,0:T(8,128)(2,1)S(1)}, u32[]{:S(2)}, u32[]{:S(2)}) %collective-permute-start.5) | collective-permute-done | bytes 49184 | tf_op jit(solution)/shard_map/ppermute | solution.py:27
  33.9 0.1 collective-permute-done.9
  34.0 0.1 select_bitcast_fusion.1
  34.0 0.0 copy-start.3
  34.0 0.0 copy-start.1
  34.1 0.1 pad_maximum_fusion
  34.2 0.0 copy-start.6
  34.2 0.2 fusion.18
  34.4 1.1 %collective-permute-start.10 = (bf16[16,256]{1,0:T(8,128)(2,1)S(1)}, bf16[16,256]{1,0:T(8,128)(2,1)S(1)}, u32[]{:S(2)}, u32[]{:S(2)}) collective-permute-start(bf16[16,256]{1,0:T(8,128)(2,1)S(1)} %get-tuple-element.25), channel_id=1, source_target_pairs={{0,24},{1,25},{2,26},{3,27},{4,28},{5,29},{6,30},{7,31},{8,16},{9,... | collective-permute-start | bytes 24584 | tf_op jit(solution)/shard_map/ppermute | solution.py:27
  35.5 1.9 %collective-permute-done.10 = bf16[16,256]{1,0:T(8,128)(2,1)S(1)} collective-permute-done((bf16[16,256]{1,0:T(8,128)(2,1)S(1)}, bf16[16,256]{1,0:T(8,128)(2,1)S(1)}, u32[]{:S(2)}, u32[]{:S(2)}) %collective-permute-start.10) | collective-permute-done | bytes 8224 | tf_op jit(solution)/shard_map/ppermute | solution.py:27
  37.4 0.2 convolution_convert_fusion
  37.7 0.0 copy-done.3
  37.7 0.2 convolution_convert_fusion.1
  37.9 1.5 %collective-permute-start.11 = (bf16[16,128]{1,0:T(8,128)(2,1)S(1)}, bf16[16,128]{1,0:T(8,128)(2,1)S(1)}, u32[]{:S(2)}, u32[]{:S(2)}) collective-permute-start(bf16[16,128]{1,0:T(8,128)(2,1)S(1)} %convolution_convert_fusion.1), channel_id=1, source_target_pairs={{0,1},{1,0},{2,3},{3,2},{4,5},{5,4},{6,7},{7,6},{8,9},{9,8},{10,11... | collective-permute-start | bytes 12296 | tf_op jit(solution)/shard_map/ppermute | solution.py:27
  39.3 2.2 %collective-permute-done.11 = bf16[16,128]{1,0:T(8,128)(2,1)S(1)} collective-permute-done((bf16[16,128]{1,0:T(8,128)(2,1)S(1)}, bf16[16,128]{1,0:T(8,128)(2,1)S(1)}, u32[]{:S(2)}, u32[]{:S(2)}) %collective-permute-start.11) | collective-permute-done | bytes 4128 | tf_op jit(solution)/shard_map/ppermute | solution.py:27
  41.5 0.9 %collective-permute-start.12 = (bf16[16,256]{1,0:T(8,128)(2,1)S(1)}, bf16[16,256]{1,0:T(8,128)(2,1)S(1)}, u32[]{:S(2)}, u32[]{:S(2)}) collective-permute-start(bf16[16,256]{1,0:T(8,128)(2,1)S(1)} %pad_maximum_fusion.5), channel_id=1, source_target_pairs={{0,2},{1,3},{2,0},{3,1},{4,6},{5,7},{6,4},{7,5},{8,10},{9,11},{10,... | collective-permute-start | bytes 24584 | tf_op jit(solution)/shard_map/ppermute | solution.py:27
  42.5 0.0 copy-done
  42.5 0.0 copy-done.1
  42.5 1.1 %fusion.3.particular_hbm = f32[16,16,256]{2,1,0:T(8,128)} fusion(bf16[16,256,256]{2,1,0:T(8,128)(2,1)S(1)} %bitcast.25, bf16[16,16,256]{2,1,0:T(8,128)(2,1)S(1)} %copy-done.1), kind=kOutput, calls=%fused_computation.13 | convolution fusion | flops 33554432 | bytes 2490368 | tf_op jit(solution)/shard_map/rlq,lqp->lrp/dot_general | solution.py:229
  43.6 0.0 copy-done.6
  43.6 0.6 %slice.23.box_ref = bf16[16,384]{1,0:T(8,128)(2,1)} slice(bf16[16,640]{1,0:T(8,128)(2,1)S(1)} %copy-done.6), slice={[0:16], [0:384]} | slice | bytes 24576 | tf_op jit(solution)/shard_map/slice | solution.py:238
  44.2 0.6 %slice.24.first_ref = bf16[16,256]{1,0:T(8,128)(2,1)} slice(bf16[16,768]{1,0:T(8,128)(2,1)S(1)} %add_convert_fusion.1), slice={[0:16], [0:256]} | slice | bytes 16384 | tf_op jit(solution)/shard_map/slice | solution.py:236
  44.8 0.5 collective-permute-done.12
  45.3 0.6 %pad_maximum_fusion.4.mid_ref = bf16[16,512]{1,0:T(8,128)(2,1)} fusion(bf16[16,256]{1,0:T(8,128)(2,1)S(1)} %get-tuple-element.20, bf16[16,256]{1,0:T(8,128)(2,1)S(1)} %get-tuple-element.19), kind=kLoop, calls=%fused_computation.32 | loop fusion | flops 32768 | bytes 32768 | tf_op jit(solution)/shard_map/concatenate | solution.py:48
  45.9 3.9 %shard_map.119 = f32[16,16,256]{2,1,0:T(8,128)} custom-call(bf16[16,256]{1,0:T(8,128)(2,1)} %slice.24.first_ref, bf16[16,512]{1,0:T(8,128)(2,1)} %pad_maximum_fusion.4.mid_ref, bf16[16,384]{1,0:T(8,128)(2,1)} %slice.23.box_ref, bf16[256,768]{1,0:T(8,128)(2,1)} %one_hbm.3, bf16[1024,640]{1,0:T(8,128)(2,1)} %down_hbm.1, bf16[1024,256]{1,0:T(8,128)(2,1)} %lift_hbm.1, ...), custom_call_target="tpu_custom_call" | custom-call | flops 35651584 | bytes 2752512 | tf_op jit(solution)/shard_map/pallas_call | solution.py:148
  (15 shorter events, 0.2 us)
Async XLA Ops:
  0.0 42.5 %copy-start = (bf16[4096,256]{1,0:T(8,128)(2,1)S(1)}, bf16[4096,256]{1,0:T(8,128)(2,1)}, u32[]{:S(2)}) copy-start(bf16[4096,256]{1,0:T(8,128)(2,1)} %param.14) | copy-start | bytes 6291460
  0.0 6.2 %copy-start.4 = (bf16[64,256]{1,0:T(8,128)(2,1)S(1)}, bf16[64,256]{1,0:T(8,128)(2,1)}, u32[]{:S(2)}) copy-start(bf16[64,256]{1,0:T(8,128)(2,1)} %param.22) | copy-start | bytes 98308
  0.0 11.0 %copy-start.5 = (bf16[64,256]{1,0:T(8,128)(2,1)S(1)}, bf16[64,256]{1,0:T(8,128)(2,1)}, u32[]{:S(2)}) copy-start(bf16[64,256]{1,0:T(8,128)(2,1)} %param.23) | copy-start | bytes 98308
  0.0 14.5 %copy-start.2 = (bf16[128,1536]{1,0:T(8,128)(2,1)S(1)}, bf16[128,1536]{1,0:T(8,128)(2,1)}, u32[]{:S(2)}) copy-start(bf16[128,1536]{1,0:T(8,128)(2,1)} %param.20) | copy-start | bytes 1179652
  3.1 5.1 %collective-permute-start = (bf16[16,768]{1,0:T(8,128)(2,1)}, bf16[16,768]{1,0:T(8,128)(2,1)S(1)}, u32[]{:S(2)}, u32[]{:S(2)}) collective-permute-start(bf16[16,768]{1,0:T(8,128)(2,1)} %get-tuple-element.9), channel_id=1, source_target_pairs={{0,1},{1,0},{2,3},{3,2},{4,5},{5,4},{6,7},{7,6},{8,9},{9,8},{10,11... | collective-permute-start | bytes 73736 | tf_op jit(solution)/shard_map/ppermute | solution.py:27
  9.0 4.7 %collective-permute-start.1 = (bf16[16,768]{1,0:T(8,128)(2,1)S(1)}, bf16[16,768]{1,0:T(8,128)(2,1)S(1)}, u32[]{:S(2)}, u32[]{:S(2)}) collective-permute-start(bf16[16,768]{1,0:T(8,128)(2,1)S(1)} %fusion.10), channel_id=1, source_target_pairs={{0,2},{1,3},{2,0},{3,1},{4,6},{5,7},{6,4},{7,5},{8,10},{9,11},{10,... | collective-permute-start | bytes 73736 | tf_op jit(solution)/shard_map/ppermute | solution.py:27
  11.1 5.7 %collective-permute-start.6 = (bf16[64,512]{1,0:T(8,128)(2,1)S(1)}, bf16[64,512]{1,0:T(8,128)(2,1)S(1)}, u32[]{:S(2)}, u32[]{:S(2)}) collective-permute-start(bf16[64,512]{1,0:T(8,128)(2,1)S(1)} %constant_dynamic-update-slice_fusion), channel_id=1, source_target_pairs={{0,4},{1,5},{2,6},{3,7},{4,0},{5,1},{6,2},{7,3},{8,12},{9,13},{10,... | collective-permute-start | bytes 196616 | tf_op jit(solution)/shard_map/ppermute | solution.py:27
  14.6 4.9 %collective-permute-start.2 = (bf16[16,1536]{1,0:T(8,128)(2,1)S(1)}, bf16[16,1536]{1,0:T(8,128)(2,1)S(1)}, u32[]{:S(2)}, u32[]{:S(2)}) collective-permute-start(bf16[16,1536]{1,0:T(8,128)(2,1)S(1)} %get-tuple-element.23), channel_id=1, source_target_pairs={{0,12},{1,13},{2,14},{3,15},{4,8},{5,9},{6,10},{7,11},{8,4},{9,5},... | collective-permute-start | bytes 147464 | tf_op jit(solution)/shard_map/ppermute | solution.py:27
  16.8 5.8 %collective-permute-start.7 = (bf16[2,64,512]{2,1,0:T(8,128)(2,1)S(1)}, bf16[2,64,512]{2,1,0:T(8,128)(2,1)S(1)}, u32[]{:S(2)}, u32[]{:S(2)}) collective-permute-start(bf16[2,64,512]{2,1,0:T(8,128)(2,1)S(1)} %pad_maximum_fusion.3), channel_id=1, source_target_pairs={{0,1},{1,0},{2,3},{3,2},{4,5},{5,4},{6,7},{7,6},{8,9},{9,8},{10,11... | collective-permute-start | bytes 393224 | tf_op jit(solution)/shard_map/ppermute | solution.py:27
  19.6 3.9 %collective-permute-start.3 = (bf16[16,1536]{1,0:T(8,128)(2,1)S(1)}, bf16[16,1536]{1,0:T(8,128)(2,1)S(1)}, u32[]{:S(2)}, u32[]{:S(2)}) collective-permute-start(bf16[16,1536]{1,0:T(8,128)(2,1)S(1)} %fusion.5), channel_id=1, source_target_pairs={{0,9},{1,8},{2,11},{3,10},{4,13},{5,12},{6,15},{7,14},{8,1},{9,0},... | collective-permute-start | bytes 147464 | tf_op jit(solution)/shard_map/ppermute | solution.py:27
  22.6 8.3 %collective-permute-start.8 = (bf16[2,2,64,512]{3,2,1,0:T(8,128)(2,1)S(1)}, bf16[2,2,64,512]{3,2,1,0:T(8,128)(2,1)S(1)}, u32[]{:S(2)}, u32[]{:S(2)}) collective-permute-start(bf16[2,2,64,512]{3,2,1,0:T(8,128)(2,1)S(1)} %pad_maximum_fusion.2), channel_id=1, source_target_pairs={{0,2},{1,3},{2,0},{3,1},{4,6},{5,7},{6,4},{7,5},{8,10},{9,11},{10,... | collective-permute-start | bytes 786440 | tf_op jit(solution)/shard_map/ppermute | solution.py:27
  23.5 8.3 %collective-permute-start.4 = (bf16[16,1536]{1,0:T(8,128)(2,1)S(1)}, bf16[16,1536]{1,0:T(8,128)(2,1)S(1)}, u32[]{:S(2)}, u32[]{:S(2)}) collective-permute-start(bf16[16,1536]{1,0:T(8,128)(2,1)S(1)} %fusion.16), channel_id=1, source_target_pairs={{0,10},{1,11},{2,8},{3,9},{4,14},{5,15},{6,12},{7,13},{8,2},{9,3},... | collective-permute-start | bytes 147464 | tf_op jit(solution)/shard_map/ppermute | solution.py:27
  31.8 2.1 %collective-permute-start.9 = (bf16[2,2,2,64,512]{4,3,2,1,0:T(8,128)(2,1)}, bf16[2,2,2,64,512]{4,3,2,1,0:T(8,128)(2,1)S(1)}, u32[]{:S(2)}, u32[]{:S(2)}) collective-permute-start(bf16[2,2,2,64,512]{4,3,2,1,0:T(8,128)(2,1)} %pad_maximum_fusion.1), channel_id=1, source_target_pairs={{0,8},{1,9},{2,10},{3,11},{4,12},{5,13},{6,14},{7,15},{8,0},{9,1},... | collective-permute-start | bytes 1572872 | tf_op jit(solution)/shard_map/ppermute | solution.py:27
  31.9 1.9 %collective-permute-start.5 = (bf16[16,1536]{1,0:T(8,128)(2,1)S(1)}, bf16[16,1536]{1,0:T(8,128)(2,1)S(1)}, u32[]{:S(2)}, u32[]{:S(2)}) collective-permute-start(bf16[16,1536]{1,0:T(8,128)(2,1)S(1)} %fusion.6), channel_id=1, source_target_pairs={{0,8},{1,9},{2,10},{3,11},{4,12},{5,13},{6,14},{7,15},{8,0},{9,1},... | collective-permute-start | bytes 147464 | tf_op jit(solution)/shard_map/ppermute | solution.py:27
  34.0 3.6 %copy-start.3 = (bf16[128,1536]{1,0:T(8,128)(2,1)S(1)}, bf16[128,1536]{1,0:T(8,128)(2,1)}, u32[]{:S(2)}) copy-start(bf16[128,1536]{1,0:T(8,128)(2,1)} %param.21) | copy-start | bytes 1179652
  34.0 8.4 %copy-start.1 = (bf16[16,16,256]{2,1,0:T(8,128)(2,1)S(1)}, bf16[16,16,256]{2,1,0:T(8,128)(2,1)}, u32[]{:S(2)}) copy-start(bf16[16,16,256]{2,1,0:T(8,128)(2,1)} %source_hbm.1) | copy-start | bytes 393220
  34.2 9.4 %copy-start.6 = (bf16[16,640]{1,0:T(8,128)(2,1)S(1)}, bf16[16,640]{1,0:T(8,128)(2,1)}, u32[]{:S(2)}) copy-start(bf16[16,640]{1,0:T(8,128)(2,1)} %get-tuple-element.10) | copy-start | bytes 61444
  34.4 3.1 %collective-permute-start.10 = (bf16[16,256]{1,0:T(8,128)(2,1)S(1)}, bf16[16,256]{1,0:T(8,128)(2,1)S(1)}, u32[]{:S(2)}, u32[]{:S(2)}) collective-permute-start(bf16[16,256]{1,0:T(8,128)(2,1)S(1)} %get-tuple-element.25), channel_id=1, source_target_pairs={{0,24},{1,25},{2,26},{3,27},{4,28},{5,29},{6,30},{7,31},{8,16},{9,... | collective-permute-start | bytes 24584 | tf_op jit(solution)/shard_map/ppermute | solution.py:27
  37.9 3.6 %collective-permute-start.11 = (bf16[16,128]{1,0:T(8,128)(2,1)S(1)}, bf16[16,128]{1,0:T(8,128)(2,1)S(1)}, u32[]{:S(2)}, u32[]{:S(2)}) collective-permute-start(bf16[16,128]{1,0:T(8,128)(2,1)S(1)} %convolution_convert_fusion.1), channel_id=1, source_target_pairs={{0,1},{1,0},{2,3},{3,2},{4,5},{5,4},{6,7},{7,6},{8,9},{9,8},{10,11... | collective-permute-start | bytes 12296 | tf_op jit(solution)/shard_map/ppermute | solution.py:27
  41.5 3.7 %collective-permute-start.12 = (bf16[16,256]{1,0:T(8,128)(2,1)S(1)}, bf16[16,256]{1,0:T(8,128)(2,1)S(1)}, u32[]{:S(2)}, u32[]{:S(2)}) collective-permute-start(bf16[16,256]{1,0:T(8,128)(2,1)S(1)} %pad_maximum_fusion.5), channel_id=1, source_target_pairs={{0,2},{1,3},{2,0},{3,1},{4,6},{5,7},{6,4},{7,5},{8,10},{9,11},{10,... | collective-permute-start | bytes 24584 | tf_op jit(solution)/shard_map/ppermute | solution.py:27

commit v6 on v1

--- a/solution.py
+++ b/solution.py
@@ -54,10 +54,6 @@
     )
 
 
-def tie(*values):
-    return lax.optimization_barrier(values)
-
-
 def per_device(
     source,
     leaf_flux,
@@ -102,7 +98,6 @@
     roots_far = swap(roots, far)
     first_sum = partner_sum(first_sum, 1)
 
-    first_sum, roots_far = tie(first_sum, roots_far)
     roots = joined_pair(roots, roots_far, place & far != 0, 0)
     roots_one = swap(roots, 1)
     first_sum = partner_sum(first_sum, near)
@@ -110,13 +105,11 @@
 
     piece = lax.dynamic_slice_in_dim(first_state, k_zero + place % quad * width, width, 1)
     second_sum = product(piece, up_two)
-    second_sum, roots_one = tie(second_sum, roots_one)
     roots = joined_pair(roots, roots_one, place & 1 != 0, 1)
     roots_near = swap(roots, near)
     second_sum = partner_sum(second_sum, far | pair)
 
     second_sum = partner_sum(second_sum, 1 | pair)
-    second_sum, roots_near = tie(second_sum, roots_near)
     roots = joined_pair(roots, roots_near, place & near != 0, 1)
     roots_pair = swap(roots, pair)
     second_sum = partner_sum(second_sum, near | pair)

time: 54.1 us -> 49 us (0.906)
  waiting for transfers between devices: 31.6 us -> 18.8 us
  starting transfers between devices: 11.4 us -> 18.3 us
  other arithmetic: 1.27 us -> 2.07 us
    ppermute x13, waiting for transfers between devices: 31.6 us -> 18.8 us  [swap(): return lax.ppermute(value, AXES, [(i, i ^ mask) for i in range(count)])]
    ppermute x13, starting transfers between devices: 11.4 us -> 18.3 us  [swap(): return lax.ppermute(value, AXES, [(i, i ^ mask) for i in range(count)])]
    convert_element_type x7 -> x6, other arithmetic: 0.07 us -> 0.9 us  [rounded(): return value.astype(jnp.bfloat16)]
  transfers between devices with their start and end apart: 13 -> 13, of which waited for: 11 -> 9; matrix products, arithmetic and copies ran while one was open for 4% -> 6% of each run, Pallas kernels for 0% -> 0%
where the time goes in v6:
time: 49 us; the launch traced here: 48.8 us
  waiting for transfers between devices  18.8 us (38%)
  starting transfers between devices  18.3 us (37%)
  matrix products  8.24 us (17%)
  other arithmetic  2.07 us (4%)
  local copies, waits for them, and re-layouts  1.19 us (2%)
    ppermute x13, waiting for transfers between devices, swap(): return lax.ppermute(value, AXES, [(i, i ^ mask) for i in range(count)])  18.8 us
    ppermute x13, starting transfers between devices, swap(): return lax.ppermute(value, AXES, [(i, i ^ mask) for i in range(count)])  18.3 us
    dot_general x5, matrix products, contract(): lax.dot_general(left, right, (((1,), (1,)), ((), ())), preferred_element_...  3.88 us
    dot_general x1, matrix products, per_device(): jnp.einsum('rlq,leq->rle', source, leaf_flux.reshape(leaves, edge_count,...  1.44 us
    dot_general x1, matrix products, per_device(): jnp.einsum('rle,leq->rlq', leaf_bound, leaf_lift.reshape(leaves, edge_cou...  1.29 us
    another operation x8, other arithmetic, joined_pair(): jnp.stack([jnp.where(upper, other, joined), jnp.where(upper, joined, othe...  1.15 us
    dot_general x1, matrix products, per_device(): jnp.einsum('rlq,lqp->rlp', source, leaf_particular.reshape(leaves, points...  1.09 us
  transfers between devices with their start and end apart: 13, of which 9 were waited for; matrix products, arithmetic and copies ran while one was open for 6% of the time, Pallas kernels for 0%

profile of v6, /device:TPU:0, one launch (start us, length us, event | category | flops | bytes accessed | tf_op | source)
XLA Modules:
  0.0 48.8 jit_solution(1624846978598819086)
XLA Ops:
  0.0 0.0 copy-start
  0.0 0.0 copy-start.5
  0.0 0.0 copy-start.6
  0.0 0.0 copy-start.7
  0.0 1.4 %fusion.1 = bf16[16,16,64]{2,0,1:T(8,128)(2,1)S(1)} fusion(bf16[16,64,256]{2,1,0:T(8,128)(2,1)} %bitcast.45, bf16[16,16,256]{2,1,0:T(8,128)(2,1)} %param.12), kind=kOutput, calls=%fused_computation.4 | convolution fusion | flops 8404992 | bytes 688128 | tf_op jit(solution)/shard_map/rlq,leq->rle/dot_general | solution.py:87
  1.5 0.0 copy-start.3
  1.5 0.1 reshape.19
  1.6 1.8 %convolution_convert_fusion.3 = bf16[16,640]{1,0:T(8,128)(2,1)S(1)} fusion(bf16[16,1024]{1,0:T(8,128)(2,1)S(1)} %reshape.19, bf16[640,1024]{1,0:T(8,128)(2,1)} %param.16), kind=kOutput, calls=%fused_computation.7 | convolution fusion | flops 20981760 | bytes 1363968 | tf_op jit(solution)/shard_map/dot_general | solution.py:10
  3.4 0.0 copy-done.5
  3.4 0.2 fusion.32
  3.6 3.0 %collective-permute-start = (bf16[16,768]{1,0:T(8,128)(2,1)S(1)}, bf16[16,768]{1,0:T(8,128)(2,1)S(1)}, u32[]{:S(2)}, u32[]{:S(2)}) collective-permute-start(bf16[16,768]{1,0:T(8,128)(2,1)S(1)} %get-tuple-element.17), channel_id=1, source_target_pairs={{0,1},{1,0},{2,3},{3,2},{4,5},{5,4},{6,7},{7,6},{8,9},{9,8},{10,11... | collective-permute-start | bytes 73736 | tf_op jit(solution)/shard_map/ppermute | solution.py:25
  6.6 0.0 copy-done.6
  6.6 1.8 %collective-permute-done = bf16[16,768]{1,0:T(8,128)(2,1)S(1)} collective-permute-done((bf16[16,768]{1,0:T(8,128)(2,1)S(1)}, bf16[16,768]{1,0:T(8,128)(2,1)S(1)}, u32[]{:S(2)}, u32[]{:S(2)}) %collective-permute-start) | collective-permute-done | bytes 24608 | tf_op jit(solution)/shard_map/ppermute | solution.py:25
  8.4 2.1 %collective-permute-start.1 = (bf16[16,768]{1,0:T(8,128)(2,1)S(1)}, bf16[16,768]{1,0:T(8,128)(2,1)S(1)}, u32[]{:S(2)}, u32[]{:S(2)}) collective-permute-start(bf16[16,768]{1,0:T(8,128)(2,1)S(1)} %fusion.13), channel_id=1, source_target_pairs={{0,2},{1,3},{2,0},{3,1},{4,6},{5,7},{6,4},{7,5},{8,10},{9,11},{10,... | collective-permute-start | bytes 73736 | tf_op jit(solution)/shard_map/ppermute | solution.py:25
  10.5 0.0 copy-done.7
  10.6 2.6 %collective-permute-start.6 = (bf16[64,512]{1,0:T(8,128)(2,1)S(1)}, bf16[64,512]{1,0:T(8,128)(2,1)S(1)}, u32[]{:S(2)}, u32[]{:S(2)}) collective-permute-start(bf16[64,512]{1,0:T(8,128)(2,1)S(1)} %constant_dynamic-update-slice_fusion), channel_id=1, source_target_pairs={{0,4},{1,5},{2,6},{3,7},{4,0},{5,1},{6,2},{7,3},{8,12},{9,13},{10,... | collective-permute-start | bytes 196616 | tf_op jit(solution)/shard_map/ppermute | solution.py:25
  13.1 0.0 collective-permute-done.1
  13.2 0.0 copy-done.3
  13.2 0.2 fusion.33
  13.3 0.1 collective-permute-start.2
  13.4 2.8 %collective-permute-done.6 = bf16[64,512]{1,0:T(8,128)(2,1)S(1)} collective-permute-done((bf16[64,512]{1,0:T(8,128)(2,1)S(1)}, bf16[64,512]{1,0:T(8,128)(2,1)S(1)}, u32[]{:S(2)}, u32[]{:S(2)}) %collective-permute-start.6) | collective-permute-done | bytes 65568 | tf_op jit(solution)/shard_map/ppermute | solution.py:25
  16.3 1.7 %collective-permute-start.7 = (bf16[2,64,512]{2,1,0:T(8,128)(2,1)S(1)}, bf16[2,64,512]{2,1,0:T(8,128)(2,1)S(1)}, u32[]{:S(2)}, u32[]{:S(2)}) collective-permute-start(bf16[2,64,512]{2,1,0:T(8,128)(2,1)S(1)} %pad_maximum_fusion.3), channel_id=1, source_target_pairs={{0,1},{1,0},{2,3},{3,2},{4,5},{5,4},{6,7},{7,6},{8,9},{9,8},{10,11... | collective-permute-start | bytes 393224 | tf_op jit(solution)/shard_map/ppermute | solution.py:25
  17.9 0.3 collective-permute-done.2
  18.3 1.2 %collective-permute-start.3 = (bf16[16,1536]{1,0:T(8,128)(2,1)S(1)}, bf16[16,1536]{1,0:T(8,128)(2,1)S(1)}, u32[]{:S(2)}, u32[]{:S(2)}) collective-permute-start(bf16[16,1536]{1,0:T(8,128)(2,1)S(1)} %fusion.7), channel_id=1, source_target_pairs={{0,9},{1,8},{2,11},{3,10},{4,13},{5,12},{6,15},{7,14},{8,1},{9,0},... | collective-permute-start | bytes 147464 | tf_op jit(solution)/shard_map/ppermute | solution.py:25
  19.4 1.9 %collective-permute-done.7 = bf16[2,64,512]{2,1,0:T(8,128)(2,1)S(1)} collective-permute-done((bf16[2,64,512]{2,1,0:T(8,128)(2,1)S(1)}, bf16[2,64,512]{2,1,0:T(8,128)(2,1)S(1)}, u32[]{:S(2)}, u32[]{:S(2)}) %collective-permute-start.7) | collective-permute-done | bytes 131104 | tf_op jit(solution)/shard_map/ppermute | solution.py:25
  21.4 1.2 %collective-permute-start.8 = (bf16[2,2,64,512]{3,2,1,0:T(8,128)(2,1)S(1)}, bf16[2,2,64,512]{3,2,1,0:T(8,128)(2,1)S(1)}, u32[]{:S(2)}, u32[]{:S(2)}) collective-permute-start(bf16[2,2,64,512]{3,2,1,0:T(8,128)(2,1)S(1)} %pad_maximum_fusion.2), channel_id=1, source_target_pairs={{0,2},{1,3},{2,0},{3,1},{4,6},{5,7},{6,4},{7,5},{8,10},{9,11},{10,... | collective-permute-start | bytes 786440 | tf_op jit(solution)/shard_map/ppermute | solution.py:25
  22.5 0.0 collective-permute-done.3
  22.6 1.0 %collective-permute-start.4 = (bf16[16,1536]{1,0:T(8,128)(2,1)S(1)}, bf16[16,1536]{1,0:T(8,128)(2,1)S(1)}, u32[]{:S(2)}, u32[]{:S(2)}) collective-permute-start(bf16[16,1536]{1,0:T(8,128)(2,1)S(1)} %fusion.31), channel_id=1, source_target_pairs={{0,10},{1,11},{2,8},{3,9},{4,14},{5,15},{6,12},{7,13},{8,2},{9,3},... | collective-permute-start | bytes 147464 | tf_op jit(solution)/shard_map/ppermute | solution.py:25
  23.5 6.1 %collective-permute-done.8 = bf16[2,2,64,512]{3,2,1,0:T(8,128)(2,1)S(1)} collective-permute-done((bf16[2,2,64,512]{3,2,1,0:T(8,128)(2,1)S(1)}, bf16[2,2,64,512]{3,2,1,0:T(8,128)(2,1)S(1)}, u32[]{:S(2)}, u32[]{:S(2)}) %collective-permute-start.8) | collective-permute-done | bytes 262176 | tf_op jit(solution)/shard_map/ppermute | solution.py:25
  29.7 0.9 %pad_maximum_fusion.1 = bf16[2,2,2,64,512]{4,3,2,1,0:T(8,128)(2,1)} fusion(bf16[2,1,2,64,512]{4,3,2,1,0:T(8,128)(2,1)S(1)} %get-tuple-element.8, bf16[2,1,2,64,512]{4,3,2,1,0:T(8,128)(2,1)S(1)} %get-tuple-element.7), kind=kLoop, calls=%fused_computation.14 | loop fusion | flops 262144 | bytes 1048576 | tf_op jit(solution)/shard_map/stack | solution.py:52
  30.5 0.0 collective-permute-start.9
  30.6 0.0 collective-permute-done.4
  30.6 0.6 %collective-permute-start.5 = (bf16[16,1536]{1,0:T(8,128)(2,1)S(1)}, bf16[16,1536]{1,0:T(8,128)(2,1)}, u32[]{:S(2)}, u32[]{:S(2)}) collective-permute-start(bf16[16,1536]{1,0:T(8,128)(2,1)S(1)} %fusion.8), channel_id=1, source_target_pairs={{0,8},{1,9},{2,10},{3,11},{4,12},{5,13},{6,14},{7,15},{8,0},{9,1},... | collective-permute-start | bytes 147464 | tf_op jit(solution)/shard_map/ppermute | solution.py:25
  31.2 1.5 %collective-permute-done.5 = bf16[16,1536]{1,0:T(8,128)(2,1)} collective-permute-done((bf16[16,1536]{1,0:T(8,128)(2,1)S(1)}, bf16[16,1536]{1,0:T(8,128)(2,1)}, u32[]{:S(2)}, u32[]{:S(2)}) %collective-permute-start.5) | collective-permute-done | bytes 49184 | tf_op jit(solution)/shard_map/ppermute | solution.py:25
  32.7 0.8 %add_convert_fusion = bf16[16,1536]{1,0:T(8,128)(2,1)S(1)} fusion(bf16[16,1536]{1,0:T(8,128)(2,1)} %collective-permute-done.5, bf16[16,1536]{1,0:T(8,128)(2,1)S(1)} %collective-permute-done.4, bf16[16,1536]{1,0:T(8,128)(2,1)S(1)} %collective-permute-done.3, f32[16,1536]{1,0:T(8,128)S(1)} %get-tuple-element.20, bf16[16,1536]{1,0:T(8,128)(2,1)S(1)} %collective-permute-done.2), kind=kLoop, calls=%fused_computation.25 | loop fusion | flops 221184 | bytes 344064 | tf_op jit(solution)/shard_map/convert_element_type | solution.py:20
  33.5 0.0 collective-permute-done.9
  33.5 0.1 select_bitcast_fusion.1
  33.6 0.0 copy-start.4
  33.6 0.1 pad_maximum_fusion
  33.7 0.0 copy-start.2
  33.7 0.2 fusion.34
  33.9 1.4 %collective-permute-start.10 = (bf16[16,256]{1,0:T(8,128)(2,1)S(1)}, bf16[16,256]{1,0:T(8,128)(2,1)S(1)}, u32[]{:S(2)}, u32[]{:S(2)}) collective-permute-start(bf16[16,256]{1,0:T(8,128)(2,1)S(1)} %get-tuple-element.21), channel_id=1, source_target_pairs={{0,24},{1,25},{2,26},{3,27},{4,28},{5,29},{6,30},{7,31},{8,16},{9,... | collective-permute-start | bytes 24584 | tf_op jit(solution)/shard_map/ppermute | solution.py:25
  35.3 1.7 %collective-permute-done.10 = bf16[16,256]{1,0:T(8,128)(2,1)S(1)} collective-permute-done((bf16[16,256]{1,0:T(8,128)(2,1)S(1)}, bf16[16,256]{1,0:T(8,128)(2,1)S(1)}, u32[]{:S(2)}, u32[]{:S(2)}) %collective-permute-start.10) | collective-permute-done | bytes 8224 | tf_op jit(solution)/shard_map/ppermute | solution.py:25
  37.0 0.2 convolution_convert_fusion.2
  37.2 0.0 copy-done.4
  37.2 0.2 convolution_convert_fusion.5
  37.4 1.7 %collective-permute-start.11 = (bf16[16,128]{1,0:T(8,128)(2,1)S(1)}, bf16[16,128]{1,0:T(8,128)(2,1)S(1)}, u32[]{:S(2)}, u32[]{:S(2)}) collective-permute-start(bf16[16,128]{1,0:T(8,128)(2,1)S(1)} %convolution_convert_fusion.5), channel_id=1, source_target_pairs={{0,1},{1,0},{2,3},{3,2},{4,5},{5,4},{6,7},{7,6},{8,9},{9,8},{10,11... | collective-permute-start | bytes 12296 | tf_op jit(solution)/shard_map/ppermute | solution.py:25
  39.2 1.9 %collective-permute-done.11 = bf16[16,128]{1,0:T(8,128)(2,1)S(1)} collective-permute-done((bf16[16,128]{1,0:T(8,128)(2,1)S(1)}, bf16[16,128]{1,0:T(8,128)(2,1)S(1)}, u32[]{:S(2)}, u32[]{:S(2)}) %collective-permute-start.11) | collective-permute-done | bytes 4128 | tf_op jit(solution)/shard_map/ppermute | solution.py:25
  41.1 1.8 %collective-permute-start.12 = (bf16[16,256]{1,0:T(8,128)(2,1)S(1)}, bf16[16,256]{1,0:T(8,128)(2,1)S(1)}, u32[]{:S(2)}, u32[]{:S(2)}) collective-permute-start(bf16[16,256]{1,0:T(8,128)(2,1)S(1)} %pad_maximum_fusion.4), channel_id=1, source_target_pairs={{0,2},{1,3},{2,0},{3,1},{4,6},{5,7},{6,4},{7,5},{8,10},{9,11},{10,... | collective-permute-start | bytes 24584 | tf_op jit(solution)/shard_map/ppermute | solution.py:25
  42.9 0.0 copy-done
  42.9 0.0 copy-done.2
  42.9 0.0 copy-start.1
  42.9 1.1 %convolution_bitcast_fusion.1 = f32[16,16,256]{2,0,1:T(8,128)} fusion(bf16[16,256,256]{2,1,0:T(8,128)(2,1)S(1)} %bitcast.42, bf16[16,16,256]{2,1,0:T(8,128)(2,1)S(1)} %copy-done.2), kind=kOutput, calls=%fused_computation.2 | convolution fusion | flops 33554432 | bytes 2490368 | tf_op jit(solution)/shard_map/rlq,lqp->rlp/dot_general | solution.py:142
  44.0 0.8 %collective-permute-done.12 = bf16[16,256]{1,0:T(8,128)(2,1)S(1)} collective-permute-done((bf16[16,256]{1,0:T(8,128)(2,1)S(1)}, bf16[16,256]{1,0:T(8,128)(2,1)S(1)}, u32[]{:S(2)}, u32[]{:S(2)}) %collective-permute-start.12) | collective-permute-done | bytes 8224 | tf_op jit(solution)/shard_map/ppermute | solution.py:25
  44.8 1.2 %convolution_convert_fusion.4 = bf16[16,256]{1,0:T(8,128)(2,1)S(1)} fusion(bf16[256,768]{1,0:T(8,128)(2,1)} %param.19, bf16[16,256]{1,0:T(8,128)(2,1)S(1)} %get-tuple-element.14, bf16[16,256]{1,0:T(8,128)(2,1)S(1)} %get-tuple-element.13, bf16[16,256]{1,0:T(8,128)(2,1)S(1)} %slice.30), kind=kOutput, calls=%fused_computation.8 | convolution fusion | flops 6369280 | bytes 425984 | tf_op jit(solution)/shard_map/dot_general | solution.py:10
  46.0 0.0 copy-done.1
  46.0 0.5 %convolution_convert_fusion.1 = bf16[16,1024]{1,0:T(8,128)(2,1)S(1)} fusion(bf16[1024,640]{1,0:T(8,128)(2,1)S(1)} %copy-done.1, bf16[16,256]{1,0:T(8,128)(2,1)S(1)} %convolution_convert_fusion.4, bf16[16,384]{1,0:T(8,128)(2,1)S(1)} %slice.28), kind=kOutput, calls=%fused_computation.5 | convolution fusion | flops 21028864 | bytes 1363968 | tf_op jit(solution)/shard_map/dot_general | solution.py:10
  46.5 0.1 reshape.21
  46.6 1.3 %fusion = f32[16,16,256]{2,0,1:T(8,128)S(1)} fusion(f32[16,16,256]{2,0,1:T(8,128)} %convolution_bitcast_fusion.1, bf16[16,64,256]{2,1,0:T(8,128)(2,1)} %bitcast.46, bf16[16,16,64]{2,1,0:T(8,128)(2,1)S(1)} %reshape.21), kind=kOutput, calls=%fused_computation.1 | convolution fusion | flops 8454144 | bytes 1081344 | tf_op jit(solution)/shard_map/rle,leq->rlq/dot_general | solution.py:136
  47.9 0.9 %copy.23 = f32[16,16,256]{2,1,0:T(8,128)} copy(f32[16,16,256]{2,0,1:T(8,128)S(1)} %fusion) | data formatting | bytes 524288 | tf_op jit(solution)/shard_map/add | solution.py:148
  (19 shorter events, 0.2 us)
Async XLA Ops:
  0.0 42.9 %copy-start = (bf16[4096,256]{1,0:T(8,128)(2,1)S(1)}, bf16[4096,256]{1,0:T(8,128)(2,1)}, u32[]{:S(2)}) copy-start(bf16[4096,256]{1,0:T(8,128)(2,1)} %param.14) | copy-start | bytes 6291460
  0.0 3.4 %copy-start.5 = (bf16[256,768]{1,0:T(8,128)(2,1)S(1)}, bf16[256,768]{1,0:T(8,128)(2,1)}, u32[]{:S(2)}) copy-start(bf16[256,768]{1,0:T(8,128)(2,1)} %param.18) | copy-start | bytes 1179652
  0.0 6.6 %copy-start.6 = (bf16[64,256]{1,0:T(8,128)(2,1)S(1)}, bf16[64,256]{1,0:T(8,128)(2,1)}, u32[]{:S(2)}) copy-start(bf16[64,256]{1,0:T(8,128)(2,1)} %param.22) | copy-start | bytes 98308
  0.0 10.5 %copy-start.7 = (bf16[64,256]{1,0:T(8,128)(2,1)S(1)}, bf16[64,256]{1,0:T(8,128)(2,1)}, u32[]{:S(2)}) copy-start(bf16[64,256]{1,0:T(8,128)(2,1)} %param.23) | copy-start | bytes 98308
  1.5 11.7 %copy-start.3 = (bf16[128,1536]{1,0:T(8,128)(2,1)S(1)}, bf16[128,1536]{1,0:T(8,128)(2,1)}, u32[]{:S(2)}) copy-start(bf16[128,1536]{1,0:T(8,128)(2,1)} %param.20) | copy-start | bytes 1179652
  3.6 4.8 %collective-permute-start = (bf16[16,768]{1,0:T(8,128)(2,1)S(1)}, bf16[16,768]{1,0:T(8,128)(2,1)S(1)}, u32[]{:S(2)}, u32[]{:S(2)}) collective-permute-start(bf16[16,768]{1,0:T(8,128)(2,1)S(1)} %get-tuple-element.17), channel_id=1, source_target_pairs={{0,1},{1,0},{2,3},{3,2},{4,5},{5,4},{6,7},{7,6},{8,9},{9,8},{10,11... | collective-permute-start | bytes 73736 | tf_op jit(solution)/shard_map/ppermute | solution.py:25
  8.4 4.7 %collective-permute-start.1 = (bf16[16,768]{1,0:T(8,128)(2,1)S(1)}, bf16[16,768]{1,0:T(8,128)(2,1)S(1)}, u32[]{:S(2)}, u32[]{:S(2)}) collective-permute-start(bf16[16,768]{1,0:T(8,128)(2,1)S(1)} %fusion.13), channel_id=1, source_target_pairs={{0,2},{1,3},{2,0},{3,1},{4,6},{5,7},{6,4},{7,5},{8,10},{9,11},{10,... | collective-permute-start | bytes 73736 | tf_op jit(solution)/shard_map/ppermute | solution.py:25
  10.6 5.7 %collective-permute-start.6 = (bf16[64,512]{1,0:T(8,128)(2,1)S(1)}, bf16[64,512]{1,0:T(8,128)(2,1)S(1)}, u32[]{:S(2)}, u32[]{:S(2)}) collective-permute-start(bf16[64,512]{1,0:T(8,128)(2,1)S(1)} %constant_dynamic-update-slice_fusion), channel_id=1, source_target_pairs={{0,4},{1,5},{2,6},{3,7},{4,0},{5,1},{6,2},{7,3},{8,12},{9,13},{10,... | collective-permute-start | bytes 196616 | tf_op jit(solution)/shard_map/ppermute | solution.py:25
  13.3 4.9 %collective-permute-start.2 = (bf16[16,1536]{1,0:T(8,128)(2,1)S(1)}, bf16[16,1536]{1,0:T(8,128)(2,1)S(1)}, u32[]{:S(2)}, u32[]{:S(2)}) collective-permute-start(bf16[16,1536]{1,0:T(8,128)(2,1)S(1)} %get-tuple-element.19), channel_id=1, source_target_pairs={{0,12},{1,13},{2,14},{3,15},{4,8},{5,9},{6,10},{7,11},{8,4},{9,5},... | collective-permute-start | bytes 147464 | tf_op jit(solution)/shard_map/ppermute | solution.py:25
  16.3 5.0 %collective-permute-start.7 = (bf16[2,64,512]{2,1,0:T(8,128)(2,1)S(1)}, bf16[2,64,512]{2,1,0:T(8,128)(2,1)S(1)}, u32[]{:S(2)}, u32[]{:S(2)}) collective-permute-start(bf16[2,64,512]{2,1,0:T(8,128)(2,1)S(1)} %pad_maximum_fusion.3), channel_id=1, source_target_pairs={{0,1},{1,0},{2,3},{3,2},{4,5},{5,4},{6,7},{7,6},{8,9},{9,8},{10,11... | collective-permute-start | bytes 393224 | tf_op jit(solution)/shard_map/ppermute | solution.py:25
  18.3 4.3 %collective-permute-start.3 = (bf16[16,1536]{1,0:T(8,128)(2,1)S(1)}, bf16[16,1536]{1,0:T(8,128)(2,1)S(1)}, u32[]{:S(2)}, u32[]{:S(2)}) collective-permute-start(bf16[16,1536]{1,0:T(8,128)(2,1)S(1)} %fusion.7), channel_id=1, source_target_pairs={{0,9},{1,8},{2,11},{3,10},{4,13},{5,12},{6,15},{7,14},{8,1},{9,0},... | collective-permute-start | bytes 147464 | tf_op jit(solution)/shard_map/ppermute | solution.py:25
  21.4 8.3 %collective-permute-start.8 = (bf16[2,2,64,512]{3,2,1,0:T(8,128)(2,1)S(1)}, bf16[2,2,64,512]{3,2,1,0:T(8,128)(2,1)S(1)}, u32[]{:S(2)}, u32[]{:S(2)}) collective-permute-start(bf16[2,2,64,512]{3,2,1,0:T(8,128)(2,1)S(1)} %pad_maximum_fusion.2), channel_id=1, source_target_pairs={{0,2},{1,3},{2,0},{3,1},{4,6},{5,7},{6,4},{7,5},{8,10},{9,11},{10,... | collective-permute-start | bytes 786440 | tf_op jit(solution)/shard_map/ppermute | solution.py:25
  22.6 8.0 %collective-permute-start.4 = (bf16[16,1536]{1,0:T(8,128)(2,1)S(1)}, bf16[16,1536]{1,0:T(8,128)(2,1)S(1)}, u32[]{:S(2)}, u32[]{:S(2)}) collective-permute-start(bf16[16,1536]{1,0:T(8,128)(2,1)S(1)} %fusion.31), channel_id=1, source_target_pairs={{0,10},{1,11},{2,8},{3,9},{4,14},{5,15},{6,12},{7,13},{8,2},{9,3},... | collective-permute-start | bytes 147464 | tf_op jit(solution)/shard_map/ppermute | solution.py:25
  30.5 2.9 %collective-permute-start.9 = (bf16[2,2,2,64,512]{4,3,2,1,0:T(8,128)(2,1)}, bf16[2,2,2,64,512]{4,3,2,1,0:T(8,128)(2,1)S(1)}, u32[]{:S(2)}, u32[]{:S(2)}) collective-permute-start(bf16[2,2,2,64,512]{4,3,2,1,0:T(8,128)(2,1)} %pad_maximum_fusion.1), channel_id=1, source_target_pairs={{0,8},{1,9},{2,10},{3,11},{4,12},{5,13},{6,14},{7,15},{8,0},{9,1},... | collective-permute-start | bytes 1572872 | tf_op jit(solution)/shard_map/ppermute | solution.py:25
  30.6 2.1 %collective-permute-start.5 = (bf16[16,1536]{1,0:T(8,128)(2,1)S(1)}, bf16[16,1536]{1,0:T(8,128)(2,1)}, u32[]{:S(2)}, u32[]{:S(2)}) collective-permute-start(bf16[16,1536]{1,0:T(8,128)(2,1)S(1)} %fusion.8), channel_id=1, source_target_pairs={{0,8},{1,9},{2,10},{3,11},{4,12},{5,13},{6,14},{7,15},{8,0},{9,1},... | collective-permute-start | bytes 147464 | tf_op jit(solution)/shard_map/ppermute | solution.py:25
  33.6 3.6 %copy-start.4 = (bf16[128,1536]{1,0:T(8,128)(2,1)S(1)}, bf16[128,1536]{1,0:T(8,128)(2,1)}, u32[]{:S(2)}) copy-start(bf16[128,1536]{1,0:T(8,128)(2,1)} %param.21) | copy-start | bytes 1179652
  33.7 9.2 %copy-start.2 = (bf16[16,16,256]{2,1,0:T(8,128)(2,1)S(1)}, bf16[16,16,256]{2,1,0:T(8,128)(2,1)}, u32[]{:S(2)}) copy-start(bf16[16,16,256]{2,1,0:T(8,128)(2,1)} %param.12) | copy-start | bytes 393220
  33.9 3.1 %collective-permute-start.10 = (bf16[16,256]{1,0:T(8,128)(2,1)S(1)}, bf16[16,256]{1,0:T(8,128)(2,1)S(1)}, u32[]{:S(2)}, u32[]{:S(2)}) collective-permute-start(bf16[16,256]{1,0:T(8,128)(2,1)S(1)} %get-tuple-element.21), channel_id=1, source_target_pairs={{0,24},{1,25},{2,26},{3,27},{4,28},{5,29},{6,30},{7,31},{8,16},{9,... | collective-permute-start | bytes 24584 | tf_op jit(solution)/shard_map/ppermute | solution.py:25
  37.4 3.6 %collective-permute-start.11 = (bf16[16,128]{1,0:T(8,128)(2,1)S(1)}, bf16[16,128]{1,0:T(8,128)(2,1)S(1)}, u32[]{:S(2)}, u32[]{:S(2)}) collective-permute-start(bf16[16,128]{1,0:T(8,128)(2,1)S(1)} %convolution_convert_fusion.5), channel_id=1, source_target_pairs={{0,1},{1,0},{2,3},{3,2},{4,5},{5,4},{6,7},{7,6},{8,9},{9,8},{10,11... | collective-permute-start | bytes 12296 | tf_op jit(solution)/shard_map/ppermute | solution.py:25
  41.1 3.7 %collective-permute-start.12 = (bf16[16,256]{1,0:T(8,128)(2,1)S(1)}, bf16[16,256]{1,0:T(8,128)(2,1)S(1)}, u32[]{:S(2)}, u32[]{:S(2)}) collective-permute-start(bf16[16,256]{1,0:T(8,128)(2,1)S(1)} %pad_maximum_fusion.4), channel_id=1, source_target_pairs={{0,2},{1,3},{2,0},{3,1},{4,6},{5,7},{6,4},{7,5},{8,10},{9,11},{10,... | collective-permute-start | bytes 24584 | tf_op jit(solution)/shard_map/ppermute | solution.py:25
  42.9 3.1 %copy-start.1 = (bf16[1024,640]{1,0:T(8,128)(2,1)S(1)}, bf16[1024,640]{1,0:T(8,128)(2,1)}, u32[]{:S(2)}) copy-start(bf16[1024,640]{1,0:T(8,128)(2,1)} %param.17) | copy-start | bytes 3932164

commit v7 on v6

--- a/solution.py
+++ b/solution.py
@@ -106,16 +106,18 @@
     piece = lax.dynamic_slice_in_dim(first_state, k_zero + place % quad * width, width, 1)
     second_sum = product(piece, up_two)
     roots = joined_pair(roots, roots_one, place & 1 != 0, 1)
-    roots_near = swap(roots, near)
+    roots_near, roots_pair = swap(roots, near), swap(roots, pair)
     second_sum = partner_sum(second_sum, far | pair)
 
     second_sum = partner_sum(second_sum, 1 | pair)
-    roots = joined_pair(roots, roots_near, place & near != 0, 1)
-    roots_pair = swap(roots, pair)
+    low = joined_pair(roots, roots_near, place & near != 0, 1)
+    high = swap(roots_near, pair)
     second_sum = partner_sum(second_sum, near | pair)
+    second_sum, high = lax.optimization_barrier((second_sum, high))
+    high = joined_pair(roots_pair, high, place & near != 0, 1)
     second_sum = partner_sum(second_sum, pair)
     second_state = rounded(second_sum)
-    roots = joined_pair(roots, roots_pair, place & pair != 0, 0)
+    roots = joined_pair(low, high, place & pair != 0, 0)
     roots = roots.reshape(-1, roots.shape[-1])
 
     root_sum = product(second_state[:, k_one:], roots[:, :root_points])

time: 49 us -> 47.8 us (0.976)
  other arithmetic: 2.07 us -> 0.47 us
    another operation x8 -> x7, other arithmetic: 1.15 us -> 0.26 us  [joined_pair(): jnp.stack([jnp.where(upper, other, joined), jnp.where(upper, joined, othe...]
    convert_element_type x6, other arithmetic: 0.9 us -> 0.07 us  [rounded(): return value.astype(jnp.bfloat16)]
    ppermute x13 -> x14, waiting for transfers between devices: 18.8 us -> 19.2 us  [swap(): return lax.ppermute(value, AXES, [(i, i ^ mask) for i in range(count)])]
    ppermute x13 -> x14, starting transfers between devices: 18.3 us -> 18.3 us  [swap(): return lax.ppermute(value, AXES, [(i, i ^ mask) for i in range(count)])]
  transfers between devices with their start and end apart: 13 -> 14, of which waited for: 9 -> 10; matrix products, arithmetic and copies ran while one was open for 6% -> 4% of each run, Pallas kernels for 0% -> 0%
where the time goes in v7:
time: 47.8 us; the launch traced here: 47.6 us
  waiting for transfers between devices  19.2 us (40%)
  starting transfers between devices  18.3 us (38%)
  matrix products  8.24 us (17%)
  local copies, waits for them, and re-layouts  1.19 us (2%)
    ppermute x14, waiting for transfers between devices, swap(): return lax.ppermute(value, AXES, [(i, i ^ mask) for i in range(count)])  19.2 us
    ppermute x14, starting transfers between devices, swap(): return lax.ppermute(value, AXES, [(i, i ^ mask) for i in range(count)])  18.3 us
    dot_general x5, matrix products, contract(): lax.dot_general(left, right, (((1,), (1,)), ((), ())), preferred_element_...  3.88 us
    dot_general x1, matrix products, per_device(): jnp.einsum('rlq,leq->rle', source, leaf_flux.reshape(leaves, edge_count,...  1.44 us
    dot_general x1, matrix products, per_device(): jnp.einsum('rle,leq->rlq', leaf_bound, leaf_lift.reshape(leaves, edge_cou...  1.29 us
    dot_general x1, matrix products, per_device(): jnp.einsum('rlq,lqp->rlp', source, leaf_particular.reshape(leaves, points...  1.09 us
  transfers between devices with their start and end apart: 14, of which 10 were waited for; matrix products, arithmetic and copies ran while one was open for 4% of the time, Pallas kernels for 0%

profile of v7, /device:TPU:0, one launch (start us, length us, event | category | flops | bytes accessed | tf_op | source)
XLA Modules:
  0.0 47.6 jit_solution(9093984900667688900)
XLA Ops:
  0.0 0.0 copy-start
  0.0 0.0 copy-start.5
  0.0 0.0 copy-start.6
  0.0 0.0 copy-start.7
  0.0 1.4 %fusion.1 = bf16[16,16,64]{2,0,1:T(8,128)(2,1)S(1)} fusion(bf16[16,64,256]{2,1,0:T(8,128)(2,1)} %bitcast.49, bf16[16,16,256]{2,1,0:T(8,128)(2,1)} %param.12), kind=kOutput, calls=%fused_computation.4 | convolution fusion | flops 8404992 | bytes 688128 | tf_op jit(solution)/shard_map/rlq,leq->rle/dot_general | solution.py:87
  1.5 0.0 copy-start.3
  1.5 0.1 reshape.137
  1.6 1.8 %convolution_convert_fusion.3 = bf16[16,640]{1,0:T(8,128)(2,1)S(1)} fusion(bf16[16,1024]{1,0:T(8,128)(2,1)S(1)} %reshape.137, bf16[640,1024]{1,0:T(8,128)(2,1)} %param.16), kind=kOutput, calls=%fused_computation.7 | convolution fusion | flops 20981760 | bytes 1363968 | tf_op jit(solution)/shard_map/dot_general | solution.py:10
  3.4 0.0 copy-done.5
  3.4 0.2 fusion.31
  3.6 3.0 %collective-permute-start = (bf16[16,768]{1,0:T(8,128)(2,1)S(1)}, bf16[16,768]{1,0:T(8,128)(2,1)S(1)}, u32[]{:S(2)}, u32[]{:S(2)}) collective-permute-start(bf16[16,768]{1,0:T(8,128)(2,1)S(1)} %get-tuple-element.23), channel_id=1, source_target_pairs={{0,1},{1,0},{2,3},{3,2},{4,5},{5,4},{6,7},{7,6},{8,9},{9,8},{10,11... | collective-permute-start | bytes 73736 | tf_op jit(solution)/shard_map/ppermute | solution.py:25
  6.6 0.0 copy-done.6
  6.6 1.8 %collective-permute-done = bf16[16,768]{1,0:T(8,128)(2,1)S(1)} collective-permute-done((bf16[16,768]{1,0:T(8,128)(2,1)S(1)}, bf16[16,768]{1,0:T(8,128)(2,1)S(1)}, u32[]{:S(2)}, u32[]{:S(2)}) %collective-permute-start) | collective-permute-done | bytes 24608 | tf_op jit(solution)/shard_map/ppermute | solution.py:25
  8.4 2.1 %collective-permute-start.1 = (bf16[16,768]{1,0:T(8,128)(2,1)S(1)}, bf16[16,768]{1,0:T(8,128)(2,1)S(1)}, u32[]{:S(2)}, u32[]{:S(2)}) collective-permute-start(bf16[16,768]{1,0:T(8,128)(2,1)S(1)} %fusion.13), channel_id=1, source_target_pairs={{0,2},{1,3},{2,0},{3,1},{4,6},{5,7},{6,4},{7,5},{8,10},{9,11},{10,... | collective-permute-start | bytes 73736 | tf_op jit(solution)/shard_map/ppermute | solution.py:25
  10.5 0.0 copy-done.7
  10.6 2.6 %collective-permute-start.5 = (bf16[64,512]{1,0:T(8,128)(2,1)S(1)}, bf16[64,512]{1,0:T(8,128)(2,1)S(1)}, u32[]{:S(2)}, u32[]{:S(2)}) collective-permute-start(bf16[64,512]{1,0:T(8,128)(2,1)S(1)} %constant_dynamic-update-slice_fusion), channel_id=1, source_target_pairs={{0,4},{1,5},{2,6},{3,7},{4,0},{5,1},{6,2},{7,3},{8,12},{9,13},{10,... | collective-permute-start | bytes 196616 | tf_op jit(solution)/shard_map/ppermute | solution.py:25
  13.1 0.0 collective-permute-done.1
  13.2 0.0 copy-done.3
  13.2 0.2 fusion.32
  13.3 0.1 collective-permute-start.2
  13.4 2.8 %collective-permute-done.5 = bf16[64,512]{1,0:T(8,128)(2,1)S(1)} collective-permute-done((bf16[64,512]{1,0:T(8,128)(2,1)S(1)}, bf16[64,512]{1,0:T(8,128)(2,1)S(1)}, u32[]{:S(2)}, u32[]{:S(2)}) %collective-permute-start.5) | collective-permute-done | bytes 65568 | tf_op jit(solution)/shard_map/ppermute | solution.py:25
  16.3 1.7 %collective-permute-start.6 = (bf16[2,64,512]{2,1,0:T(8,128)(2,1)S(1)}, bf16[2,64,512]{2,1,0:T(8,128)(2,1)S(1)}, u32[]{:S(2)}, u32[]{:S(2)}) collective-permute-start(bf16[2,64,512]{2,1,0:T(8,128)(2,1)S(1)} %pad_maximum_fusion.4), channel_id=1, source_target_pairs={{0,1},{1,0},{2,3},{3,2},{4,5},{5,4},{6,7},{7,6},{8,9},{9,8},{10,11... | collective-permute-start | bytes 393224 | tf_op jit(solution)/shard_map/ppermute | solution.py:25
  17.9 0.3 collective-permute-done.2
  18.3 1.2 %collective-permute-start.3 = (bf16[16,1536]{1,0:T(8,128)(2,1)S(1)}, bf16[16,1536]{1,0:T(8,128)(2,1)S(1)}, u32[]{:S(2)}, u32[]{:S(2)}) collective-permute-start(bf16[16,1536]{1,0:T(8,128)(2,1)S(1)} %fusion.7), channel_id=1, source_target_pairs={{0,9},{1,8},{2,11},{3,10},{4,13},{5,12},{6,15},{7,14},{8,1},{9,0},... | collective-permute-start | bytes 147464 | tf_op jit(solution)/shard_map/ppermute | solution.py:25
  19.4 1.9 %collective-permute-done.6 = bf16[2,64,512]{2,1,0:T(8,128)(2,1)S(1)} collective-permute-done((bf16[2,64,512]{2,1,0:T(8,128)(2,1)S(1)}, bf16[2,64,512]{2,1,0:T(8,128)(2,1)S(1)}, u32[]{:S(2)}, u32[]{:S(2)}) %collective-permute-start.6) | collective-permute-done | bytes 131104 | tf_op jit(solution)/shard_map/ppermute | solution.py:25
  21.4 1.2 %collective-permute-start.7 = (bf16[2,2,64,512]{3,2,1,0:T(8,128)(2,1)S(1)}, bf16[2,2,64,512]{3,2,1,0:T(8,128)(2,1)S(1)}, u32[]{:S(2)}, u32[]{:S(2)}) collective-permute-start(bf16[2,2,64,512]{3,2,1,0:T(8,128)(2,1)S(1)} %pad_maximum_fusion.3), channel_id=1, source_target_pairs={{0,2},{1,3},{2,0},{3,1},{4,6},{5,7},{6,4},{7,5},{8,10},{9,11},{10,... | collective-permute-start | bytes 786440 | tf_op jit(solution)/shard_map/ppermute | solution.py:25
  22.5 0.0 collective-permute-done.3
  22.6 1.0 %collective-permute-start.4 = (bf16[16,1536]{1,0:T(8,128)(2,1)S(1)}, bf16[16,1536]{1,0:T(8,128)(2,1)S(1)}, u32[]{:S(2)}, u32[]{:S(2)}) collective-permute-start(bf16[16,1536]{1,0:T(8,128)(2,1)S(1)} %fusion.12), channel_id=1, source_target_pairs={{0,10},{1,11},{2,8},{3,9},{4,14},{5,15},{6,12},{7,13},{8,2},{9,3},... | collective-permute-start | bytes 147464 | tf_op jit(solution)/shard_map/ppermute | solution.py:25
  23.5 0.4 collective-permute-start.10
  23.9 5.7 %collective-permute-done.7 = bf16[2,2,64,512]{3,2,1,0:T(8,128)(2,1)S(1)} collective-permute-done((bf16[2,2,64,512]{3,2,1,0:T(8,128)(2,1)S(1)}, bf16[2,2,64,512]{3,2,1,0:T(8,128)(2,1)S(1)}, u32[]{:S(2)}, u32[]{:S(2)}) %collective-permute-start.7) | collective-permute-done | bytes 262176 | tf_op jit(solution)/shard_map/ppermute | solution.py:25
  29.6 0.0 collective-permute-start.8
  29.7 0.0 collective-permute-done.4
  29.7 1.5 %collective-permute-done.8 = bf16[2,2,64,512]{3,2,1,0:T(8,128)(2,1)S(1)} collective-permute-done((bf16[2,2,64,512]{3,2,1,0:T(8,128)(2,1)S(1)}, bf16[2,2,64,512]{3,2,1,0:T(8,128)(2,1)S(1)}, u32[]{:S(2)}, u32[]{:S(2)}) %collective-permute-start.8) | collective-permute-done | bytes 262176 | tf_op jit(solution)/shard_map/ppermute | solution.py:25
  31.2 0.2 collective-permute-start.9
  31.4 0.0 collective-permute-done.10
  31.4 0.1 broadcast_select_fusion.1
  31.5 0.0 copy-start.4
  31.5 0.1 pad_maximum_fusion
  31.6 0.0 copy-start.2
  31.6 0.8 %collective-permute-done.9 = bf16[16,1536]{1,0:T(8,128)(2,1)S(1)} collective-permute-done((bf16[16,1536]{1,0:T(8,128)(2,1)S(1)}, bf16[16,1536]{1,0:T(8,128)(2,1)S(1)}, u32[]{:S(2)}, u32[]{:S(2)}) %collective-permute-start.9) | collective-permute-done | bytes 49184 | tf_op jit(solution)/shard_map/ppermute | solution.py:25
  32.5 0.2 fusion.33
  32.7 1.4 %collective-permute-start.11 = (bf16[16,256]{1,0:T(8,128)(2,1)S(1)}, bf16[16,256]{1,0:T(8,128)(2,1)S(1)}, u32[]{:S(2)}, u32[]{:S(2)}) collective-permute-start(bf16[16,256]{1,0:T(8,128)(2,1)S(1)} %get-tuple-element.27), channel_id=1, source_target_pairs={{0,24},{1,25},{2,26},{3,27},{4,28},{5,29},{6,30},{7,31},{8,16},{9,... | collective-permute-start | bytes 24584 | tf_op jit(solution)/shard_map/ppermute | solution.py:25
  34.1 1.6 %collective-permute-done.11 = bf16[16,256]{1,0:T(8,128)(2,1)S(1)} collective-permute-done((bf16[16,256]{1,0:T(8,128)(2,1)S(1)}, bf16[16,256]{1,0:T(8,128)(2,1)S(1)}, u32[]{:S(2)}, u32[]{:S(2)}) %collective-permute-start.11) | collective-permute-done | bytes 8224 | tf_op jit(solution)/shard_map/ppermute | solution.py:25
  35.8 0.2 convolution_convert_fusion.2
  36.0 0.0 copy-done.4
  36.0 0.2 convolution_convert_fusion.5
  36.2 1.7 %collective-permute-start.12 = (bf16[16,128]{1,0:T(8,128)(2,1)S(1)}, bf16[16,128]{1,0:T(8,128)(2,1)S(1)}, u32[]{:S(2)}, u32[]{:S(2)}) collective-permute-start(bf16[16,128]{1,0:T(8,128)(2,1)S(1)} %convolution_convert_fusion.5), channel_id=1, source_target_pairs={{0,1},{1,0},{2,3},{3,2},{4,5},{5,4},{6,7},{7,6},{8,9},{9,8},{10,11... | collective-permute-start | bytes 12296 | tf_op jit(solution)/shard_map/ppermute | solution.py:25
  37.9 1.9 %collective-permute-done.12 = bf16[16,128]{1,0:T(8,128)(2,1)S(1)} collective-permute-done((bf16[16,128]{1,0:T(8,128)(2,1)S(1)}, bf16[16,128]{1,0:T(8,128)(2,1)S(1)}, u32[]{:S(2)}, u32[]{:S(2)}) %collective-permute-start.12) | collective-permute-done | bytes 4128 | tf_op jit(solution)/shard_map/ppermute | solution.py:25
  39.9 1.8 %collective-permute-start.13 = (bf16[16,256]{1,0:T(8,128)(2,1)S(1)}, bf16[16,256]{1,0:T(8,128)(2,1)S(1)}, u32[]{:S(2)}, u32[]{:S(2)}) collective-permute-start(bf16[16,256]{1,0:T(8,128)(2,1)S(1)} %pad_maximum_fusion.5), channel_id=1, source_target_pairs={{0,2},{1,3},{2,0},{3,1},{4,6},{5,7},{6,4},{7,5},{8,10},{9,11},{10,... | collective-permute-start | bytes 24584 | tf_op jit(solution)/shard_map/ppermute | solution.py:25
  41.7 0.0 copy-done
  41.7 0.0 copy-done.2
  41.7 0.0 copy-start.1
  41.7 1.1 %convolution_bitcast_fusion.1 = f32[16,16,256]{2,0,1:T(8,128)} fusion(bf16[16,256,256]{2,1,0:T(8,128)(2,1)S(1)} %bitcast.46, bf16[16,16,256]{2,1,0:T(8,128)(2,1)S(1)} %copy-done.2), kind=kOutput, calls=%fused_computation.2 | convolution fusion | flops 33554432 | bytes 2490368 | tf_op jit(solution)/shard_map/rlq,lqp->rlp/dot_general | solution.py:144
  42.8 0.8 %collective-permute-done.13 = bf16[16,256]{1,0:T(8,128)(2,1)S(1)} collective-permute-done((bf16[16,256]{1,0:T(8,128)(2,1)S(1)}, bf16[16,256]{1,0:T(8,128)(2,1)S(1)}, u32[]{:S(2)}, u32[]{:S(2)}) %collective-permute-start.13) | collective-permute-done | bytes 8224 | tf_op jit(solution)/shard_map/ppermute | solution.py:25
  43.6 1.2 %convolution_convert_fusion.4 = bf16[16,256]{1,0:T(8,128)(2,1)S(1)} fusion(bf16[256,768]{1,0:T(8,128)(2,1)} %param.19, bf16[16,256]{1,0:T(8,128)(2,1)S(1)} %get-tuple-element.20, bf16[16,256]{1,0:T(8,128)(2,1)S(1)} %get-tuple-element.19, bf16[16,256]{1,0:T(8,128)(2,1)S(1)} %slice.30), kind=kOutput, calls=%fused_computation.8 | convolution fusion | flops 6369280 | bytes 425984 | tf_op jit(solution)/shard_map/dot_general | solution.py:10
  44.8 0.0 copy-done.1
  44.8 0.5 %convolution_convert_fusion.1 = bf16[16,1024]{1,0:T(8,128)(2,1)S(1)} fusion(bf16[1024,640]{1,0:T(8,128)(2,1)S(1)} %copy-done.1, bf16[16,256]{1,0:T(8,128)(2,1)S(1)} %convolution_convert_fusion.4, bf16[16,384]{1,0:T(8,128)(2,1)S(1)} %slice.28), kind=kOutput, calls=%fused_computation.5 | convolution fusion | flops 21028864 | bytes 1363968 | tf_op jit(solution)/shard_map/dot_general | solution.py:10
  45.3 0.1 reshape.139
  45.4 1.3 %fusion = f32[16,16,256]{2,0,1:T(8,128)S(1)} fusion(f32[16,16,256]{2,0,1:T(8,128)} %convolution_bitcast_fusion.1, bf16[16,64,256]{2,1,0:T(8,128)(2,1)} %bitcast.50, bf16[16,16,64]{2,1,0:T(8,128)(2,1)S(1)} %reshape.139), kind=kOutput, calls=%fused_computation.1 | convolution fusion | flops 8454144 | bytes 1081344 | tf_op jit(solution)/shard_map/rle,leq->rlq/dot_general | solution.py:138
  46.7 0.9 %copy.25 = f32[16,16,256]{2,1,0:T(8,128)} copy(f32[16,16,256]{2,0,1:T(8,128)S(1)} %fusion) | data formatting | bytes 524288 | tf_op jit(solution)/shard_map/add | solution.py:150
  (22 shorter events, 0.3 us)
Async XLA Ops:
  0.0 41.7 %copy-start = (bf16[4096,256]{1,0:T(8,128)(2,1)S(1)}, bf16[4096,256]{1,0:T(8,128)(2,1)}, u32[]{:S(2)}) copy-start(bf16[4096,256]{1,0:T(8,128)(2,1)} %param.14) | copy-start | bytes 6291460
  0.0 3.4 %copy-start.5 = (bf16[256,768]{1,0:T(8,128)(2,1)S(1)}, bf16[256,768]{1,0:T(8,128)(2,1)}, u32[]{:S(2)}) copy-start(bf16[256,768]{1,0:T(8,128)(2,1)} %param.18) | copy-start | bytes 1179652
  0.0 6.6 %copy-start.6 = (bf16[64,256]{1,0:T(8,128)(2,1)S(1)}, bf16[64,256]{1,0:T(8,128)(2,1)}, u32[]{:S(2)}) copy-start(bf16[64,256]{1,0:T(8,128)(2,1)} %param.22) | copy-start | bytes 98308
  0.0 10.5 %copy-start.7 = (bf16[64,256]{1,0:T(8,128)(2,1)S(1)}, bf16[64,256]{1,0:T(8,128)(2,1)}, u32[]{:S(2)}) copy-start(bf16[64,256]{1,0:T(8,128)(2,1)} %param.23) | copy-start | bytes 98308
  1.5 11.7 %copy-start.3 = (bf16[128,1536]{1,0:T(8,128)(2,1)S(1)}, bf16[128,1536]{1,0:T(8,128)(2,1)}, u32[]{:S(2)}) copy-start(bf16[128,1536]{1,0:T(8,128)(2,1)} %param.20) | copy-start | bytes 1179652
  3.6 4.8 %collective-permute-start = (bf16[16,768]{1,0:T(8,128)(2,1)S(1)}, bf16[16,768]{1,0:T(8,128)(2,1)S(1)}, u32[]{:S(2)}, u32[]{:S(2)}) collective-permute-start(bf16[16,768]{1,0:T(8,128)(2,1)S(1)} %get-tuple-element.23), channel_id=1, source_target_pairs={{0,1},{1,0},{2,3},{3,2},{4,5},{5,4},{6,7},{7,6},{8,9},{9,8},{10,11... | collective-permute-start | bytes 73736 | tf_op jit(solution)/shard_map/ppermute | solution.py:25
  8.4 4.7 %collective-permute-start.1 = (bf16[16,768]{1,0:T(8,128)(2,1)S(1)}, bf16[16,768]{1,0:T(8,128)(2,1)S(1)}, u32[]{:S(2)}, u32[]{:S(2)}) collective-permute-start(bf16[16,768]{1,0:T(8,128)(2,1)S(1)} %fusion.13), channel_id=1, source_target_pairs={{0,2},{1,3},{2,0},{3,1},{4,6},{5,7},{6,4},{7,5},{8,10},{9,11},{10,... | collective-permute-start | bytes 73736 | tf_op jit(solution)/shard_map/ppermute | solution.py:25
  10.6 5.7 %collective-permute-start.5 = (bf16[64,512]{1,0:T(8,128)(2,1)S(1)}, bf16[64,512]{1,0:T(8,128)(2,1)S(1)}, u32[]{:S(2)}, u32[]{:S(2)}) collective-permute-start(bf16[64,512]{1,0:T(8,128)(2,1)S(1)} %constant_dynamic-update-slice_fusion), channel_id=1, source_target_pairs={{0,4},{1,5},{2,6},{3,7},{4,0},{5,1},{6,2},{7,3},{8,12},{9,13},{10,... | collective-permute-start | bytes 196616 | tf_op jit(solution)/shard_map/ppermute | solution.py:25
  13.3 4.9 %collective-permute-start.2 = (bf16[16,1536]{1,0:T(8,128)(2,1)S(1)}, bf16[16,1536]{1,0:T(8,128)(2,1)S(1)}, u32[]{:S(2)}, u32[]{:S(2)}) collective-permute-start(bf16[16,1536]{1,0:T(8,128)(2,1)S(1)} %get-tuple-element.25), channel_id=1, source_target_pairs={{0,12},{1,13},{2,14},{3,15},{4,8},{5,9},{6,10},{7,11},{8,4},{9,5},... | collective-permute-start | bytes 147464 | tf_op jit(solution)/shard_map/ppermute | solution.py:25
  16.3 5.0 %collective-permute-start.6 = (bf16[2,64,512]{2,1,0:T(8,128)(2,1)S(1)}, bf16[2,64,512]{2,1,0:T(8,128)(2,1)S(1)}, u32[]{:S(2)}, u32[]{:S(2)}) collective-permute-start(bf16[2,64,512]{2,1,0:T(8,128)(2,1)S(1)} %pad_maximum_fusion.4), channel_id=1, source_target_pairs={{0,1},{1,0},{2,3},{3,2},{4,5},{5,4},{6,7},{7,6},{8,9},{9,8},{10,11... | collective-permute-start | bytes 393224 | tf_op jit(solution)/shard_map/ppermute | solution.py:25
  18.3 4.3 %collective-permute-start.3 = (bf16[16,1536]{1,0:T(8,128)(2,1)S(1)}, bf16[16,1536]{1,0:T(8,128)(2,1)S(1)}, u32[]{:S(2)}, u32[]{:S(2)}) collective-permute-start(bf16[16,1536]{1,0:T(8,128)(2,1)S(1)} %fusion.7), channel_id=1, source_target_pairs={{0,9},{1,8},{2,11},{3,10},{4,13},{5,12},{6,15},{7,14},{8,1},{9,0},... | collective-permute-start | bytes 147464 | tf_op jit(solution)/shard_map/ppermute | solution.py:25
  21.4 8.3 %collective-permute-start.7 = (bf16[2,2,64,512]{3,2,1,0:T(8,128)(2,1)S(1)}, bf16[2,2,64,512]{3,2,1,0:T(8,128)(2,1)S(1)}, u32[]{:S(2)}, u32[]{:S(2)}) collective-permute-start(bf16[2,2,64,512]{3,2,1,0:T(8,128)(2,1)S(1)} %pad_maximum_fusion.3), channel_id=1, source_target_pairs={{0,2},{1,3},{2,0},{3,1},{4,6},{5,7},{6,4},{7,5},{8,10},{9,11},{10,... | collective-permute-start | bytes 786440 | tf_op jit(solution)/shard_map/ppermute | solution.py:25
  22.6 7.1 %collective-permute-start.4 = (bf16[16,1536]{1,0:T(8,128)(2,1)S(1)}, bf16[16,1536]{1,0:T(8,128)(2,1)S(1)}, u32[]{:S(2)}, u32[]{:S(2)}) collective-permute-start(bf16[16,1536]{1,0:T(8,128)(2,1)S(1)} %fusion.12), channel_id=1, source_target_pairs={{0,10},{1,11},{2,8},{3,9},{4,14},{5,15},{6,12},{7,13},{8,2},{9,3},... | collective-permute-start | bytes 147464 | tf_op jit(solution)/shard_map/ppermute | solution.py:25
  23.5 7.8 %collective-permute-start.10 = (bf16[2,2,64,512]{3,2,1,0:T(8,128)(2,1)S(1)}, bf16[2,2,64,512]{3,2,1,0:T(8,128)(2,1)S(1)}, u32[]{:S(2)}, u32[]{:S(2)}) collective-permute-start(bf16[2,2,64,512]{3,2,1,0:T(8,128)(2,1)S(1)} %pad_maximum_fusion.3), channel_id=1, source_target_pairs={{0,8},{1,9},{2,10},{3,11},{4,12},{5,13},{6,14},{7,15},{8,0},{9,1},... | collective-permute-start | bytes 786440 | tf_op jit(solution)/shard_map/ppermute | solution.py:25
  29.6 1.5 %collective-permute-start.8 = (bf16[2,2,64,512]{3,2,1,0:T(8,128)(2,1)S(1)}, bf16[2,2,64,512]{3,2,1,0:T(8,128)(2,1)S(1)}, u32[]{:S(2)}, u32[]{:S(2)}) collective-permute-start(bf16[2,2,64,512]{3,2,1,0:T(8,128)(2,1)S(1)} %collective-permute-done.7), channel_id=1, source_target_pairs={{0,8},{1,9},{2,10},{3,11},{4,12},{5,13},{6,14},{7,15},{8,0},{9,1},... | collective-permute-start | bytes 786440 | tf_op jit(solution)/shard_map/ppermute | solution.py:25
  31.2 1.3 %collective-permute-start.9 = (bf16[16,1536]{1,0:T(8,128)(2,1)S(1)}, bf16[16,1536]{1,0:T(8,128)(2,1)S(1)}, u32[]{:S(2)}, u32[]{:S(2)}) collective-permute-start(bf16[16,1536]{1,0:T(8,128)(2,1)S(1)} %convert_element_type.86), channel_id=1, source_target_pairs={{0,8},{1,9},{2,10},{3,11},{4,12},{5,13},{6,14},{7,15},{8,0},{9,1},... | collective-permute-start | bytes 147464 | tf_op jit(solution)/shard_map/ppermute | solution.py:25
  31.5 4.5 %copy-start.4 = (bf16[128,1536]{1,0:T(8,128)(2,1)S(1)}, bf16[128,1536]{1,0:T(8,128)(2,1)}, u32[]{:S(2)}) copy-start(bf16[128,1536]{1,0:T(8,128)(2,1)} %param.21) | copy-start | bytes 1179652
  31.6 10.0 %copy-start.2 = (bf16[16,16,256]{2,1,0:T(8,128)(2,1)S(1)}, bf16[16,16,256]{2,1,0:T(8,128)(2,1)}, u32[]{:S(2)}) copy-start(bf16[16,16,256]{2,1,0:T(8,128)(2,1)} %param.12) | copy-start | bytes 393220
  32.7 3.1 %collective-permute-start.11 = (bf16[16,256]{1,0:T(8,128)(2,1)S(1)}, bf16[16,256]{1,0:T(8,128)(2,1)S(1)}, u32[]{:S(2)}, u32[]{:S(2)}) collective-permute-start(bf16[16,256]{1,0:T(8,128)(2,1)S(1)} %get-tuple-element.27), channel_id=1, source_target_pairs={{0,24},{1,25},{2,26},{3,27},{4,28},{5,29},{6,30},{7,31},{8,16},{9,... | collective-permute-start | bytes 24584 | tf_op jit(solution)/shard_map/ppermute | solution.py:25
  36.2 3.6 %collective-permute-start.12 = (bf16[16,128]{1,0:T(8,128)(2,1)S(1)}, bf16[16,128]{1,0:T(8,128)(2,1)S(1)}, u32[]{:S(2)}, u32[]{:S(2)}) collective-permute-start(bf16[16,128]{1,0:T(8,128)(2,1)S(1)} %convolution_convert_fusion.5), channel_id=1, source_target_pairs={{0,1},{1,0},{2,3},{3,2},{4,5},{5,4},{6,7},{7,6},{8,9},{9,8},{10,11... | collective-permute-start | bytes 12296 | tf_op jit(solution)/shard_map/ppermute | solution.py:25
  39.9 3.7 %collective-permute-start.13 = (bf16[16,256]{1,0:T(8,128)(2,1)S(1)}, bf16[16,256]{1,0:T(8,128)(2,1)S(1)}, u32[]{:S(2)}, u32[]{:S(2)}) collective-permute-start(bf16[16,256]{1,0:T(8,128)(2,1)S(1)} %pad_maximum_fusion.5), channel_id=1, source_target_pairs={{0,2},{1,3},{2,0},{3,1},{4,6},{5,7},{6,4},{7,5},{8,10},{9,11},{10,... | collective-permute-start | bytes 24584 | tf_op jit(solution)/shard_map/ppermute | solution.py:25
  41.7 3.1 %copy-start.1 = (bf16[1024,640]{1,0:T(8,128)(2,1)S(1)}, bf16[1024,640]{1,0:T(8,128)(2,1)}, u32[]{:S(2)}) copy-start(bf16[1024,640]{1,0:T(8,128)(2,1)} %param.17) | copy-start | bytes 3932164

commit v8 on v7

--- a/solution.py
+++ b/solution.py
@@ -99,6 +99,7 @@
     first_sum = partner_sum(first_sum, 1)
 
     roots = joined_pair(roots, roots_far, place & far != 0, 0)
+    roots = swap(swap(roots, pair), pair)
     roots_one = swap(roots, 1)
     first_sum = partner_sum(first_sum, near)
     first_state = rounded(first_sum)

time: 47.8 us -> 48.6 us (1.017)
  waiting for transfers between devices: 19.2 us -> 20.5 us
  starting transfers between devices: 18.3 us -> 17.8 us
    ppermute x14 -> x16, waiting for transfers between devices: 19.2 us -> 20.5 us  [swap(): return lax.ppermute(value, AXES, [(i, i ^ mask) for i in range(count)])]
    ppermute x14 -> x16, starting transfers between devices: 18.3 us -> 17.8 us  [swap(): return lax.ppermute(value, AXES, [(i, i ^ mask) for i in range(count)])]
  transfers between devices with their start and end apart: 14 -> 16, of which waited for: 10 -> 11; matrix products, arithmetic and copies ran while one was open for 4% -> 4% of each run, Pallas kernels for 0% -> 0%
where the time goes in v8:
time: 48.6 us; the launch traced here: 48.5 us
  waiting for transfers between devices  20.5 us (42%)
  starting transfers between devices  17.8 us (37%)
  matrix products  8.28 us (17%)
  local copies, waits for them, and re-layouts  1.2 us (2%)
    ppermute x16, waiting for transfers between devices, swap(): return lax.ppermute(value, AXES, [(i, i ^ mask) for i in range(count)])  20.5 us
    ppermute x16, starting transfers between devices, swap(): return lax.ppermute(value, AXES, [(i, i ^ mask) for i in range(count)])  17.8 us
    dot_general x5, matrix products, contract(): lax.dot_general(left, right, (((1,), (1,)), ((), ())), preferred_element_...  3.93 us
    dot_general x1, matrix products, per_device(): jnp.einsum('rlq,leq->rle', source, leaf_flux.reshape(leaves, edge_count,...  1.44 us
    dot_general x1, matrix products, per_device(): jnp.einsum('rle,leq->rlq', leaf_bound, leaf_lift.reshape(leaves, edge_cou...  1.29 us
    dot_general x1, matrix products, per_device(): jnp.einsum('rlq,lqp->rlp', source, leaf_particular.reshape(leaves, points...  1.09 us
  transfers between devices with their start and end apart: 16, of which 11 were waited for; matrix products, arithmetic and copies ran while one was open for 4% of the time, Pallas kernels for 0%

profile of v8, /device:TPU:0, one launch (start us, length us, event | category | flops | bytes accessed | tf_op | source)
XLA Modules:
  0.0 48.5 jit_solution(12642443990254857849)
XLA Ops:
  0.0 0.0 copy-start
  0.0 0.0 copy-start.5
  0.0 0.0 copy-start.6
  0.0 0.0 copy-start.7
  0.0 1.4 %fusion.1 = bf16[16,16,64]{2,0,1:T(8,128)(2,1)S(1)} fusion(bf16[16,64,256]{2,1,0:T(8,128)(2,1)} %bitcast.49, bf16[16,16,256]{2,1,0:T(8,128)(2,1)} %param.12), kind=kOutput, calls=%fused_computation.4 | convolution fusion | flops 8404992 | bytes 688128 | tf_op jit(solution)/shard_map/rlq,leq->rle/dot_general | solution.py:87
  1.5 0.1 reshape.137
  1.6 0.0 copy-start.3
  1.6 1.8 %convolution_convert_fusion.3 = bf16[16,640]{1,0:T(8,128)(2,1)S(1)} fusion(bf16[16,1024]{1,0:T(8,128)(2,1)S(1)} %reshape.137, bf16[640,1024]{1,0:T(8,128)(2,1)} %param.16), kind=kOutput, calls=%fused_computation.7 | convolution fusion | flops 20981760 | bytes 1363968 | tf_op jit(solution)/shard_map/dot_general | solution.py:10
  3.4 0.0 copy-done.5
  3.4 0.2 fusion.31
  3.6 3.0 %collective-permute-start = (bf16[16,768]{1,0:T(8,128)(2,1)S(1)}, bf16[16,768]{1,0:T(8,128)(2,1)S(1)}, u32[]{:S(2)}, u32[]{:S(2)}) collective-permute-start(bf16[16,768]{1,0:T(8,128)(2,1)S(1)} %get-tuple-element.23), channel_id=1, source_target_pairs={{0,1},{1,0},{2,3},{3,2},{4,5},{5,4},{6,7},{7,6},{8,9},{9,8},{10,11... | collective-permute-start | bytes 73736 | tf_op jit(solution)/shard_map/ppermute | solution.py:25
  6.6 0.0 copy-done.6
  6.7 0.0 copy-done.7
  6.7 2.7 %collective-permute-start.5 = (bf16[64,512]{1,0:T(8,128)(2,1)S(1)}, bf16[64,512]{1,0:T(8,128)(2,1)S(1)}, u32[]{:S(2)}, u32[]{:S(2)}) collective-permute-start(bf16[64,512]{1,0:T(8,128)(2,1)S(1)} %constant_dynamic-update-slice_fusion), channel_id=1, source_target_pairs={{0,4},{1,5},{2,6},{3,7},{4,0},{5,1},{6,2},{7,3},{8,12},{9,13},{10,... | collective-permute-start | bytes 196616 | tf_op jit(solution)/shard_map/ppermute | solution.py:25
  9.3 0.0 collective-permute-done
  9.3 1.6 %collective-permute-start.1 = (bf16[16,768]{1,0:T(8,128)(2,1)S(1)}, bf16[16,768]{1,0:T(8,128)(2,1)S(1)}, u32[]{:S(2)}, u32[]{:S(2)}) collective-permute-start(bf16[16,768]{1,0:T(8,128)(2,1)S(1)} %fusion.13), channel_id=1, source_target_pairs={{0,2},{1,3},{2,0},{3,1},{4,6},{5,7},{6,4},{7,5},{8,10},{9,11},{10,... | collective-permute-start | bytes 73736 | tf_op jit(solution)/shard_map/ppermute | solution.py:25
  11.0 1.3 %collective-permute-done.5 = bf16[64,512]{1,0:T(8,128)(2,1)S(1)} collective-permute-done((bf16[64,512]{1,0:T(8,128)(2,1)S(1)}, bf16[64,512]{1,0:T(8,128)(2,1)S(1)}, u32[]{:S(2)}, u32[]{:S(2)}) %collective-permute-start.5) | collective-permute-done | bytes 65568 | tf_op jit(solution)/shard_map/ppermute | solution.py:25
  12.3 0.1 collective-permute-start.6
  12.4 0.9 %collective-permute-done.1 = bf16[16,768]{1,0:T(8,128)(2,1)S(1)} collective-permute-done((bf16[16,768]{1,0:T(8,128)(2,1)S(1)}, bf16[16,768]{1,0:T(8,128)(2,1)S(1)}, u32[]{:S(2)}, u32[]{:S(2)}) %collective-permute-start.1) | collective-permute-done | bytes 24608 | tf_op jit(solution)/shard_map/ppermute | solution.py:25
  13.2 0.4 collective-permute-done.6
  13.7 0.1 collective-permute-start.7
  13.8 0.0 copy-done.3
  13.8 0.2 fusion.32
  14.0 2.6 %collective-permute-start.2 = (bf16[16,1536]{1,0:T(8,128)(2,1)S(1)}, bf16[16,1536]{1,0:T(8,128)(2,1)S(1)}, u32[]{:S(2)}, u32[]{:S(2)}) collective-permute-start(bf16[16,1536]{1,0:T(8,128)(2,1)S(1)} %get-tuple-element.25), channel_id=1, source_target_pairs={{0,12},{1,13},{2,14},{3,15},{4,8},{5,9},{6,10},{7,11},{8,4},{9,5},... | collective-permute-start | bytes 147464 | tf_op jit(solution)/shard_map/ppermute | solution.py:25
  16.6 0.0 collective-permute-done.7
  16.6 0.8 %collective-permute-start.8 = (bf16[2,64,512]{2,1,0:T(8,128)(2,1)S(1)}, bf16[2,64,512]{2,1,0:T(8,128)(2,1)S(1)}, u32[]{:S(2)}, u32[]{:S(2)}) collective-permute-start(bf16[2,64,512]{2,1,0:T(8,128)(2,1)S(1)} %collective-permute-done.7), channel_id=1, source_target_pairs={{0,1},{1,0},{2,3},{3,2},{4,5},{5,4},{6,7},{7,6},{8,9},{9,8},{10,11... | collective-permute-start | bytes 393224 | tf_op jit(solution)/shard_map/ppermute | solution.py:25
  17.4 1.1 %collective-permute-done.2 = bf16[16,1536]{1,0:T(8,128)(2,1)S(1)} collective-permute-done((bf16[16,1536]{1,0:T(8,128)(2,1)S(1)}, bf16[16,1536]{1,0:T(8,128)(2,1)S(1)}, u32[]{:S(2)}, u32[]{:S(2)}) %collective-permute-start.2) | collective-permute-done | bytes 49184 | tf_op jit(solution)/shard_map/ppermute | solution.py:25
  18.5 0.8 %collective-permute-start.3 = (bf16[16,1536]{1,0:T(8,128)(2,1)S(1)}, bf16[16,1536]{1,0:T(8,128)(2,1)S(1)}, u32[]{:S(2)}, u32[]{:S(2)}) collective-permute-start(bf16[16,1536]{1,0:T(8,128)(2,1)S(1)} %fusion.7), channel_id=1, source_target_pairs={{0,9},{1,8},{2,11},{3,10},{4,13},{5,12},{6,15},{7,14},{8,1},{9,0},... | collective-permute-start | bytes 147464 | tf_op jit(solution)/shard_map/ppermute | solution.py:25
  19.3 3.4 %collective-permute-done.8 = bf16[2,64,512]{2,1,0:T(8,128)(2,1)S(1)} collective-permute-done((bf16[2,64,512]{2,1,0:T(8,128)(2,1)S(1)}, bf16[2,64,512]{2,1,0:T(8,128)(2,1)S(1)}, u32[]{:S(2)}, u32[]{:S(2)}) %collective-permute-start.8) | collective-permute-done | bytes 131104 | tf_op jit(solution)/shard_map/ppermute | solution.py:25
  22.8 1.6 %collective-permute-start.9 = (bf16[2,2,64,512]{3,2,1,0:T(8,128)(2,1)S(1)}, bf16[2,2,64,512]{3,2,1,0:T(8,128)(2,1)S(1)}, u32[]{:S(2)}, u32[]{:S(2)}) collective-permute-start(bf16[2,2,64,512]{3,2,1,0:T(8,128)(2,1)S(1)} %pad_maximum_fusion.3), channel_id=1, source_target_pairs={{0,2},{1,3},{2,0},{3,1},{4,6},{5,7},{6,4},{7,5},{8,10},{9,11},{10,... | collective-permute-start | bytes 786440 | tf_op jit(solution)/shard_map/ppermute | solution.py:25
  24.4 0.0 collective-permute-done.3
  24.4 0.3 collective-permute-start.4
  24.7 0.4 collective-permute-start.12
  25.1 5.4 %collective-permute-done.9 = bf16[2,2,64,512]{3,2,1,0:T(8,128)(2,1)S(1)} collective-permute-done((bf16[2,2,64,512]{3,2,1,0:T(8,128)(2,1)S(1)}, bf16[2,2,64,512]{3,2,1,0:T(8,128)(2,1)S(1)}, u32[]{:S(2)}, u32[]{:S(2)}) %collective-permute-start.9) | collective-permute-done | bytes 262176 | tf_op jit(solution)/shard_map/ppermute | solution.py:25
  30.5 0.0 collective-permute-start.10
  30.5 0.0 collective-permute-done.4
  30.6 1.5 %collective-permute-done.10 = bf16[2,2,64,512]{3,2,1,0:T(8,128)(2,1)S(1)} collective-permute-done((bf16[2,2,64,512]{3,2,1,0:T(8,128)(2,1)S(1)}, bf16[2,2,64,512]{3,2,1,0:T(8,128)(2,1)S(1)}, u32[]{:S(2)}, u32[]{:S(2)}) %collective-permute-start.10) | collective-permute-done | bytes 262176 | tf_op jit(solution)/shard_map/ppermute | solution.py:25
  32.1 0.2 collective-permute-start.11
  32.2 0.0 collective-permute-done.12
  32.3 0.1 broadcast_select_fusion.1
  32.4 0.0 copy-start.4
  32.4 0.1 pad_maximum_fusion
  32.5 0.0 copy-start.2
  32.5 0.8 %collective-permute-done.11 = bf16[16,1536]{1,0:T(8,128)(2,1)S(1)} collective-permute-done((bf16[16,1536]{1,0:T(8,128)(2,1)S(1)}, bf16[16,1536]{1,0:T(8,128)(2,1)S(1)}, u32[]{:S(2)}, u32[]{:S(2)}) %collective-permute-start.11) | collective-permute-done | bytes 49184 | tf_op jit(solution)/shard_map/ppermute | solution.py:25
  33.4 0.2 fusion.33
  33.6 1.3 %collective-permute-start.13 = (bf16[16,256]{1,0:T(8,128)(2,1)S(1)}, bf16[16,256]{1,0:T(8,128)(2,1)S(1)}, u32[]{:S(2)}, u32[]{:S(2)}) collective-permute-start(bf16[16,256]{1,0:T(8,128)(2,1)S(1)} %get-tuple-element.27), channel_id=1, source_target_pairs={{0,24},{1,25},{2,26},{3,27},{4,28},{5,29},{6,30},{7,31},{8,16},{9,... | collective-permute-start | bytes 24584 | tf_op jit(solution)/shard_map/ppermute | solution.py:25
  34.8 1.8 %collective-permute-done.13 = bf16[16,256]{1,0:T(8,128)(2,1)S(1)} collective-permute-done((bf16[16,256]{1,0:T(8,128)(2,1)S(1)}, bf16[16,256]{1,0:T(8,128)(2,1)S(1)}, u32[]{:S(2)}, u32[]{:S(2)}) %collective-permute-start.13) | collective-permute-done | bytes 8224 | tf_op jit(solution)/shard_map/ppermute | solution.py:25
  36.6 0.2 convolution_convert_fusion.2
  36.9 0.0 copy-done.4
  36.9 0.2 convolution_convert_fusion.5
  37.1 0.5 %collective-permute-start.14 = (bf16[16,128]{1,0:T(8,128)(2,1)S(1)}, bf16[16,128]{1,0:T(8,128)(2,1)S(1)}, u32[]{:S(2)}, u32[]{:S(2)}) collective-permute-start(bf16[16,128]{1,0:T(8,128)(2,1)S(1)} %convolution_convert_fusion.5), channel_id=1, source_target_pairs={{0,1},{1,0},{2,3},{3,2},{4,5},{5,4},{6,7},{7,6},{8,9},{9,8},{10,11... | collective-permute-start | bytes 12296 | tf_op jit(solution)/shard_map/ppermute | solution.py:25
  37.6 3.1 %collective-permute-done.14 = bf16[16,128]{1,0:T(8,128)(2,1)S(1)} collective-permute-done((bf16[16,128]{1,0:T(8,128)(2,1)S(1)}, bf16[16,128]{1,0:T(8,128)(2,1)S(1)}, u32[]{:S(2)}, u32[]{:S(2)}) %collective-permute-start.14) | collective-permute-done | bytes 4128 | tf_op jit(solution)/shard_map/ppermute | solution.py:25
  40.7 1.8 %collective-permute-start.15 = (bf16[16,256]{1,0:T(8,128)(2,1)S(1)}, bf16[16,256]{1,0:T(8,128)(2,1)S(1)}, u32[]{:S(2)}, u32[]{:S(2)}) collective-permute-start(bf16[16,256]{1,0:T(8,128)(2,1)S(1)} %pad_maximum_fusion.5), channel_id=1, source_target_pairs={{0,2},{1,3},{2,0},{3,1},{4,6},{5,7},{6,4},{7,5},{8,10},{9,11},{10,... | collective-permute-start | bytes 24584 | tf_op jit(solution)/shard_map/ppermute | solution.py:25
  42.5 0.0 copy-done
  42.5 0.0 copy-done.2
  42.6 0.0 copy-start.1
  42.6 1.1 %convolution_bitcast_fusion.1 = f32[16,16,256]{2,0,1:T(8,128)} fusion(bf16[16,256,256]{2,1,0:T(8,128)(2,1)S(1)} %bitcast.46, bf16[16,16,256]{2,1,0:T(8,128)(2,1)S(1)} %copy-done.2), kind=kOutput, calls=%fused_computation.2 | convolution fusion | flops 33554432 | bytes 2490368 | tf_op jit(solution)/shard_map/rlq,lqp->rlp/dot_general | solution.py:145
  43.7 0.8 %collective-permute-done.15 = bf16[16,256]{1,0:T(8,128)(2,1)S(1)} collective-permute-done((bf16[16,256]{1,0:T(8,128)(2,1)S(1)}, bf16[16,256]{1,0:T(8,128)(2,1)S(1)}, u32[]{:S(2)}, u32[]{:S(2)}) %collective-permute-start.15) | collective-permute-done | bytes 8224 | tf_op jit(solution)/shard_map/ppermute | solution.py:25
  44.5 1.2 %convolution_convert_fusion.4 = bf16[16,256]{1,0:T(8,128)(2,1)S(1)} fusion(bf16[256,768]{1,0:T(8,128)(2,1)} %param.19, bf16[16,256]{1,0:T(8,128)(2,1)S(1)} %get-tuple-element.20, bf16[16,256]{1,0:T(8,128)(2,1)S(1)} %get-tuple-element.19, bf16[16,256]{1,0:T(8,128)(2,1)S(1)} %slice.30), kind=kOutput, calls=%fused_computation.8 | convolution fusion | flops 6369280 | bytes 425984 | tf_op jit(solution)/shard_map/dot_general | solution.py:10
  45.6 0.0 copy-done.1
  45.6 0.5 %convolution_convert_fusion.1 = bf16[16,1024]{1,0:T(8,128)(2,1)S(1)} fusion(bf16[1024,640]{1,0:T(8,128)(2,1)S(1)} %copy-done.1, bf16[16,256]{1,0:T(8,128)(2,1)S(1)} %convolution_convert_fusion.4, bf16[16,384]{1,0:T(8,128)(2,1)S(1)} %slice.28), kind=kOutput, calls=%fused_computation.5 | convolution fusion | flops 21028864 | bytes 1363968 | tf_op jit(solution)/shard_map/dot_general | solution.py:10
  46.2 0.1 reshape.139
  46.3 1.3 %fusion = f32[16,16,256]{2,0,1:T(8,128)S(1)} fusion(f32[16,16,256]{2,0,1:T(8,128)} %convolution_bitcast_fusion.1, bf16[16,64,256]{2,1,0:T(8,128)(2,1)} %bitcast.50, bf16[16,16,64]{2,1,0:T(8,128)(2,1)S(1)} %reshape.139), kind=kOutput, calls=%fused_computation.1 | convolution fusion | flops 8454144 | bytes 1081344 | tf_op jit(solution)/shard_map/rle,leq->rlq/dot_general | solution.py:139
  47.6 0.9 %copy.25 = f32[16,16,256]{2,1,0:T(8,128)} copy(f32[16,16,256]{2,0,1:T(8,128)S(1)} %fusion) | data formatting | bytes 524288 | tf_op jit(solution)/shard_map/add | solution.py:151
  (22 shorter events, 0.3 us)
Async XLA Ops:
  0.0 42.5 %copy-start = (bf16[4096,256]{1,0:T(8,128)(2,1)S(1)}, bf16[4096,256]{1,0:T(8,128)(2,1)}, u32[]{:S(2)}) copy-start(bf16[4096,256]{1,0:T(8,128)(2,1)} %param.14) | copy-start | bytes 6291460
  0.0 3.4 %copy-start.5 = (bf16[256,768]{1,0:T(8,128)(2,1)S(1)}, bf16[256,768]{1,0:T(8,128)(2,1)}, u32[]{:S(2)}) copy-start(bf16[256,768]{1,0:T(8,128)(2,1)} %param.18) | copy-start | bytes 1179652
  0.0 6.6 %copy-start.6 = (bf16[64,256]{1,0:T(8,128)(2,1)S(1)}, bf16[64,256]{1,0:T(8,128)(2,1)}, u32[]{:S(2)}) copy-start(bf16[64,256]{1,0:T(8,128)(2,1)} %param.22) | copy-start | bytes 98308
  0.0 6.6 %copy-start.7 = (bf16[64,256]{1,0:T(8,128)(2,1)S(1)}, bf16[64,256]{1,0:T(8,128)(2,1)}, u32[]{:S(2)}) copy-start(bf16[64,256]{1,0:T(8,128)(2,1)} %param.23) | copy-start | bytes 98308
  1.6 12.2 %copy-start.3 = (bf16[128,1536]{1,0:T(8,128)(2,1)S(1)}, bf16[128,1536]{1,0:T(8,128)(2,1)}, u32[]{:S(2)}) copy-start(bf16[128,1536]{1,0:T(8,128)(2,1)} %param.20) | copy-start | bytes 1179652
  3.6 5.7 %collective-permute-start = (bf16[16,768]{1,0:T(8,128)(2,1)S(1)}, bf16[16,768]{1,0:T(8,128)(2,1)S(1)}, u32[]{:S(2)}, u32[]{:S(2)}) collective-permute-start(bf16[16,768]{1,0:T(8,128)(2,1)S(1)} %get-tuple-element.23), channel_id=1, source_target_pairs={{0,1},{1,0},{2,3},{3,2},{4,5},{5,4},{6,7},{7,6},{8,9},{9,8},{10,11... | collective-permute-start | bytes 73736 | tf_op jit(solution)/shard_map/ppermute | solution.py:25
  6.7 5.6 %collective-permute-start.5 = (bf16[64,512]{1,0:T(8,128)(2,1)S(1)}, bf16[64,512]{1,0:T(8,128)(2,1)S(1)}, u32[]{:S(2)}, u32[]{:S(2)}) collective-permute-start(bf16[64,512]{1,0:T(8,128)(2,1)S(1)} %constant_dynamic-update-slice_fusion), channel_id=1, source_target_pairs={{0,4},{1,5},{2,6},{3,7},{4,0},{5,1},{6,2},{7,3},{8,12},{9,13},{10,... | collective-permute-start | bytes 196616 | tf_op jit(solution)/shard_map/ppermute | solution.py:25
  9.3 3.9 %collective-permute-start.1 = (bf16[16,768]{1,0:T(8,128)(2,1)S(1)}, bf16[16,768]{1,0:T(8,128)(2,1)S(1)}, u32[]{:S(2)}, u32[]{:S(2)}) collective-permute-start(bf16[16,768]{1,0:T(8,128)(2,1)S(1)} %fusion.13), channel_id=1, source_target_pairs={{0,2},{1,3},{2,0},{3,1},{4,6},{5,7},{6,4},{7,5},{8,10},{9,11},{10,... | collective-permute-start | bytes 73736 | tf_op jit(solution)/shard_map/ppermute | solution.py:25
  12.3 1.4 %collective-permute-start.6 = (bf16[2,64,512]{2,1,0:T(8,128)(2,1)S(1)}, bf16[2,64,512]{2,1,0:T(8,128)(2,1)S(1)}, u32[]{:S(2)}, u32[]{:S(2)}) collective-permute-start(bf16[2,64,512]{2,1,0:T(8,128)(2,1)S(1)} %pad_maximum_fusion.4), channel_id=1, source_target_pairs={{0,8},{1,9},{2,10},{3,11},{4,12},{5,13},{6,14},{7,15},{8,0},{9,1},... | collective-permute-start | bytes 393224 | tf_op jit(solution)/shard_map/ppermute | solution.py:25
  13.7 2.9 %collective-permute-start.7 = (bf16[2,64,512]{2,1,0:T(8,128)(2,1)S(1)}, bf16[2,64,512]{2,1,0:T(8,128)(2,1)S(1)}, u32[]{:S(2)}, u32[]{:S(2)}) collective-permute-start(bf16[2,64,512]{2,1,0:T(8,128)(2,1)S(1)} %collective-permute-done.6), channel_id=1, source_target_pairs={{0,8},{1,9},{2,10},{3,11},{4,12},{5,13},{6,14},{7,15},{8,0},{9,1},... | collective-permute-start | bytes 393224 | tf_op jit(solution)/shard_map/ppermute | solution.py:25
  14.0 4.5 %collective-permute-start.2 = (bf16[16,1536]{1,0:T(8,128)(2,1)S(1)}, bf16[16,1536]{1,0:T(8,128)(2,1)S(1)}, u32[]{:S(2)}, u32[]{:S(2)}) collective-permute-start(bf16[16,1536]{1,0:T(8,128)(2,1)S(1)} %get-tuple-element.25), channel_id=1, source_target_pairs={{0,12},{1,13},{2,14},{3,15},{4,8},{5,9},{6,10},{7,11},{8,4},{9,5},... | collective-permute-start | bytes 147464 | tf_op jit(solution)/shard_map/ppermute | solution.py:25
  16.6 6.1 %collective-permute-start.8 = (bf16[2,64,512]{2,1,0:T(8,128)(2,1)S(1)}, bf16[2,64,512]{2,1,0:T(8,128)(2,1)S(1)}, u32[]{:S(2)}, u32[]{:S(2)}) collective-permute-start(bf16[2,64,512]{2,1,0:T(8,128)(2,1)S(1)} %collective-permute-done.7), channel_id=1, source_target_pairs={{0,1},{1,0},{2,3},{3,2},{4,5},{5,4},{6,7},{7,6},{8,9},{9,8},{10,11... | collective-permute-start | bytes 393224 | tf_op jit(solution)/shard_map/ppermute | solution.py:25
  18.5 5.9 %collective-permute-start.3 = (bf16[16,1536]{1,0:T(8,128)(2,1)S(1)}, bf16[16,1536]{1,0:T(8,128)(2,1)S(1)}, u32[]{:S(2)}, u32[]{:S(2)}) collective-permute-start(bf16[16,1536]{1,0:T(8,128)(2,1)S(1)} %fusion.7), channel_id=1, source_target_pairs={{0,9},{1,8},{2,11},{3,10},{4,13},{5,12},{6,15},{7,14},{8,1},{9,0},... | collective-permute-start | bytes 147464 | tf_op jit(solution)/shard_map/ppermute | solution.py:25
  22.8 7.8 %collective-permute-start.9 = (bf16[2,2,64,512]{3,2,1,0:T(8,128)(2,1)S(1)}, bf16[2,2,64,512]{3,2,1,0:T(8,128)(2,1)S(1)}, u32[]{:S(2)}, u32[]{:S(2)}) collective-permute-start(bf16[2,2,64,512]{3,2,1,0:T(8,128)(2,1)S(1)} %pad_maximum_fusion.3), channel_id=1, source_target_pairs={{0,2},{1,3},{2,0},{3,1},{4,6},{5,7},{6,4},{7,5},{8,10},{9,11},{10,... | collective-permute-start | bytes 786440 | tf_op jit(solution)/shard_map/ppermute | solution.py:25
  24.4 6.1 %collective-permute-start.4 = (bf16[16,1536]{1,0:T(8,128)(2,1)S(1)}, bf16[16,1536]{1,0:T(8,128)(2,1)S(1)}, u32[]{:S(2)}, u32[]{:S(2)}) collective-permute-start(bf16[16,1536]{1,0:T(8,128)(2,1)S(1)} %fusion.12), channel_id=1, source_target_pairs={{0,10},{1,11},{2,8},{3,9},{4,14},{5,15},{6,12},{7,13},{8,2},{9,3},... | collective-permute-start | bytes 147464 | tf_op jit(solution)/shard_map/ppermute | solution.py:25
  24.7 7.5 %collective-permute-start.12 = (bf16[2,2,64,512]{3,2,1,0:T(8,128)(2,1)S(1)}, bf16[2,2,64,512]{3,2,1,0:T(8,128)(2,1)S(1)}, u32[]{:S(2)}, u32[]{:S(2)}) collective-permute-start(bf16[2,2,64,512]{3,2,1,0:T(8,128)(2,1)S(1)} %pad_maximum_fusion.3), channel_id=1, source_target_pairs={{0,8},{1,9},{2,10},{3,11},{4,12},{5,13},{6,14},{7,15},{8,0},{9,1},... | collective-permute-start | bytes 786440 | tf_op jit(solution)/shard_map/ppermute | solution.py:25
  30.5 1.5 %collective-permute-start.10 = (bf16[2,2,64,512]{3,2,1,0:T(8,128)(2,1)S(1)}, bf16[2,2,64,512]{3,2,1,0:T(8,128)(2,1)S(1)}, u32[]{:S(2)}, u32[]{:S(2)}) collective-permute-start(bf16[2,2,64,512]{3,2,1,0:T(8,128)(2,1)S(1)} %collective-permute-done.9), channel_id=1, source_target_pairs={{0,8},{1,9},{2,10},{3,11},{4,12},{5,13},{6,14},{7,15},{8,0},{9,1},... | collective-permute-start | bytes 786440 | tf_op jit(solution)/shard_map/ppermute | solution.py:25
  32.1 1.3 %collective-permute-start.11 = (bf16[16,1536]{1,0:T(8,128)(2,1)S(1)}, bf16[16,1536]{1,0:T(8,128)(2,1)S(1)}, u32[]{:S(2)}, u32[]{:S(2)}) collective-permute-start(bf16[16,1536]{1,0:T(8,128)(2,1)S(1)} %convert_element_type.86), channel_id=1, source_target_pairs={{0,8},{1,9},{2,10},{3,11},{4,12},{5,13},{6,14},{7,15},{8,0},{9,1},... | collective-permute-start | bytes 147464 | tf_op jit(solution)/shard_map/ppermute | solution.py:25
  32.4 4.5 %copy-start.4 = (bf16[128,1536]{1,0:T(8,128)(2,1)S(1)}, bf16[128,1536]{1,0:T(8,128)(2,1)}, u32[]{:S(2)}) copy-start(bf16[128,1536]{1,0:T(8,128)(2,1)} %param.21) | copy-start | bytes 1179652
  32.5 10.0 %copy-start.2 = (bf16[16,16,256]{2,1,0:T(8,128)(2,1)S(1)}, bf16[16,16,256]{2,1,0:T(8,128)(2,1)}, u32[]{:S(2)}) copy-start(bf16[16,16,256]{2,1,0:T(8,128)(2,1)} %param.12) | copy-start | bytes 393220
  33.6 3.1 %collective-permute-start.13 = (bf16[16,256]{1,0:T(8,128)(2,1)S(1)}, bf16[16,256]{1,0:T(8,128)(2,1)S(1)}, u32[]{:S(2)}, u32[]{:S(2)}) collective-permute-start(bf16[16,256]{1,0:T(8,128)(2,1)S(1)} %get-tuple-element.27), channel_id=1, source_target_pairs={{0,24},{1,25},{2,26},{3,27},{4,28},{5,29},{6,30},{7,31},{8,16},{9,... | collective-permute-start | bytes 24584 | tf_op jit(solution)/shard_map/ppermute | solution.py:25
  37.1 3.6 %collective-permute-start.14 = (bf16[16,128]{1,0:T(8,128)(2,1)S(1)}, bf16[16,128]{1,0:T(8,128)(2,1)S(1)}, u32[]{:S(2)}, u32[]{:S(2)}) collective-permute-start(bf16[16,128]{1,0:T(8,128)(2,1)S(1)} %convolution_convert_fusion.5), channel_id=1, source_target_pairs={{0,1},{1,0},{2,3},{3,2},{4,5},{5,4},{6,7},{7,6},{8,9},{9,8},{10,11... | collective-permute-start | bytes 12296 | tf_op jit(solution)/shard_map/ppermute | solution.py:25
  40.7 3.7 %collective-permute-start.15 = (bf16[16,256]{1,0:T(8,128)(2,1)S(1)}, bf16[16,256]{1,0:T(8,128)(2,1)S(1)}, u32[]{:S(2)}, u32[]{:S(2)}) collective-permute-start(bf16[16,256]{1,0:T(8,128)(2,1)S(1)} %pad_maximum_fusion.5), channel_id=1, source_target_pairs={{0,2},{1,3},{2,0},{3,1},{4,6},{5,7},{6,4},{7,5},{8,10},{9,11},{10,... | collective-permute-start | bytes 24584 | tf_op jit(solution)/shard_map/ppermute | solution.py:25
  42.6 3.1 %copy-start.1 = (bf16[1024,640]{1,0:T(8,128)(2,1)S(1)}, bf16[1024,640]{1,0:T(8,128)(2,1)}, u32[]{:S(2)}) copy-start(bf16[1024,640]{1,0:T(8,128)(2,1)} %param.17) | copy-start | bytes 3932164

commit v9 on v7

--- a/solution.py
+++ b/solution.py
@@ -52,6 +52,13 @@
     return jnp.stack(
         [jnp.where(upper, other, joined), jnp.where(upper, joined, other)], axis=axis
     )
+
+
+def diagonal(rows, leaves):
+    columns = rows.shape[2]
+    leaf = jnp.arange(columns) // (columns // leaves)
+    kept = jnp.where(leaf == jnp.arange(leaves)[:, None], rows, jnp.zeros((), rows.dtype))
+    return kept.reshape(-1, columns)
 
 
 def per_device(
@@ -134,20 +141,16 @@
 
     box_bound = rounded(contract(first_input, down_one))
     box_input = jnp.concatenate([box_state[:, :inner_dev], box_bound], axis=1)
-    leaf_bound = rounded(contract(box_input, box_down)).reshape(rhs_count, leaves, edge_count)
-    lifted = jnp.einsum(
-        "rle,leq->rlq",
-        leaf_bound,
-        leaf_lift.reshape(leaves, edge_count, points),
-        preferred_element_type=jnp.float32,
-    )
+    leaf_bound = rounded(contract(box_input, box_down))
+    edges = diagonal(leaf_bound[:, None, :], leaves)
+    lifted = product(edges, leaf_lift)
     particular = jnp.einsum(
         "rlq,lqp->rlp",
         source,
         leaf_particular.reshape(leaves, points, points),
         preferred_element_type=jnp.float32,
     )
-    return lifted + particular
+    return lifted.reshape(particular.shape) + particular
 
 
 def solution(mesh):

time: 47.8 us -> 46.5 us (0.973)
  local copies, waits for them, and re-layouts: 1.19 us -> 0.2 us
    dot_general x1 -> x0, matrix products: 1.29 us -> none  [per_device(): jnp.einsum('rle,leq->rlq', leaf_bound, leaf_lift.reshape(leaves, edge_cou...]
    dot_general x3 -> x4, matrix products: 0.53 us -> 1.6 us  [product(): return jnp.dot(left, right, preferred_element_type=jnp.float32)]
    add x1 -> x0, local copies, waits for them, and re-layouts: 0.86 us -> none  [per_device(): return lifted + particular]
where the time goes in v9:
time: 46.5 us; the launch traced here: 46.4 us
  waiting for transfers between devices  19.1 us (41%)
  starting transfers between devices  18.3 us (39%)
  matrix products  8.02 us (17%)
  other arithmetic  0.49 us (1%)
    ppermute x14, waiting for transfers between devices, swap(): return lax.ppermute(value, AXES, [(i, i ^ mask) for i in range(count)])  19.1 us
    ppermute x14, starting transfers between devices, swap(): return lax.ppermute(value, AXES, [(i, i ^ mask) for i in range(count)])  18.3 us
    dot_general x5, matrix products, contract(): lax.dot_general(left, right, (((1,), (1,)), ((), ())), preferred_element_...  3.88 us
    dot_general x4, matrix products, product(): return jnp.dot(left, right, preferred_element_type=jnp.float32)  1.6 us
    dot_general x1, matrix products, per_device(): jnp.einsum('rlq,leq->rle', source, leaf_flux.reshape(leaves, edge_count,...  1.44 us
    dot_general x1, matrix products, per_device(): jnp.einsum('rlq,lqp->rlp', source, leaf_particular.reshape(leaves, points...  1.09 us
  transfers between devices with their start and end apart: 14, of which 10 were waited for; matrix products, arithmetic and copies ran while one was open for 4% of the time, Pallas kernels for 0%

profile of v9, /device:TPU:0, one launch (start us, length us, event | category | flops | bytes accessed | tf_op | source)
XLA Modules:
  0.0 46.4 jit_solution(15067588461695305908)
XLA Ops:
  0.0 0.0 copy-start
  0.0 0.0 copy-start.5
  0.0 0.0 copy-start.7
  0.0 0.0 copy-start.8
  0.0 1.4 %fusion = bf16[16,16,64]{2,0,1:T(8,128)(2,1)S(1)} fusion(bf16[16,64,256]{2,1,0:T(8,128)(2,1)} %bitcast.46, bf16[16,16,256]{2,1,0:T(8,128)(2,1)} %param.12), kind=kOutput, calls=%fused_computation.2 | convolution fusion | flops 8404992 | bytes 688128 | tf_op jit(solution)/shard_map/rlq,leq->rle/dot_general | solution.py:94
  1.5 0.0 copy-start.3
  1.5 0.1 reshape.150
  1.6 1.8 %convolution_convert_fusion.3 = bf16[16,640]{1,0:T(8,128)(2,1)S(1)} fusion(bf16[16,1024]{1,0:T(8,128)(2,1)S(1)} %reshape.150, bf16[640,1024]{1,0:T(8,128)(2,1)} %param.16), kind=kOutput, calls=%fused_computation.5 | convolution fusion | flops 20981760 | bytes 1363968 | tf_op jit(solution)/shard_map/dot_general | solution.py:10
  3.4 0.0 copy-done.5
  3.4 0.2 fusion.39
  3.6 3.0 %collective-permute-start = (bf16[16,768]{1,0:T(8,128)(2,1)S(1)}, bf16[16,768]{1,0:T(8,128)(2,1)S(1)}, u32[]{:S(2)}, u32[]{:S(2)}) collective-permute-start(bf16[16,768]{1,0:T(8,128)(2,1)S(1)} %get-tuple-element.23), channel_id=1, source_target_pairs={{0,1},{1,0},{2,3},{3,2},{4,5},{5,4},{6,7},{7,6},{8,9},{9,8},{10,11... | collective-permute-start | bytes 73736 | tf_op jit(solution)/shard_map/ppermute | solution.py:25
  6.6 0.0 copy-done.7
  6.6 1.8 %collective-permute-done = bf16[16,768]{1,0:T(8,128)(2,1)S(1)} collective-permute-done((bf16[16,768]{1,0:T(8,128)(2,1)S(1)}, bf16[16,768]{1,0:T(8,128)(2,1)S(1)}, u32[]{:S(2)}, u32[]{:S(2)}) %collective-permute-start) | collective-permute-done | bytes 24608 | tf_op jit(solution)/shard_map/ppermute | solution.py:25
  8.4 2.1 %collective-permute-start.1 = (bf16[16,768]{1,0:T(8,128)(2,1)S(1)}, bf16[16,768]{1,0:T(8,128)(2,1)S(1)}, u32[]{:S(2)}, u32[]{:S(2)}) collective-permute-start(bf16[16,768]{1,0:T(8,128)(2,1)S(1)} %fusion.17), channel_id=1, source_target_pairs={{0,2},{1,3},{2,0},{3,1},{4,6},{5,7},{6,4},{7,5},{8,10},{9,11},{10,... | collective-permute-start | bytes 73736 | tf_op jit(solution)/shard_map/ppermute | solution.py:25
  10.5 0.0 copy-done.8
  10.6 2.6 %collective-permute-start.5 = (bf16[64,512]{1,0:T(8,128)(2,1)S(1)}, bf16[64,512]{1,0:T(8,128)(2,1)S(1)}, u32[]{:S(2)}, u32[]{:S(2)}) collective-permute-start(bf16[64,512]{1,0:T(8,128)(2,1)S(1)} %constant_dynamic-update-slice_fusion), channel_id=1, source_target_pairs={{0,4},{1,5},{2,6},{3,7},{4,0},{5,1},{6,2},{7,3},{8,12},{9,13},{10,... | collective-permute-start | bytes 196616 | tf_op jit(solution)/shard_map/ppermute | solution.py:25
  13.1 0.0 collective-permute-done.1
  13.2 0.0 copy-done.3
  13.2 0.2 fusion.40
  13.3 0.1 collective-permute-start.2
  13.4 2.8 %collective-permute-done.5 = bf16[64,512]{1,0:T(8,128)(2,1)S(1)} collective-permute-done((bf16[64,512]{1,0:T(8,128)(2,1)S(1)}, bf16[64,512]{1,0:T(8,128)(2,1)S(1)}, u32[]{:S(2)}, u32[]{:S(2)}) %collective-permute-start.5) | collective-permute-done | bytes 65568 | tf_op jit(solution)/shard_map/ppermute | solution.py:25
  16.3 1.7 %collective-permute-start.6 = (bf16[2,64,512]{2,1,0:T(8,128)(2,1)S(1)}, bf16[2,64,512]{2,1,0:T(8,128)(2,1)S(1)}, u32[]{:S(2)}, u32[]{:S(2)}) collective-permute-start(bf16[2,64,512]{2,1,0:T(8,128)(2,1)S(1)} %pad_maximum_fusion.4), channel_id=1, source_target_pairs={{0,1},{1,0},{2,3},{3,2},{4,5},{5,4},{6,7},{7,6},{8,9},{9,8},{10,11... | collective-permute-start | bytes 393224 | tf_op jit(solution)/shard_map/ppermute | solution.py:25
  17.9 0.3 collective-permute-done.2
  18.3 1.2 %collective-permute-start.3 = (bf16[16,1536]{1,0:T(8,128)(2,1)S(1)}, bf16[16,1536]{1,0:T(8,128)(2,1)S(1)}, u32[]{:S(2)}, u32[]{:S(2)}) collective-permute-start(bf16[16,1536]{1,0:T(8,128)(2,1)S(1)} %fusion.12), channel_id=1, source_target_pairs={{0,9},{1,8},{2,11},{3,10},{4,13},{5,12},{6,15},{7,14},{8,1},{9,0},... | collective-permute-start | bytes 147464 | tf_op jit(solution)/shard_map/ppermute | solution.py:25
  19.4 1.9 %collective-permute-done.6 = bf16[2,64,512]{2,1,0:T(8,128)(2,1)S(1)} collective-permute-done((bf16[2,64,512]{2,1,0:T(8,128)(2,1)S(1)}, bf16[2,64,512]{2,1,0:T(8,128)(2,1)S(1)}, u32[]{:S(2)}, u32[]{:S(2)}) %collective-permute-start.6) | collective-permute-done | bytes 131104 | tf_op jit(solution)/shard_map/ppermute | solution.py:25
  21.4 1.2 %collective-permute-start.7 = (bf16[2,2,64,512]{3,2,1,0:T(8,128)(2,1)S(1)}, bf16[2,2,64,512]{3,2,1,0:T(8,128)(2,1)S(1)}, u32[]{:S(2)}, u32[]{:S(2)}) collective-permute-start(bf16[2,2,64,512]{3,2,1,0:T(8,128)(2,1)S(1)} %pad_maximum_fusion.3), channel_id=1, source_target_pairs={{0,2},{1,3},{2,0},{3,1},{4,6},{5,7},{6,4},{7,5},{8,10},{9,11},{10,... | collective-permute-start | bytes 786440 | tf_op jit(solution)/shard_map/ppermute | solution.py:25
  22.5 0.0 collective-permute-done.3
  22.6 1.0 %collective-permute-start.4 = (bf16[16,1536]{1,0:T(8,128)(2,1)S(1)}, bf16[16,1536]{1,0:T(8,128)(2,1)S(1)}, u32[]{:S(2)}, u32[]{:S(2)}) collective-permute-start(bf16[16,1536]{1,0:T(8,128)(2,1)S(1)} %fusion.16), channel_id=1, source_target_pairs={{0,10},{1,11},{2,8},{3,9},{4,14},{5,15},{6,12},{7,13},{8,2},{9,3},... | collective-permute-start | bytes 147464 | tf_op jit(solution)/shard_map/ppermute | solution.py:25
  23.5 0.4 collective-permute-start.10
  23.9 5.7 %collective-permute-done.7 = bf16[2,2,64,512]{3,2,1,0:T(8,128)(2,1)S(1)} collective-permute-done((bf16[2,2,64,512]{3,2,1,0:T(8,128)(2,1)S(1)}, bf16[2,2,64,512]{3,2,1,0:T(8,128)(2,1)S(1)}, u32[]{:S(2)}, u32[]{:S(2)}) %collective-permute-start.7) | collective-permute-done | bytes 262176 | tf_op jit(solution)/shard_map/ppermute | solution.py:25
  29.6 0.0 collective-permute-start.8
  29.7 0.0 collective-permute-done.4
  29.7 1.5 %collective-permute-done.8 = bf16[2,2,64,512]{3,2,1,0:T(8,128)(2,1)S(1)} collective-permute-done((bf16[2,2,64,512]{3,2,1,0:T(8,128)(2,1)S(1)}, bf16[2,2,64,512]{3,2,1,0:T(8,128)(2,1)S(1)}, u32[]{:S(2)}, u32[]{:S(2)}) %collective-permute-start.8) | collective-permute-done | bytes 262176 | tf_op jit(solution)/shard_map/ppermute | solution.py:25
  31.2 0.2 collective-permute-start.9
  31.4 0.0 collective-permute-done.10
  31.4 0.1 broadcast_select_fusion.1
  31.5 0.0 copy-start.2
  31.5 0.1 pad_maximum_fusion
  31.6 0.9 %collective-permute-done.9 = bf16[16,1536]{1,0:T(8,128)(2,1)S(1)} collective-permute-done((bf16[16,1536]{1,0:T(8,128)(2,1)S(1)}, bf16[16,1536]{1,0:T(8,128)(2,1)S(1)}, u32[]{:S(2)}, u32[]{:S(2)}) %collective-permute-start.9) | collective-permute-done | bytes 49184 | tf_op jit(solution)/shard_map/ppermute | solution.py:25
  32.5 0.2 fusion.41
  32.7 1.4 %collective-permute-start.11 = (bf16[16,256]{1,0:T(8,128)(2,1)S(1)}, bf16[16,256]{1,0:T(8,128)(2,1)S(1)}, u32[]{:S(2)}, u32[]{:S(2)}) collective-permute-start(bf16[16,256]{1,0:T(8,128)(2,1)S(1)} %get-tuple-element.27), channel_id=1, source_target_pairs={{0,24},{1,25},{2,26},{3,27},{4,28},{5,29},{6,30},{7,31},{8,16},{9,... | collective-permute-start | bytes 24584 | tf_op jit(solution)/shard_map/ppermute | solution.py:25
  34.1 0.0 copy-done
  34.1 0.0 copy-done.2
  34.1 0.0 copy-start.4
  34.1 1.1 %fusion.9 = f32[16,256,16]{1,2,0:T(8,128)} fusion(bf16[16,256,256]{2,1,0:T(8,128)(2,1)S(1)} %bitcast.43, bf16[16,16,256]{2,1,0:T(8,128)(2,1)S(1)} %copy-done.2), kind=kOutput, calls=%fused_computation.29 | convolution fusion | flops 33554432 | bytes 2490368 | tf_op jit(solution)/shard_map/rlq,lqp->rlp/dot_general | solution.py:147
  35.2 0.0 copy-start.1
  35.2 0.5 %collective-permute-done.11 = bf16[16,256]{1,0:T(8,128)(2,1)S(1)} collective-permute-done((bf16[16,256]{1,0:T(8,128)(2,1)S(1)}, bf16[16,256]{1,0:T(8,128)(2,1)S(1)}, u32[]{:S(2)}, u32[]{:S(2)}) %collective-permute-start.11) | collective-permute-done | bytes 8224 | tf_op jit(solution)/shard_map/ppermute | solution.py:25
  35.8 0.2 convolution_convert_fusion.2
  36.0 0.0 copy-done.4
  36.0 0.2 convolution_convert_fusion.5
  36.2 1.7 %collective-permute-start.12 = (bf16[16,128]{1,0:T(8,128)(2,1)S(1)}, bf16[16,128]{1,0:T(8,128)(2,1)S(1)}, u32[]{:S(2)}, u32[]{:S(2)}) collective-permute-start(bf16[16,128]{1,0:T(8,128)(2,1)S(1)} %convolution_convert_fusion.5), channel_id=1, source_target_pairs={{0,1},{1,0},{2,3},{3,2},{4,5},{5,4},{6,7},{7,6},{8,9},{9,8},{10,11... | collective-permute-start | bytes 12296 | tf_op jit(solution)/shard_map/ppermute | solution.py:25
  37.9 1.9 %collective-permute-done.12 = bf16[16,128]{1,0:T(8,128)(2,1)S(1)} collective-permute-done((bf16[16,128]{1,0:T(8,128)(2,1)S(1)}, bf16[16,128]{1,0:T(8,128)(2,1)S(1)}, u32[]{:S(2)}, u32[]{:S(2)}) %collective-permute-start.12) | collective-permute-done | bytes 4128 | tf_op jit(solution)/shard_map/ppermute | solution.py:25
  39.9 1.8 %collective-permute-start.13 = (bf16[16,256]{1,0:T(8,128)(2,1)S(1)}, bf16[16,256]{1,0:T(8,128)(2,1)S(1)}, u32[]{:S(2)}, u32[]{:S(2)}) collective-permute-start(bf16[16,256]{1,0:T(8,128)(2,1)S(1)} %pad_maximum_fusion.5), channel_id=1, source_target_pairs={{0,2},{1,3},{2,0},{3,1},{4,6},{5,7},{6,4},{7,5},{8,10},{9,11},{10,... | collective-permute-start | bytes 24584 | tf_op jit(solution)/shard_map/ppermute | solution.py:25
  41.7 0.0 copy-start.6
  41.7 0.0 copy-start.9
  41.8 1.8 %collective-permute-done.13 = bf16[16,256]{1,0:T(8,128)(2,1)S(1)} collective-permute-done((bf16[16,256]{1,0:T(8,128)(2,1)S(1)}, bf16[16,256]{1,0:T(8,128)(2,1)S(1)}, u32[]{:S(2)}, u32[]{:S(2)}) %collective-permute-start.13) | collective-permute-done | bytes 8224 | tf_op jit(solution)/shard_map/ppermute | solution.py:25
  43.6 1.2 %convolution_convert_fusion.4 = bf16[16,256]{1,0:T(8,128)(2,1)S(1)} fusion(bf16[256,768]{1,0:T(8,128)(2,1)} %param.19, bf16[16,256]{1,0:T(8,128)(2,1)S(1)} %get-tuple-element.20, bf16[16,256]{1,0:T(8,128)(2,1)S(1)} %get-tuple-element.19, bf16[16,256]{1,0:T(8,128)(2,1)S(1)} %slice.30), kind=kOutput, calls=%fused_computation.6 | convolution fusion | flops 6369280 | bytes 425984 | tf_op jit(solution)/shard_map/dot_general | solution.py:10
  44.8 0.0 copy-done.1
  44.8 0.5 %convolution_convert_fusion.1 = bf16[16,1024]{1,0:T(8,128)(2,1)S(1)} fusion(bf16[1024,640]{1,0:T(8,128)(2,1)S(1)} %copy-done.1, bf16[16,256]{1,0:T(8,128)(2,1)S(1)} %convolution_convert_fusion.4, bf16[16,384]{1,0:T(8,128)(2,1)S(1)} %slice.28), kind=kOutput, calls=%fused_computation.3 | convolution fusion | flops 21028864 | bytes 1363968 | tf_op jit(solution)/shard_map/dot_general | solution.py:10
  45.3 0.0 copy-done.6
  45.3 0.0 copy-done.9
  45.3 1.1 %convolution_add_fusion = f32[16,16,256]{2,1,0:T(8,128)} fusion(bf16[1024,256]{1,0:T(8,128)(2,1)S(1)} %copy-done.9, pred[16,1024]{1,0:T(8,128)(4,1)S(1)} %iota_compare_fusion, f32[16,256,16]{1,2,0:T(8,128)S(1)} %copy-done.6, bf16[16,1024]{1,0:T(8,128)(2,1)S(1)} %convolution_convert_fusion.1), kind=kOutput, calls=%fused_computation | convolution fusion | flops 134545408 | bytes 1097728 | tf_op jit(solution)/shard_map/dot_general | solution.py:16
  (24 shorter events, 0.3 us)
Async XLA Ops:
  0.0 34.1 %copy-start = (bf16[4096,256]{1,0:T(8,128)(2,1)S(1)}, bf16[4096,256]{1,0:T(8,128)(2,1)}, u32[]{:S(2)}) copy-start(bf16[4096,256]{1,0:T(8,128)(2,1)} %param.14) | copy-start | bytes 6291460
  0.0 3.4 %copy-start.5 = (bf16[256,768]{1,0:T(8,128)(2,1)S(1)}, bf16[256,768]{1,0:T(8,128)(2,1)}, u32[]{:S(2)}) copy-start(bf16[256,768]{1,0:T(8,128)(2,1)} %param.18) | copy-start | bytes 1179652
  0.0 6.6 %copy-start.7 = (bf16[64,256]{1,0:T(8,128)(2,1)S(1)}, bf16[64,256]{1,0:T(8,128)(2,1)}, u32[]{:S(2)}) copy-start(bf16[64,256]{1,0:T(8,128)(2,1)} %param.22) | copy-start | bytes 98308
  0.0 10.5 %copy-start.8 = (bf16[64,256]{1,0:T(8,128)(2,1)S(1)}, bf16[64,256]{1,0:T(8,128)(2,1)}, u32[]{:S(2)}) copy-start(bf16[64,256]{1,0:T(8,128)(2,1)} %param.23) | copy-start | bytes 98308
  1.5 11.7 %copy-start.3 = (bf16[128,1536]{1,0:T(8,128)(2,1)S(1)}, bf16[128,1536]{1,0:T(8,128)(2,1)}, u32[]{:S(2)}) copy-start(bf16[128,1536]{1,0:T(8,128)(2,1)} %param.20) | copy-start | bytes 1179652
  3.6 4.8 %collective-permute-start = (bf16[16,768]{1,0:T(8,128)(2,1)S(1)}, bf16[16,768]{1,0:T(8,128)(2,1)S(1)}, u32[]{:S(2)}, u32[]{:S(2)}) collective-permute-start(bf16[16,768]{1,0:T(8,128)(2,1)S(1)} %get-tuple-element.23), channel_id=1, source_target_pairs={{0,1},{1,0},{2,3},{3,2},{4,5},{5,4},{6,7},{7,6},{8,9},{9,8},{10,11... | collective-permute-start | bytes 73736 | tf_op jit(solution)/shard_map/ppermute | solution.py:25
  8.4 4.7 %collective-permute-start.1 = (bf16[16,768]{1,0:T(8,128)(2,1)S(1)}, bf16[16,768]{1,0:T(8,128)(2,1)S(1)}, u32[]{:S(2)}, u32[]{:S(2)}) collective-permute-start(bf16[16,768]{1,0:T(8,128)(2,1)S(1)} %fusion.17), channel_id=1, source_target_pairs={{0,2},{1,3},{2,0},{3,1},{4,6},{5,7},{6,4},{7,5},{8,10},{9,11},{10,... | collective-permute-start | bytes 73736 | tf_op jit(solution)/shard_map/ppermute | solution.py:25
  10.6 5.7 %collective-permute-start.5 = (bf16[64,512]{1,0:T(8,128)(2,1)S(1)}, bf16[64,512]{1,0:T(8,128)(2,1)S(1)}, u32[]{:S(2)}, u32[]{:S(2)}) collective-permute-start(bf16[64,512]{1,0:T(8,128)(2,1)S(1)} %constant_dynamic-update-slice_fusion), channel_id=1, source_target_pairs={{0,4},{1,5},{2,6},{3,7},{4,0},{5,1},{6,2},{7,3},{8,12},{9,13},{10,... | collective-permute-start | bytes 196616 | tf_op jit(solution)/shard_map/ppermute | solution.py:25
  13.3 4.9 %collective-permute-start.2 = (bf16[16,1536]{1,0:T(8,128)(2,1)S(1)}, bf16[16,1536]{1,0:T(8,128)(2,1)S(1)}, u32[]{:S(2)}, u32[]{:S(2)}) collective-permute-start(bf16[16,1536]{1,0:T(8,128)(2,1)S(1)} %get-tuple-element.25), channel_id=1, source_target_pairs={{0,12},{1,13},{2,14},{3,15},{4,8},{5,9},{6,10},{7,11},{8,4},{9,5},... | collective-permute-start | bytes 147464 | tf_op jit(solution)/shard_map/ppermute | solution.py:25
  16.3 5.0 %collective-permute-start.6 = (bf16[2,64,512]{2,1,0:T(8,128)(2,1)S(1)}, bf16[2,64,512]{2,1,0:T(8,128)(2,1)S(1)}, u32[]{:S(2)}, u32[]{:S(2)}) collective-permute-start(bf16[2,64,512]{2,1,0:T(8,128)(2,1)S(1)} %pad_maximum_fusion.4), channel_id=1, source_target_pairs={{0,1},{1,0},{2,3},{3,2},{4,5},{5,4},{6,7},{7,6},{8,9},{9,8},{10,11... | collective-permute-start | bytes 393224 | tf_op jit(solution)/shard_map/ppermute | solution.py:25
  18.3 4.3 %collective-permute-start.3 = (bf16[16,1536]{1,0:T(8,128)(2,1)S(1)}, bf16[16,1536]{1,0:T(8,128)(2,1)S(1)}, u32[]{:S(2)}, u32[]{:S(2)}) collective-permute-start(bf16[16,1536]{1,0:T(8,128)(2,1)S(1)} %fusion.12), channel_id=1, source_target_pairs={{0,9},{1,8},{2,11},{3,10},{4,13},{5,12},{6,15},{7,14},{8,1},{9,0},... | collective-permute-start | bytes 147464 | tf_op jit(solution)/shard_map/ppermute | solution.py:25
  21.4 8.3 %collective-permute-start.7 = (bf16[2,2,64,512]{3,2,1,0:T(8,128)(2,1)S(1)}, bf16[2,2,64,512]{3,2,1,0:T(8,128)(2,1)S(1)}, u32[]{:S(2)}, u32[]{:S(2)}) collective-permute-start(bf16[2,2,64,512]{3,2,1,0:T(8,128)(2,1)S(1)} %pad_maximum_fusion.3), channel_id=1, source_target_pairs={{0,2},{1,3},{2,0},{3,1},{4,6},{5,7},{6,4},{7,5},{8,10},{9,11},{10,... | collective-permute-start | bytes 786440 | tf_op jit(solution)/shard_map/ppermute | solution.py:25
  22.6 7.1 %collective-permute-start.4 = (bf16[16,1536]{1,0:T(8,128)(2,1)S(1)}, bf16[16,1536]{1,0:T(8,128)(2,1)S(1)}, u32[]{:S(2)}, u32[]{:S(2)}) collective-permute-start(bf16[16,1536]{1,0:T(8,128)(2,1)S(1)} %fusion.16), channel_id=1, source_target_pairs={{0,10},{1,11},{2,8},{3,9},{4,14},{5,15},{6,12},{7,13},{8,2},{9,3},... | collective-permute-start | bytes 147464 | tf_op jit(solution)/shard_map/ppermute | solution.py:25
  23.5 7.8 %collective-permute-start.10 = (bf16[2,2,64,512]{3,2,1,0:T(8,128)(2,1)S(1)}, bf16[2,2,64,512]{3,2,1,0:T(8,128)(2,1)S(1)}, u32[]{:S(2)}, u32[]{:S(2)}) collective-permute-start(bf16[2,2,64,512]{3,2,1,0:T(8,128)(2,1)S(1)} %pad_maximum_fusion.3), channel_id=1, source_target_pairs={{0,8},{1,9},{2,10},{3,11},{4,12},{5,13},{6,14},{7,15},{8,0},{9,1},... | collective-permute-start | bytes 786440 | tf_op jit(solution)/shard_map/ppermute | solution.py:25
  29.6 1.5 %collective-permute-start.8 = (bf16[2,2,64,512]{3,2,1,0:T(8,128)(2,1)S(1)}, bf16[2,2,64,512]{3,2,1,0:T(8,128)(2,1)S(1)}, u32[]{:S(2)}, u32[]{:S(2)}) collective-permute-start(bf16[2,2,64,512]{3,2,1,0:T(8,128)(2,1)S(1)} %collective-permute-done.7), channel_id=1, source_target_pairs={{0,8},{1,9},{2,10},{3,11},{4,12},{5,13},{6,14},{7,15},{8,0},{9,1},... | collective-permute-start | bytes 786440 | tf_op jit(solution)/shard_map/ppermute | solution.py:25
  31.2 1.3 %collective-permute-start.9 = (bf16[16,1536]{1,0:T(8,128)(2,1)S(1)}, bf16[16,1536]{1,0:T(8,128)(2,1)S(1)}, u32[]{:S(2)}, u32[]{:S(2)}) collective-permute-start(bf16[16,1536]{1,0:T(8,128)(2,1)S(1)} %convert_element_type.86), channel_id=1, source_target_pairs={{0,8},{1,9},{2,10},{3,11},{4,12},{5,13},{6,14},{7,15},{8,0},{9,1},... | collective-permute-start | bytes 147464 | tf_op jit(solution)/shard_map/ppermute | solution.py:25
  31.5 2.6 %copy-start.2 = (bf16[16,16,256]{2,1,0:T(8,128)(2,1)S(1)}, bf16[16,16,256]{2,1,0:T(8,128)(2,1)}, u32[]{:S(2)}) copy-start(bf16[16,16,256]{2,1,0:T(8,128)(2,1)} %param.12) | copy-start | bytes 393220
  32.7 3.1 %collective-permute-start.11 = (bf16[16,256]{1,0:T(8,128)(2,1)S(1)}, bf16[16,256]{1,0:T(8,128)(2,1)S(1)}, u32[]{:S(2)}, u32[]{:S(2)}) collective-permute-start(bf16[16,256]{1,0:T(8,128)(2,1)S(1)} %get-tuple-element.27), channel_id=1, source_target_pairs={{0,24},{1,25},{2,26},{3,27},{4,28},{5,29},{6,30},{7,31},{8,16},{9,... | collective-permute-start | bytes 24584 | tf_op jit(solution)/shard_map/ppermute | solution.py:25
  34.1 1.9 %copy-start.4 = (bf16[128,1536]{1,0:T(8,128)(2,1)S(1)}, bf16[128,1536]{1,0:T(8,128)(2,1)}, u32[]{:S(2)}) copy-start(bf16[128,1536]{1,0:T(8,128)(2,1)} %param.21) | copy-start | bytes 1179652
  35.2 9.5 %copy-start.1 = (bf16[1024,640]{1,0:T(8,128)(2,1)S(1)}, bf16[1024,640]{1,0:T(8,128)(2,1)}, u32[]{:S(2)}) copy-start(bf16[1024,640]{1,0:T(8,128)(2,1)} %param.17) | copy-start | bytes 3932164
  36.2 3.6 %collective-permute-start.12 = (bf16[16,128]{1,0:T(8,128)(2,1)S(1)}, bf16[16,128]{1,0:T(8,128)(2,1)S(1)}, u32[]{:S(2)}, u32[]{:S(2)}) collective-permute-start(bf16[16,128]{1,0:T(8,128)(2,1)S(1)} %convolution_convert_fusion.5), channel_id=1, source_target_pairs={{0,1},{1,0},{2,3},{3,2},{4,5},{5,4},{6,7},{7,6},{8,9},{9,8},{10,11... | collective-permute-start | bytes 12296 | tf_op jit(solution)/shard_map/ppermute | solution.py:25
  39.9 3.7 %collective-permute-start.13 = (bf16[16,256]{1,0:T(8,128)(2,1)S(1)}, bf16[16,256]{1,0:T(8,128)(2,1)S(1)}, u32[]{:S(2)}, u32[]{:S(2)}) collective-permute-start(bf16[16,256]{1,0:T(8,128)(2,1)S(1)} %pad_maximum_fusion.5), channel_id=1, source_target_pairs={{0,2},{1,3},{2,0},{3,1},{4,6},{5,7},{6,4},{7,5},{8,10},{9,11},{10,... | collective-permute-start | bytes 24584 | tf_op jit(solution)/shard_map/ppermute | solution.py:25
  41.7 3.6 %copy-start.6 = (f32[16,256,16]{1,2,0:T(8,128)S(1)}, f32[16,256,16]{1,2,0:T(8,128)}, u32[]{:S(2)}) copy-start(f32[16,256,16]{1,2,0:T(8,128)} %fusion.9) | copy-start | bytes 786436
  41.7 3.6 %copy-start.9 = (bf16[1024,256]{1,0:T(8,128)(2,1)S(1)}, bf16[1024,256]{1,0:T(8,128)(2,1)}, u32[]{:S(2)}) copy-start(bf16[1024,256]{1,0:T(8,128)(2,1)} %param.15) | copy-start | bytes 1572868

commit v10 on v9

--- a/solution.py
+++ b/solution.py
@@ -61,6 +61,13 @@
     return kept.reshape(-1, columns)
 
 
+def family_rows(own, own_near, other, other_near, near, pair, place):
+    own = joined_pair(own, own_near, place & near != 0, 1)
+    other = joined_pair(other, other_near, place & near != 0, 1)
+    rows = joined_pair(own, other, place & pair != 0, 0)
+    return rows.reshape(-1, rows.shape[-1])
+
+
 def per_device(
     source,
     leaf_flux,
@@ -112,27 +119,29 @@
 
     piece = lax.dynamic_slice_in_dim(first_state, k_zero + place % quad * width, width, 1)
     second_sum = product(piece, up_two)
+    second_sum = partner_sum(second_sum, far | pair)
+    second_sum, roots_one = lax.optimization_barrier((second_sum, roots_one))
     roots = joined_pair(roots, roots_one, place & 1 != 0, 1)
-    roots_near, roots_pair = swap(roots, near), swap(roots, pair)
-    second_sum = partner_sum(second_sum, far | pair)
-
+    up_part, down_part = roots[..., :root_points], roots[..., root_points:]
+    up_near, up_pair = swap(up_part, near), swap(up_part, pair)
+    second_sum = partner_sum(second_sum, near | pair)
+    second_sum, up_near = lax.optimization_barrier((second_sum, up_near))
+    down_near, down_pair = swap(down_part, near), swap(down_part, pair)
+    up_high = swap(up_near, pair)
+    down_high = swap(down_near, pair)
     second_sum = partner_sum(second_sum, 1 | pair)
-    low = joined_pair(roots, roots_near, place & near != 0, 1)
-    high = swap(roots_near, pair)
-    second_sum = partner_sum(second_sum, near | pair)
-    second_sum, high = lax.optimization_barrier((second_sum, high))
-    high = joined_pair(roots_pair, high, place & near != 0, 1)
+    second_sum, up_high = lax.optimization_barrier((second_sum, up_high))
     second_sum = partner_sum(second_sum, pair)
     second_state = rounded(second_sum)
-    roots = joined_pair(low, high, place & pair != 0, 0)
-    roots = roots.reshape(-1, roots.shape[-1])
+    up_rows = family_rows(up_part, up_near, up_pair, up_high, near, pair, place)
+    down_rows = family_rows(down_part, down_near, down_pair, down_high, near, pair, place)
 
-    root_sum = product(second_state[:, k_one:], roots[:, :root_points])
+    root_sum = product(second_state[:, k_one:], up_rows)
     for bit in bits_of(family, count):
         root_sum = partner_sum(root_sum, bit | pair)
     root_state = rounded(root_sum)
 
-    top_bound = rounded(contract(root_state, roots[:, root_points:]))
+    top_bound = rounded(contract(root_state, down_rows))
     second_input = jnp.concatenate([second_state[:, :k_one], top_bound], axis=1)
     mid_bound = rounded(contract(second_input, down_two))
     mid_bound = placed([mid_bound, swap(mid_bound, 1)], place, 1)

time: 46.5 us -> 47.1 us (1.013)
  waiting for transfers between devices: 19.1 us -> 19.6 us
    ppermute x14 -> x17, waiting for transfers between devices: 19.1 us -> 19.6 us  [swap(): return lax.ppermute(value, AXES, [(i, i ^ mask) for i in range(count)])]
    ppermute x14 -> x17, starting transfers between devices: 18.3 us -> 18.1 us  [swap(): return lax.ppermute(value, AXES, [(i, i ^ mask) for i in range(count)])]
  transfers between devices with their start and end apart: 14 -> 17, of which waited for: 10 -> 10; matrix products, arithmetic and copies ran while one was open for 4% -> 4% of each run, Pallas kernels for 0% -> 0%
where the time goes in v10:
time: 47.1 us; the launch traced here: 46.9 us
  waiting for transfers between devices  19.6 us (42%)
  starting transfers between devices  18.1 us (38%)
  matrix products  8.01 us (17%)
  other arithmetic  0.5 us (1%)
    ppermute x17, waiting for transfers between devices, swap(): return lax.ppermute(value, AXES, [(i, i ^ mask) for i in range(count)])  19.6 us
    ppermute x17, starting transfers between devices, swap(): return lax.ppermute(value, AXES, [(i, i ^ mask) for i in range(count)])  18.1 us
    dot_general x5, matrix products, contract(): lax.dot_general(left, right, (((1,), (1,)), ((), ())), preferred_element_...  3.88 us
    dot_general x4, matrix products, product(): return jnp.dot(left, right, preferred_element_type=jnp.float32)  1.6 us
    dot_general x1, matrix products, per_device(): jnp.einsum('rlq,leq->rle', source, leaf_flux.reshape(leaves, edge_count,...  1.44 us
    dot_general x1, matrix products, per_device(): jnp.einsum('rlq,lqp->rlp', source, leaf_particular.reshape(leaves, points...  1.09 us
  transfers between devices with their start and end apart: 17, of which 10 were waited for; matrix products, arithmetic and copies ran while one was open for 4% of the time, Pallas kernels for 0%

profile of v10, /device:TPU:0, one launch (start us, length us, event | category | flops | bytes accessed | tf_op | source)
XLA Modules:
  0.0 46.9 jit_solution(11701308558431033392)
XLA Ops:
  0.0 0.0 copy-start
  0.0 1.4 %fusion = bf16[16,16,64]{2,0,1:T(8,128)(2,1)S(1)} fusion(bf16[16,64,256]{2,1,0:T(8,128)(2,1)} %bitcast.57, bf16[16,16,256]{2,1,0:T(8,128)(2,1)} %param.12), kind=kOutput, calls=%fused_computation.2 | convolution fusion | flops 8404992 | bytes 688128 | tf_op jit(solution)/shard_map/rlq,leq->rle/dot_general | solution.py:101
  1.5 0.0 copy-start.2
  1.5 0.1 reshape.271
  1.6 1.8 %convolution_convert_fusion.3 = bf16[16,640]{1,0:T(8,128)(2,1)S(1)} fusion(bf16[16,1024]{1,0:T(8,128)(2,1)S(1)} %reshape.271, bf16[640,1024]{1,0:T(8,128)(2,1)} %param.16), kind=kOutput, calls=%fused_computation.5 | convolution fusion | flops 20981760 | bytes 1363968 | tf_op jit(solution)/shard_map/dot_general | solution.py:10
  3.4 0.0 copy-done.5
  3.4 0.2 fusion.36
  3.6 3.0 %collective-permute-start = (bf16[16,768]{1,0:T(8,128)(2,1)S(1)}, bf16[16,768]{1,0:T(8,128)(2,1)S(1)}, u32[]{:S(2)}, u32[]{:S(2)}) collective-permute-start(bf16[16,768]{1,0:T(8,128)(2,1)S(1)} %get-tuple-element.39), channel_id=1, source_target_pairs={{0,1},{1,0},{2,3},{3,2},{4,5},{5,4},{6,7},{7,6},{8,9},{9,8},{10,11... | collective-permute-start | bytes 73736 | tf_op jit(solution)/shard_map/ppermute | solution.py:25
  6.6 0.0 copy-done.7
  6.6 0.0 copy-done.8
  6.6 2.7 %collective-permute-start.3 = (bf16[64,512]{1,0:T(8,128)(2,1)S(1)}, bf16[64,512]{1,0:T(8,128)(2,1)S(1)}, u32[]{:S(2)}, u32[]{:S(2)}) collective-permute-start(bf16[64,512]{1,0:T(8,128)(2,1)S(1)} %constant_dynamic-update-slice_fusion), channel_id=1, source_target_pairs={{0,4},{1,5},{2,6},{3,7},{4,0},{5,1},{6,2},{7,3},{8,12},{9,13},{10,... | collective-permute-start | bytes 196616 | tf_op jit(solution)/shard_map/ppermute | solution.py:25
  9.3 0.0 collective-permute-done
  9.3 1.6 %collective-permute-start.1 = (bf16[16,768]{1,0:T(8,128)(2,1)S(1)}, bf16[16,768]{1,0:T(8,128)(2,1)S(1)}, u32[]{:S(2)}, u32[]{:S(2)}) collective-permute-start(bf16[16,768]{1,0:T(8,128)(2,1)S(1)} %fusion.13), channel_id=1, source_target_pairs={{0,2},{1,3},{2,0},{3,1},{4,6},{5,7},{6,4},{7,5},{8,10},{9,11},{10,... | collective-permute-start | bytes 73736 | tf_op jit(solution)/shard_map/ppermute | solution.py:25
  10.9 0.0 copy-done
  10.9 0.0 copy-done.2
  10.9 1.1 %fusion.7 = f32[16,256,16]{1,2,0:T(8,128)} fusion(bf16[16,256,256]{2,1,0:T(8,128)(2,1)S(1)} %bitcast.54, bf16[16,16,256]{2,1,0:T(8,128)(2,1)S(1)} %copy-done.2), kind=kOutput, calls=%fused_computation.38 | convolution fusion | flops 33554432 | bytes 2490368 | tf_op jit(solution)/shard_map/rlq,lqp->rlp/dot_general | solution.py:156
  12.0 1.1 %collective-permute-done.1 = bf16[16,768]{1,0:T(8,128)(2,1)S(1)} collective-permute-done((bf16[16,768]{1,0:T(8,128)(2,1)S(1)}, bf16[16,768]{1,0:T(8,128)(2,1)S(1)}, u32[]{:S(2)}, u32[]{:S(2)}) %collective-permute-start.1) | collective-permute-done | bytes 24608 | tf_op jit(solution)/shard_map/ppermute | solution.py:25
  13.2 0.0 copy-done.3
  13.2 0.2 fusion.37
  13.4 0.1 collective-permute-start.2
  13.4 0.0 collective-permute-done.3
  13.5 1.2 %collective-permute-start.4 = (bf16[2,64,512]{2,1,0:T(8,128)(2,1)S(1)}, bf16[2,64,512]{2,1,0:T(8,128)(2,1)S(1)}, u32[]{:S(2)}, u32[]{:S(2)}) collective-permute-start(bf16[2,64,512]{2,1,0:T(8,128)(2,1)S(1)} %pad_maximum_fusion.7), channel_id=1, source_target_pairs={{0,1},{1,0},{2,3},{3,2},{4,5},{5,4},{6,7},{7,6},{8,9},{9,8},{10,11... | collective-permute-start | bytes 393224 | tf_op jit(solution)/shard_map/ppermute | solution.py:25
  14.7 3.5 %collective-permute-done.2 = bf16[16,1536]{1,0:T(8,128)(2,1)S(1)} collective-permute-done((bf16[16,1536]{1,0:T(8,128)(2,1)S(1)}, bf16[16,1536]{1,0:T(8,128)(2,1)S(1)}, u32[]{:S(2)}, u32[]{:S(2)}) %collective-permute-start.2) | collective-permute-done | bytes 49184 | tf_op jit(solution)/shard_map/ppermute | solution.py:25
  18.3 0.3 collective-permute-done.4
  18.6 2.7 %collective-permute-start.5 = (bf16[16,1536]{1,0:T(8,128)(2,1)S(1)}, bf16[16,1536]{1,0:T(8,128)(2,1)S(1)}, u32[]{:S(2)}, u32[]{:S(2)}) collective-permute-start(bf16[16,1536]{1,0:T(8,128)(2,1)S(1)} %convert_element_type.82), channel_id=1, source_target_pairs={{0,10},{1,11},{2,8},{3,9},{4,14},{5,15},{6,12},{7,13},{8,2},{9,3},... | collective-permute-start | bytes 147464 | tf_op jit(solution)/shard_map/ppermute | solution.py:25
  21.4 0.2 collective-permute-start.6
  21.6 0.0 collective-permute-start.10
  21.6 1.9 %collective-permute-start.12 = (bf16[2,2,64,256]{3,2,1,0:T(8,128)(2,1)S(1)}, bf16[2,2,64,256]{3,2,1,0:T(8,128)(2,1)S(1)}, u32[]{:S(2)}, u32[]{:S(2)}) collective-permute-start(bf16[2,2,64,256]{3,2,1,0:T(8,128)(2,1)S(1)} %get-tuple-element.26), channel_id=1, source_target_pairs={{0,2},{1,3},{2,0},{3,1},{4,6},{5,7},{6,4},{7,5},{8,10},{9,11},{10,... | collective-permute-start | bytes 393224 | tf_op jit(solution)/shard_map/ppermute | solution.py:25
  23.4 0.2 collective-permute-start.14
  23.7 0.0 collective-permute-done.5
  23.7 4.1 %collective-permute-done.6 = bf16[2,2,64,256]{3,2,1,0:T(8,128)(2,1)S(1)} collective-permute-done((bf16[2,2,64,256]{3,2,1,0:T(8,128)(2,1)S(1)}, bf16[2,2,64,256]{3,2,1,0:T(8,128)(2,1)S(1)}, u32[]{:S(2)}, u32[]{:S(2)}) %collective-permute-start.6) | collective-permute-done | bytes 131104 | tf_op jit(solution)/shard_map/ppermute | solution.py:25
  27.8 0.1 collective-permute-start.7
  27.9 1.3 %collective-permute-start.8 = (bf16[2,2,64,256]{3,2,1,0:T(8,128)(2,1)S(1)}, bf16[2,2,64,256]{3,2,1,0:T(8,128)(2,1)S(1)}, u32[]{:S(2)}, u32[]{:S(2)}) collective-permute-start(bf16[2,2,64,256]{3,2,1,0:T(8,128)(2,1)S(1)} %collective-permute-done.6), channel_id=1, source_target_pairs={{0,8},{1,9},{2,10},{3,11},{4,12},{5,13},{6,14},{7,15},{8,0},{9,1},... | collective-permute-start | bytes 393224 | tf_op jit(solution)/shard_map/ppermute | solution.py:25
  29.2 0.1 collective-permute-done.12
  29.3 0.0 collective-permute-start.13
  29.3 2.3 %collective-permute-done.7 = bf16[16,1536]{1,0:T(8,128)(2,1)S(1)} collective-permute-done((bf16[16,1536]{1,0:T(8,128)(2,1)S(1)}, bf16[16,1536]{1,0:T(8,128)(2,1)S(1)}, u32[]{:S(2)}, u32[]{:S(2)}) %collective-permute-start.7) | collective-permute-done | bytes 49184 | tf_op jit(solution)/shard_map/ppermute | solution.py:25
  31.7 0.0 collective-permute-done.8
  31.7 0.1 collective-permute-start.9
  31.8 0.0 collective-permute-done.10
  31.8 0.1 broadcast_select_fusion.1
  31.9 0.1 pad_maximum_fusion
  32.0 0.0 collective-permute-done.14
  32.0 0.0 collective-permute-done.13
  32.0 0.1 broadcast_select_fusion.3
  32.1 0.9 %collective-permute-done.9 = bf16[16,1536]{1,0:T(8,128)(2,1)S(1)} collective-permute-done((bf16[16,1536]{1,0:T(8,128)(2,1)S(1)}, bf16[16,1536]{1,0:T(8,128)(2,1)S(1)}, u32[]{:S(2)}, u32[]{:S(2)}) %collective-permute-start.9) | collective-permute-done | bytes 49184 | tf_op jit(solution)/shard_map/ppermute | solution.py:25
  33.0 0.2 fusion.38
  33.2 1.3 %collective-permute-start.11 = (bf16[16,256]{1,0:T(8,128)(2,1)S(1)}, bf16[16,256]{1,0:T(8,128)(2,1)S(1)}, u32[]{:S(2)}, u32[]{:S(2)}) collective-permute-start(bf16[16,256]{1,0:T(8,128)(2,1)S(1)} %get-tuple-element.43), channel_id=1, source_target_pairs={{0,24},{1,25},{2,26},{3,27},{4,28},{5,29},{6,30},{7,31},{8,16},{9,... | collective-permute-start | bytes 24584 | tf_op jit(solution)/shard_map/ppermute | solution.py:25
  34.5 0.1 pad_maximum_fusion.1
  34.5 0.0 copy-start.1
  34.6 1.7 %collective-permute-done.11 = bf16[16,256]{1,0:T(8,128)(2,1)S(1)} collective-permute-done((bf16[16,256]{1,0:T(8,128)(2,1)S(1)}, bf16[16,256]{1,0:T(8,128)(2,1)S(1)}, u32[]{:S(2)}, u32[]{:S(2)}) %collective-permute-start.11) | collective-permute-done | bytes 8224 | tf_op jit(solution)/shard_map/ppermute | solution.py:25
  36.3 0.2 convolution_convert_fusion.2
  36.5 0.0 copy-done.4
  36.5 0.2 convolution_convert_fusion.5
  36.7 1.0 %collective-permute-start.15 = (bf16[16,128]{1,0:T(8,128)(2,1)S(1)}, bf16[16,128]{1,0:T(8,128)(2,1)S(1)}, u32[]{:S(2)}, u32[]{:S(2)}) collective-permute-start(bf16[16,128]{1,0:T(8,128)(2,1)S(1)} %convolution_convert_fusion.5), channel_id=1, source_target_pairs={{0,1},{1,0},{2,3},{3,2},{4,5},{5,4},{6,7},{7,6},{8,9},{9,8},{10,11... | collective-permute-start | bytes 12296 | tf_op jit(solution)/shard_map/ppermute | solution.py:25
  37.7 2.7 %collective-permute-done.15 = bf16[16,128]{1,0:T(8,128)(2,1)S(1)} collective-permute-done((bf16[16,128]{1,0:T(8,128)(2,1)S(1)}, bf16[16,128]{1,0:T(8,128)(2,1)S(1)}, u32[]{:S(2)}, u32[]{:S(2)}) %collective-permute-start.15) | collective-permute-done | bytes 4128 | tf_op jit(solution)/shard_map/ppermute | solution.py:25
  40.4 0.8 %collective-permute-start.16 = (bf16[16,256]{1,0:T(8,128)(2,1)S(1)}, bf16[16,256]{1,0:T(8,128)(2,1)S(1)}, u32[]{:S(2)}, u32[]{:S(2)}) collective-permute-start(bf16[16,256]{1,0:T(8,128)(2,1)S(1)} %pad_maximum_fusion.8), channel_id=1, source_target_pairs={{0,2},{1,3},{2,0},{3,1},{4,6},{5,7},{6,4},{7,5},{8,10},{9,11},{10,... | collective-permute-start | bytes 24584 | tf_op jit(solution)/shard_map/ppermute | solution.py:25
  41.3 0.0 copy-start.6
  41.3 0.0 copy-start.9
  41.3 2.8 %collective-permute-done.16 = bf16[16,256]{1,0:T(8,128)(2,1)S(1)} collective-permute-done((bf16[16,256]{1,0:T(8,128)(2,1)S(1)}, bf16[16,256]{1,0:T(8,128)(2,1)S(1)}, u32[]{:S(2)}, u32[]{:S(2)}) %collective-permute-start.16) | collective-permute-done | bytes 8224 | tf_op jit(solution)/shard_map/ppermute | solution.py:25
  44.1 1.2 %convolution_convert_fusion.4 = bf16[16,256]{1,0:T(8,128)(2,1)S(1)} fusion(bf16[256,768]{1,0:T(8,128)(2,1)} %param.19, bf16[16,256]{1,0:T(8,128)(2,1)S(1)} %get-tuple-element.36, bf16[16,256]{1,0:T(8,128)(2,1)S(1)} %get-tuple-element.35, bf16[16,256]{1,0:T(8,128)(2,1)S(1)} %slice.30), kind=kOutput, calls=%fused_computation.6 | convolution fusion | flops 6369280 | bytes 425984 | tf_op jit(solution)/shard_map/dot_general | solution.py:10
  45.3 0.0 copy-done.1
  45.3 0.5 %convolution_convert_fusion.1 = bf16[16,1024]{1,0:T(8,128)(2,1)S(1)} fusion(bf16[1024,640]{1,0:T(8,128)(2,1)S(1)} %copy-done.1, bf16[16,256]{1,0:T(8,128)(2,1)S(1)} %convolution_convert_fusion.4, bf16[16,384]{1,0:T(8,128)(2,1)S(1)} %slice.28), kind=kOutput, calls=%fused_computation.3 | convolution fusion | flops 21028864 | bytes 1363968 | tf_op jit(solution)/shard_map/dot_general | solution.py:10
  45.8 0.0 copy-done.6
  45.8 1.1 %convolution_add_fusion = f32[16,16,256]{2,1,0:T(8,128)} fusion(bf16[1024,256]{1,0:T(8,128)(2,1)S(1)} %copy-done.9, pred[16,1024]{1,0:T(8,128)(4,1)S(1)} %iota_compare_fusion, f32[16,256,16]{1,2,0:T(8,128)S(1)} %copy-done.6, bf16[16,1024]{1,0:T(8,128)(2,1)S(1)} %convolution_convert_fusion.1), kind=kOutput, calls=%fused_computation | convolution fusion | flops 134545408 | bytes 1097728 | tf_op jit(solution)/shard_map/dot_general | solution.py:16
  (35 shorter events, 0.4 us)
Async XLA Ops:
  0.0 10.9 %copy-start = (bf16[4096,256]{1,0:T(8,128)(2,1)S(1)}, bf16[4096,256]{1,0:T(8,128)(2,1)}, u32[]{:S(2)}) copy-start(bf16[4096,256]{1,0:T(8,128)(2,1)} %param.14) | copy-start | bytes 6291460
  0.0 3.4 %copy-start.5 = (bf16[256,768]{1,0:T(8,128)(2,1)S(1)}, bf16[256,768]{1,0:T(8,128)(2,1)}, u32[]{:S(2)}) copy-start(bf16[256,768]{1,0:T(8,128)(2,1)} %param.18) | copy-start | bytes 1179652
  0.0 6.6 %copy-start.7 = (bf16[64,256]{1,0:T(8,128)(2,1)S(1)}, bf16[64,256]{1,0:T(8,128)(2,1)}, u32[]{:S(2)}) copy-start(bf16[64,256]{1,0:T(8,128)(2,1)} %param.22) | copy-start | bytes 98308
  0.0 6.6 %copy-start.8 = (bf16[64,256]{1,0:T(8,128)(2,1)S(1)}, bf16[64,256]{1,0:T(8,128)(2,1)}, u32[]{:S(2)}) copy-start(bf16[64,256]{1,0:T(8,128)(2,1)} %param.23) | copy-start | bytes 98308
  1.5 9.5 %copy-start.2 = (bf16[16,16,256]{2,1,0:T(8,128)(2,1)S(1)}, bf16[16,16,256]{2,1,0:T(8,128)(2,1)}, u32[]{:S(2)}) copy-start(bf16[16,16,256]{2,1,0:T(8,128)(2,1)} %param.12) | copy-start | bytes 393220
  3.6 5.7 %collective-permute-start = (bf16[16,768]{1,0:T(8,128)(2,1)S(1)}, bf16[16,768]{1,0:T(8,128)(2,1)S(1)}, u32[]{:S(2)}, u32[]{:S(2)}) collective-permute-start(bf16[16,768]{1,0:T(8,128)(2,1)S(1)} %get-tuple-element.39), channel_id=1, source_target_pairs={{0,1},{1,0},{2,3},{3,2},{4,5},{5,4},{6,7},{7,6},{8,9},{9,8},{10,11... | collective-permute-start | bytes 73736 | tf_op jit(solution)/shard_map/ppermute | solution.py:25
  6.6 6.8 %collective-permute-start.3 = (bf16[64,512]{1,0:T(8,128)(2,1)S(1)}, bf16[64,512]{1,0:T(8,128)(2,1)S(1)}, u32[]{:S(2)}, u32[]{:S(2)}) collective-permute-start(bf16[64,512]{1,0:T(8,128)(2,1)S(1)} %constant_dynamic-update-slice_fusion), channel_id=1, source_target_pairs={{0,4},{1,5},{2,6},{3,7},{4,0},{5,1},{6,2},{7,3},{8,12},{9,13},{10,... | collective-permute-start | bytes 196616 | tf_op jit(solution)/shard_map/ppermute | solution.py:25
  9.3 3.9 %collective-permute-start.1 = (bf16[16,768]{1,0:T(8,128)(2,1)S(1)}, bf16[16,768]{1,0:T(8,128)(2,1)S(1)}, u32[]{:S(2)}, u32[]{:S(2)}) collective-permute-start(bf16[16,768]{1,0:T(8,128)(2,1)S(1)} %fusion.13), channel_id=1, source_target_pairs={{0,2},{1,3},{2,0},{3,1},{4,6},{5,7},{6,4},{7,5},{8,10},{9,11},{10,... | collective-permute-start | bytes 73736 | tf_op jit(solution)/shard_map/ppermute | solution.py:25
  10.9 2.3 %copy-start.3 = (bf16[128,1536]{1,0:T(8,128)(2,1)S(1)}, bf16[128,1536]{1,0:T(8,128)(2,1)}, u32[]{:S(2)}) copy-start(bf16[128,1536]{1,0:T(8,128)(2,1)} %param.20) | copy-start | bytes 1179652
  13.4 4.9 %collective-permute-start.2 = (bf16[16,1536]{1,0:T(8,128)(2,1)S(1)}, bf16[16,1536]{1,0:T(8,128)(2,1)S(1)}, u32[]{:S(2)}, u32[]{:S(2)}) collective-permute-start(bf16[16,1536]{1,0:T(8,128)(2,1)S(1)} %get-tuple-element.41), channel_id=1, source_target_pairs={{0,12},{1,13},{2,14},{3,15},{4,8},{5,9},{6,10},{7,11},{8,4},{9,5},... | collective-permute-start | bytes 147464 | tf_op jit(solution)/shard_map/ppermute | solution.py:25
  13.5 5.1 %collective-permute-start.4 = (bf16[2,64,512]{2,1,0:T(8,128)(2,1)S(1)}, bf16[2,64,512]{2,1,0:T(8,128)(2,1)S(1)}, u32[]{:S(2)}, u32[]{:S(2)}) collective-permute-start(bf16[2,64,512]{2,1,0:T(8,128)(2,1)S(1)} %pad_maximum_fusion.7), channel_id=1, source_target_pairs={{0,1},{1,0},{2,3},{3,2},{4,5},{5,4},{6,7},{7,6},{8,9},{9,8},{10,11... | collective-permute-start | bytes 393224 | tf_op jit(solution)/shard_map/ppermute | solution.py:25
  18.6 5.1 %collective-permute-start.5 = (bf16[16,1536]{1,0:T(8,128)(2,1)S(1)}, bf16[16,1536]{1,0:T(8,128)(2,1)S(1)}, u32[]{:S(2)}, u32[]{:S(2)}) collective-permute-start(bf16[16,1536]{1,0:T(8,128)(2,1)S(1)} %convert_element_type.82), channel_id=1, source_target_pairs={{0,10},{1,11},{2,8},{3,9},{4,14},{5,15},{6,12},{7,13},{8,2},{9,3},... | collective-permute-start | bytes 147464 | tf_op jit(solution)/shard_map/ppermute | solution.py:25
  21.4 6.5 %collective-permute-start.6 = (bf16[2,2,64,256]{3,2,1,0:T(8,128)(2,1)S(1)}, bf16[2,2,64,256]{3,2,1,0:T(8,128)(2,1)S(1)}, u32[]{:S(2)}, u32[]{:S(2)}) collective-permute-start(bf16[2,2,64,256]{3,2,1,0:T(8,128)(2,1)S(1)} %get-tuple-element.25), channel_id=1, source_target_pairs={{0,2},{1,3},{2,0},{3,1},{4,6},{5,7},{6,4},{7,5},{8,10},{9,11},{10,... | collective-permute-start | bytes 393224 | tf_op jit(solution)/shard_map/ppermute | solution.py:25
  21.6 10.2 %collective-permute-start.10 = (bf16[2,2,64,256]{3,2,1,0:T(8,128)(2,1)S(1)}, bf16[2,2,64,256]{3,2,1,0:T(8,128)(2,1)S(1)}, u32[]{:S(2)}, u32[]{:S(2)}) collective-permute-start(bf16[2,2,64,256]{3,2,1,0:T(8,128)(2,1)S(1)} %get-tuple-element.25), channel_id=1, source_target_pairs={{0,8},{1,9},{2,10},{3,11},{4,12},{5,13},{6,14},{7,15},{8,0},{9,1},... | collective-permute-start | bytes 393224 | tf_op jit(solution)/shard_map/ppermute | solution.py:25
  21.6 7.7 %collective-permute-start.12 = (bf16[2,2,64,256]{3,2,1,0:T(8,128)(2,1)S(1)}, bf16[2,2,64,256]{3,2,1,0:T(8,128)(2,1)S(1)}, u32[]{:S(2)}, u32[]{:S(2)}) collective-permute-start(bf16[2,2,64,256]{3,2,1,0:T(8,128)(2,1)S(1)} %get-tuple-element.26), channel_id=1, source_target_pairs={{0,2},{1,3},{2,0},{3,1},{4,6},{5,7},{6,4},{7,5},{8,10},{9,11},{10,... | collective-permute-start | bytes 393224 | tf_op jit(solution)/shard_map/ppermute | solution.py:25
  23.4 8.5 %collective-permute-start.14 = (bf16[2,2,64,256]{3,2,1,0:T(8,128)(2,1)S(1)}, bf16[2,2,64,256]{3,2,1,0:T(8,128)(2,1)S(1)}, u32[]{:S(2)}, u32[]{:S(2)}) collective-permute-start(bf16[2,2,64,256]{3,2,1,0:T(8,128)(2,1)S(1)} %get-tuple-element.26), channel_id=1, source_target_pairs={{0,8},{1,9},{2,10},{3,11},{4,12},{5,13},{6,14},{7,15},{8,0},{9,1},... | collective-permute-start | bytes 393224 | tf_op jit(solution)/shard_map/ppermute | solution.py:25
  27.8 3.8 %collective-permute-start.7 = (bf16[16,1536]{1,0:T(8,128)(2,1)S(1)}, bf16[16,1536]{1,0:T(8,128)(2,1)S(1)}, u32[]{:S(2)}, u32[]{:S(2)}) collective-permute-start(bf16[16,1536]{1,0:T(8,128)(2,1)S(1)} %convert_element_type.84), channel_id=1, source_target_pairs={{0,9},{1,8},{2,11},{3,10},{4,13},{5,12},{6,15},{7,14},{8,1},{9,0},... | collective-permute-start | bytes 147464 | tf_op jit(solution)/shard_map/ppermute | solution.py:25
  27.9 3.8 %collective-permute-start.8 = (bf16[2,2,64,256]{3,2,1,0:T(8,128)(2,1)S(1)}, bf16[2,2,64,256]{3,2,1,0:T(8,128)(2,1)S(1)}, u32[]{:S(2)}, u32[]{:S(2)}) collective-permute-start(bf16[2,2,64,256]{3,2,1,0:T(8,128)(2,1)S(1)} %collective-permute-done.6), channel_id=1, source_target_pairs={{0,8},{1,9},{2,10},{3,11},{4,12},{5,13},{6,14},{7,15},{8,0},{9,1},... | collective-permute-start | bytes 393224 | tf_op jit(solution)/shard_map/ppermute | solution.py:25
  29.3 2.7 %collective-permute-start.13 = (bf16[2,2,64,256]{3,2,1,0:T(8,128)(2,1)S(1)}, bf16[2,2,64,256]{3,2,1,0:T(8,128)(2,1)S(1)}, u32[]{:S(2)}, u32[]{:S(2)}) collective-permute-start(bf16[2,2,64,256]{3,2,1,0:T(8,128)(2,1)S(1)} %collective-permute-done.12), channel_id=1, source_target_pairs={{0,8},{1,9},{2,10},{3,11},{4,12},{5,13},{6,14},{7,15},{8,0},{9,1},... | collective-permute-start | bytes 393224 | tf_op jit(solution)/shard_map/ppermute | solution.py:25
  31.7 1.3 %collective-permute-start.9 = (bf16[16,1536]{1,0:T(8,128)(2,1)S(1)}, bf16[16,1536]{1,0:T(8,128)(2,1)S(1)}, u32[]{:S(2)}, u32[]{:S(2)}) collective-permute-start(bf16[16,1536]{1,0:T(8,128)(2,1)S(1)} %convert_element_type.86), channel_id=1, source_target_pairs={{0,8},{1,9},{2,10},{3,11},{4,12},{5,13},{6,14},{7,15},{8,0},{9,1},... | collective-permute-start | bytes 147464 | tf_op jit(solution)/shard_map/ppermute | solution.py:25
  33.2 3.1 %collective-permute-start.11 = (bf16[16,256]{1,0:T(8,128)(2,1)S(1)}, bf16[16,256]{1,0:T(8,128)(2,1)S(1)}, u32[]{:S(2)}, u32[]{:S(2)}) collective-permute-start(bf16[16,256]{1,0:T(8,128)(2,1)S(1)} %get-tuple-element.43), channel_id=1, source_target_pairs={{0,24},{1,25},{2,26},{3,27},{4,28},{5,29},{6,30},{7,31},{8,16},{9,... | collective-permute-start | bytes 24584 | tf_op jit(solution)/shard_map/ppermute | solution.py:25
  34.5 2.1 %copy-start.4 = (bf16[128,1536]{1,0:T(8,128)(2,1)S(1)}, bf16[128,1536]{1,0:T(8,128)(2,1)}, u32[]{:S(2)}) copy-start(bf16[128,1536]{1,0:T(8,128)(2,1)} %param.21) | copy-start | bytes 1179652
  34.5 10.8 %copy-start.1 = (bf16[1024,640]{1,0:T(8,128)(2,1)S(1)}, bf16[1024,640]{1,0:T(8,128)(2,1)}, u32[]{:S(2)}) copy-start(bf16[1024,640]{1,0:T(8,128)(2,1)} %param.17) | copy-start | bytes 3932164
  36.7 3.6 %collective-permute-start.15 = (bf16[16,128]{1,0:T(8,128)(2,1)S(1)}, bf16[16,128]{1,0:T(8,128)(2,1)S(1)}, u32[]{:S(2)}, u32[]{:S(2)}) collective-permute-start(bf16[16,128]{1,0:T(8,128)(2,1)S(1)} %convolution_convert_fusion.5), channel_id=1, source_target_pairs={{0,1},{1,0},{2,3},{3,2},{4,5},{5,4},{6,7},{7,6},{8,9},{9,8},{10,11... | collective-permute-start | bytes 12296 | tf_op jit(solution)/shard_map/ppermute | solution.py:25
  40.4 3.7 %collective-permute-start.16 = (bf16[16,256]{1,0:T(8,128)(2,1)S(1)}, bf16[16,256]{1,0:T(8,128)(2,1)S(1)}, u32[]{:S(2)}, u32[]{:S(2)}) collective-permute-start(bf16[16,256]{1,0:T(8,128)(2,1)S(1)} %pad_maximum_fusion.8), channel_id=1, source_target_pairs={{0,2},{1,3},{2,0},{3,1},{4,6},{5,7},{6,4},{7,5},{8,10},{9,11},{10,... | collective-permute-start | bytes 24584 | tf_op jit(solution)/shard_map/ppermute | solution.py:25
  41.3 4.5 %copy-start.6 = (f32[16,256,16]{1,2,0:T(8,128)S(1)}, f32[16,256,16]{1,2,0:T(8,128)}, u32[]{:S(2)}) copy-start(f32[16,256,16]{1,2,0:T(8,128)} %fusion.7) | copy-start | bytes 786436
  41.3 4.5 %copy-start.9 = (bf16[1024,256]{1,0:T(8,128)(2,1)S(1)}, bf16[1024,256]{1,0:T(8,128)(2,1)}, u32[]{:S(2)}) copy-start(bf16[1024,256]{1,0:T(8,128)(2,1)} %param.15) | copy-start | bytes 1572868

commit v11 on v9

--- a/solution.py
+++ b/solution.py
@@ -120,7 +120,8 @@
     low = joined_pair(roots, roots_near, place & near != 0, 1)
     high = swap(roots_near, pair)
     second_sum = partner_sum(second_sum, near | pair)
-    second_sum, high = lax.optimization_barrier((second_sum, high))
+    kept = jnp.where(place < 0, -down_one, down_one)
+    second_sum, high, kept = lax.optimization_barrier((second_sum, high, kept))
     high = joined_pair(roots_pair, high, place & near != 0, 1)
     second_sum = partner_sum(second_sum, pair)
     second_state = rounded(second_sum)
@@ -139,7 +140,7 @@
     mid_bound = placed([mid_bound, swap(mid_bound, near)], place // near, 1)
     first_input = jnp.concatenate([first_state[:, :k_zero], mid_bound], axis=1)
 
-    box_bound = rounded(contract(first_input, down_one))
+    box_bound = rounded(contract(first_input, kept))
     box_input = jnp.concatenate([box_state[:, :inner_dev], box_bound], axis=1)
     leaf_bound = rounded(contract(box_input, box_down))
     edges = diagonal(leaf_bound[:, None, :], leaves)

time: 46.5 us -> 46.9 us (level)
  other arithmetic: 0.49 us -> 1.94 us
  waiting for transfers between devices: 19.1 us -> 18.4 us
    add x1, other arithmetic: 0.02 us -> 0.82 us  [partner_sum(): return total + swap(rounded(total), mask).astype(jnp.float32)]
    ppermute x14, waiting for transfers between devices: 19.1 us -> 18.4 us  [swap(): return lax.ppermute(value, AXES, [(i, i ^ mask) for i in range(count)])]
    dot_general x1, matrix products: 1.09 us -> 0.38 us  [per_device(): jnp.einsum('rlq,lqp->rlp', source, leaf_particular.reshape(leaves, points...]
    convert_element_type x6, other arithmetic: 0.07 us -> 0.69 us  [rounded(): return value.astype(jnp.bfloat16)]
  transfers between devices with their start and end apart: 14 -> 14, of which waited for: 10 -> 10; matrix products, arithmetic and copies ran while one was open for 4% -> 5% of each run, Pallas kernels for 0% -> 0%
where the time goes in v11:
time: 46.9 us; the launch traced here: 46.7 us
  waiting for transfers between devices  18.4 us (39%)
  starting transfers between devices  18.3 us (39%)
  matrix products  7.64 us (16%)
  other arithmetic  1.94 us (4%)
    ppermute x14, waiting for transfers between devices, swap(): return lax.ppermute(value, AXES, [(i, i ^ mask) for i in range(count)])  18.4 us
    ppermute x14, starting transfers between devices, swap(): return lax.ppermute(value, AXES, [(i, i ^ mask) for i in range(count)])  18.3 us
    dot_general x5, matrix products, contract(): lax.dot_general(left, right, (((1,), (1,)), ((), ())), preferred_element_...  4.21 us
    dot_general x4, matrix products, product(): return jnp.dot(left, right, preferred_element_type=jnp.float32)  1.62 us
    dot_general x1, matrix products, per_device(): jnp.einsum('rlq,leq->rle', source, leaf_flux.reshape(leaves, edge_count,...  1.44 us
  transfers between devices with their start and end apart: 14, of which 10 were waited for; matrix products, arithmetic and copies ran while one was open for 5% of the time, Pallas kernels for 0%

profile of v11, /device:TPU:0, one launch (start us, length us, event | category | flops | bytes accessed | tf_op | source)
XLA Modules:
  0.0 46.7 jit_solution(14131563490609802681)
XLA Ops:
  0.0 0.0 copy-start
  0.0 0.0 copy-start.4
  0.0 0.0 copy-start.6
  0.0 0.0 copy-start.7
  0.0 1.4 %fusion = bf16[16,16,64]{2,0,1:T(8,128)(2,1)S(1)} fusion(bf16[16,64,256]{2,1,0:T(8,128)(2,1)} %bitcast.46, bf16[16,16,256]{2,1,0:T(8,128)(2,1)} %param.12), kind=kOutput, calls=%fused_computation.2 | convolution fusion | flops 8404992 | bytes 688128 | tf_op jit(solution)/shard_map/rlq,leq->rle/dot_general | solution.py:94
  1.5 0.0 copy-start.2
  1.5 0.1 reshape.150
  1.6 1.8 %convolution_convert_fusion.3 = bf16[16,640]{1,0:T(8,128)(2,1)S(1)} fusion(bf16[16,1024]{1,0:T(8,128)(2,1)S(1)} %reshape.150, bf16[640,1024]{1,0:T(8,128)(2,1)} %param.16), kind=kOutput, calls=%fused_computation.5 | convolution fusion | flops 20981760 | bytes 1363968 | tf_op jit(solution)/shard_map/dot_general | solution.py:10
  3.4 0.0 copy-done.4
  3.4 0.2 fusion.39
  3.6 3.0 %collective-permute-start = (bf16[16,768]{1,0:T(8,128)(2,1)S(1)}, bf16[16,768]{1,0:T(8,128)(2,1)S(1)}, u32[]{:S(2)}, u32[]{:S(2)}) collective-permute-start(bf16[16,768]{1,0:T(8,128)(2,1)S(1)} %get-tuple-element.25), channel_id=1, source_target_pairs={{0,1},{1,0},{2,3},{3,2},{4,5},{5,4},{6,7},{7,6},{8,9},{9,8},{10,11... | collective-permute-start | bytes 73736 | tf_op jit(solution)/shard_map/ppermute | solution.py:25
  6.6 0.0 copy-done.6
  6.6 1.8 %collective-permute-done = bf16[16,768]{1,0:T(8,128)(2,1)S(1)} collective-permute-done((bf16[16,768]{1,0:T(8,128)(2,1)S(1)}, bf16[16,768]{1,0:T(8,128)(2,1)S(1)}, u32[]{:S(2)}, u32[]{:S(2)}) %collective-permute-start) | collective-permute-done | bytes 24608 | tf_op jit(solution)/shard_map/ppermute | solution.py:25
  8.4 2.1 %collective-permute-start.1 = (bf16[16,768]{1,0:T(8,128)(2,1)S(1)}, bf16[16,768]{1,0:T(8,128)(2,1)S(1)}, u32[]{:S(2)}, u32[]{:S(2)}) collective-permute-start(bf16[16,768]{1,0:T(8,128)(2,1)S(1)} %fusion.17), channel_id=1, source_target_pairs={{0,2},{1,3},{2,0},{3,1},{4,6},{5,7},{6,4},{7,5},{8,10},{9,11},{10,... | collective-permute-start | bytes 73736 | tf_op jit(solution)/shard_map/ppermute | solution.py:25
  10.5 0.0 copy-done.7
  10.6 2.6 %collective-permute-start.5 = (bf16[64,512]{1,0:T(8,128)(2,1)S(1)}, bf16[64,512]{1,0:T(8,128)(2,1)S(1)}, u32[]{:S(2)}, u32[]{:S(2)}) collective-permute-start(bf16[64,512]{1,0:T(8,128)(2,1)S(1)} %constant_dynamic-update-slice_fusion), channel_id=1, source_target_pairs={{0,4},{1,5},{2,6},{3,7},{4,0},{5,1},{6,2},{7,3},{8,12},{9,13},{10,... | collective-permute-start | bytes 196616 | tf_op jit(solution)/shard_map/ppermute | solution.py:25
  13.1 0.0 collective-permute-done.1
  13.2 0.0 copy-done.2
  13.2 0.0 copy-start.5
  13.2 0.2 fusion.40
  13.3 0.1 collective-permute-start.2
  13.4 2.8 %collective-permute-done.5 = bf16[64,512]{1,0:T(8,128)(2,1)S(1)} collective-permute-done((bf16[64,512]{1,0:T(8,128)(2,1)S(1)}, bf16[64,512]{1,0:T(8,128)(2,1)S(1)}, u32[]{:S(2)}, u32[]{:S(2)}) %collective-permute-start.5) | collective-permute-done | bytes 65568 | tf_op jit(solution)/shard_map/ppermute | solution.py:25
  16.3 1.7 %collective-permute-start.6 = (bf16[2,64,512]{2,1,0:T(8,128)(2,1)S(1)}, bf16[2,64,512]{2,1,0:T(8,128)(2,1)S(1)}, u32[]{:S(2)}, u32[]{:S(2)}) collective-permute-start(bf16[2,64,512]{2,1,0:T(8,128)(2,1)S(1)} %pad_maximum_fusion.4), channel_id=1, source_target_pairs={{0,1},{1,0},{2,3},{3,2},{4,5},{5,4},{6,7},{7,6},{8,9},{9,8},{10,11... | collective-permute-start | bytes 393224 | tf_op jit(solution)/shard_map/ppermute | solution.py:25
  17.9 0.3 collective-permute-done.2
  18.3 1.2 %collective-permute-start.3 = (bf16[16,1536]{1,0:T(8,128)(2,1)S(1)}, bf16[16,1536]{1,0:T(8,128)(2,1)S(1)}, u32[]{:S(2)}, u32[]{:S(2)}) collective-permute-start(bf16[16,1536]{1,0:T(8,128)(2,1)S(1)} %fusion.12), channel_id=1, source_target_pairs={{0,9},{1,8},{2,11},{3,10},{4,13},{5,12},{6,15},{7,14},{8,1},{9,0},... | collective-permute-start | bytes 147464 | tf_op jit(solution)/shard_map/ppermute | solution.py:25
  19.5 1.8 %collective-permute-done.6 = bf16[2,64,512]{2,1,0:T(8,128)(2,1)S(1)} collective-permute-done((bf16[2,64,512]{2,1,0:T(8,128)(2,1)S(1)}, bf16[2,64,512]{2,1,0:T(8,128)(2,1)S(1)}, u32[]{:S(2)}, u32[]{:S(2)}) %collective-permute-start.6) | collective-permute-done | bytes 131104 | tf_op jit(solution)/shard_map/ppermute | solution.py:25
  21.4 1.2 %collective-permute-start.7 = (bf16[2,2,64,512]{3,2,1,0:T(8,128)(2,1)S(1)}, bf16[2,2,64,512]{3,2,1,0:T(8,128)(2,1)S(1)}, u32[]{:S(2)}, u32[]{:S(2)}) collective-permute-start(bf16[2,2,64,512]{3,2,1,0:T(8,128)(2,1)S(1)} %pad_maximum_fusion.3), channel_id=1, source_target_pairs={{0,2},{1,3},{2,0},{3,1},{4,6},{5,7},{6,4},{7,5},{8,10},{9,11},{10,... | collective-permute-start | bytes 786440 | tf_op jit(solution)/shard_map/ppermute | solution.py:25
  22.5 0.0 collective-permute-done.3
  22.5 0.6 %fusion.16 = bf16[16,1536]{1,0:T(8,128)(2,1)} fusion(bf16[16,1536]{1,0:T(8,128)(2,1)S(1)} %collective-permute-done.3, f32[16,1536]{1,0:T(8,128)S(1)} %get-tuple-element.28, bf16[16,1536]{1,0:T(8,128)(2,1)S(1)} %collective-permute-done.2), kind=kLoop, calls=%fused_computation.46 | loop fusion | flops 122880 | bytes 245760 | tf_op jit(solution)/shard_map/convert_element_type | solution.py:20
  23.2 0.9 %collective-permute-start.4 = (bf16[16,1536]{1,0:T(8,128)(2,1)}, bf16[16,1536]{1,0:T(8,128)(2,1)}, u32[]{:S(2)}, u32[]{:S(2)}) collective-permute-start(bf16[16,1536]{1,0:T(8,128)(2,1)} %fusion.16), channel_id=1, source_target_pairs={{0,10},{1,11},{2,8},{3,9},{4,14},{5,15},{6,12},{7,13},{8,2},{9,3},... | collective-permute-start | bytes 147464 | tf_op jit(solution)/shard_map/ppermute | solution.py:25
  24.1 0.0 copy-done.5
  24.1 0.5 collective-permute-start.10
  24.6 5.1 %collective-permute-done.7 = bf16[2,2,64,512]{3,2,1,0:T(8,128)(2,1)S(1)} collective-permute-done((bf16[2,2,64,512]{3,2,1,0:T(8,128)(2,1)S(1)}, bf16[2,2,64,512]{3,2,1,0:T(8,128)(2,1)S(1)}, u32[]{:S(2)}, u32[]{:S(2)}) %collective-permute-start.7) | collective-permute-done | bytes 262176 | tf_op jit(solution)/shard_map/ppermute | solution.py:25
  29.6 0.0 collective-permute-start.8
  29.6 0.0 collective-permute-done.4
  29.6 0.8 %convert_add_fusion = f32[16,1536]{1,0:T(8,128)S(1)} fusion(bf16[16,1536]{1,0:T(8,128)(2,1)} %collective-permute-done.4, bf16[16,1536]{1,0:T(8,128)(2,1)S(1)} %collective-permute-done.3, f32[16,1536]{1,0:T(8,128)S(1)} %get-tuple-element.28, bf16[16,1536]{1,0:T(8,128)(2,1)S(1)} %collective-permute-done.2), kind=kLoop, calls=%fused_computation.34 | loop fusion | flops 147456 | bytes 344064 | tf_op jit(solution)/shard_map/add | solution.py:29
  30.5 0.7 %collective-permute-done.8 = bf16[2,2,64,512]{3,2,1,0:T(8,128)(2,1)S(1)} collective-permute-done((bf16[2,2,64,512]{3,2,1,0:T(8,128)(2,1)S(1)}, bf16[2,2,64,512]{3,2,1,0:T(8,128)(2,1)S(1)}, u32[]{:S(2)}, u32[]{:S(2)}) %collective-permute-start.8) | collective-permute-done | bytes 262176 | tf_op jit(solution)/shard_map/ppermute | solution.py:25
  31.2 0.2 collective-permute-start.9
  31.3 0.0 collective-permute-done.10
  31.4 0.1 broadcast_select_fusion.1
  31.5 0.0 copy-start.1
  31.5 0.1 pad_maximum_fusion
  31.6 0.9 %collective-permute-done.9 = bf16[16,1536]{1,0:T(8,128)(2,1)S(1)} collective-permute-done((bf16[16,1536]{1,0:T(8,128)(2,1)S(1)}, bf16[16,1536]{1,0:T(8,128)(2,1)S(1)}, u32[]{:S(2)}, u32[]{:S(2)}) %collective-permute-start.9) | collective-permute-done | bytes 49184 | tf_op jit(solution)/shard_map/ppermute | solution.py:25
  32.5 0.2 fusion.41
  32.7 1.4 %collective-permute-start.11 = (bf16[16,256]{1,0:T(8,128)(2,1)S(1)}, bf16[16,256]{1,0:T(8,128)(2,1)S(1)}, u32[]{:S(2)}, u32[]{:S(2)}) collective-permute-start(bf16[16,256]{1,0:T(8,128)(2,1)S(1)} %get-tuple-element.29), channel_id=1, source_target_pairs={{0,24},{1,25},{2,26},{3,27},{4,28},{5,29},{6,30},{7,31},{8,16},{9,... | collective-permute-start | bytes 24584 | tf_op jit(solution)/shard_map/ppermute | solution.py:25
  34.1 0.0 copy-done
  34.1 0.0 copy-done.1
  34.1 0.0 copy-start.3
  34.1 0.4 fusion.9
  34.5 1.3 %collective-permute-done.11 = bf16[16,256]{1,0:T(8,128)(2,1)S(1)} collective-permute-done((bf16[16,256]{1,0:T(8,128)(2,1)S(1)}, bf16[16,256]{1,0:T(8,128)(2,1)S(1)}, u32[]{:S(2)}, u32[]{:S(2)}) %collective-permute-start.11) | collective-permute-done | bytes 8224 | tf_op jit(solution)/shard_map/ppermute | solution.py:25
  35.8 0.2 convolution_convert_fusion.2
  36.0 0.0 copy-done.3
  36.0 0.0 copy-start.8
  36.0 0.2 convolution_convert_fusion.5
  36.2 1.7 %collective-permute-start.12 = (bf16[16,128]{1,0:T(8,128)(2,1)S(1)}, bf16[16,128]{1,0:T(8,128)(2,1)S(1)}, u32[]{:S(2)}, u32[]{:S(2)}) collective-permute-start(bf16[16,128]{1,0:T(8,128)(2,1)S(1)} %convolution_convert_fusion.5), channel_id=1, source_target_pairs={{0,1},{1,0},{2,3},{3,2},{4,5},{5,4},{6,7},{7,6},{8,9},{9,8},{10,11... | collective-permute-start | bytes 12296 | tf_op jit(solution)/shard_map/ppermute | solution.py:25
  37.9 1.9 %collective-permute-done.12 = bf16[16,128]{1,0:T(8,128)(2,1)S(1)} collective-permute-done((bf16[16,128]{1,0:T(8,128)(2,1)S(1)}, bf16[16,128]{1,0:T(8,128)(2,1)S(1)}, u32[]{:S(2)}, u32[]{:S(2)}) %collective-permute-start.12) | collective-permute-done | bytes 4128 | tf_op jit(solution)/shard_map/ppermute | solution.py:25
  39.9 1.8 %collective-permute-start.13 = (bf16[16,256]{1,0:T(8,128)(2,1)S(1)}, bf16[16,256]{1,0:T(8,128)(2,1)S(1)}, u32[]{:S(2)}, u32[]{:S(2)}) collective-permute-start(bf16[16,256]{1,0:T(8,128)(2,1)S(1)} %pad_maximum_fusion.5), channel_id=1, source_target_pairs={{0,2},{1,3},{2,0},{3,1},{4,6},{5,7},{6,4},{7,5},{8,10},{9,11},{10,... | collective-permute-start | bytes 24584 | tf_op jit(solution)/shard_map/ppermute | solution.py:25
  41.7 1.9 %collective-permute-done.13 = bf16[16,256]{1,0:T(8,128)(2,1)S(1)} collective-permute-done((bf16[16,256]{1,0:T(8,128)(2,1)S(1)}, bf16[16,256]{1,0:T(8,128)(2,1)S(1)}, u32[]{:S(2)}, u32[]{:S(2)}) %collective-permute-start.13) | collective-permute-done | bytes 8224 | tf_op jit(solution)/shard_map/ppermute | solution.py:25
  43.6 0.2 convolution_convert_fusion.4
  43.8 1.8 %convolution_convert_fusion.1 = bf16[16,1024]{1,0:T(8,128)(2,1)S(1)} fusion(bf16[1024,640]{1,0:T(8,128)(2,1)} %param.17, bf16[16,256]{1,0:T(8,128)(2,1)S(1)} %convolution_convert_fusion.4, bf16[16,384]{1,0:T(8,128)(2,1)S(1)} %slice.28), kind=kOutput, calls=%fused_computation.3 | convolution fusion | flops 21028864 | bytes 1363968 | tf_op jit(solution)/shard_map/dot_general | solution.py:10
  45.6 0.0 copy-done.8
  45.6 1.1 %convolution_add_fusion = f32[16,16,256]{2,1,0:T(8,128)} fusion(bf16[1024,256]{1,0:T(8,128)(2,1)S(1)} %copy-done.8, pred[16,1024]{1,0:T(8,128)(4,1)S(1)} %iota_compare_fusion, f32[16,256,16]{1,2,0:T(8,128)S(1)} %fusion.9, bf16[16,1024]{1,0:T(8,128)(2,1)S(1)} %convolution_convert_fusion.1), kind=kOutput, calls=%fused_computation | convolution fusion | flops 134545408 | bytes 1097728 | tf_op jit(solution)/shard_map/dot_general | solution.py:16
  (23 shorter events, 0.3 us)
Async XLA Ops:
  0.0 34.1 %copy-start = (bf16[4096,256]{1,0:T(8,128)(2,1)S(1)}, bf16[4096,256]{1,0:T(8,128)(2,1)}, u32[]{:S(2)}) copy-start(bf16[4096,256]{1,0:T(8,128)(2,1)} %param.14) | copy-start | bytes 6291460
  0.0 3.4 %copy-start.4 = (bf16[256,768]{1,0:T(8,128)(2,1)S(1)}, bf16[256,768]{1,0:T(8,128)(2,1)}, u32[]{:S(2)}) copy-start(bf16[256,768]{1,0:T(8,128)(2,1)} %param.18) | copy-start | bytes 1179652
  0.0 6.6 %copy-start.6 = (bf16[64,256]{1,0:T(8,128)(2,1)S(1)}, bf16[64,256]{1,0:T(8,128)(2,1)}, u32[]{:S(2)}) copy-start(bf16[64,256]{1,0:T(8,128)(2,1)} %param.22) | copy-start | bytes 98308
  0.0 10.5 %copy-start.7 = (bf16[64,256]{1,0:T(8,128)(2,1)S(1)}, bf16[64,256]{1,0:T(8,128)(2,1)}, u32[]{:S(2)}) copy-start(bf16[64,256]{1,0:T(8,128)(2,1)} %param.23) | copy-start | bytes 98308
  1.5 11.7 %copy-start.2 = (bf16[128,1536]{1,0:T(8,128)(2,1)S(1)}, bf16[128,1536]{1,0:T(8,128)(2,1)}, u32[]{:S(2)}) copy-start(bf16[128,1536]{1,0:T(8,128)(2,1)} %param.20) | copy-start | bytes 1179652
  3.6 4.8 %collective-permute-start = (bf16[16,768]{1,0:T(8,128)(2,1)S(1)}, bf16[16,768]{1,0:T(8,128)(2,1)S(1)}, u32[]{:S(2)}, u32[]{:S(2)}) collective-permute-start(bf16[16,768]{1,0:T(8,128)(2,1)S(1)} %get-tuple-element.25), channel_id=1, source_target_pairs={{0,1},{1,0},{2,3},{3,2},{4,5},{5,4},{6,7},{7,6},{8,9},{9,8},{10,11... | collective-permute-start | bytes 73736 | tf_op jit(solution)/shard_map/ppermute | solution.py:25
  8.4 4.7 %collective-permute-start.1 = (bf16[16,768]{1,0:T(8,128)(2,1)S(1)}, bf16[16,768]{1,0:T(8,128)(2,1)S(1)}, u32[]{:S(2)}, u32[]{:S(2)}) collective-permute-start(bf16[16,768]{1,0:T(8,128)(2,1)S(1)} %fusion.17), channel_id=1, source_target_pairs={{0,2},{1,3},{2,0},{3,1},{4,6},{5,7},{6,4},{7,5},{8,10},{9,11},{10,... | collective-permute-start | bytes 73736 | tf_op jit(solution)/shard_map/ppermute | solution.py:25
  10.6 5.7 %collective-permute-start.5 = (bf16[64,512]{1,0:T(8,128)(2,1)S(1)}, bf16[64,512]{1,0:T(8,128)(2,1)S(1)}, u32[]{:S(2)}, u32[]{:S(2)}) collective-permute-start(bf16[64,512]{1,0:T(8,128)(2,1)S(1)} %constant_dynamic-update-slice_fusion), channel_id=1, source_target_pairs={{0,4},{1,5},{2,6},{3,7},{4,0},{5,1},{6,2},{7,3},{8,12},{9,13},{10,... | collective-permute-start | bytes 196616 | tf_op jit(solution)/shard_map/ppermute | solution.py:25
  13.2 10.9 %copy-start.5 = (bf16[256,768]{1,0:T(8,128)(2,1)S(1)}, bf16[256,768]{1,0:T(8,128)(2,1)}, u32[]{:S(2)}) copy-start(bf16[256,768]{1,0:T(8,128)(2,1)} %param.19) | copy-start | bytes 1179652
  13.3 4.9 %collective-permute-start.2 = (bf16[16,1536]{1,0:T(8,128)(2,1)S(1)}, bf16[16,1536]{1,0:T(8,128)(2,1)S(1)}, u32[]{:S(2)}, u32[]{:S(2)}) collective-permute-start(bf16[16,1536]{1,0:T(8,128)(2,1)S(1)} %get-tuple-element.27), channel_id=1, source_target_pairs={{0,12},{1,13},{2,14},{3,15},{4,8},{5,9},{6,10},{7,11},{8,4},{9,5},... | collective-permute-start | bytes 147464 | tf_op jit(solution)/shard_map/ppermute | solution.py:25
  16.3 5.0 %collective-permute-start.6 = (bf16[2,64,512]{2,1,0:T(8,128)(2,1)S(1)}, bf16[2,64,512]{2,1,0:T(8,128)(2,1)S(1)}, u32[]{:S(2)}, u32[]{:S(2)}) collective-permute-start(bf16[2,64,512]{2,1,0:T(8,128)(2,1)S(1)} %pad_maximum_fusion.4), channel_id=1, source_target_pairs={{0,1},{1,0},{2,3},{3,2},{4,5},{5,4},{6,7},{7,6},{8,9},{9,8},{10,11... | collective-permute-start | bytes 393224 | tf_op jit(solution)/shard_map/ppermute | solution.py:25
  18.3 4.3 %collective-permute-start.3 = (bf16[16,1536]{1,0:T(8,128)(2,1)S(1)}, bf16[16,1536]{1,0:T(8,128)(2,1)S(1)}, u32[]{:S(2)}, u32[]{:S(2)}) collective-permute-start(bf16[16,1536]{1,0:T(8,128)(2,1)S(1)} %fusion.12), channel_id=1, source_target_pairs={{0,9},{1,8},{2,11},{3,10},{4,13},{5,12},{6,15},{7,14},{8,1},{9,0},... | collective-permute-start | bytes 147464 | tf_op jit(solution)/shard_map/ppermute | solution.py:25
  21.4 8.3 %collective-permute-start.7 = (bf16[2,2,64,512]{3,2,1,0:T(8,128)(2,1)S(1)}, bf16[2,2,64,512]{3,2,1,0:T(8,128)(2,1)S(1)}, u32[]{:S(2)}, u32[]{:S(2)}) collective-permute-start(bf16[2,2,64,512]{3,2,1,0:T(8,128)(2,1)S(1)} %pad_maximum_fusion.3), channel_id=1, source_target_pairs={{0,2},{1,3},{2,0},{3,1},{4,6},{5,7},{6,4},{7,5},{8,10},{9,11},{10,... | collective-permute-start | bytes 786440 | tf_op jit(solution)/shard_map/ppermute | solution.py:25
  23.2 6.5 %collective-permute-start.4 = (bf16[16,1536]{1,0:T(8,128)(2,1)}, bf16[16,1536]{1,0:T(8,128)(2,1)}, u32[]{:S(2)}, u32[]{:S(2)}) collective-permute-start(bf16[16,1536]{1,0:T(8,128)(2,1)} %fusion.16), channel_id=1, source_target_pairs={{0,10},{1,11},{2,8},{3,9},{4,14},{5,15},{6,12},{7,13},{8,2},{9,3},... | collective-permute-start | bytes 147464 | tf_op jit(solution)/shard_map/ppermute | solution.py:25
  24.1 7.2 %collective-permute-start.10 = (bf16[2,2,64,512]{3,2,1,0:T(8,128)(2,1)S(1)}, bf16[2,2,64,512]{3,2,1,0:T(8,128)(2,1)S(1)}, u32[]{:S(2)}, u32[]{:S(2)}) collective-permute-start(bf16[2,2,64,512]{3,2,1,0:T(8,128)(2,1)S(1)} %pad_maximum_fusion.3), channel_id=1, source_target_pairs={{0,8},{1,9},{2,10},{3,11},{4,12},{5,13},{6,14},{7,15},{8,0},{9,1},... | collective-permute-start | bytes 786440 | tf_op jit(solution)/shard_map/ppermute | solution.py:25
  29.6 1.5 %collective-permute-start.8 = (bf16[2,2,64,512]{3,2,1,0:T(8,128)(2,1)S(1)}, bf16[2,2,64,512]{3,2,1,0:T(8,128)(2,1)S(1)}, u32[]{:S(2)}, u32[]{:S(2)}) collective-permute-start(bf16[2,2,64,512]{3,2,1,0:T(8,128)(2,1)S(1)} %collective-permute-done.7), channel_id=1, source_target_pairs={{0,8},{1,9},{2,10},{3,11},{4,12},{5,13},{6,14},{7,15},{8,0},{9,1},... | collective-permute-start | bytes 786440 | tf_op jit(solution)/shard_map/ppermute | solution.py:25
  31.2 1.3 %collective-permute-start.9 = (bf16[16,1536]{1,0:T(8,128)(2,1)S(1)}, bf16[16,1536]{1,0:T(8,128)(2,1)S(1)}, u32[]{:S(2)}, u32[]{:S(2)}) collective-permute-start(bf16[16,1536]{1,0:T(8,128)(2,1)S(1)} %convert_element_type.86), channel_id=1, source_target_pairs={{0,8},{1,9},{2,10},{3,11},{4,12},{5,13},{6,14},{7,15},{8,0},{9,1},... | collective-permute-start | bytes 147464 | tf_op jit(solution)/shard_map/ppermute | solution.py:25
  31.5 2.6 %copy-start.1 = (bf16[16,16,256]{2,1,0:T(8,128)(2,1)S(1)}, bf16[16,16,256]{2,1,0:T(8,128)(2,1)}, u32[]{:S(2)}) copy-start(bf16[16,16,256]{2,1,0:T(8,128)(2,1)} %param.12) | copy-start | bytes 393220
  32.7 3.1 %collective-permute-start.11 = (bf16[16,256]{1,0:T(8,128)(2,1)S(1)}, bf16[16,256]{1,0:T(8,128)(2,1)S(1)}, u32[]{:S(2)}, u32[]{:S(2)}) collective-permute-start(bf16[16,256]{1,0:T(8,128)(2,1)S(1)} %get-tuple-element.29), channel_id=1, source_target_pairs={{0,24},{1,25},{2,26},{3,27},{4,28},{5,29},{6,30},{7,31},{8,16},{9,... | collective-permute-start | bytes 24584 | tf_op jit(solution)/shard_map/ppermute | solution.py:25
  34.1 1.9 %copy-start.3 = (bf16[128,1536]{1,0:T(8,128)(2,1)S(1)}, bf16[128,1536]{1,0:T(8,128)(2,1)}, u32[]{:S(2)}) copy-start(bf16[128,1536]{1,0:T(8,128)(2,1)} %param.21) | copy-start | bytes 1179652
  36.0 9.6 %copy-start.8 = (bf16[1024,256]{1,0:T(8,128)(2,1)S(1)}, bf16[1024,256]{1,0:T(8,128)(2,1)}, u32[]{:S(2)}) copy-start(bf16[1024,256]{1,0:T(8,128)(2,1)} %param.15) | copy-start | bytes 1572868
  36.2 3.6 %collective-permute-start.12 = (bf16[16,128]{1,0:T(8,128)(2,1)S(1)}, bf16[16,128]{1,0:T(8,128)(2,1)S(1)}, u32[]{:S(2)}, u32[]{:S(2)}) collective-permute-start(bf16[16,128]{1,0:T(8,128)(2,1)S(1)} %convolution_convert_fusion.5), channel_id=1, source_target_pairs={{0,1},{1,0},{2,3},{3,2},{4,5},{5,4},{6,7},{7,6},{8,9},{9,8},{10,11... | collective-permute-start | bytes 12296 | tf_op jit(solution)/shard_map/ppermute | solution.py:25
  39.9 3.7 %collective-permute-start.13 = (bf16[16,256]{1,0:T(8,128)(2,1)S(1)}, bf16[16,256]{1,0:T(8,128)(2,1)S(1)}, u32[]{:S(2)}, u32[]{:S(2)}) collective-permute-start(bf16[16,256]{1,0:T(8,128)(2,1)S(1)} %pad_maximum_fusion.5), channel_id=1, source_target_pairs={{0,2},{1,3},{2,0},{3,1},{4,6},{5,7},{6,4},{7,5},{8,10},{9,11},{10,... | collective-permute-start | bytes 24584 | tf_op jit(solution)/shard_map/ppermute | solution.py:25

commit v12 on v11

--- a/solution.py
+++ b/solution.py
@@ -121,7 +121,10 @@
     high = swap(roots_near, pair)
     second_sum = partner_sum(second_sum, near | pair)
     kept = jnp.where(place < 0, -down_one, down_one)
-    second_sum, high, kept = lax.optimization_barrier((second_sum, high, kept))
+    kept_down = jnp.where(place < 0, -box_down, box_down)
+    second_sum, high, kept, kept_down = lax.optimization_barrier(
+        (second_sum, high, kept, kept_down)
+    )
     high = joined_pair(roots_pair, high, place & near != 0, 1)
     second_sum = partner_sum(second_sum, pair)
     second_state = rounded(second_sum)
@@ -142,7 +145,7 @@
 
     box_bound = rounded(contract(first_input, kept))
     box_input = jnp.concatenate([box_state[:, :inner_dev], box_bound], axis=1)
-    leaf_bound = rounded(contract(box_input, box_down))
+    leaf_bound = rounded(contract(box_input, kept_down))
     edges = diagonal(leaf_bound[:, None, :], leaves)
     lifted = product(edges, leaf_lift)
     particular = jnp.einsum(

time: 46.9 us -> 51.2 us (1.092)
  other arithmetic: 1.94 us -> 6.8 us
  starting transfers between devices: 18.3 us -> 14.5 us
  local copies, waits for them, and re-layouts: 0.2 us -> 2.7 us
  matrix products: 7.64 us -> 9.08 us
  waiting for transfers between devices: 18.4 us -> 17.4 us
    ppermute x14, starting transfers between devices: 18.3 us -> 14.5 us  [swap(): return lax.ppermute(value, AXES, [(i, i ^ mask) for i in range(count)])]
    another operation x7, other arithmetic: 0.26 us -> 2.88 us  [joined_pair(): jnp.stack([jnp.where(upper, other, joined), jnp.where(upper, joined, othe...]
    unnamed x19 -> x29, local copies, waits for them, and re-layouts: 0.05 us -> 1.92 us
    select_n x0 -> x1, other arithmetic: none -> 1.47 us  [per_device(): kept_down = jnp.where(place < 0, -box_down, box_down)]
    dot_general x4, matrix products: 1.62 us -> 2.66 us  [product(): return jnp.dot(left, right, preferred_element_type=jnp.float32)]
    ppermute x14, waiting for transfers between devices: 18.4 us -> 17.4 us  [swap(): return lax.ppermute(value, AXES, [(i, i ^ mask) for i in range(count)])]
    select_n x1, other arithmetic: 0.03 us -> 0.78 us  [per_device(): kept = jnp.where(place < 0, -down_one, down_one)]
    dot_general x1, matrix products: 0.38 us -> 1.09 us  [per_device(): jnp.einsum('rlq,lqp->rlp', source, leaf_particular.reshape(leaves, points...]
  transfers between devices with their start and end apart: 14 -> 14, of which waited for: 10 -> 8; matrix products, arithmetic and copies ran while one was open for 5% -> 20% of each run, Pallas kernels for 0% -> 0%
where the time goes in v12:
time: 51.2 us; the launch traced here: 50.8 us
  waiting for transfers between devices  17.4 us (34%)
  starting transfers between devices  14.5 us (28%)
  matrix products  9.08 us (18%)
  other arithmetic  6.8 us (13%)
  local copies, waits for them, and re-layouts  2.7 us (5%)
    ppermute x14, waiting for transfers between devices, swap(): return lax.ppermute(value, AXES, [(i, i ^ mask) for i in range(count)])  17.4 us
    ppermute x14, starting transfers between devices, swap(): return lax.ppermute(value, AXES, [(i, i ^ mask) for i in range(count)])  14.5 us
    dot_general x5, matrix products, contract(): lax.dot_general(left, right, (((1,), (1,)), ((), ())), preferred_element_...  3.89 us
    another operation x7, other arithmetic, joined_pair(): jnp.stack([jnp.where(upper, other, joined), jnp.where(upper, joined, othe...  2.88 us
    dot_general x4, matrix products, product(): return jnp.dot(left, right, preferred_element_type=jnp.float32)  2.66 us
    unnamed x29, local copies, waits for them, and re-layouts  1.92 us
    select_n x1, other arithmetic, per_device(): kept_down = jnp.where(place < 0, -box_down, box_down)  1.47 us
    dot_general x1, matrix products, per_device(): jnp.einsum('rlq,leq->rle', source, leaf_flux.reshape(leaves, edge_count,...  1.44 us
  transfers between devices with their start and end apart: 14, of which 8 were waited for; matrix products, arithmetic and copies ran while one was open for 20% of the time, Pallas kernels for 0%

profile of v12, /device:TPU:0, one launch (start us, length us, event | category | flops | bytes accessed | tf_op | source)
XLA Modules:
  0.0 50.8 jit_solution(5641203225859078895)
XLA Ops:
  0.0 0.0 copy-start
  0.0 1.4 %fusion = bf16[16,16,64]{2,0,1:T(8,128)(2,1)S(1)} fusion(bf16[16,64,256]{2,1,0:T(8,128)(2,1)} %bitcast.46, bf16[16,16,256]{2,1,0:T(8,128)(2,1)} %param.12), kind=kOutput, calls=%fused_computation.3 | convolution fusion | flops 8404992 | bytes 688128 | tf_op jit(solution)/shard_map/rlq,leq->rle/dot_general | solution.py:94
  1.5 0.1 reshape.150
  1.6 1.8 %convolution_convert_fusion.3 = bf16[16,640]{1,0:T(8,128)(2,1)S(1)} fusion(bf16[16,1024]{1,0:T(8,128)(2,1)S(1)} %reshape.150, bf16[640,1024]{1,0:T(8,128)(2,1)} %param.16), kind=kOutput, calls=%fused_computation.6 | convolution fusion | flops 20981760 | bytes 1363968 | tf_op jit(solution)/shard_map/dot_general | solution.py:10
  3.4 0.0 copy-done.5
  3.4 0.2 fusion.39
  3.6 3.0 %collective-permute-start = (bf16[16,768]{1,0:T(8,128)(2,1)S(1)}, bf16[16,768]{1,0:T(8,128)(2,1)S(1)}, u32[]{:S(2)}, u32[]{:S(2)}) collective-permute-start(bf16[16,768]{1,0:T(8,128)(2,1)S(1)} %get-tuple-element.27), channel_id=1, source_target_pairs={{0,1},{1,0},{2,3},{3,2},{4,5},{5,4},{6,7},{7,6},{8,9},{9,8},{10,11... | collective-permute-start | bytes 73736 | tf_op jit(solution)/shard_map/ppermute | solution.py:25
  6.6 0.0 copy-done.11
  6.6 0.6 %constant_dynamic-update-slice_fusion.1 = bf16[64,512]{1,0:T(8,128)(2,1)} fusion(bf16[64,256]{1,0:T(8,128)(2,1)S(1)} %copy-done.11), kind=kLoop, calls=%fused_computation.68 | loop fusion | bytes 65536
  7.2 0.0 copy-done.12
  7.2 0.6 %constant_dynamic-update-slice_fusion = bf16[64,512]{1,0:T(8,128)(2,1)} fusion(bf16[64,512]{1,0:T(8,128)(2,1)} %constant_dynamic-update-slice_fusion.1, bf16[64,256]{1,0:T(8,128)(2,1)S(1)} %copy-done.12), kind=kLoop, calls=%fused_computation.67 | loop fusion | bytes 65536 | tf_op jit(solution)/shard_map/concatenate | solution.py:104
  7.8 2.6 %collective-permute-start.5 = (bf16[64,512]{1,0:T(8,128)(2,1)}, bf16[64,512]{1,0:T(8,128)(2,1)}, u32[]{:S(2)}, u32[]{:S(2)}) collective-permute-start(bf16[64,512]{1,0:T(8,128)(2,1)} %constant_dynamic-update-slice_fusion), channel_id=1, source_target_pairs={{0,4},{1,5},{2,6},{3,7},{4,0},{5,1},{6,2},{7,3},{8,12},{9,13},{10,... | collective-permute-start | bytes 196616 | tf_op jit(solution)/shard_map/ppermute | solution.py:25
  10.4 0.0 collective-permute-done
  10.4 0.0 copy-done.9
  10.4 1.6 %collective-permute-start.1 = (bf16[16,768]{1,0:T(8,128)(2,1)S(1)}, bf16[16,768]{1,0:T(8,128)(2,1)S(1)}, u32[]{:S(2)}, u32[]{:S(2)}) collective-permute-start(bf16[16,768]{1,0:T(8,128)(2,1)S(1)} %fusion.17), channel_id=1, source_target_pairs={{0,2},{1,3},{2,0},{3,1},{4,6},{5,7},{6,4},{7,5},{8,10},{9,11},{10,... | collective-permute-start | bytes 73736 | tf_op jit(solution)/shard_map/ppermute | solution.py:25
  12.1 1.5 %negate_select_fusion = bf16[1024,640]{1,0:T(8,128)(2,1)S(1)} fusion(bf16[1024,640]{1,0:T(8,128)(2,1)} %param.17, pred[]{:T(512)S(6)} %rem.32), kind=kLoop, calls=%fused_computation | loop fusion | flops 1310720 | bytes 2621441 | tf_op jit(solution)/shard_map/jit(_where)/select_n | solution.py:124
  13.6 0.8 %collective-permute-done.1 = bf16[16,768]{1,0:T(8,128)(2,1)S(1)} collective-permute-done((bf16[16,768]{1,0:T(8,128)(2,1)S(1)}, bf16[16,768]{1,0:T(8,128)(2,1)S(1)}, u32[]{:S(2)}, u32[]{:S(2)}) %collective-permute-start.1) | collective-permute-done | bytes 24608 | tf_op jit(solution)/shard_map/ppermute | solution.py:25
  14.4 0.0 copy-start.6
  14.4 1.2 %fusion.40 = (bf16[16,1536]{1,0:T(8,128)(2,1)S(1)}, f32[16,1536]{1,0:T(8,128)S(1)}) fusion(bf16[128,1536]{1,0:T(8,128)(2,1)} %param.20, bf16[16,768]{1,0:T(8,128)(2,1)S(1)} %add_convert_fusion.1, s32[]{:T(128)S(6)} %select_n.144), kind=kOutput, calls=%fused_computation.83 | convolution fusion | flops 6316032 | bytes 544772 | tf_op jit(solution)/shard_map/dot_general | solution.py:16
  15.6 0.1 collective-permute-start.2
  15.7 0.0 collective-permute-done.5
  15.7 0.9 %select_bitcast_fusion.7 = (bf16[1,64,512]{2,1,0:T(8,128)(2,1)S(1)}, bf16[1,64,512]{2,1,0:T(8,128)(2,1)S(1)}) fusion(bf16[64,512]{1,0:T(8,128)(2,1)} %collective-permute-done.5, bf16[64,512]{1,0:T(8,128)(2,1)} %constant_dynamic-update-slice_fusion, pred[]{:T(512)S(6)} %ne.64), kind=kLoop, calls=%fused_computation.40 | loop fusion | flops 65536 | bytes 262145 | tf_op jit(solution)/shard_map/stack | solution.py:52
  16.6 0.6 %collective-permute-start.6 = (bf16[2,64,512]{2,1,0:T(8,128)(2,1)S(1)}, bf16[2,64,512]{2,1,0:T(8,128)(2,1)S(1)}, u32[]{:S(2)}, u32[]{:S(2)}) collective-permute-start(bf16[2,64,512]{2,1,0:T(8,128)(2,1)S(1)} %pad_maximum_fusion.4), channel_id=1, source_target_pairs={{0,1},{1,0},{2,3},{3,2},{4,5},{5,4},{6,7},{7,6},{8,9},{9,8},{10,11... | collective-permute-start | bytes 393224 | tf_op jit(solution)/shard_map/ppermute | solution.py:25
  17.2 3.2 %collective-permute-done.2 = bf16[16,1536]{1,0:T(8,128)(2,1)S(1)} collective-permute-done((bf16[16,1536]{1,0:T(8,128)(2,1)S(1)}, bf16[16,1536]{1,0:T(8,128)(2,1)S(1)}, u32[]{:S(2)}, u32[]{:S(2)}) %collective-permute-start.2) | collective-permute-done | bytes 49184 | tf_op jit(solution)/shard_map/ppermute | solution.py:25
  20.4 0.1 collective-permute-start.3
  20.4 2.4 %collective-permute-done.6 = bf16[2,64,512]{2,1,0:T(8,128)(2,1)S(1)} collective-permute-done((bf16[2,64,512]{2,1,0:T(8,128)(2,1)S(1)}, bf16[2,64,512]{2,1,0:T(8,128)(2,1)S(1)}, u32[]{:S(2)}, u32[]{:S(2)}) %collective-permute-start.6) | collective-permute-done | bytes 131104 | tf_op jit(solution)/shard_map/ppermute | solution.py:25
  22.9 0.6 %copy-done.1 = bf16[2,1,64,512]{3,2,1,0:T(8,128)(2,1)} copy-done((bf16[2,1,64,512]{3,2,1,0:T(8,128)(2,1)}, bf16[2,1,64,512]{3,2,1,0:T(8,128)(2,1)S(1)}, u32[]{:S(2)}) %copy-start.1) | copy-done | bytes 131096
  23.5 0.7 %pad_maximum_fusion.3 = bf16[2,2,64,512]{3,2,1,0:T(8,128)(2,1)} fusion(bf16[2,1,64,512]{3,2,1,0:T(8,128)(2,1)S(1)} %get-tuple-element.20, bf16[2,1,64,512]{3,2,1,0:T(8,128)(2,1)S(1)} %get-tuple-element.19), kind=kLoop, calls=%fused_computation.21 | loop fusion | flops 131072 | bytes 524288 | tf_op jit(solution)/shard_map/stack | solution.py:52
  24.2 1.5 %collective-permute-start.7 = (bf16[2,2,64,512]{3,2,1,0:T(8,128)(2,1)}, bf16[2,2,64,512]{3,2,1,0:T(8,128)(2,1)}, u32[]{:S(2)}, u32[]{:S(2)}) collective-permute-start(bf16[2,2,64,512]{3,2,1,0:T(8,128)(2,1)} %pad_maximum_fusion.3), channel_id=1, source_target_pairs={{0,2},{1,3},{2,0},{3,1},{4,6},{5,7},{6,4},{7,5},{8,10},{9,11},{10,... | collective-permute-start | bytes 786440 | tf_op jit(solution)/shard_map/ppermute | solution.py:25
  25.8 0.0 collective-permute-done.3
  25.8 0.6 %copy-done.8 = bf16[16,1536]{1,0:T(8,128)(2,1)} copy-done((bf16[16,1536]{1,0:T(8,128)(2,1)}, bf16[16,1536]{1,0:T(8,128)(2,1)S(1)}, u32[]{:S(2)}) %copy-start.8) | copy-done | bytes 49176
  26.4 0.6 %fusion.16 = bf16[16,1536]{1,0:T(8,128)(2,1)} fusion(bf16[16,1536]{1,0:T(8,128)(2,1)S(1)} %collective-permute-done.3, f32[16,1536]{1,0:T(8,128)S(1)} %get-tuple-element.30, bf16[16,1536]{1,0:T(8,128)(2,1)S(1)} %collective-permute-done.2), kind=kLoop, calls=%fused_computation.47 | loop fusion | flops 122880 | bytes 245760 | tf_op jit(solution)/shard_map/convert_element_type | solution.py:20
  27.0 0.0 collective-permute-start.4
  27.0 0.8 %negate_select_fusion.1 = bf16[256,768]{1,0:T(8,128)(2,1)} fusion(bf16[256,768]{1,0:T(8,128)(2,1)S(1)} %copy-done.6, pred[]{:T(512)S(6)} %rem.32), kind=kLoop, calls=%fused_computation.10 | loop fusion | flops 393216 | bytes 786433 | tf_op jit(solution)/shard_map/jit(_where)/select_n | solution.py:123
  27.8 0.6 %collective-permute-start.10 = (bf16[2,2,64,512]{3,2,1,0:T(8,128)(2,1)}, bf16[2,2,64,512]{3,2,1,0:T(8,128)(2,1)S(1)}, u32[]{:S(2)}, u32[]{:S(2)}) collective-permute-start(bf16[2,2,64,512]{3,2,1,0:T(8,128)(2,1)} %pad_maximum_fusion.3), channel_id=1, source_target_pairs={{0,8},{1,9},{2,10},{3,11},{4,12},{5,13},{6,14},{7,15},{8,0},{9,1},... | collective-permute-start | bytes 786440 | tf_op jit(solution)/shard_map/ppermute | solution.py:25
  28.4 5.1 %collective-permute-done.7 = bf16[2,2,64,512]{3,2,1,0:T(8,128)(2,1)} collective-permute-done((bf16[2,2,64,512]{3,2,1,0:T(8,128)(2,1)}, bf16[2,2,64,512]{3,2,1,0:T(8,128)(2,1)}, u32[]{:S(2)}, u32[]{:S(2)}) %collective-permute-start.7) | collective-permute-done | bytes 262176 | tf_op jit(solution)/shard_map/ppermute | solution.py:25
  33.5 0.0 collective-permute-start.8
  33.5 0.0 collective-permute-done.4
  33.5 0.8 %convert_add_fusion = f32[16,1536]{1,0:T(8,128)S(1)} fusion(bf16[16,1536]{1,0:T(8,128)(2,1)} %collective-permute-done.4, bf16[16,1536]{1,0:T(8,128)(2,1)} %copy-done.8, f32[16,1536]{1,0:T(8,128)S(1)} %get-tuple-element.30, bf16[16,1536]{1,0:T(8,128)(2,1)S(1)} %collective-permute-done.2), kind=kLoop, calls=%fused_computation.35 | loop fusion | flops 147456 | bytes 344064 | tf_op jit(solution)/shard_map/add | solution.py:29
  34.3 1.1 %select_bitcast_fusion.1 = (bf16[1,2,1,2,64,512]{5,4,3,2,1,0:T(8,128)(2,1)S(1)}, bf16[1,2,1,2,64,512]{5,4,3,2,1,0:T(8,128)(2,1)S(1)}) fusion(bf16[2,2,64,512]{3,2,1,0:T(8,128)(2,1)} %collective-permute-done.7, pred[]{:T(512)S(6)} %ne.66, bf16[2,1,64,512]{3,2,1,0:T(8,128)(2,1)} %copy-done.2, bf16[2,1,64,512]{3,2,1,0:T(8,128)(2,1)} %copy-done.1), kind=kLoop, calls=%fused_computation.25 | loop fusion | flops 393216 | bytes 1048577 | tf_op jit(solution)/shard_map/stack | solution.py:52
  35.4 0.0 collective-permute-done.8
  35.5 0.6 %collective-permute-start.9 = (bf16[16,1536]{1,0:T(8,128)(2,1)S(1)}, bf16[16,1536]{1,0:T(8,128)(2,1)S(1)}, u32[]{:S(2)}, u32[]{:S(2)}) collective-permute-start(bf16[16,1536]{1,0:T(8,128)(2,1)S(1)} %convert_element_type.86), channel_id=1, source_target_pairs={{0,8},{1,9},{2,10},{3,11},{4,12},{5,13},{6,14},{7,15},{8,0},{9,1},... | collective-permute-start | bytes 147464 | tf_op jit(solution)/shard_map/ppermute | solution.py:25
  36.0 0.0 collective-permute-done.10
  36.1 0.1 broadcast_select_fusion.1
  36.2 0.0 copy-start.3
  36.2 0.1 pad_maximum_fusion
  36.3 0.6 %collective-permute-done.9 = bf16[16,1536]{1,0:T(8,128)(2,1)S(1)} collective-permute-done((bf16[16,1536]{1,0:T(8,128)(2,1)S(1)}, bf16[16,1536]{1,0:T(8,128)(2,1)S(1)}, u32[]{:S(2)}, u32[]{:S(2)}) %collective-permute-start.9) | collective-permute-done | bytes 49184 | tf_op jit(solution)/shard_map/ppermute | solution.py:25
  36.9 0.2 fusion.41
  37.1 1.5 %collective-permute-start.11 = (bf16[16,256]{1,0:T(8,128)(2,1)S(1)}, bf16[16,256]{1,0:T(8,128)(2,1)S(1)}, u32[]{:S(2)}, u32[]{:S(2)}) collective-permute-start(bf16[16,256]{1,0:T(8,128)(2,1)S(1)} %get-tuple-element.31), channel_id=1, source_target_pairs={{0,24},{1,25},{2,26},{3,27},{4,28},{5,29},{6,30},{7,31},{8,16},{9,... | collective-permute-start | bytes 24584 | tf_op jit(solution)/shard_map/ppermute | solution.py:25
  38.6 0.0 copy-done.3
  38.6 1.1 %fusion.9 = f32[16,256,16]{1,2,0:T(8,128)} fusion(bf16[16,256,256]{2,1,0:T(8,128)(2,1)S(1)} %bitcast.43, bf16[16,16,256]{2,1,0:T(8,128)(2,1)S(1)} %copy-done.3), kind=kOutput, calls=%fused_computation.31 | convolution fusion | flops 33554432 | bytes 2490368 | tf_op jit(solution)/shard_map/rlq,lqp->rlp/dot_general | solution.py:151
  39.7 0.5 %collective-permute-done.11 = bf16[16,256]{1,0:T(8,128)(2,1)S(1)} collective-permute-done((bf16[16,256]{1,0:T(8,128)(2,1)S(1)}, bf16[16,256]{1,0:T(8,128)(2,1)S(1)}, u32[]{:S(2)}, u32[]{:S(2)}) %collective-permute-start.11) | collective-permute-done | bytes 8224 | tf_op jit(solution)/shard_map/ppermute | solution.py:25
  40.2 0.2 convolution_convert_fusion.2
  40.4 0.2 convolution_convert_fusion.5
  40.6 0.7 %collective-permute-start.12 = (bf16[16,128]{1,0:T(8,128)(2,1)S(1)}, bf16[16,128]{1,0:T(8,128)(2,1)S(1)}, u32[]{:S(2)}, u32[]{:S(2)}) collective-permute-start(bf16[16,128]{1,0:T(8,128)(2,1)S(1)} %convolution_convert_fusion.5), channel_id=1, source_target_pairs={{0,1},{1,0},{2,3},{3,2},{4,5},{5,4},{6,7},{7,6},{8,9},{9,8},{10,11... | collective-permute-start | bytes 12296 | tf_op jit(solution)/shard_map/ppermute | solution.py:25
  41.4 2.9 %collective-permute-done.12 = bf16[16,128]{1,0:T(8,128)(2,1)S(1)} collective-permute-done((bf16[16,128]{1,0:T(8,128)(2,1)S(1)}, bf16[16,128]{1,0:T(8,128)(2,1)S(1)}, u32[]{:S(2)}, u32[]{:S(2)}) %collective-permute-start.12) | collective-permute-done | bytes 4128 | tf_op jit(solution)/shard_map/ppermute | solution.py:25
  44.3 1.7 %collective-permute-start.13 = (bf16[16,256]{1,0:T(8,128)(2,1)S(1)}, bf16[16,256]{1,0:T(8,128)(2,1)S(1)}, u32[]{:S(2)}, u32[]{:S(2)}) collective-permute-start(bf16[16,256]{1,0:T(8,128)(2,1)S(1)} %pad_maximum_fusion.5), channel_id=1, source_target_pairs={{0,2},{1,3},{2,0},{3,1},{4,6},{5,7},{6,4},{7,5},{8,10},{9,11},{10,... | collective-permute-start | bytes 24584 | tf_op jit(solution)/shard_map/ppermute | solution.py:25
  46.0 0.0 copy-start.7
  46.0 0.0 copy-start.13
  46.0 2.0 %collective-permute-done.13 = bf16[16,256]{1,0:T(8,128)(2,1)S(1)} collective-permute-done((bf16[16,256]{1,0:T(8,128)(2,1)S(1)}, bf16[16,256]{1,0:T(8,128)(2,1)S(1)}, u32[]{:S(2)}, u32[]{:S(2)}) %collective-permute-start.13) | collective-permute-done | bytes 8224 | tf_op jit(solution)/shard_map/ppermute | solution.py:25
  48.0 0.0 slice-done.1
  48.0 1.2 %convolution_convert_fusion.4 = bf16[16,256]{1,0:T(8,128)(2,1)S(1)} fusion(bf16[256,768]{1,0:T(8,128)(2,1)} %negate_select_fusion.1, bf16[16,256]{1,0:T(8,128)(2,1)S(1)} %get-tuple-element.24, bf16[16,256]{1,0:T(8,128)(2,1)S(1)} %get-tuple-element.23, bf16[16,256]{1,0:T(8,128)(2,1)S(1)} %slice-done.1), kind=kOutput, calls=%fused_computation.7 | convolution fusion | flops 6369280 | bytes 425984 | tf_op jit(solution)/shard_map/dot_general | solution.py:10
  49.2 0.5 %convolution_convert_fusion.1 = bf16[16,1024]{1,0:T(8,128)(2,1)S(1)} fusion(bf16[1024,640]{1,0:T(8,128)(2,1)S(1)} %negate_select_fusion, bf16[16,256]{1,0:T(8,128)(2,1)S(1)} %convolution_convert_fusion.4, bf16[16,384]{1,0:T(8,128)(2,1)S(1)} %slice-done), kind=kOutput, calls=%fused_computation.4 | convolution fusion | flops 21028864 | bytes 1363968 | tf_op jit(solution)/shard_map/dot_general | solution.py:10
  49.7 1.1 %convolution_add_fusion = f32[16,16,256]{2,1,0:T(8,128)} fusion(bf16[1024,256]{1,0:T(8,128)(2,1)S(1)} %copy-done.13, pred[16,1024]{1,0:T(8,128)(4,1)S(1)} %iota_compare_fusion, f32[16,256,16]{1,2,0:T(8,128)S(1)} %copy-done.7, bf16[16,1024]{1,0:T(8,128)(2,1)S(1)} %convolution_convert_fusion.1), kind=kOutput, calls=%fused_computation.1 | convolution fusion | flops 134545408 | bytes 1097728 | tf_op jit(solution)/shard_map/dot_general | solution.py:16
  (34 shorter events, 0.2 us)
Async XLA Ops:
  0.0 38.6 %copy-start = (bf16[4096,256]{1,0:T(8,128)(2,1)S(1)}, bf16[4096,256]{1,0:T(8,128)(2,1)}, u32[]{:S(2)}) copy-start(bf16[4096,256]{1,0:T(8,128)(2,1)} %param.14) | copy-start | bytes 6291460
  0.0 3.4 %copy-start.5 = (bf16[256,768]{1,0:T(8,128)(2,1)S(1)}, bf16[256,768]{1,0:T(8,128)(2,1)}, u32[]{:S(2)}) copy-start(bf16[256,768]{1,0:T(8,128)(2,1)} %param.18) | copy-start | bytes 1179652
  0.0 6.6 %copy-start.11 = (bf16[64,256]{1,0:T(8,128)(2,1)S(1)}, bf16[64,256]{1,0:T(8,128)(2,1)}, u32[]{:S(2)}) copy-start(bf16[64,256]{1,0:T(8,128)(2,1)} %param.22) | copy-start | bytes 98308
  0.0 7.2 %copy-start.12 = (bf16[64,256]{1,0:T(8,128)(2,1)S(1)}, bf16[64,256]{1,0:T(8,128)(2,1)}, u32[]{:S(2)}) copy-start(bf16[64,256]{1,0:T(8,128)(2,1)} %param.23) | copy-start | bytes 98308
  3.4 7.1 %copy-start.9 = (bf16[16,640]{1,0:T(8,128)(2,1)}, bf16[16,640]{1,0:T(8,128)(2,1)S(1)}, u32[]{:S(2)}) copy-start(bf16[16,640]{1,0:T(8,128)(2,1)S(1)} %convolution_convert_fusion.3) | copy-start | bytes 61444
  3.6 6.9 %collective-permute-start = (bf16[16,768]{1,0:T(8,128)(2,1)S(1)}, bf16[16,768]{1,0:T(8,128)(2,1)S(1)}, u32[]{:S(2)}, u32[]{:S(2)}) collective-permute-start(bf16[16,768]{1,0:T(8,128)(2,1)S(1)} %get-tuple-element.27), channel_id=1, source_target_pairs={{0,1},{1,0},{2,3},{3,2},{4,5},{5,4},{6,7},{7,6},{8,9},{9,8},{10,11... | collective-permute-start | bytes 73736 | tf_op jit(solution)/shard_map/ppermute | solution.py:25
  7.8 7.8 %collective-permute-start.5 = (bf16[64,512]{1,0:T(8,128)(2,1)}, bf16[64,512]{1,0:T(8,128)(2,1)}, u32[]{:S(2)}, u32[]{:S(2)}) collective-permute-start(bf16[64,512]{1,0:T(8,128)(2,1)} %constant_dynamic-update-slice_fusion), channel_id=1, source_target_pairs={{0,4},{1,5},{2,6},{3,7},{4,0},{5,1},{6,2},{7,3},{8,12},{9,13},{10,... | collective-permute-start | bytes 196616 | tf_op jit(solution)/shard_map/ppermute | solution.py:25
  10.4 3.9 %collective-permute-start.1 = (bf16[16,768]{1,0:T(8,128)(2,1)S(1)}, bf16[16,768]{1,0:T(8,128)(2,1)S(1)}, u32[]{:S(2)}, u32[]{:S(2)}) collective-permute-start(bf16[16,768]{1,0:T(8,128)(2,1)S(1)} %fusion.17), channel_id=1, source_target_pairs={{0,2},{1,3},{2,0},{3,1},{4,6},{5,7},{6,4},{7,5},{8,10},{9,11},{10,... | collective-permute-start | bytes 73736 | tf_op jit(solution)/shard_map/ppermute | solution.py:25
  14.4 2.2 %copy-start.10 = (bf16[16,768]{1,0:T(8,128)(2,1)}, bf16[16,768]{1,0:T(8,128)(2,1)S(1)}, u32[]{:S(2)}) copy-start(bf16[16,768]{1,0:T(8,128)(2,1)S(1)} %add_convert_fusion.1) | copy-start | bytes 73732
  14.4 12.7 %copy-start.6 = (bf16[256,768]{1,0:T(8,128)(2,1)S(1)}, bf16[256,768]{1,0:T(8,128)(2,1)}, u32[]{:S(2)}) copy-start(bf16[256,768]{1,0:T(8,128)(2,1)} %param.19) | copy-start | bytes 1179652
  15.6 4.8 %collective-permute-start.2 = (bf16[16,1536]{1,0:T(8,128)(2,1)S(1)}, bf16[16,1536]{1,0:T(8,128)(2,1)S(1)}, u32[]{:S(2)}, u32[]{:S(2)}) collective-permute-start(bf16[16,1536]{1,0:T(8,128)(2,1)S(1)} %get-tuple-element.29), channel_id=1, source_target_pairs={{0,12},{1,13},{2,14},{3,15},{4,8},{5,9},{6,10},{7,11},{8,4},{9,5},... | collective-permute-start | bytes 147464 | tf_op jit(solution)/shard_map/ppermute | solution.py:25
  16.6 6.3 %collective-permute-start.6 = (bf16[2,64,512]{2,1,0:T(8,128)(2,1)S(1)}, bf16[2,64,512]{2,1,0:T(8,128)(2,1)S(1)}, u32[]{:S(2)}, u32[]{:S(2)}) collective-permute-start(bf16[2,64,512]{2,1,0:T(8,128)(2,1)S(1)} %pad_maximum_fusion.4), channel_id=1, source_target_pairs={{0,1},{1,0},{2,3},{3,2},{4,5},{5,4},{6,7},{7,6},{8,9},{9,8},{10,11... | collective-permute-start | bytes 393224 | tf_op jit(solution)/shard_map/ppermute | solution.py:25
  20.4 5.4 %collective-permute-start.3 = (bf16[16,1536]{1,0:T(8,128)(2,1)S(1)}, bf16[16,1536]{1,0:T(8,128)(2,1)S(1)}, u32[]{:S(2)}, u32[]{:S(2)}) collective-permute-start(bf16[16,1536]{1,0:T(8,128)(2,1)S(1)} %fusion.12), channel_id=1, source_target_pairs={{0,9},{1,8},{2,11},{3,10},{4,13},{5,12},{6,15},{7,14},{8,1},{9,0},... | collective-permute-start | bytes 147464 | tf_op jit(solution)/shard_map/ppermute | solution.py:25
  22.9 0.6 %copy-start.1 = (bf16[2,1,64,512]{3,2,1,0:T(8,128)(2,1)}, bf16[2,1,64,512]{3,2,1,0:T(8,128)(2,1)S(1)}, u32[]{:S(2)}) copy-start(bf16[2,1,64,512]{3,2,1,0:T(8,128)(2,1)S(1)} %get-tuple-element.19) | copy-start | bytes 393220
  22.9 1.4 %copy-start.2 = (bf16[2,1,64,512]{3,2,1,0:T(8,128)(2,1)}, bf16[2,1,64,512]{3,2,1,0:T(8,128)(2,1)S(1)}, u32[]{:S(2)}) copy-start(bf16[2,1,64,512]{3,2,1,0:T(8,128)(2,1)S(1)} %get-tuple-element.20) | copy-start | bytes 393220
  24.2 9.2 %collective-permute-start.7 = (bf16[2,2,64,512]{3,2,1,0:T(8,128)(2,1)}, bf16[2,2,64,512]{3,2,1,0:T(8,128)(2,1)}, u32[]{:S(2)}, u32[]{:S(2)}) collective-permute-start(bf16[2,2,64,512]{3,2,1,0:T(8,128)(2,1)} %pad_maximum_fusion.3), channel_id=1, source_target_pairs={{0,2},{1,3},{2,0},{3,1},{4,6},{5,7},{6,4},{7,5},{8,10},{9,11},{10,... | collective-permute-start | bytes 786440 | tf_op jit(solution)/shard_map/ppermute | solution.py:25
  25.8 0.6 %copy-start.8 = (bf16[16,1536]{1,0:T(8,128)(2,1)}, bf16[16,1536]{1,0:T(8,128)(2,1)S(1)}, u32[]{:S(2)}) copy-start(bf16[16,1536]{1,0:T(8,128)(2,1)S(1)} %collective-permute-done.3) | copy-start | bytes 147460
  27.0 6.5 %collective-permute-start.4 = (bf16[16,1536]{1,0:T(8,128)(2,1)}, bf16[16,1536]{1,0:T(8,128)(2,1)}, u32[]{:S(2)}, u32[]{:S(2)}) collective-permute-start(bf16[16,1536]{1,0:T(8,128)(2,1)} %fusion.16), channel_id=1, source_target_pairs={{0,10},{1,11},{2,8},{3,9},{4,14},{5,15},{6,12},{7,13},{8,2},{9,3},... | collective-permute-start | bytes 147464 | tf_op jit(solution)/shard_map/ppermute | solution.py:25
  27.8 8.2 %collective-permute-start.10 = (bf16[2,2,64,512]{3,2,1,0:T(8,128)(2,1)}, bf16[2,2,64,512]{3,2,1,0:T(8,128)(2,1)S(1)}, u32[]{:S(2)}, u32[]{:S(2)}) collective-permute-start(bf16[2,2,64,512]{3,2,1,0:T(8,128)(2,1)} %pad_maximum_fusion.3), channel_id=1, source_target_pairs={{0,8},{1,9},{2,10},{3,11},{4,12},{5,13},{6,14},{7,15},{8,0},{9,1},... | collective-permute-start | bytes 786440 | tf_op jit(solution)/shard_map/ppermute | solution.py:25
  33.5 1.9 %collective-permute-start.8 = (bf16[2,2,64,512]{3,2,1,0:T(8,128)(2,1)}, bf16[2,2,64,512]{3,2,1,0:T(8,128)(2,1)S(1)}, u32[]{:S(2)}, u32[]{:S(2)}) collective-permute-start(bf16[2,2,64,512]{3,2,1,0:T(8,128)(2,1)} %collective-permute-done.7), channel_id=1, source_target_pairs={{0,8},{1,9},{2,10},{3,11},{4,12},{5,13},{6,14},{7,15},{8,0},{9,1},... | collective-permute-start | bytes 786440 | tf_op jit(solution)/shard_map/ppermute | solution.py:25
  35.5 1.5 %collective-permute-start.9 = (bf16[16,1536]{1,0:T(8,128)(2,1)S(1)}, bf16[16,1536]{1,0:T(8,128)(2,1)S(1)}, u32[]{:S(2)}, u32[]{:S(2)}) collective-permute-start(bf16[16,1536]{1,0:T(8,128)(2,1)S(1)} %convert_element_type.86), channel_id=1, source_target_pairs={{0,8},{1,9},{2,10},{3,11},{4,12},{5,13},{6,14},{7,15},{8,0},{9,1},... | collective-permute-start | bytes 147464 | tf_op jit(solution)/shard_map/ppermute | solution.py:25
  36.2 2.4 %copy-start.3 = (bf16[16,16,256]{2,1,0:T(8,128)(2,1)S(1)}, bf16[16,16,256]{2,1,0:T(8,128)(2,1)}, u32[]{:S(2)}) copy-start(bf16[16,16,256]{2,1,0:T(8,128)(2,1)} %param.12) | copy-start | bytes 393220
  37.1 3.1 %collective-permute-start.11 = (bf16[16,256]{1,0:T(8,128)(2,1)S(1)}, bf16[16,256]{1,0:T(8,128)(2,1)S(1)}, u32[]{:S(2)}, u32[]{:S(2)}) collective-permute-start(bf16[16,256]{1,0:T(8,128)(2,1)S(1)} %get-tuple-element.31), channel_id=1, source_target_pairs={{0,24},{1,25},{2,26},{3,27},{4,28},{5,29},{6,30},{7,31},{8,16},{9,... | collective-permute-start | bytes 24584 | tf_op jit(solution)/shard_map/ppermute | solution.py:25
  38.6 1.9 %copy-start.4 = (bf16[128,1536]{1,0:T(8,128)(2,1)S(1)}, bf16[128,1536]{1,0:T(8,128)(2,1)}, u32[]{:S(2)}) copy-start(bf16[128,1536]{1,0:T(8,128)(2,1)} %param.21) | copy-start | bytes 1179652
  38.6 9.4 %slice-start.1 = ((bf16[16,768]{1,0:T(8,128)(2,1)}), bf16[16,256]{1,0:T(8,128)(2,1)S(1)}, s32[]{:S(2)}) async-start(bf16[16,768]{1,0:T(8,128)(2,1)} %copy-done.10), calls=%async_computation.1 | async-start | bytes 16384 | tf_op jit(solution)/shard_map/slice | solution.py:144
  39.7 9.5 %slice-start = ((bf16[16,640]{1,0:T(8,128)(2,1)}), bf16[16,384]{1,0:T(8,128)(2,1)S(1)}, s32[]{:S(2)}) async-start(bf16[16,640]{1,0:T(8,128)(2,1)} %copy-done.9), calls=%async_computation | async-start | bytes 24576 | tf_op jit(solution)/shard_map/slice | solution.py:147
  40.6 3.6 %collective-permute-start.12 = (bf16[16,128]{1,0:T(8,128)(2,1)S(1)}, bf16[16,128]{1,0:T(8,128)(2,1)S(1)}, u32[]{:S(2)}, u32[]{:S(2)}) collective-permute-start(bf16[16,128]{1,0:T(8,128)(2,1)S(1)} %convolution_convert_fusion.5), channel_id=1, source_target_pairs={{0,1},{1,0},{2,3},{3,2},{4,5},{5,4},{6,7},{7,6},{8,9},{9,8},{10,11... | collective-permute-start | bytes 12296 | tf_op jit(solution)/shard_map/ppermute | solution.py:25
  44.3 3.7 %collective-permute-start.13 = (bf16[16,256]{1,0:T(8,128)(2,1)S(1)}, bf16[16,256]{1,0:T(8,128)(2,1)S(1)}, u32[]{:S(2)}, u32[]{:S(2)}) collective-permute-start(bf16[16,256]{1,0:T(8,128)(2,1)S(1)} %pad_maximum_fusion.5), channel_id=1, source_target_pairs={{0,2},{1,3},{2,0},{3,1},{4,6},{5,7},{6,4},{7,5},{8,10},{9,11},{10,... | collective-permute-start | bytes 24584 | tf_op jit(solution)/shard_map/ppermute | solution.py:25
  46.0 3.7 %copy-start.7 = (f32[16,256,16]{1,2,0:T(8,128)S(1)}, f32[16,256,16]{1,2,0:T(8,128)}, u32[]{:S(2)}) copy-start(f32[16,256,16]{1,2,0:T(8,128)} %fusion.9) | copy-start | bytes 786436
  46.0 3.7 %copy-start.13 = (bf16[1024,256]{1,0:T(8,128)(2,1)S(1)}, bf16[1024,256]{1,0:T(8,128)(2,1)}, u32[]{:S(2)}) copy-start(bf16[1024,256]{1,0:T(8,128)(2,1)} %param.15) | copy-start | bytes 1572868

commit v13 on v9

--- a/solution.py
+++ b/solution.py
@@ -116,10 +116,10 @@
     roots_near, roots_pair = swap(roots, near), swap(roots, pair)
     second_sum = partner_sum(second_sum, far | pair)
 
-    second_sum = partner_sum(second_sum, 1 | pair)
+    second_sum = partner_sum(second_sum, near | pair)
     low = joined_pair(roots, roots_near, place & near != 0, 1)
     high = swap(roots_near, pair)
-    second_sum = partner_sum(second_sum, near | pair)
+    second_sum = partner_sum(second_sum, 1 | pair)
     second_sum, high = lax.optimization_barrier((second_sum, high))
     high = joined_pair(roots_pair, high, place & near != 0, 1)
     second_sum = partner_sum(second_sum, pair)

time: 46.5 us -> 46 us (0.989)
  waiting for transfers between devices: 19.1 us -> 17.9 us
  starting transfers between devices: 18.3 us -> 19 us
    ppermute x14, waiting for transfers between devices: 19.1 us -> 17.9 us  [swap(): return lax.ppermute(value, AXES, [(i, i ^ mask) for i in range(count)])]
    ppermute x14, starting transfers between devices: 18.3 us -> 19 us  [swap(): return lax.ppermute(value, AXES, [(i, i ^ mask) for i in range(count)])]
where the time goes in v13:
time: 46 us; the launch traced here: 45.8 us
  starting transfers between devices  19 us (41%)
  waiting for transfers between devices  17.9 us (39%)
  matrix products  8.02 us (17%)
  other arithmetic  0.49 us (1%)
    ppermute x14, starting transfers between devices, swap(): return lax.ppermute(value, AXES, [(i, i ^ mask) for i in range(count)])  19 us
    ppermute x14, waiting for transfers between devices, swap(): return lax.ppermute(value, AXES, [(i, i ^ mask) for i in range(count)])  17.9 us
    dot_general x5, matrix products, contract(): lax.dot_general(left, right, (((1,), (1,)), ((), ())), preferred_element_...  3.88 us
    dot_general x4, matrix products, product(): return jnp.dot(left, right, preferred_element_type=jnp.float32)  1.6 us
    dot_general x1, matrix products, per_device(): jnp.einsum('rlq,leq->rle', source, leaf_flux.reshape(leaves, edge_count,...  1.44 us
    dot_general x1, matrix products, per_device(): jnp.einsum('rlq,lqp->rlp', source, leaf_particular.reshape(leaves, points...  1.09 us
  transfers between devices with their start and end apart: 14, of which 10 were waited for; matrix products, arithmetic and copies ran while one was open for 4% of the time, Pallas kernels for 0%

profile of v13, /device:TPU:0, one launch (start us, length us, event | category | flops | bytes accessed | tf_op | source)
XLA Modules:
  0.0 45.8 jit_solution(4182541621266773624)
XLA Ops:
  0.0 0.0 copy-start
  0.0 0.0 copy-start.5
  0.0 0.0 copy-start.7
  0.0 0.0 copy-start.8
  0.0 1.4 %fusion = bf16[16,16,64]{2,0,1:T(8,128)(2,1)S(1)} fusion(bf16[16,64,256]{2,1,0:T(8,128)(2,1)} %bitcast.46, bf16[16,16,256]{2,1,0:T(8,128)(2,1)} %param.12), kind=kOutput, calls=%fused_computation.2 | convolution fusion | flops 8404992 | bytes 688128 | tf_op jit(solution)/shard_map/rlq,leq->rle/dot_general | solution.py:94
  1.5 0.0 copy-start.3
  1.5 0.1 reshape.150
  1.6 1.8 %convolution_convert_fusion.3 = bf16[16,640]{1,0:T(8,128)(2,1)S(1)} fusion(bf16[16,1024]{1,0:T(8,128)(2,1)S(1)} %reshape.150, bf16[640,1024]{1,0:T(8,128)(2,1)} %param.16), kind=kOutput, calls=%fused_computation.5 | convolution fusion | flops 20981760 | bytes 1363968 | tf_op jit(solution)/shard_map/dot_general | solution.py:10
  3.4 0.0 copy-done.5
  3.4 0.2 fusion.39
  3.6 3.0 %collective-permute-start = (bf16[16,768]{1,0:T(8,128)(2,1)S(1)}, bf16[16,768]{1,0:T(8,128)(2,1)S(1)}, u32[]{:S(2)}, u32[]{:S(2)}) collective-permute-start(bf16[16,768]{1,0:T(8,128)(2,1)S(1)} %get-tuple-element.23), channel_id=1, source_target_pairs={{0,1},{1,0},{2,3},{3,2},{4,5},{5,4},{6,7},{7,6},{8,9},{9,8},{10,11... | collective-permute-start | bytes 73736 | tf_op jit(solution)/shard_map/ppermute | solution.py:25
  6.6 0.0 copy-done.7
  6.6 1.8 %collective-permute-done = bf16[16,768]{1,0:T(8,128)(2,1)S(1)} collective-permute-done((bf16[16,768]{1,0:T(8,128)(2,1)S(1)}, bf16[16,768]{1,0:T(8,128)(2,1)S(1)}, u32[]{:S(2)}, u32[]{:S(2)}) %collective-permute-start) | collective-permute-done | bytes 24608 | tf_op jit(solution)/shard_map/ppermute | solution.py:25
  8.4 2.1 %collective-permute-start.1 = (bf16[16,768]{1,0:T(8,128)(2,1)S(1)}, bf16[16,768]{1,0:T(8,128)(2,1)S(1)}, u32[]{:S(2)}, u32[]{:S(2)}) collective-permute-start(bf16[16,768]{1,0:T(8,128)(2,1)S(1)} %fusion.17), channel_id=1, source_target_pairs={{0,2},{1,3},{2,0},{3,1},{4,6},{5,7},{6,4},{7,5},{8,10},{9,11},{10,... | collective-permute-start | bytes 73736 | tf_op jit(solution)/shard_map/ppermute | solution.py:25
  10.5 0.0 copy-done.8
  10.6 2.6 %collective-permute-start.5 = (bf16[64,512]{1,0:T(8,128)(2,1)S(1)}, bf16[64,512]{1,0:T(8,128)(2,1)S(1)}, u32[]{:S(2)}, u32[]{:S(2)}) collective-permute-start(bf16[64,512]{1,0:T(8,128)(2,1)S(1)} %constant_dynamic-update-slice_fusion), channel_id=1, source_target_pairs={{0,4},{1,5},{2,6},{3,7},{4,0},{5,1},{6,2},{7,3},{8,12},{9,13},{10,... | collective-permute-start | bytes 196616 | tf_op jit(solution)/shard_map/ppermute | solution.py:25
  13.1 0.0 collective-permute-done.1
  13.2 0.0 copy-done.3
  13.2 0.2 fusion.40
  13.3 0.1 collective-permute-start.2
  13.4 2.8 %collective-permute-done.5 = bf16[64,512]{1,0:T(8,128)(2,1)S(1)} collective-permute-done((bf16[64,512]{1,0:T(8,128)(2,1)S(1)}, bf16[64,512]{1,0:T(8,128)(2,1)S(1)}, u32[]{:S(2)}, u32[]{:S(2)}) %collective-permute-start.5) | collective-permute-done | bytes 65568 | tf_op jit(solution)/shard_map/ppermute | solution.py:25
  16.3 1.7 %collective-permute-start.6 = (bf16[2,64,512]{2,1,0:T(8,128)(2,1)S(1)}, bf16[2,64,512]{2,1,0:T(8,128)(2,1)S(1)}, u32[]{:S(2)}, u32[]{:S(2)}) collective-permute-start(bf16[2,64,512]{2,1,0:T(8,128)(2,1)S(1)} %pad_maximum_fusion.4), channel_id=1, source_target_pairs={{0,1},{1,0},{2,3},{3,2},{4,5},{5,4},{6,7},{7,6},{8,9},{9,8},{10,11... | collective-permute-start | bytes 393224 | tf_op jit(solution)/shard_map/ppermute | solution.py:25
  17.9 0.3 collective-permute-done.2
  18.3 1.3 %collective-permute-start.3 = (bf16[16,1536]{1,0:T(8,128)(2,1)S(1)}, bf16[16,1536]{1,0:T(8,128)(2,1)S(1)}, u32[]{:S(2)}, u32[]{:S(2)}) collective-permute-start(bf16[16,1536]{1,0:T(8,128)(2,1)S(1)} %fusion.12), channel_id=1, source_target_pairs={{0,10},{1,11},{2,8},{3,9},{4,14},{5,15},{6,12},{7,13},{8,2},{9,3},... | collective-permute-start | bytes 147464 | tf_op jit(solution)/shard_map/ppermute | solution.py:25
  19.6 1.7 %collective-permute-done.6 = bf16[2,64,512]{2,1,0:T(8,128)(2,1)S(1)} collective-permute-done((bf16[2,64,512]{2,1,0:T(8,128)(2,1)S(1)}, bf16[2,64,512]{2,1,0:T(8,128)(2,1)S(1)}, u32[]{:S(2)}, u32[]{:S(2)}) %collective-permute-start.6) | collective-permute-done | bytes 131104 | tf_op jit(solution)/shard_map/ppermute | solution.py:25
  21.4 1.2 %collective-permute-start.7 = (bf16[2,2,64,512]{3,2,1,0:T(8,128)(2,1)S(1)}, bf16[2,2,64,512]{3,2,1,0:T(8,128)(2,1)S(1)}, u32[]{:S(2)}, u32[]{:S(2)}) collective-permute-start(bf16[2,2,64,512]{3,2,1,0:T(8,128)(2,1)S(1)} %pad_maximum_fusion.3), channel_id=1, source_target_pairs={{0,2},{1,3},{2,0},{3,1},{4,6},{5,7},{6,4},{7,5},{8,10},{9,11},{10,... | collective-permute-start | bytes 786440 | tf_op jit(solution)/shard_map/ppermute | solution.py:25
  22.5 0.0 collective-permute-done.3
  22.6 1.2 %collective-permute-start.4 = (bf16[16,1536]{1,0:T(8,128)(2,1)S(1)}, bf16[16,1536]{1,0:T(8,128)(2,1)S(1)}, u32[]{:S(2)}, u32[]{:S(2)}) collective-permute-start(bf16[16,1536]{1,0:T(8,128)(2,1)S(1)} %fusion.16), channel_id=1, source_target_pairs={{0,9},{1,8},{2,11},{3,10},{4,13},{5,12},{6,15},{7,14},{8,1},{9,0},... | collective-permute-start | bytes 147464 | tf_op jit(solution)/shard_map/ppermute | solution.py:25
  23.8 0.7 %collective-permute-start.10 = (bf16[2,2,64,512]{3,2,1,0:T(8,128)(2,1)S(1)}, bf16[2,2,64,512]{3,2,1,0:T(8,128)(2,1)S(1)}, u32[]{:S(2)}, u32[]{:S(2)}) collective-permute-start(bf16[2,2,64,512]{3,2,1,0:T(8,128)(2,1)S(1)} %pad_maximum_fusion.3), channel_id=1, source_target_pairs={{0,8},{1,9},{2,10},{3,11},{4,12},{5,13},{6,14},{7,15},{8,0},{9,1},... | collective-permute-start | bytes 786440 | tf_op jit(solution)/shard_map/ppermute | solution.py:25
  24.4 4.7 %collective-permute-done.7 = bf16[2,2,64,512]{3,2,1,0:T(8,128)(2,1)S(1)} collective-permute-done((bf16[2,2,64,512]{3,2,1,0:T(8,128)(2,1)S(1)}, bf16[2,2,64,512]{3,2,1,0:T(8,128)(2,1)S(1)}, u32[]{:S(2)}, u32[]{:S(2)}) %collective-permute-start.7) | collective-permute-done | bytes 262176 | tf_op jit(solution)/shard_map/ppermute | solution.py:25
  29.1 0.0 collective-permute-start.8
  29.1 0.0 collective-permute-done.4
  29.2 1.5 %collective-permute-done.8 = bf16[2,2,64,512]{3,2,1,0:T(8,128)(2,1)S(1)} collective-permute-done((bf16[2,2,64,512]{3,2,1,0:T(8,128)(2,1)S(1)}, bf16[2,2,64,512]{3,2,1,0:T(8,128)(2,1)S(1)}, u32[]{:S(2)}, u32[]{:S(2)}) %collective-permute-start.8) | collective-permute-done | bytes 262176 | tf_op jit(solution)/shard_map/ppermute | solution.py:25
  30.7 0.2 collective-permute-start.9
  30.8 0.0 collective-permute-done.10
  30.9 0.1 broadcast_select_fusion.1
  31.0 0.0 copy-start.2
  31.0 0.1 pad_maximum_fusion
  31.1 0.9 %collective-permute-done.9 = bf16[16,1536]{1,0:T(8,128)(2,1)S(1)} collective-permute-done((bf16[16,1536]{1,0:T(8,128)(2,1)S(1)}, bf16[16,1536]{1,0:T(8,128)(2,1)S(1)}, u32[]{:S(2)}, u32[]{:S(2)}) %collective-permute-start.9) | collective-permute-done | bytes 49184 | tf_op jit(solution)/shard_map/ppermute | solution.py:25
  32.0 0.2 fusion.41
  32.2 1.4 %collective-permute-start.11 = (bf16[16,256]{1,0:T(8,128)(2,1)S(1)}, bf16[16,256]{1,0:T(8,128)(2,1)S(1)}, u32[]{:S(2)}, u32[]{:S(2)}) collective-permute-start(bf16[16,256]{1,0:T(8,128)(2,1)S(1)} %get-tuple-element.27), channel_id=1, source_target_pairs={{0,24},{1,25},{2,26},{3,27},{4,28},{5,29},{6,30},{7,31},{8,16},{9,... | collective-permute-start | bytes 24584 | tf_op jit(solution)/shard_map/ppermute | solution.py:25
  33.6 0.0 copy-done
  33.6 0.0 copy-done.2
  33.6 0.0 copy-start.4
  33.6 1.1 %fusion.9 = f32[16,256,16]{1,2,0:T(8,128)} fusion(bf16[16,256,256]{2,1,0:T(8,128)(2,1)S(1)} %bitcast.43, bf16[16,16,256]{2,1,0:T(8,128)(2,1)S(1)} %copy-done.2), kind=kOutput, calls=%fused_computation.29 | convolution fusion | flops 33554432 | bytes 2490368 | tf_op jit(solution)/shard_map/rlq,lqp->rlp/dot_general | solution.py:147
  34.7 0.0 copy-start.1
  34.7 0.5 %collective-permute-done.11 = bf16[16,256]{1,0:T(8,128)(2,1)S(1)} collective-permute-done((bf16[16,256]{1,0:T(8,128)(2,1)S(1)}, bf16[16,256]{1,0:T(8,128)(2,1)S(1)}, u32[]{:S(2)}, u32[]{:S(2)}) %collective-permute-start.11) | collective-permute-done | bytes 8224 | tf_op jit(solution)/shard_map/ppermute | solution.py:25
  35.2 0.2 convolution_convert_fusion.2
  35.5 0.0 copy-done.4
  35.5 0.2 convolution_convert_fusion.5
  35.7 1.7 %collective-permute-start.12 = (bf16[16,128]{1,0:T(8,128)(2,1)S(1)}, bf16[16,128]{1,0:T(8,128)(2,1)S(1)}, u32[]{:S(2)}, u32[]{:S(2)}) collective-permute-start(bf16[16,128]{1,0:T(8,128)(2,1)S(1)} %convolution_convert_fusion.5), channel_id=1, source_target_pairs={{0,1},{1,0},{2,3},{3,2},{4,5},{5,4},{6,7},{7,6},{8,9},{9,8},{10,11... | collective-permute-start | bytes 12296 | tf_op jit(solution)/shard_map/ppermute | solution.py:25
  37.4 1.9 %collective-permute-done.12 = bf16[16,128]{1,0:T(8,128)(2,1)S(1)} collective-permute-done((bf16[16,128]{1,0:T(8,128)(2,1)S(1)}, bf16[16,128]{1,0:T(8,128)(2,1)S(1)}, u32[]{:S(2)}, u32[]{:S(2)}) %collective-permute-start.12) | collective-permute-done | bytes 4128 | tf_op jit(solution)/shard_map/ppermute | solution.py:25
  39.3 1.8 %collective-permute-start.13 = (bf16[16,256]{1,0:T(8,128)(2,1)S(1)}, bf16[16,256]{1,0:T(8,128)(2,1)S(1)}, u32[]{:S(2)}, u32[]{:S(2)}) collective-permute-start(bf16[16,256]{1,0:T(8,128)(2,1)S(1)} %pad_maximum_fusion.5), channel_id=1, source_target_pairs={{0,2},{1,3},{2,0},{3,1},{4,6},{5,7},{6,4},{7,5},{8,10},{9,11},{10,... | collective-permute-start | bytes 24584 | tf_op jit(solution)/shard_map/ppermute | solution.py:25
  41.2 0.0 copy-start.6
  41.2 0.0 copy-start.9
  41.2 1.8 %collective-permute-done.13 = bf16[16,256]{1,0:T(8,128)(2,1)S(1)} collective-permute-done((bf16[16,256]{1,0:T(8,128)(2,1)S(1)}, bf16[16,256]{1,0:T(8,128)(2,1)S(1)}, u32[]{:S(2)}, u32[]{:S(2)}) %collective-permute-start.13) | collective-permute-done | bytes 8224 | tf_op jit(solution)/shard_map/ppermute | solution.py:25
  43.1 1.2 %convolution_convert_fusion.4 = bf16[16,256]{1,0:T(8,128)(2,1)S(1)} fusion(bf16[256,768]{1,0:T(8,128)(2,1)} %param.19, bf16[16,256]{1,0:T(8,128)(2,1)S(1)} %get-tuple-element.20, bf16[16,256]{1,0:T(8,128)(2,1)S(1)} %get-tuple-element.19, bf16[16,256]{1,0:T(8,128)(2,1)S(1)} %slice.30), kind=kOutput, calls=%fused_computation.6 | convolution fusion | flops 6369280 | bytes 425984 | tf_op jit(solution)/shard_map/dot_general | solution.py:10
  44.2 0.0 copy-done.1
  44.2 0.5 %convolution_convert_fusion.1 = bf16[16,1024]{1,0:T(8,128)(2,1)S(1)} fusion(bf16[1024,640]{1,0:T(8,128)(2,1)S(1)} %copy-done.1, bf16[16,256]{1,0:T(8,128)(2,1)S(1)} %convolution_convert_fusion.4, bf16[16,384]{1,0:T(8,128)(2,1)S(1)} %slice.28), kind=kOutput, calls=%fused_computation.3 | convolution fusion | flops 21028864 | bytes 1363968 | tf_op jit(solution)/shard_map/dot_general | solution.py:10
  44.8 0.0 copy-done.6
  44.8 0.0 copy-done.9
  44.8 1.1 %convolution_add_fusion = f32[16,16,256]{2,1,0:T(8,128)} fusion(bf16[1024,256]{1,0:T(8,128)(2,1)S(1)} %copy-done.9, pred[16,1024]{1,0:T(8,128)(4,1)S(1)} %iota_compare_fusion, f32[16,256,16]{1,2,0:T(8,128)S(1)} %copy-done.6, bf16[16,1024]{1,0:T(8,128)(2,1)S(1)} %convolution_convert_fusion.1), kind=kOutput, calls=%fused_computation | convolution fusion | flops 134545408 | bytes 1097728 | tf_op jit(solution)/shard_map/dot_general | solution.py:16
  (24 shorter events, 0.3 us)
Async XLA Ops:
  0.0 33.6 %copy-start = (bf16[4096,256]{1,0:T(8,128)(2,1)S(1)}, bf16[4096,256]{1,0:T(8,128)(2,1)}, u32[]{:S(2)}) copy-start(bf16[4096,256]{1,0:T(8,128)(2,1)} %param.14) | copy-start | bytes 6291460
  0.0 3.4 %copy-start.5 = (bf16[256,768]{1,0:T(8,128)(2,1)S(1)}, bf16[256,768]{1,0:T(8,128)(2,1)}, u32[]{:S(2)}) copy-start(bf16[256,768]{1,0:T(8,128)(2,1)} %param.18) | copy-start | bytes 1179652
  0.0 6.6 %copy-start.7 = (bf16[64,256]{1,0:T(8,128)(2,1)S(1)}, bf16[64,256]{1,0:T(8,128)(2,1)}, u32[]{:S(2)}) copy-start(bf16[64,256]{1,0:T(8,128)(2,1)} %param.22) | copy-start | bytes 98308
  0.0 10.5 %copy-start.8 = (bf16[64,256]{1,0:T(8,128)(2,1)S(1)}, bf16[64,256]{1,0:T(8,128)(2,1)}, u32[]{:S(2)}) copy-start(bf16[64,256]{1,0:T(8,128)(2,1)} %param.23) | copy-start | bytes 98308
  1.5 11.7 %copy-start.3 = (bf16[128,1536]{1,0:T(8,128)(2,1)S(1)}, bf16[128,1536]{1,0:T(8,128)(2,1)}, u32[]{:S(2)}) copy-start(bf16[128,1536]{1,0:T(8,128)(2,1)} %param.20) | copy-start | bytes 1179652
  3.6 4.8 %collective-permute-start = (bf16[16,768]{1,0:T(8,128)(2,1)S(1)}, bf16[16,768]{1,0:T(8,128)(2,1)S(1)}, u32[]{:S(2)}, u32[]{:S(2)}) collective-permute-start(bf16[16,768]{1,0:T(8,128)(2,1)S(1)} %get-tuple-element.23), channel_id=1, source_target_pairs={{0,1},{1,0},{2,3},{3,2},{4,5},{5,4},{6,7},{7,6},{8,9},{9,8},{10,11... | collective-permute-start | bytes 73736 | tf_op jit(solution)/shard_map/ppermute | solution.py:25
  8.4 4.7 %collective-permute-start.1 = (bf16[16,768]{1,0:T(8,128)(2,1)S(1)}, bf16[16,768]{1,0:T(8,128)(2,1)S(1)}, u32[]{:S(2)}, u32[]{:S(2)}) collective-permute-start(bf16[16,768]{1,0:T(8,128)(2,1)S(1)} %fusion.17), channel_id=1, source_target_pairs={{0,2},{1,3},{2,0},{3,1},{4,6},{5,7},{6,4},{7,5},{8,10},{9,11},{10,... | collective-permute-start | bytes 73736 | tf_op jit(solution)/shard_map/ppermute | solution.py:25
  10.6 5.7 %collective-permute-start.5 = (bf16[64,512]{1,0:T(8,128)(2,1)S(1)}, bf16[64,512]{1,0:T(8,128)(2,1)S(1)}, u32[]{:S(2)}, u32[]{:S(2)}) collective-permute-start(bf16[64,512]{1,0:T(8,128)(2,1)S(1)} %constant_dynamic-update-slice_fusion), channel_id=1, source_target_pairs={{0,4},{1,5},{2,6},{3,7},{4,0},{5,1},{6,2},{7,3},{8,12},{9,13},{10,... | collective-permute-start | bytes 196616 | tf_op jit(solution)/shard_map/ppermute | solution.py:25
  13.3 4.9 %collective-permute-start.2 = (bf16[16,1536]{1,0:T(8,128)(2,1)S(1)}, bf16[16,1536]{1,0:T(8,128)(2,1)S(1)}, u32[]{:S(2)}, u32[]{:S(2)}) collective-permute-start(bf16[16,1536]{1,0:T(8,128)(2,1)S(1)} %get-tuple-element.25), channel_id=1, source_target_pairs={{0,12},{1,13},{2,14},{3,15},{4,8},{5,9},{6,10},{7,11},{8,4},{9,5},... | collective-permute-start | bytes 147464 | tf_op jit(solution)/shard_map/ppermute | solution.py:25
  16.3 5.0 %collective-permute-start.6 = (bf16[2,64,512]{2,1,0:T(8,128)(2,1)S(1)}, bf16[2,64,512]{2,1,0:T(8,128)(2,1)S(1)}, u32[]{:S(2)}, u32[]{:S(2)}) collective-permute-start(bf16[2,64,512]{2,1,0:T(8,128)(2,1)S(1)} %pad_maximum_fusion.4), channel_id=1, source_target_pairs={{0,1},{1,0},{2,3},{3,2},{4,5},{5,4},{6,7},{7,6},{8,9},{9,8},{10,11... | collective-permute-start | bytes 393224 | tf_op jit(solution)/shard_map/ppermute | solution.py:25
  18.3 4.3 %collective-permute-start.3 = (bf16[16,1536]{1,0:T(8,128)(2,1)S(1)}, bf16[16,1536]{1,0:T(8,128)(2,1)S(1)}, u32[]{:S(2)}, u32[]{:S(2)}) collective-permute-start(bf16[16,1536]{1,0:T(8,128)(2,1)S(1)} %fusion.12), channel_id=1, source_target_pairs={{0,10},{1,11},{2,8},{3,9},{4,14},{5,15},{6,12},{7,13},{8,2},{9,3},... | collective-permute-start | bytes 147464 | tf_op jit(solution)/shard_map/ppermute | solution.py:25
  21.4 7.8 %collective-permute-start.7 = (bf16[2,2,64,512]{3,2,1,0:T(8,128)(2,1)S(1)}, bf16[2,2,64,512]{3,2,1,0:T(8,128)(2,1)S(1)}, u32[]{:S(2)}, u32[]{:S(2)}) collective-permute-start(bf16[2,2,64,512]{3,2,1,0:T(8,128)(2,1)S(1)} %pad_maximum_fusion.3), channel_id=1, source_target_pairs={{0,2},{1,3},{2,0},{3,1},{4,6},{5,7},{6,4},{7,5},{8,10},{9,11},{10,... | collective-permute-start | bytes 786440 | tf_op jit(solution)/shard_map/ppermute | solution.py:25
  22.6 6.6 %collective-permute-start.4 = (bf16[16,1536]{1,0:T(8,128)(2,1)S(1)}, bf16[16,1536]{1,0:T(8,128)(2,1)S(1)}, u32[]{:S(2)}, u32[]{:S(2)}) collective-permute-start(bf16[16,1536]{1,0:T(8,128)(2,1)S(1)} %fusion.16), channel_id=1, source_target_pairs={{0,9},{1,8},{2,11},{3,10},{4,13},{5,12},{6,15},{7,14},{8,1},{9,0},... | collective-permute-start | bytes 147464 | tf_op jit(solution)/shard_map/ppermute | solution.py:25
  23.8 7.1 %collective-permute-start.10 = (bf16[2,2,64,512]{3,2,1,0:T(8,128)(2,1)S(1)}, bf16[2,2,64,512]{3,2,1,0:T(8,128)(2,1)S(1)}, u32[]{:S(2)}, u32[]{:S(2)}) collective-permute-start(bf16[2,2,64,512]{3,2,1,0:T(8,128)(2,1)S(1)} %pad_maximum_fusion.3), channel_id=1, source_target_pairs={{0,8},{1,9},{2,10},{3,11},{4,12},{5,13},{6,14},{7,15},{8,0},{9,1},... | collective-permute-start | bytes 786440 | tf_op jit(solution)/shard_map/ppermute | solution.py:25
  29.1 1.5 %collective-permute-start.8 = (bf16[2,2,64,512]{3,2,1,0:T(8,128)(2,1)S(1)}, bf16[2,2,64,512]{3,2,1,0:T(8,128)(2,1)S(1)}, u32[]{:S(2)}, u32[]{:S(2)}) collective-permute-start(bf16[2,2,64,512]{3,2,1,0:T(8,128)(2,1)S(1)} %collective-permute-done.7), channel_id=1, source_target_pairs={{0,8},{1,9},{2,10},{3,11},{4,12},{5,13},{6,14},{7,15},{8,0},{9,1},... | collective-permute-start | bytes 786440 | tf_op jit(solution)/shard_map/ppermute | solution.py:25
  30.7 1.3 %collective-permute-start.9 = (bf16[16,1536]{1,0:T(8,128)(2,1)S(1)}, bf16[16,1536]{1,0:T(8,128)(2,1)S(1)}, u32[]{:S(2)}, u32[]{:S(2)}) collective-permute-start(bf16[16,1536]{1,0:T(8,128)(2,1)S(1)} %convert_element_type.86), channel_id=1, source_target_pairs={{0,8},{1,9},{2,10},{3,11},{4,12},{5,13},{6,14},{7,15},{8,0},{9,1},... | collective-permute-start | bytes 147464 | tf_op jit(solution)/shard_map/ppermute | solution.py:25
  31.0 2.6 %copy-start.2 = (bf16[16,16,256]{2,1,0:T(8,128)(2,1)S(1)}, bf16[16,16,256]{2,1,0:T(8,128)(2,1)}, u32[]{:S(2)}) copy-start(bf16[16,16,256]{2,1,0:T(8,128)(2,1)} %param.12) | copy-start | bytes 393220
  32.2 3.1 %collective-permute-start.11 = (bf16[16,256]{1,0:T(8,128)(2,1)S(1)}, bf16[16,256]{1,0:T(8,128)(2,1)S(1)}, u32[]{:S(2)}, u32[]{:S(2)}) collective-permute-start(bf16[16,256]{1,0:T(8,128)(2,1)S(1)} %get-tuple-element.27), channel_id=1, source_target_pairs={{0,24},{1,25},{2,26},{3,27},{4,28},{5,29},{6,30},{7,31},{8,16},{9,... | collective-permute-start | bytes 24584 | tf_op jit(solution)/shard_map/ppermute | solution.py:25
  33.6 1.9 %copy-start.4 = (bf16[128,1536]{1,0:T(8,128)(2,1)S(1)}, bf16[128,1536]{1,0:T(8,128)(2,1)}, u32[]{:S(2)}) copy-start(bf16[128,1536]{1,0:T(8,128)(2,1)} %param.21) | copy-start | bytes 1179652
  34.7 9.5 %copy-start.1 = (bf16[1024,640]{1,0:T(8,128)(2,1)S(1)}, bf16[1024,640]{1,0:T(8,128)(2,1)}, u32[]{:S(2)}) copy-start(bf16[1024,640]{1,0:T(8,128)(2,1)} %param.17) | copy-start | bytes 3932164
  35.7 3.6 %collective-permute-start.12 = (bf16[16,128]{1,0:T(8,128)(2,1)S(1)}, bf16[16,128]{1,0:T(8,128)(2,1)S(1)}, u32[]{:S(2)}, u32[]{:S(2)}) collective-permute-start(bf16[16,128]{1,0:T(8,128)(2,1)S(1)} %convolution_convert_fusion.5), channel_id=1, source_target_pairs={{0,1},{1,0},{2,3},{3,2},{4,5},{5,4},{6,7},{7,6},{8,9},{9,8},{10,11... | collective-permute-start | bytes 12296 | tf_op jit(solution)/shard_map/ppermute | solution.py:25
  39.3 3.7 %collective-permute-start.13 = (bf16[16,256]{1,0:T(8,128)(2,1)S(1)}, bf16[16,256]{1,0:T(8,128)(2,1)S(1)}, u32[]{:S(2)}, u32[]{:S(2)}) collective-permute-start(bf16[16,256]{1,0:T(8,128)(2,1)S(1)} %pad_maximum_fusion.5), channel_id=1, source_target_pairs={{0,2},{1,3},{2,0},{3,1},{4,6},{5,7},{6,4},{7,5},{8,10},{9,11},{10,... | collective-permute-start | bytes 24584 | tf_op jit(solution)/shard_map/ppermute | solution.py:25
  41.2 3.6 %copy-start.6 = (f32[16,256,16]{1,2,0:T(8,128)S(1)}, f32[16,256,16]{1,2,0:T(8,128)}, u32[]{:S(2)}) copy-start(f32[16,256,16]{1,2,0:T(8,128)} %fusion.9) | copy-start | bytes 786436
  41.2 3.6 %copy-start.9 = (bf16[1024,256]{1,0:T(8,128)(2,1)S(1)}, bf16[1024,256]{1,0:T(8,128)(2,1)}, u32[]{:S(2)}) copy-start(bf16[1024,256]{1,0:T(8,128)(2,1)} %param.15) | copy-start | bytes 1572868

commit v14 on v13

--- a/solution.py
+++ b/solution.py
@@ -114,9 +114,9 @@
     second_sum = product(piece, up_two)
     roots = joined_pair(roots, roots_one, place & 1 != 0, 1)
     roots_near, roots_pair = swap(roots, near), swap(roots, pair)
+    second_sum = partner_sum(second_sum, near | pair)
+
     second_sum = partner_sum(second_sum, far | pair)
-
-    second_sum = partner_sum(second_sum, near | pair)
     low = joined_pair(roots, roots_near, place & near != 0, 1)
     high = swap(roots_near, pair)
     second_sum = partner_sum(second_sum, 1 | pair)

time: 46 us -> 46.2 us (level)
  waiting for transfers between devices: 17.9 us -> 22.5 us
  starting transfers between devices: 19 us -> 14.6 us
    ppermute x14, waiting for transfers between devices: 17.9 us -> 22.5 us  [swap(): return lax.ppermute(value, AXES, [(i, i ^ mask) for i in range(count)])]
    ppermute x14, starting transfers between devices: 19 us -> 14.6 us  [swap(): return lax.ppermute(value, AXES, [(i, i ^ mask) for i in range(count)])]
where the time goes in v14:
time: 46.2 us; the launch traced here: 46 us
  waiting for transfers between devices  22.5 us (49%)
  starting transfers between devices  14.6 us (32%)
  matrix products  8.02 us (17%)
  other arithmetic  0.49 us (1%)
    ppermute x14, waiting for transfers between devices, swap(): return lax.ppermute(value, AXES, [(i, i ^ mask) for i in range(count)])  22.5 us
    ppermute x14, starting transfers between devices, swap(): return lax.ppermute(value, AXES, [(i, i ^ mask) for i in range(count)])  14.6 us
    dot_general x5, matrix products, contract(): lax.dot_general(left, right, (((1,), (1,)), ((), ())), preferred_element_...  3.88 us
    dot_general x4, matrix products, product(): return jnp.dot(left, right, preferred_element_type=jnp.float32)  1.6 us
    dot_general x1, matrix products, per_device(): jnp.einsum('rlq,leq->rle', source, leaf_flux.reshape(leaves, edge_count,...  1.44 us
    dot_general x1, matrix products, per_device(): jnp.einsum('rlq,lqp->rlp', source, leaf_particular.reshape(leaves, points...  1.09 us
  transfers between devices with their start and end apart: 14, of which 10 were waited for; matrix products, arithmetic and copies ran while one was open for 4% of the time, Pallas kernels for 0%

profile of v14, /device:TPU:0, one launch (start us, length us, event | category | flops | bytes accessed | tf_op | source)
XLA Modules:
  0.0 46.0 jit_solution(17328183815307745788)
XLA Ops:
  0.0 0.0 copy-start
  0.0 0.0 copy-start.5
  0.0 0.0 copy-start.7
  0.0 0.0 copy-start.8
  0.0 1.4 %fusion = bf16[16,16,64]{2,0,1:T(8,128)(2,1)S(1)} fusion(bf16[16,64,256]{2,1,0:T(8,128)(2,1)} %bitcast.46, bf16[16,16,256]{2,1,0:T(8,128)(2,1)} %param.12), kind=kOutput, calls=%fused_computation.2 | convolution fusion | flops 8404992 | bytes 688128 | tf_op jit(solution)/shard_map/rlq,leq->rle/dot_general | solution.py:94
  1.5 0.0 copy-start.3
  1.5 0.1 reshape.150
  1.6 1.8 %convolution_convert_fusion.3 = bf16[16,640]{1,0:T(8,128)(2,1)S(1)} fusion(bf16[16,1024]{1,0:T(8,128)(2,1)S(1)} %reshape.150, bf16[640,1024]{1,0:T(8,128)(2,1)} %param.16), kind=kOutput, calls=%fused_computation.5 | convolution fusion | flops 20981760 | bytes 1363968 | tf_op jit(solution)/shard_map/dot_general | solution.py:10
  3.4 0.0 copy-done.5
  3.4 0.2 fusion.39
  3.6 3.0 %collective-permute-start = (bf16[16,768]{1,0:T(8,128)(2,1)S(1)}, bf16[16,768]{1,0:T(8,128)(2,1)S(1)}, u32[]{:S(2)}, u32[]{:S(2)}) collective-permute-start(bf16[16,768]{1,0:T(8,128)(2,1)S(1)} %get-tuple-element.23), channel_id=1, source_target_pairs={{0,1},{1,0},{2,3},{3,2},{4,5},{5,4},{6,7},{7,6},{8,9},{9,8},{10,11... | collective-permute-start | bytes 73736 | tf_op jit(solution)/shard_map/ppermute | solution.py:25
  6.6 0.0 copy-done.7
  6.6 1.8 %collective-permute-done = bf16[16,768]{1,0:T(8,128)(2,1)S(1)} collective-permute-done((bf16[16,768]{1,0:T(8,128)(2,1)S(1)}, bf16[16,768]{1,0:T(8,128)(2,1)S(1)}, u32[]{:S(2)}, u32[]{:S(2)}) %collective-permute-start) | collective-permute-done | bytes 24608 | tf_op jit(solution)/shard_map/ppermute | solution.py:25
  8.4 2.1 %collective-permute-start.1 = (bf16[16,768]{1,0:T(8,128)(2,1)S(1)}, bf16[16,768]{1,0:T(8,128)(2,1)S(1)}, u32[]{:S(2)}, u32[]{:S(2)}) collective-permute-start(bf16[16,768]{1,0:T(8,128)(2,1)S(1)} %fusion.17), channel_id=1, source_target_pairs={{0,2},{1,3},{2,0},{3,1},{4,6},{5,7},{6,4},{7,5},{8,10},{9,11},{10,... | collective-permute-start | bytes 73736 | tf_op jit(solution)/shard_map/ppermute | solution.py:25
  10.5 0.0 copy-done.8
  10.6 2.6 %collective-permute-start.5 = (bf16[64,512]{1,0:T(8,128)(2,1)S(1)}, bf16[64,512]{1,0:T(8,128)(2,1)S(1)}, u32[]{:S(2)}, u32[]{:S(2)}) collective-permute-start(bf16[64,512]{1,0:T(8,128)(2,1)S(1)} %constant_dynamic-update-slice_fusion), channel_id=1, source_target_pairs={{0,4},{1,5},{2,6},{3,7},{4,0},{5,1},{6,2},{7,3},{8,12},{9,13},{10,... | collective-permute-start | bytes 196616 | tf_op jit(solution)/shard_map/ppermute | solution.py:25
  13.1 0.0 collective-permute-done.1
  13.2 0.0 copy-done.3
  13.2 0.2 fusion.40
  13.3 0.1 collective-permute-start.2
  13.4 2.8 %collective-permute-done.5 = bf16[64,512]{1,0:T(8,128)(2,1)S(1)} collective-permute-done((bf16[64,512]{1,0:T(8,128)(2,1)S(1)}, bf16[64,512]{1,0:T(8,128)(2,1)S(1)}, u32[]{:S(2)}, u32[]{:S(2)}) %collective-permute-start.5) | collective-permute-done | bytes 65568 | tf_op jit(solution)/shard_map/ppermute | solution.py:25
  16.3 1.7 %collective-permute-start.6 = (bf16[2,64,512]{2,1,0:T(8,128)(2,1)S(1)}, bf16[2,64,512]{2,1,0:T(8,128)(2,1)S(1)}, u32[]{:S(2)}, u32[]{:S(2)}) collective-permute-start(bf16[2,64,512]{2,1,0:T(8,128)(2,1)S(1)} %pad_maximum_fusion.4), channel_id=1, source_target_pairs={{0,1},{1,0},{2,3},{3,2},{4,5},{5,4},{6,7},{7,6},{8,9},{9,8},{10,11... | collective-permute-start | bytes 393224 | tf_op jit(solution)/shard_map/ppermute | solution.py:25
  17.9 0.0 collective-permute-done.2
  18.0 1.4 %collective-permute-start.3 = (bf16[16,1536]{1,0:T(8,128)(2,1)S(1)}, bf16[16,1536]{1,0:T(8,128)(2,1)S(1)}, u32[]{:S(2)}, u32[]{:S(2)}) collective-permute-start(bf16[16,1536]{1,0:T(8,128)(2,1)S(1)} %fusion.12), channel_id=1, source_target_pairs={{0,12},{1,13},{2,14},{3,15},{4,8},{5,9},{6,10},{7,11},{8,4},{9,5},... | collective-permute-start | bytes 147464 | tf_op jit(solution)/shard_map/ppermute | solution.py:25
  19.3 2.0 %collective-permute-done.6 = bf16[2,64,512]{2,1,0:T(8,128)(2,1)S(1)} collective-permute-done((bf16[2,64,512]{2,1,0:T(8,128)(2,1)S(1)}, bf16[2,64,512]{2,1,0:T(8,128)(2,1)S(1)}, u32[]{:S(2)}, u32[]{:S(2)}) %collective-permute-start.6) | collective-permute-done | bytes 131104 | tf_op jit(solution)/shard_map/ppermute | solution.py:25
  21.4 0.1 collective-permute-start.7
  21.4 2.4 %collective-permute-done.3 = bf16[16,1536]{1,0:T(8,128)(2,1)S(1)} collective-permute-done((bf16[16,1536]{1,0:T(8,128)(2,1)S(1)}, bf16[16,1536]{1,0:T(8,128)(2,1)S(1)}, u32[]{:S(2)}, u32[]{:S(2)}) %collective-permute-start.3) | collective-permute-done | bytes 49184 | tf_op jit(solution)/shard_map/ppermute | solution.py:25
  23.9 0.7 %collective-permute-start.4 = (bf16[16,1536]{1,0:T(8,128)(2,1)S(1)}, bf16[16,1536]{1,0:T(8,128)(2,1)S(1)}, u32[]{:S(2)}, u32[]{:S(2)}) collective-permute-start(bf16[16,1536]{1,0:T(8,128)(2,1)S(1)} %fusion.16), channel_id=1, source_target_pairs={{0,9},{1,8},{2,11},{3,10},{4,13},{5,12},{6,15},{7,14},{8,1},{9,0},... | collective-permute-start | bytes 147464 | tf_op jit(solution)/shard_map/ppermute | solution.py:25
  24.6 0.4 collective-permute-start.10
  25.0 4.3 %collective-permute-done.7 = bf16[2,2,64,512]{3,2,1,0:T(8,128)(2,1)S(1)} collective-permute-done((bf16[2,2,64,512]{3,2,1,0:T(8,128)(2,1)S(1)}, bf16[2,2,64,512]{3,2,1,0:T(8,128)(2,1)S(1)}, u32[]{:S(2)}, u32[]{:S(2)}) %collective-permute-start.7) | collective-permute-done | bytes 262176 | tf_op jit(solution)/shard_map/ppermute | solution.py:25
  29.3 0.0 collective-permute-start.8
  29.3 0.0 collective-permute-done.4
  29.4 1.5 %collective-permute-done.8 = bf16[2,2,64,512]{3,2,1,0:T(8,128)(2,1)S(1)} collective-permute-done((bf16[2,2,64,512]{3,2,1,0:T(8,128)(2,1)S(1)}, bf16[2,2,64,512]{3,2,1,0:T(8,128)(2,1)S(1)}, u32[]{:S(2)}, u32[]{:S(2)}) %collective-permute-start.8) | collective-permute-done | bytes 262176 | tf_op jit(solution)/shard_map/ppermute | solution.py:25
  30.9 0.2 collective-permute-start.9
  31.0 0.0 collective-permute-done.10
  31.1 0.1 broadcast_select_fusion.1
  31.2 0.0 copy-start.2
  31.2 0.1 pad_maximum_fusion
  31.3 0.9 %collective-permute-done.9 = bf16[16,1536]{1,0:T(8,128)(2,1)S(1)} collective-permute-done((bf16[16,1536]{1,0:T(8,128)(2,1)S(1)}, bf16[16,1536]{1,0:T(8,128)(2,1)S(1)}, u32[]{:S(2)}, u32[]{:S(2)}) %collective-permute-start.9) | collective-permute-done | bytes 49184 | tf_op jit(solution)/shard_map/ppermute | solution.py:25
  32.2 0.2 fusion.41
  32.4 1.3 %collective-permute-start.11 = (bf16[16,256]{1,0:T(8,128)(2,1)S(1)}, bf16[16,256]{1,0:T(8,128)(2,1)S(1)}, u32[]{:S(2)}, u32[]{:S(2)}) collective-permute-start(bf16[16,256]{1,0:T(8,128)(2,1)S(1)} %get-tuple-element.27), channel_id=1, source_target_pairs={{0,24},{1,25},{2,26},{3,27},{4,28},{5,29},{6,30},{7,31},{8,16},{9,... | collective-permute-start | bytes 24584 | tf_op jit(solution)/shard_map/ppermute | solution.py:25
  33.6 0.0 copy-done
  33.6 0.0 copy-done.2
  33.6 0.0 copy-start.4
  33.6 1.1 %fusion.9 = f32[16,256,16]{1,2,0:T(8,128)} fusion(bf16[16,256,256]{2,1,0:T(8,128)(2,1)S(1)} %bitcast.43, bf16[16,16,256]{2,1,0:T(8,128)(2,1)S(1)} %copy-done.2), kind=kOutput, calls=%fused_computation.29 | convolution fusion | flops 33554432 | bytes 2490368 | tf_op jit(solution)/shard_map/rlq,lqp->rlp/dot_general | solution.py:147
  34.7 0.0 copy-start.1
  34.7 0.7 %collective-permute-done.11 = bf16[16,256]{1,0:T(8,128)(2,1)S(1)} collective-permute-done((bf16[16,256]{1,0:T(8,128)(2,1)S(1)}, bf16[16,256]{1,0:T(8,128)(2,1)S(1)}, u32[]{:S(2)}, u32[]{:S(2)}) %collective-permute-start.11) | collective-permute-done | bytes 8224 | tf_op jit(solution)/shard_map/ppermute | solution.py:25
  35.4 0.2 convolution_convert_fusion.2
  35.7 0.0 copy-done.4
  35.7 0.2 convolution_convert_fusion.5
  35.9 0.9 %collective-permute-start.12 = (bf16[16,128]{1,0:T(8,128)(2,1)S(1)}, bf16[16,128]{1,0:T(8,128)(2,1)S(1)}, u32[]{:S(2)}, u32[]{:S(2)}) collective-permute-start(bf16[16,128]{1,0:T(8,128)(2,1)S(1)} %convolution_convert_fusion.5), channel_id=1, source_target_pairs={{0,1},{1,0},{2,3},{3,2},{4,5},{5,4},{6,7},{7,6},{8,9},{9,8},{10,11... | collective-permute-start | bytes 12296 | tf_op jit(solution)/shard_map/ppermute | solution.py:25
  36.8 2.8 %collective-permute-done.12 = bf16[16,128]{1,0:T(8,128)(2,1)S(1)} collective-permute-done((bf16[16,128]{1,0:T(8,128)(2,1)S(1)}, bf16[16,128]{1,0:T(8,128)(2,1)S(1)}, u32[]{:S(2)}, u32[]{:S(2)}) %collective-permute-start.12) | collective-permute-done | bytes 4128 | tf_op jit(solution)/shard_map/ppermute | solution.py:25
  39.5 0.3 collective-permute-start.13
  39.9 0.0 copy-start.6
  39.9 0.0 copy-start.9
  39.9 3.3 %collective-permute-done.13 = bf16[16,256]{1,0:T(8,128)(2,1)S(1)} collective-permute-done((bf16[16,256]{1,0:T(8,128)(2,1)S(1)}, bf16[16,256]{1,0:T(8,128)(2,1)S(1)}, u32[]{:S(2)}, u32[]{:S(2)}) %collective-permute-start.13) | collective-permute-done | bytes 8224 | tf_op jit(solution)/shard_map/ppermute | solution.py:25
  43.3 1.2 %convolution_convert_fusion.4 = bf16[16,256]{1,0:T(8,128)(2,1)S(1)} fusion(bf16[256,768]{1,0:T(8,128)(2,1)} %param.19, bf16[16,256]{1,0:T(8,128)(2,1)S(1)} %get-tuple-element.20, bf16[16,256]{1,0:T(8,128)(2,1)S(1)} %get-tuple-element.19, bf16[16,256]{1,0:T(8,128)(2,1)S(1)} %slice.30), kind=kOutput, calls=%fused_computation.6 | convolution fusion | flops 6369280 | bytes 425984 | tf_op jit(solution)/shard_map/dot_general | solution.py:10
  44.4 0.0 copy-done.1
  44.4 0.5 %convolution_convert_fusion.1 = bf16[16,1024]{1,0:T(8,128)(2,1)S(1)} fusion(bf16[1024,640]{1,0:T(8,128)(2,1)S(1)} %copy-done.1, bf16[16,256]{1,0:T(8,128)(2,1)S(1)} %convolution_convert_fusion.4, bf16[16,384]{1,0:T(8,128)(2,1)S(1)} %slice.28), kind=kOutput, calls=%fused_computation.3 | convolution fusion | flops 21028864 | bytes 1363968 | tf_op jit(solution)/shard_map/dot_general | solution.py:10
  45.0 0.0 copy-done.6
  45.0 0.0 copy-done.9
  45.0 1.1 %convolution_add_fusion = f32[16,16,256]{2,1,0:T(8,128)} fusion(bf16[1024,256]{1,0:T(8,128)(2,1)S(1)} %copy-done.9, pred[16,1024]{1,0:T(8,128)(4,1)S(1)} %iota_compare_fusion, f32[16,256,16]{1,2,0:T(8,128)S(1)} %copy-done.6, bf16[16,1024]{1,0:T(8,128)(2,1)S(1)} %convolution_convert_fusion.1), kind=kOutput, calls=%fused_computation | convolution fusion | flops 134545408 | bytes 1097728 | tf_op jit(solution)/shard_map/dot_general | solution.py:16
  (24 shorter events, 0.3 us)
Async XLA Ops:
  0.0 33.6 %copy-start = (bf16[4096,256]{1,0:T(8,128)(2,1)S(1)}, bf16[4096,256]{1,0:T(8,128)(2,1)}, u32[]{:S(2)}) copy-start(bf16[4096,256]{1,0:T(8,128)(2,1)} %param.14) | copy-start | bytes 6291460
  0.0 3.4 %copy-start.5 = (bf16[256,768]{1,0:T(8,128)(2,1)S(1)}, bf16[256,768]{1,0:T(8,128)(2,1)}, u32[]{:S(2)}) copy-start(bf16[256,768]{1,0:T(8,128)(2,1)} %param.18) | copy-start | bytes 1179652
  0.0 6.6 %copy-start.7 = (bf16[64,256]{1,0:T(8,128)(2,1)S(1)}, bf16[64,256]{1,0:T(8,128)(2,1)}, u32[]{:S(2)}) copy-start(bf16[64,256]{1,0:T(8,128)(2,1)} %param.22) | copy-start | bytes 98308
  0.0 10.5 %copy-start.8 = (bf16[64,256]{1,0:T(8,128)(2,1)S(1)}, bf16[64,256]{1,0:T(8,128)(2,1)}, u32[]{:S(2)}) copy-start(bf16[64,256]{1,0:T(8,128)(2,1)} %param.23) | copy-start | bytes 98308
  1.5 11.7 %copy-start.3 = (bf16[128,1536]{1,0:T(8,128)(2,1)S(1)}, bf16[128,1536]{1,0:T(8,128)(2,1)}, u32[]{:S(2)}) copy-start(bf16[128,1536]{1,0:T(8,128)(2,1)} %param.20) | copy-start | bytes 1179652
  3.6 4.8 %collective-permute-start = (bf16[16,768]{1,0:T(8,128)(2,1)S(1)}, bf16[16,768]{1,0:T(8,128)(2,1)S(1)}, u32[]{:S(2)}, u32[]{:S(2)}) collective-permute-start(bf16[16,768]{1,0:T(8,128)(2,1)S(1)} %get-tuple-element.23), channel_id=1, source_target_pairs={{0,1},{1,0},{2,3},{3,2},{4,5},{5,4},{6,7},{7,6},{8,9},{9,8},{10,11... | collective-permute-start | bytes 73736 | tf_op jit(solution)/shard_map/ppermute | solution.py:25
  8.4 4.7 %collective-permute-start.1 = (bf16[16,768]{1,0:T(8,128)(2,1)S(1)}, bf16[16,768]{1,0:T(8,128)(2,1)S(1)}, u32[]{:S(2)}, u32[]{:S(2)}) collective-permute-start(bf16[16,768]{1,0:T(8,128)(2,1)S(1)} %fusion.17), channel_id=1, source_target_pairs={{0,2},{1,3},{2,0},{3,1},{4,6},{5,7},{6,4},{7,5},{8,10},{9,11},{10,... | collective-permute-start | bytes 73736 | tf_op jit(solution)/shard_map/ppermute | solution.py:25
  10.6 5.7 %collective-permute-start.5 = (bf16[64,512]{1,0:T(8,128)(2,1)S(1)}, bf16[64,512]{1,0:T(8,128)(2,1)S(1)}, u32[]{:S(2)}, u32[]{:S(2)}) collective-permute-start(bf16[64,512]{1,0:T(8,128)(2,1)S(1)} %constant_dynamic-update-slice_fusion), channel_id=1, source_target_pairs={{0,4},{1,5},{2,6},{3,7},{4,0},{5,1},{6,2},{7,3},{8,12},{9,13},{10,... | collective-permute-start | bytes 196616 | tf_op jit(solution)/shard_map/ppermute | solution.py:25
  13.3 4.6 %collective-permute-start.2 = (bf16[16,1536]{1,0:T(8,128)(2,1)S(1)}, bf16[16,1536]{1,0:T(8,128)(2,1)S(1)}, u32[]{:S(2)}, u32[]{:S(2)}) collective-permute-start(bf16[16,1536]{1,0:T(8,128)(2,1)S(1)} %get-tuple-element.25), channel_id=1, source_target_pairs={{0,10},{1,11},{2,8},{3,9},{4,14},{5,15},{6,12},{7,13},{8,2},{9,3},... | collective-permute-start | bytes 147464 | tf_op jit(solution)/shard_map/ppermute | solution.py:25
  16.3 5.0 %collective-permute-start.6 = (bf16[2,64,512]{2,1,0:T(8,128)(2,1)S(1)}, bf16[2,64,512]{2,1,0:T(8,128)(2,1)S(1)}, u32[]{:S(2)}, u32[]{:S(2)}) collective-permute-start(bf16[2,64,512]{2,1,0:T(8,128)(2,1)S(1)} %pad_maximum_fusion.4), channel_id=1, source_target_pairs={{0,1},{1,0},{2,3},{3,2},{4,5},{5,4},{6,7},{7,6},{8,9},{9,8},{10,11... | collective-permute-start | bytes 393224 | tf_op jit(solution)/shard_map/ppermute | solution.py:25
  18.0 5.9 %collective-permute-start.3 = (bf16[16,1536]{1,0:T(8,128)(2,1)S(1)}, bf16[16,1536]{1,0:T(8,128)(2,1)S(1)}, u32[]{:S(2)}, u32[]{:S(2)}) collective-permute-start(bf16[16,1536]{1,0:T(8,128)(2,1)S(1)} %fusion.12), channel_id=1, source_target_pairs={{0,12},{1,13},{2,14},{3,15},{4,8},{5,9},{6,10},{7,11},{8,4},{9,5},... | collective-permute-start | bytes 147464 | tf_op jit(solution)/shard_map/ppermute | solution.py:25
  21.4 8.0 %collective-permute-start.7 = (bf16[2,2,64,512]{3,2,1,0:T(8,128)(2,1)S(1)}, bf16[2,2,64,512]{3,2,1,0:T(8,128)(2,1)S(1)}, u32[]{:S(2)}, u32[]{:S(2)}) collective-permute-start(bf16[2,2,64,512]{3,2,1,0:T(8,128)(2,1)S(1)} %pad_maximum_fusion.3), channel_id=1, source_target_pairs={{0,2},{1,3},{2,0},{3,1},{4,6},{5,7},{6,4},{7,5},{8,10},{9,11},{10,... | collective-permute-start | bytes 786440 | tf_op jit(solution)/shard_map/ppermute | solution.py:25
  23.9 5.4 %collective-permute-start.4 = (bf16[16,1536]{1,0:T(8,128)(2,1)S(1)}, bf16[16,1536]{1,0:T(8,128)(2,1)S(1)}, u32[]{:S(2)}, u32[]{:S(2)}) collective-permute-start(bf16[16,1536]{1,0:T(8,128)(2,1)S(1)} %fusion.16), channel_id=1, source_target_pairs={{0,9},{1,8},{2,11},{3,10},{4,13},{5,12},{6,15},{7,14},{8,1},{9,0},... | collective-permute-start | bytes 147464 | tf_op jit(solution)/shard_map/ppermute | solution.py:25
  24.6 6.4 %collective-permute-start.10 = (bf16[2,2,64,512]{3,2,1,0:T(8,128)(2,1)S(1)}, bf16[2,2,64,512]{3,2,1,0:T(8,128)(2,1)S(1)}, u32[]{:S(2)}, u32[]{:S(2)}) collective-permute-start(bf16[2,2,64,512]{3,2,1,0:T(8,128)(2,1)S(1)} %pad_maximum_fusion.3), channel_id=1, source_target_pairs={{0,8},{1,9},{2,10},{3,11},{4,12},{5,13},{6,14},{7,15},{8,0},{9,1},... | collective-permute-start | bytes 786440 | tf_op jit(solution)/shard_map/ppermute | solution.py:25
  29.3 1.5 %collective-permute-start.8 = (bf16[2,2,64,512]{3,2,1,0:T(8,128)(2,1)S(1)}, bf16[2,2,64,512]{3,2,1,0:T(8,128)(2,1)S(1)}, u32[]{:S(2)}, u32[]{:S(2)}) collective-permute-start(bf16[2,2,64,512]{3,2,1,0:T(8,128)(2,1)S(1)} %collective-permute-done.7), channel_id=1, source_target_pairs={{0,8},{1,9},{2,10},{3,11},{4,12},{5,13},{6,14},{7,15},{8,0},{9,1},... | collective-permute-start | bytes 786440 | tf_op jit(solution)/shard_map/ppermute | solution.py:25
  30.9 1.3 %collective-permute-start.9 = (bf16[16,1536]{1,0:T(8,128)(2,1)S(1)}, bf16[16,1536]{1,0:T(8,128)(2,1)S(1)}, u32[]{:S(2)}, u32[]{:S(2)}) collective-permute-start(bf16[16,1536]{1,0:T(8,128)(2,1)S(1)} %convert_element_type.86), channel_id=1, source_target_pairs={{0,8},{1,9},{2,10},{3,11},{4,12},{5,13},{6,14},{7,15},{8,0},{9,1},... | collective-permute-start | bytes 147464 | tf_op jit(solution)/shard_map/ppermute | solution.py:25
  31.2 2.4 %copy-start.2 = (bf16[16,16,256]{2,1,0:T(8,128)(2,1)S(1)}, bf16[16,16,256]{2,1,0:T(8,128)(2,1)}, u32[]{:S(2)}) copy-start(bf16[16,16,256]{2,1,0:T(8,128)(2,1)} %param.12) | copy-start | bytes 393220
  32.4 3.1 %collective-permute-start.11 = (bf16[16,256]{1,0:T(8,128)(2,1)S(1)}, bf16[16,256]{1,0:T(8,128)(2,1)S(1)}, u32[]{:S(2)}, u32[]{:S(2)}) collective-permute-start(bf16[16,256]{1,0:T(8,128)(2,1)S(1)} %get-tuple-element.27), channel_id=1, source_target_pairs={{0,24},{1,25},{2,26},{3,27},{4,28},{5,29},{6,30},{7,31},{8,16},{9,... | collective-permute-start | bytes 24584 | tf_op jit(solution)/shard_map/ppermute | solution.py:25
  33.6 2.0 %copy-start.4 = (bf16[128,1536]{1,0:T(8,128)(2,1)S(1)}, bf16[128,1536]{1,0:T(8,128)(2,1)}, u32[]{:S(2)}) copy-start(bf16[128,1536]{1,0:T(8,128)(2,1)} %param.21) | copy-start | bytes 1179652
  34.7 9.7 %copy-start.1 = (bf16[1024,640]{1,0:T(8,128)(2,1)S(1)}, bf16[1024,640]{1,0:T(8,128)(2,1)}, u32[]{:S(2)}) copy-start(bf16[1024,640]{1,0:T(8,128)(2,1)} %param.17) | copy-start | bytes 3932164
  35.9 3.6 %collective-permute-start.12 = (bf16[16,128]{1,0:T(8,128)(2,1)S(1)}, bf16[16,128]{1,0:T(8,128)(2,1)S(1)}, u32[]{:S(2)}, u32[]{:S(2)}) collective-permute-start(bf16[16,128]{1,0:T(8,128)(2,1)S(1)} %convolution_convert_fusion.5), channel_id=1, source_target_pairs={{0,1},{1,0},{2,3},{3,2},{4,5},{5,4},{6,7},{7,6},{8,9},{9,8},{10,11... | collective-permute-start | bytes 12296 | tf_op jit(solution)/shard_map/ppermute | solution.py:25
  39.5 3.7 %collective-permute-start.13 = (bf16[16,256]{1,0:T(8,128)(2,1)S(1)}, bf16[16,256]{1,0:T(8,128)(2,1)S(1)}, u32[]{:S(2)}, u32[]{:S(2)}) collective-permute-start(bf16[16,256]{1,0:T(8,128)(2,1)S(1)} %pad_maximum_fusion.5), channel_id=1, source_target_pairs={{0,2},{1,3},{2,0},{3,1},{4,6},{5,7},{6,4},{7,5},{8,10},{9,11},{10,... | collective-permute-start | bytes 24584 | tf_op jit(solution)/shard_map/ppermute | solution.py:25
  39.9 5.1 %copy-start.6 = (f32[16,256,16]{1,2,0:T(8,128)S(1)}, f32[16,256,16]{1,2,0:T(8,128)}, u32[]{:S(2)}) copy-start(f32[16,256,16]{1,2,0:T(8,128)} %fusion.9) | copy-start | bytes 786436
  39.9 5.0 %copy-start.9 = (bf16[1024,256]{1,0:T(8,128)(2,1)S(1)}, bf16[1024,256]{1,0:T(8,128)(2,1)}, u32[]{:S(2)}) copy-start(bf16[1024,256]{1,0:T(8,128)(2,1)} %param.15) | copy-start | bytes 1572868

commit v15 on v13

--- a/solution.py
+++ b/solution.py
@@ -135,8 +135,9 @@
     top_bound = rounded(contract(root_state, roots[:, root_points:]))
     second_input = jnp.concatenate([second_state[:, :k_one], top_bound], axis=1)
     mid_bound = rounded(contract(second_input, down_two))
-    mid_bound = placed([mid_bound, swap(mid_bound, 1)], place, 1)
-    mid_bound = placed([mid_bound, swap(mid_bound, near)], place // near, 1)
+    mid_bound = placed(
+        [mid_bound] + [swap(mid_bound, mask) for mask in range(1, quad)], place, 1
+    )
     first_input = jnp.concatenate([first_state[:, :k_zero], mid_bound], axis=1)
 
     box_bound = rounded(contract(first_input, down_one))

time: 46 us -> 48.2 us (1.048)
  waiting for transfers between devices: 17.9 us -> 23.5 us
  matrix products: 8.02 us -> 6.33 us
  starting transfers between devices: 19 us -> 17.4 us
    ppermute x14 -> x15, waiting for transfers between devices: 17.9 us -> 23.5 us  [swap(): return lax.ppermute(value, AXES, [(i, i ^ mask) for i in range(count)])]
    ppermute x14 -> x15, starting transfers between devices: 19 us -> 17.4 us  [swap(): return lax.ppermute(value, AXES, [(i, i ^ mask) for i in range(count)])]
    dot_general x5, matrix products: 3.88 us -> 2.89 us  [contract(): lax.dot_general(left, right, (((1,), (1,)), ((), ())), preferred_element_...]
    dot_general x1, matrix products: 1.09 us -> 0.38 us  [per_device(): jnp.einsum('rlq,lqp->rlp', source, leaf_particular.reshape(leaves, points...]
  transfers between devices with their start and end apart: 14 -> 15, of which waited for: 10 -> 10; matrix products, arithmetic and copies ran while one was open for 4% -> 2% of each run, Pallas kernels for 0% -> 0%
where the time goes in v15:
time: 48.2 us; the launch traced here: 48.1 us
  waiting for transfers between devices  23.5 us (49%)
  starting transfers between devices  17.4 us (36%)
  matrix products  6.33 us (13%)
  other arithmetic  0.49 us (1%)
    ppermute x15, waiting for transfers between devices, swap(): return lax.ppermute(value, AXES, [(i, i ^ mask) for i in range(count)])  23.5 us
    ppermute x15, starting transfers between devices, swap(): return lax.ppermute(value, AXES, [(i, i ^ mask) for i in range(count)])  17.4 us
    dot_general x5, matrix products, contract(): lax.dot_general(left, right, (((1,), (1,)), ((), ())), preferred_element_...  2.89 us
    dot_general x4, matrix products, product(): return jnp.dot(left, right, preferred_element_type=jnp.float32)  1.62 us
    dot_general x1, matrix products, per_device(): jnp.einsum('rlq,leq->rle', source, leaf_flux.reshape(leaves, edge_count,...  1.44 us
  transfers between devices with their start and end apart: 15, of which 10 were waited for; matrix products, arithmetic and copies ran while one was open for 2% of the time, Pallas kernels for 0%

profile of v15, /device:TPU:0, one launch (start us, length us, event | category | flops | bytes accessed | tf_op | source)
XLA Modules:
  0.0 48.1 jit_solution(17497891835451690127)
XLA Ops:
  0.0 0.0 copy-start
  0.0 0.0 copy-start.6
  0.0 0.0 copy-start.7
  0.0 0.0 copy-start.8
  0.0 1.4 %fusion = bf16[16,16,64]{2,0,1:T(8,128)(2,1)S(1)} fusion(bf16[16,64,256]{2,1,0:T(8,128)(2,1)} %bitcast.46, bf16[16,16,256]{2,1,0:T(8,128)(2,1)} %param.12), kind=kOutput, calls=%fused_computation.2 | convolution fusion | flops 8404992 | bytes 688128 | tf_op jit(solution)/shard_map/rlq,leq->rle/dot_general | solution.py:94
  1.5 0.0 copy-start.3
  1.5 0.1 reshape.150
  1.6 1.8 %convolution_convert_fusion.3 = bf16[16,640]{1,0:T(8,128)(2,1)S(1)} fusion(bf16[16,1024]{1,0:T(8,128)(2,1)S(1)} %reshape.150, bf16[640,1024]{1,0:T(8,128)(2,1)} %param.16), kind=kOutput, calls=%fused_computation.5 | convolution fusion | flops 20981760 | bytes 1363968 | tf_op jit(solution)/shard_map/dot_general | solution.py:10
  3.4 0.0 copy-done.6
  3.4 0.2 fusion.39
  3.6 3.0 %collective-permute-start = (bf16[16,768]{1,0:T(8,128)(2,1)S(1)}, bf16[16,768]{1,0:T(8,128)(2,1)S(1)}, u32[]{:S(2)}, u32[]{:S(2)}) collective-permute-start(bf16[16,768]{1,0:T(8,128)(2,1)S(1)} %get-tuple-element.25), channel_id=1, source_target_pairs={{0,1},{1,0},{2,3},{3,2},{4,5},{5,4},{6,7},{7,6},{8,9},{9,8},{10,11... | collective-permute-start | bytes 73736 | tf_op jit(solution)/shard_map/ppermute | solution.py:25
  6.6 0.0 copy-done.7
  6.6 1.8 %collective-permute-done = bf16[16,768]{1,0:T(8,128)(2,1)S(1)} collective-permute-done((bf16[16,768]{1,0:T(8,128)(2,1)S(1)}, bf16[16,768]{1,0:T(8,128)(2,1)S(1)}, u32[]{:S(2)}, u32[]{:S(2)}) %collective-permute-start) | collective-permute-done | bytes 24608 | tf_op jit(solution)/shard_map/ppermute | solution.py:25
  8.4 2.1 %collective-permute-start.1 = (bf16[16,768]{1,0:T(8,128)(2,1)S(1)}, bf16[16,768]{1,0:T(8,128)(2,1)S(1)}, u32[]{:S(2)}, u32[]{:S(2)}) collective-permute-start(bf16[16,768]{1,0:T(8,128)(2,1)S(1)} %fusion.17), channel_id=1, source_target_pairs={{0,2},{1,3},{2,0},{3,1},{4,6},{5,7},{6,4},{7,5},{8,10},{9,11},{10,... | collective-permute-start | bytes 73736 | tf_op jit(solution)/shard_map/ppermute | solution.py:25
  10.5 0.0 copy-done.8
  10.6 2.6 %collective-permute-start.5 = (bf16[64,512]{1,0:T(8,128)(2,1)S(1)}, bf16[64,512]{1,0:T(8,128)(2,1)S(1)}, u32[]{:S(2)}, u32[]{:S(2)}) collective-permute-start(bf16[64,512]{1,0:T(8,128)(2,1)S(1)} %constant_dynamic-update-slice_fusion), channel_id=1, source_target_pairs={{0,4},{1,5},{2,6},{3,7},{4,0},{5,1},{6,2},{7,3},{8,12},{9,13},{10,... | collective-permute-start | bytes 196616 | tf_op jit(solution)/shard_map/ppermute | solution.py:25
  13.1 0.0 collective-permute-done.1
  13.2 0.0 copy-done.3
  13.2 0.0 copy-start.2
  13.2 0.2 fusion.40
  13.3 0.1 collective-permute-start.2
  13.4 2.8 %collective-permute-done.5 = bf16[64,512]{1,0:T(8,128)(2,1)S(1)} collective-permute-done((bf16[64,512]{1,0:T(8,128)(2,1)S(1)}, bf16[64,512]{1,0:T(8,128)(2,1)S(1)}, u32[]{:S(2)}, u32[]{:S(2)}) %collective-permute-start.5) | collective-permute-done | bytes 65568 | tf_op jit(solution)/shard_map/ppermute | solution.py:25
  16.2 2.0 %collective-permute-done.2 = bf16[16,1536]{1,0:T(8,128)(2,1)S(1)} collective-permute-done((bf16[16,1536]{1,0:T(8,128)(2,1)S(1)}, bf16[16,1536]{1,0:T(8,128)(2,1)S(1)}, u32[]{:S(2)}, u32[]{:S(2)}) %collective-permute-start.2) | collective-permute-done | bytes 49184 | tf_op jit(solution)/shard_map/ppermute | solution.py:25
  18.3 1.3 %collective-permute-start.3 = (bf16[16,1536]{1,0:T(8,128)(2,1)S(1)}, bf16[16,1536]{1,0:T(8,128)(2,1)S(1)}, u32[]{:S(2)}, u32[]{:S(2)}) collective-permute-start(bf16[16,1536]{1,0:T(8,128)(2,1)S(1)} %fusion.12), channel_id=1, source_target_pairs={{0,10},{1,11},{2,8},{3,9},{4,14},{5,15},{6,12},{7,13},{8,2},{9,3},... | collective-permute-start | bytes 147464 | tf_op jit(solution)/shard_map/ppermute | solution.py:25
  19.6 1.6 %collective-permute-start.6 = (bf16[2,64,512]{2,1,0:T(8,128)(2,1)S(1)}, bf16[2,64,512]{2,1,0:T(8,128)(2,1)S(1)}, u32[]{:S(2)}, u32[]{:S(2)}) collective-permute-start(bf16[2,64,512]{2,1,0:T(8,128)(2,1)S(1)} %pad_maximum_fusion.4), channel_id=1, source_target_pairs={{0,1},{1,0},{2,3},{3,2},{4,5},{5,4},{6,7},{7,6},{8,9},{9,8},{10,11... | collective-permute-start | bytes 393224 | tf_op jit(solution)/shard_map/ppermute | solution.py:25
  21.2 1.0 %collective-permute-done.3 = bf16[16,1536]{1,0:T(8,128)(2,1)S(1)} collective-permute-done((bf16[16,1536]{1,0:T(8,128)(2,1)S(1)}, bf16[16,1536]{1,0:T(8,128)(2,1)S(1)}, u32[]{:S(2)}, u32[]{:S(2)}) %collective-permute-start.3) | collective-permute-done | bytes 49184 | tf_op jit(solution)/shard_map/ppermute | solution.py:25
  22.2 1.3 %collective-permute-start.4 = (bf16[16,1536]{1,0:T(8,128)(2,1)S(1)}, bf16[16,1536]{1,0:T(8,128)(2,1)S(1)}, u32[]{:S(2)}, u32[]{:S(2)}) collective-permute-start(bf16[16,1536]{1,0:T(8,128)(2,1)S(1)} %fusion.16), channel_id=1, source_target_pairs={{0,9},{1,8},{2,11},{3,10},{4,13},{5,12},{6,15},{7,14},{8,1},{9,0},... | collective-permute-start | bytes 147464 | tf_op jit(solution)/shard_map/ppermute | solution.py:25
  23.5 2.2 %collective-permute-done.6 = bf16[2,64,512]{2,1,0:T(8,128)(2,1)S(1)} collective-permute-done((bf16[2,64,512]{2,1,0:T(8,128)(2,1)S(1)}, bf16[2,64,512]{2,1,0:T(8,128)(2,1)S(1)}, u32[]{:S(2)}, u32[]{:S(2)}) %collective-permute-start.6) | collective-permute-done | bytes 131104 | tf_op jit(solution)/shard_map/ppermute | solution.py:25
  25.8 0.3 collective-permute-start.7
  26.1 0.0 copy-done
  26.1 0.0 copy-done.2
  26.1 0.4 fusion.9
  26.5 0.0 collective-permute-start.10
  26.5 7.0 %collective-permute-done.7 = bf16[2,2,64,512]{3,2,1,0:T(8,128)(2,1)S(1)} collective-permute-done((bf16[2,2,64,512]{3,2,1,0:T(8,128)(2,1)S(1)}, bf16[2,2,64,512]{3,2,1,0:T(8,128)(2,1)S(1)}, u32[]{:S(2)}, u32[]{:S(2)}) %collective-permute-start.7) | collective-permute-done | bytes 262176 | tf_op jit(solution)/shard_map/ppermute | solution.py:25
  33.5 0.0 collective-permute-start.8
  33.5 0.0 collective-permute-done.4
  33.6 1.4 %collective-permute-done.8 = bf16[2,2,64,512]{3,2,1,0:T(8,128)(2,1)S(1)} collective-permute-done((bf16[2,2,64,512]{3,2,1,0:T(8,128)(2,1)S(1)}, bf16[2,2,64,512]{3,2,1,0:T(8,128)(2,1)S(1)}, u32[]{:S(2)}, u32[]{:S(2)}) %collective-permute-start.8) | collective-permute-done | bytes 262176 | tf_op jit(solution)/shard_map/ppermute | solution.py:25
  35.1 0.2 collective-permute-start.9
  35.2 0.0 collective-permute-done.10
  35.3 0.1 broadcast_select_fusion.1
  35.4 0.0 copy-start.4
  35.4 0.1 pad_maximum_fusion
  35.5 0.0 copy-start.5
  35.5 0.0 copy-start.1
  35.5 0.8 %collective-permute-done.9 = bf16[16,1536]{1,0:T(8,128)(2,1)S(1)} collective-permute-done((bf16[16,1536]{1,0:T(8,128)(2,1)S(1)}, bf16[16,1536]{1,0:T(8,128)(2,1)S(1)}, u32[]{:S(2)}, u32[]{:S(2)}) %collective-permute-start.9) | collective-permute-done | bytes 49184 | tf_op jit(solution)/shard_map/ppermute | solution.py:25
  36.4 0.2 fusion.41
  36.6 1.3 %collective-permute-start.11 = (bf16[16,256]{1,0:T(8,128)(2,1)S(1)}, bf16[16,256]{1,0:T(8,128)(2,1)S(1)}, u32[]{:S(2)}, u32[]{:S(2)}) collective-permute-start(bf16[16,256]{1,0:T(8,128)(2,1)S(1)} %get-tuple-element.29), channel_id=1, source_target_pairs={{0,24},{1,25},{2,26},{3,27},{4,28},{5,29},{6,30},{7,31},{8,16},{9,... | collective-permute-start | bytes 24584 | tf_op jit(solution)/shard_map/ppermute | solution.py:25
  37.8 1.8 %collective-permute-done.11 = bf16[16,256]{1,0:T(8,128)(2,1)S(1)} collective-permute-done((bf16[16,256]{1,0:T(8,128)(2,1)S(1)}, bf16[16,256]{1,0:T(8,128)(2,1)S(1)}, u32[]{:S(2)}, u32[]{:S(2)}) %collective-permute-start.11) | collective-permute-done | bytes 8224 | tf_op jit(solution)/shard_map/ppermute | solution.py:25
  39.6 0.2 convolution_convert_fusion.2
  39.9 0.0 copy-done.4
  39.9 0.0 copy-start.9
  39.9 0.2 convolution_convert_fusion.5
  40.1 1.6 %collective-permute-start.14 = (bf16[16,128]{1,0:T(8,128)(2,1)S(1)}, bf16[16,128]{1,0:T(8,128)(2,1)S(1)}, u32[]{:S(2)}, u32[]{:S(2)}) collective-permute-start(bf16[16,128]{1,0:T(8,128)(2,1)S(1)} %convolution_convert_fusion.5), channel_id=1, source_target_pairs={{0,1},{1,0},{2,3},{3,2},{4,5},{5,4},{6,7},{7,6},{8,9},{9,8},{10,11... | collective-permute-start | bytes 12296 | tf_op jit(solution)/shard_map/ppermute | solution.py:25
  41.7 0.5 %collective-permute-start.12 = (bf16[16,128]{1,0:T(8,128)(2,1)S(1)}, bf16[16,128]{1,0:T(8,128)(2,1)S(1)}, u32[]{:S(2)}, u32[]{:S(2)}) collective-permute-start(bf16[16,128]{1,0:T(8,128)(2,1)S(1)} %convolution_convert_fusion.5), channel_id=1, source_target_pairs={{0,3},{1,2},{2,1},{3,0},{4,7},{5,6},{6,5},{7,4},{8,11},{9,10},{10,... | collective-permute-start | bytes 12296 | tf_op jit(solution)/shard_map/ppermute | solution.py:25
  42.2 1.5 %collective-permute-start.13 = (bf16[16,128]{1,0:T(8,128)(2,1)S(1)}, bf16[16,128]{1,0:T(8,128)(2,1)S(1)}, u32[]{:S(2)}, u32[]{:S(2)}) collective-permute-start(bf16[16,128]{1,0:T(8,128)(2,1)S(1)} %convolution_convert_fusion.5), channel_id=1, source_target_pairs={{0,2},{1,3},{2,0},{3,1},{4,6},{5,7},{6,4},{7,5},{8,10},{9,11},{10,... | collective-permute-start | bytes 12296 | tf_op jit(solution)/shard_map/ppermute | solution.py:25
  43.7 0.0 collective-permute-done.14
  43.7 2.5 %collective-permute-done.12 = bf16[16,128]{1,0:T(8,128)(2,1)S(1)} collective-permute-done((bf16[16,128]{1,0:T(8,128)(2,1)S(1)}, bf16[16,128]{1,0:T(8,128)(2,1)S(1)}, u32[]{:S(2)}, u32[]{:S(2)}) %collective-permute-start.12) | collective-permute-done | bytes 4128 | tf_op jit(solution)/shard_map/ppermute | solution.py:25
  46.3 0.0 collective-permute-done.13
  46.3 0.0 copy-done.5
  46.3 0.2 convolution_convert_fusion.4
  46.5 0.0 copy-done.1
  46.5 0.5 %convolution_convert_fusion.1 = bf16[16,1024]{1,0:T(8,128)(2,1)S(1)} fusion(bf16[1024,640]{1,0:T(8,128)(2,1)S(1)} %copy-done.1, bf16[16,256]{1,0:T(8,128)(2,1)S(1)} %convolution_convert_fusion.4, bf16[16,384]{1,0:T(8,128)(2,1)S(1)} %slice.28), kind=kOutput, calls=%fused_computation.3 | convolution fusion | flops 21028864 | bytes 1363968 | tf_op jit(solution)/shard_map/dot_general | solution.py:10
  47.0 0.0 copy-done.9
  47.0 1.1 %convolution_add_fusion = f32[16,16,256]{2,1,0:T(8,128)} fusion(bf16[1024,256]{1,0:T(8,128)(2,1)S(1)} %copy-done.9, pred[16,1024]{1,0:T(8,128)(4,1)S(1)} %iota_compare_fusion, f32[16,256,16]{1,2,0:T(8,128)S(1)} %fusion.9, bf16[16,1024]{1,0:T(8,128)(2,1)S(1)} %convolution_convert_fusion.1), kind=kOutput, calls=%fused_computation | convolution fusion | flops 134545408 | bytes 1097728 | tf_op jit(solution)/shard_map/dot_general | solution.py:16
  (24 shorter events, 0.3 us)
Async XLA Ops:
  0.0 26.1 %copy-start = (bf16[4096,256]{1,0:T(8,128)(2,1)S(1)}, bf16[4096,256]{1,0:T(8,128)(2,1)}, u32[]{:S(2)}) copy-start(bf16[4096,256]{1,0:T(8,128)(2,1)} %param.14) | copy-start | bytes 6291460
  0.0 3.4 %copy-start.6 = (bf16[256,768]{1,0:T(8,128)(2,1)S(1)}, bf16[256,768]{1,0:T(8,128)(2,1)}, u32[]{:S(2)}) copy-start(bf16[256,768]{1,0:T(8,128)(2,1)} %param.18) | copy-start | bytes 1179652
  0.0 6.6 %copy-start.7 = (bf16[64,256]{1,0:T(8,128)(2,1)S(1)}, bf16[64,256]{1,0:T(8,128)(2,1)}, u32[]{:S(2)}) copy-start(bf16[64,256]{1,0:T(8,128)(2,1)} %param.22) | copy-start | bytes 98308
  0.0 10.5 %copy-start.8 = (bf16[64,256]{1,0:T(8,128)(2,1)S(1)}, bf16[64,256]{1,0:T(8,128)(2,1)}, u32[]{:S(2)}) copy-start(bf16[64,256]{1,0:T(8,128)(2,1)} %param.23) | copy-start | bytes 98308
  1.5 11.7 %copy-start.3 = (bf16[128,1536]{1,0:T(8,128)(2,1)S(1)}, bf16[128,1536]{1,0:T(8,128)(2,1)}, u32[]{:S(2)}) copy-start(bf16[128,1536]{1,0:T(8,128)(2,1)} %param.20) | copy-start | bytes 1179652
  3.6 4.8 %collective-permute-start = (bf16[16,768]{1,0:T(8,128)(2,1)S(1)}, bf16[16,768]{1,0:T(8,128)(2,1)S(1)}, u32[]{:S(2)}, u32[]{:S(2)}) collective-permute-start(bf16[16,768]{1,0:T(8,128)(2,1)S(1)} %get-tuple-element.25), channel_id=1, source_target_pairs={{0,1},{1,0},{2,3},{3,2},{4,5},{5,4},{6,7},{7,6},{8,9},{9,8},{10,11... | collective-permute-start | bytes 73736 | tf_op jit(solution)/shard_map/ppermute | solution.py:25
  8.4 4.7 %collective-permute-start.1 = (bf16[16,768]{1,0:T(8,128)(2,1)S(1)}, bf16[16,768]{1,0:T(8,128)(2,1)S(1)}, u32[]{:S(2)}, u32[]{:S(2)}) collective-permute-start(bf16[16,768]{1,0:T(8,128)(2,1)S(1)} %fusion.17), channel_id=1, source_target_pairs={{0,2},{1,3},{2,0},{3,1},{4,6},{5,7},{6,4},{7,5},{8,10},{9,11},{10,... | collective-permute-start | bytes 73736 | tf_op jit(solution)/shard_map/ppermute | solution.py:25
  10.6 5.7 %collective-permute-start.5 = (bf16[64,512]{1,0:T(8,128)(2,1)S(1)}, bf16[64,512]{1,0:T(8,128)(2,1)S(1)}, u32[]{:S(2)}, u32[]{:S(2)}) collective-permute-start(bf16[64,512]{1,0:T(8,128)(2,1)S(1)} %constant_dynamic-update-slice_fusion), channel_id=1, source_target_pairs={{0,4},{1,5},{2,6},{3,7},{4,0},{5,1},{6,2},{7,3},{8,12},{9,13},{10,... | collective-permute-start | bytes 196616 | tf_op jit(solution)/shard_map/ppermute | solution.py:25
  13.2 12.9 %copy-start.2 = (bf16[16,16,256]{2,1,0:T(8,128)(2,1)S(1)}, bf16[16,16,256]{2,1,0:T(8,128)(2,1)}, u32[]{:S(2)}) copy-start(bf16[16,16,256]{2,1,0:T(8,128)(2,1)} %param.12) | copy-start | bytes 393220
  13.3 4.9 %collective-permute-start.2 = (bf16[16,1536]{1,0:T(8,128)(2,1)S(1)}, bf16[16,1536]{1,0:T(8,128)(2,1)S(1)}, u32[]{:S(2)}, u32[]{:S(2)}) collective-permute-start(bf16[16,1536]{1,0:T(8,128)(2,1)S(1)} %get-tuple-element.27), channel_id=1, source_target_pairs={{0,12},{1,13},{2,14},{3,15},{4,8},{5,9},{6,10},{7,11},{8,4},{9,5},... | collective-permute-start | bytes 147464 | tf_op jit(solution)/shard_map/ppermute | solution.py:25
  18.3 3.9 %collective-permute-start.3 = (bf16[16,1536]{1,0:T(8,128)(2,1)S(1)}, bf16[16,1536]{1,0:T(8,128)(2,1)S(1)}, u32[]{:S(2)}, u32[]{:S(2)}) collective-permute-start(bf16[16,1536]{1,0:T(8,128)(2,1)S(1)} %fusion.12), channel_id=1, source_target_pairs={{0,10},{1,11},{2,8},{3,9},{4,14},{5,15},{6,12},{7,13},{8,2},{9,3},... | collective-permute-start | bytes 147464 | tf_op jit(solution)/shard_map/ppermute | solution.py:25
  19.6 6.1 %collective-permute-start.6 = (bf16[2,64,512]{2,1,0:T(8,128)(2,1)S(1)}, bf16[2,64,512]{2,1,0:T(8,128)(2,1)S(1)}, u32[]{:S(2)}, u32[]{:S(2)}) collective-permute-start(bf16[2,64,512]{2,1,0:T(8,128)(2,1)S(1)} %pad_maximum_fusion.4), channel_id=1, source_target_pairs={{0,1},{1,0},{2,3},{3,2},{4,5},{5,4},{6,7},{7,6},{8,9},{9,8},{10,11... | collective-permute-start | bytes 393224 | tf_op jit(solution)/shard_map/ppermute | solution.py:25
  22.2 11.3 %collective-permute-start.4 = (bf16[16,1536]{1,0:T(8,128)(2,1)S(1)}, bf16[16,1536]{1,0:T(8,128)(2,1)S(1)}, u32[]{:S(2)}, u32[]{:S(2)}) collective-permute-start(bf16[16,1536]{1,0:T(8,128)(2,1)S(1)} %fusion.16), channel_id=1, source_target_pairs={{0,9},{1,8},{2,11},{3,10},{4,13},{5,12},{6,15},{7,14},{8,1},{9,0},... | collective-permute-start | bytes 147464 | tf_op jit(solution)/shard_map/ppermute | solution.py:25
  25.8 7.8 %collective-permute-start.7 = (bf16[2,2,64,512]{3,2,1,0:T(8,128)(2,1)S(1)}, bf16[2,2,64,512]{3,2,1,0:T(8,128)(2,1)S(1)}, u32[]{:S(2)}, u32[]{:S(2)}) collective-permute-start(bf16[2,2,64,512]{3,2,1,0:T(8,128)(2,1)S(1)} %pad_maximum_fusion.3), channel_id=1, source_target_pairs={{0,2},{1,3},{2,0},{3,1},{4,6},{5,7},{6,4},{7,5},{8,10},{9,11},{10,... | collective-permute-start | bytes 786440 | tf_op jit(solution)/shard_map/ppermute | solution.py:25
  26.5 8.8 %collective-permute-start.10 = (bf16[2,2,64,512]{3,2,1,0:T(8,128)(2,1)S(1)}, bf16[2,2,64,512]{3,2,1,0:T(8,128)(2,1)S(1)}, u32[]{:S(2)}, u32[]{:S(2)}) collective-permute-start(bf16[2,2,64,512]{3,2,1,0:T(8,128)(2,1)S(1)} %pad_maximum_fusion.3), channel_id=1, source_target_pairs={{0,8},{1,9},{2,10},{3,11},{4,12},{5,13},{6,14},{7,15},{8,0},{9,1},... | collective-permute-start | bytes 786440 | tf_op jit(solution)/shard_map/ppermute | solution.py:25
  33.5 1.5 %collective-permute-start.8 = (bf16[2,2,64,512]{3,2,1,0:T(8,128)(2,1)S(1)}, bf16[2,2,64,512]{3,2,1,0:T(8,128)(2,1)S(1)}, u32[]{:S(2)}, u32[]{:S(2)}) collective-permute-start(bf16[2,2,64,512]{3,2,1,0:T(8,128)(2,1)S(1)} %collective-permute-done.7), channel_id=1, source_target_pairs={{0,8},{1,9},{2,10},{3,11},{4,12},{5,13},{6,14},{7,15},{8,0},{9,1},... | collective-permute-start | bytes 786440 | tf_op jit(solution)/shard_map/ppermute | solution.py:25
  35.1 1.3 %collective-permute-start.9 = (bf16[16,1536]{1,0:T(8,128)(2,1)S(1)}, bf16[16,1536]{1,0:T(8,128)(2,1)S(1)}, u32[]{:S(2)}, u32[]{:S(2)}) collective-permute-start(bf16[16,1536]{1,0:T(8,128)(2,1)S(1)} %convert_element_type.86), channel_id=1, source_target_pairs={{0,8},{1,9},{2,10},{3,11},{4,12},{5,13},{6,14},{7,15},{8,0},{9,1},... | collective-permute-start | bytes 147464 | tf_op jit(solution)/shard_map/ppermute | solution.py:25
  35.4 4.5 %copy-start.4 = (bf16[128,1536]{1,0:T(8,128)(2,1)S(1)}, bf16[128,1536]{1,0:T(8,128)(2,1)}, u32[]{:S(2)}) copy-start(bf16[128,1536]{1,0:T(8,128)(2,1)} %param.21) | copy-start | bytes 1179652
  35.5 10.8 %copy-start.5 = (bf16[256,768]{1,0:T(8,128)(2,1)S(1)}, bf16[256,768]{1,0:T(8,128)(2,1)}, u32[]{:S(2)}) copy-start(bf16[256,768]{1,0:T(8,128)(2,1)} %param.19) | copy-start | bytes 1179652
  35.5 11.0 %copy-start.1 = (bf16[1024,640]{1,0:T(8,128)(2,1)S(1)}, bf16[1024,640]{1,0:T(8,128)(2,1)}, u32[]{:S(2)}) copy-start(bf16[1024,640]{1,0:T(8,128)(2,1)} %param.17) | copy-start | bytes 3932164
  36.6 3.1 %collective-permute-start.11 = (bf16[16,256]{1,0:T(8,128)(2,1)S(1)}, bf16[16,256]{1,0:T(8,128)(2,1)S(1)}, u32[]{:S(2)}, u32[]{:S(2)}) collective-permute-start(bf16[16,256]{1,0:T(8,128)(2,1)S(1)} %get-tuple-element.29), channel_id=1, source_target_pairs={{0,24},{1,25},{2,26},{3,27},{4,28},{5,29},{6,30},{7,31},{8,16},{9,... | collective-permute-start | bytes 24584 | tf_op jit(solution)/shard_map/ppermute | solution.py:25
  39.9 7.1 %copy-start.9 = (bf16[1024,256]{1,0:T(8,128)(2,1)S(1)}, bf16[1024,256]{1,0:T(8,128)(2,1)}, u32[]{:S(2)}) copy-start(bf16[1024,256]{1,0:T(8,128)(2,1)} %param.15) | copy-start | bytes 1572868
  40.1 3.6 %collective-permute-start.14 = (bf16[16,128]{1,0:T(8,128)(2,1)S(1)}, bf16[16,128]{1,0:T(8,128)(2,1)S(1)}, u32[]{:S(2)}, u32[]{:S(2)}) collective-permute-start(bf16[16,128]{1,0:T(8,128)(2,1)S(1)} %convolution_convert_fusion.5), channel_id=1, source_target_pairs={{0,1},{1,0},{2,3},{3,2},{4,5},{5,4},{6,7},{7,6},{8,9},{9,8},{10,11... | collective-permute-start | bytes 12296 | tf_op jit(solution)/shard_map/ppermute | solution.py:25
  41.7 4.6 %collective-permute-start.12 = (bf16[16,128]{1,0:T(8,128)(2,1)S(1)}, bf16[16,128]{1,0:T(8,128)(2,1)S(1)}, u32[]{:S(2)}, u32[]{:S(2)}) collective-permute-start(bf16[16,128]{1,0:T(8,128)(2,1)S(1)} %convolution_convert_fusion.5), channel_id=1, source_target_pairs={{0,3},{1,2},{2,1},{3,0},{4,7},{5,6},{6,5},{7,4},{8,11},{9,10},{10,... | collective-permute-start | bytes 12296 | tf_op jit(solution)/shard_map/ppermute | solution.py:25
  42.2 4.1 %collective-permute-start.13 = (bf16[16,128]{1,0:T(8,128)(2,1)S(1)}, bf16[16,128]{1,0:T(8,128)(2,1)S(1)}, u32[]{:S(2)}, u32[]{:S(2)}) collective-permute-start(bf16[16,128]{1,0:T(8,128)(2,1)S(1)} %convolution_convert_fusion.5), channel_id=1, source_target_pairs={{0,2},{1,3},{2,0},{3,1},{4,6},{5,7},{6,4},{7,5},{8,10},{9,11},{10,... | collective-permute-start | bytes 12296 | tf_op jit(solution)/shard_map/ppermute | solution.py:25

commit v16 on v13

--- a/solution.py
+++ b/solution.py
@@ -106,6 +106,7 @@
     first_sum = partner_sum(first_sum, 1)
 
     roots = joined_pair(roots, roots_far, place & far != 0, 0)
+    roots = swap(swap(roots, pair), pair)
     roots_one = swap(roots, 1)
     first_sum = partner_sum(first_sum, near)
     first_state = rounded(first_sum)

time: 46 us -> 46.9 us (1.020)
  waiting for transfers between devices: 17.9 us -> 18.4 us
    ppermute x14 -> x16, waiting for transfers between devices: 17.9 us -> 18.4 us  [swap(): return lax.ppermute(value, AXES, [(i, i ^ mask) for i in range(count)])]
    ppermute x14 -> x16, starting transfers between devices: 19 us -> 19.3 us  [swap(): return lax.ppermute(value, AXES, [(i, i ^ mask) for i in range(count)])]
  transfers between devices with their start and end apart: 14 -> 16, of which waited for: 10 -> 11; matrix products, arithmetic and copies ran while one was open for 4% -> 4% of each run, Pallas kernels for 0% -> 0%
where the time goes in v16:
time: 46.9 us; the launch traced here: 46.7 us
  starting transfers between devices  19.3 us (41%)
  waiting for transfers between devices  18.4 us (39%)
  matrix products  8.06 us (17%)
  other arithmetic  0.49 us (1%)
    ppermute x16, starting transfers between devices, swap(): return lax.ppermute(value, AXES, [(i, i ^ mask) for i in range(count)])  19.3 us
    ppermute x16, waiting for transfers between devices, swap(): return lax.ppermute(value, AXES, [(i, i ^ mask) for i in range(count)])  18.4 us
    dot_general x5, matrix products, contract(): lax.dot_general(left, right, (((1,), (1,)), ((), ())), preferred_element_...  3.93 us
    dot_general x4, matrix products, product(): return jnp.dot(left, right, preferred_element_type=jnp.float32)  1.6 us
    dot_general x1, matrix products, per_device(): jnp.einsum('rlq,leq->rle', source, leaf_flux.reshape(leaves, edge_count,...  1.44 us
    dot_general x1, matrix products, per_device(): jnp.einsum('rlq,lqp->rlp', source, leaf_particular.reshape(leaves, points...  1.09 us
  transfers between devices with their start and end apart: 16, of which 11 were waited for; matrix products, arithmetic and copies ran while one was open for 4% of the time, Pallas kernels for 0%

profile of v16, /device:TPU:0, one launch (start us, length us, event | category | flops | bytes accessed | tf_op | source)
XLA Modules:
  0.0 46.7 jit_solution(9980873649452945975)
XLA Ops:
  0.0 0.0 copy-start
  0.0 0.0 copy-start.5
  0.0 0.0 copy-start.7
  0.0 0.0 copy-start.8
  0.0 1.4 %fusion = bf16[16,16,64]{2,0,1:T(8,128)(2,1)S(1)} fusion(bf16[16,64,256]{2,1,0:T(8,128)(2,1)} %bitcast.46, bf16[16,16,256]{2,1,0:T(8,128)(2,1)} %param.12), kind=kOutput, calls=%fused_computation.2 | convolution fusion | flops 8404992 | bytes 688128 | tf_op jit(solution)/shard_map/rlq,leq->rle/dot_general | solution.py:94
  1.5 0.1 reshape.150
  1.6 0.0 copy-start.3
  1.6 1.8 %convolution_convert_fusion.3 = bf16[16,640]{1,0:T(8,128)(2,1)S(1)} fusion(bf16[16,1024]{1,0:T(8,128)(2,1)S(1)} %reshape.150, bf16[640,1024]{1,0:T(8,128)(2,1)} %param.16), kind=kOutput, calls=%fused_computation.5 | convolution fusion | flops 20981760 | bytes 1363968 | tf_op jit(solution)/shard_map/dot_general | solution.py:10
  3.4 0.0 copy-done.5
  3.4 0.2 fusion.39
  3.6 3.0 %collective-permute-start = (bf16[16,768]{1,0:T(8,128)(2,1)S(1)}, bf16[16,768]{1,0:T(8,128)(2,1)S(1)}, u32[]{:S(2)}, u32[]{:S(2)}) collective-permute-start(bf16[16,768]{1,0:T(8,128)(2,1)S(1)} %get-tuple-element.23), channel_id=1, source_target_pairs={{0,1},{1,0},{2,3},{3,2},{4,5},{5,4},{6,7},{7,6},{8,9},{9,8},{10,11... | collective-permute-start | bytes 73736 | tf_op jit(solution)/shard_map/ppermute | solution.py:25
  6.6 0.0 copy-done.7
  6.7 0.0 copy-done.8
  6.7 2.7 %collective-permute-start.5 = (bf16[64,512]{1,0:T(8,128)(2,1)S(1)}, bf16[64,512]{1,0:T(8,128)(2,1)S(1)}, u32[]{:S(2)}, u32[]{:S(2)}) collective-permute-start(bf16[64,512]{1,0:T(8,128)(2,1)S(1)} %constant_dynamic-update-slice_fusion), channel_id=1, source_target_pairs={{0,4},{1,5},{2,6},{3,7},{4,0},{5,1},{6,2},{7,3},{8,12},{9,13},{10,... | collective-permute-start | bytes 196616 | tf_op jit(solution)/shard_map/ppermute | solution.py:25
  9.3 0.0 collective-permute-done
  9.3 1.6 %collective-permute-start.1 = (bf16[16,768]{1,0:T(8,128)(2,1)S(1)}, bf16[16,768]{1,0:T(8,128)(2,1)S(1)}, u32[]{:S(2)}, u32[]{:S(2)}) collective-permute-start(bf16[16,768]{1,0:T(8,128)(2,1)S(1)} %fusion.17), channel_id=1, source_target_pairs={{0,2},{1,3},{2,0},{3,1},{4,6},{5,7},{6,4},{7,5},{8,10},{9,11},{10,... | collective-permute-start | bytes 73736 | tf_op jit(solution)/shard_map/ppermute | solution.py:25
  11.0 1.3 %collective-permute-done.5 = bf16[64,512]{1,0:T(8,128)(2,1)S(1)} collective-permute-done((bf16[64,512]{1,0:T(8,128)(2,1)S(1)}, bf16[64,512]{1,0:T(8,128)(2,1)S(1)}, u32[]{:S(2)}, u32[]{:S(2)}) %collective-permute-start.5) | collective-permute-done | bytes 65568 | tf_op jit(solution)/shard_map/ppermute | solution.py:25
  12.3 0.1 collective-permute-start.6
  12.4 0.9 %collective-permute-done.1 = bf16[16,768]{1,0:T(8,128)(2,1)S(1)} collective-permute-done((bf16[16,768]{1,0:T(8,128)(2,1)S(1)}, bf16[16,768]{1,0:T(8,128)(2,1)S(1)}, u32[]{:S(2)}, u32[]{:S(2)}) %collective-permute-start.1) | collective-permute-done | bytes 24608 | tf_op jit(solution)/shard_map/ppermute | solution.py:25
  13.2 0.4 collective-permute-done.6
  13.7 0.1 collective-permute-start.7
  13.8 0.0 copy-done.3
  13.8 0.2 fusion.40
  14.0 2.6 %collective-permute-start.2 = (bf16[16,1536]{1,0:T(8,128)(2,1)S(1)}, bf16[16,1536]{1,0:T(8,128)(2,1)S(1)}, u32[]{:S(2)}, u32[]{:S(2)}) collective-permute-start(bf16[16,1536]{1,0:T(8,128)(2,1)S(1)} %get-tuple-element.25), channel_id=1, source_target_pairs={{0,12},{1,13},{2,14},{3,15},{4,8},{5,9},{6,10},{7,11},{8,4},{9,5},... | collective-permute-start | bytes 147464 | tf_op jit(solution)/shard_map/ppermute | solution.py:25
  16.6 0.0 collective-permute-done.7
  16.6 0.8 %collective-permute-start.8 = (bf16[2,64,512]{2,1,0:T(8,128)(2,1)S(1)}, bf16[2,64,512]{2,1,0:T(8,128)(2,1)S(1)}, u32[]{:S(2)}, u32[]{:S(2)}) collective-permute-start(bf16[2,64,512]{2,1,0:T(8,128)(2,1)S(1)} %collective-permute-done.7), channel_id=1, source_target_pairs={{0,1},{1,0},{2,3},{3,2},{4,5},{5,4},{6,7},{7,6},{8,9},{9,8},{10,11... | collective-permute-start | bytes 393224 | tf_op jit(solution)/shard_map/ppermute | solution.py:25
  17.4 1.1 %collective-permute-done.2 = bf16[16,1536]{1,0:T(8,128)(2,1)S(1)} collective-permute-done((bf16[16,1536]{1,0:T(8,128)(2,1)S(1)}, bf16[16,1536]{1,0:T(8,128)(2,1)S(1)}, u32[]{:S(2)}, u32[]{:S(2)}) %collective-permute-start.2) | collective-permute-done | bytes 49184 | tf_op jit(solution)/shard_map/ppermute | solution.py:25
  18.5 2.0 %collective-permute-start.3 = (bf16[16,1536]{1,0:T(8,128)(2,1)S(1)}, bf16[16,1536]{1,0:T(8,128)(2,1)S(1)}, u32[]{:S(2)}, u32[]{:S(2)}) collective-permute-start(bf16[16,1536]{1,0:T(8,128)(2,1)S(1)} %fusion.12), channel_id=1, source_target_pairs={{0,10},{1,11},{2,8},{3,9},{4,14},{5,15},{6,12},{7,13},{8,2},{9,3},... | collective-permute-start | bytes 147464 | tf_op jit(solution)/shard_map/ppermute | solution.py:25
  20.5 1.7 %collective-permute-done.8 = bf16[2,64,512]{2,1,0:T(8,128)(2,1)S(1)} collective-permute-done((bf16[2,64,512]{2,1,0:T(8,128)(2,1)S(1)}, bf16[2,64,512]{2,1,0:T(8,128)(2,1)S(1)}, u32[]{:S(2)}, u32[]{:S(2)}) %collective-permute-start.8) | collective-permute-done | bytes 131104 | tf_op jit(solution)/shard_map/ppermute | solution.py:25
  22.2 2.0 %collective-permute-start.9 = (bf16[2,2,64,512]{3,2,1,0:T(8,128)(2,1)S(1)}, bf16[2,2,64,512]{3,2,1,0:T(8,128)(2,1)S(1)}, u32[]{:S(2)}, u32[]{:S(2)}) collective-permute-start(bf16[2,2,64,512]{3,2,1,0:T(8,128)(2,1)S(1)} %pad_maximum_fusion.3), channel_id=1, source_target_pairs={{0,2},{1,3},{2,0},{3,1},{4,6},{5,7},{6,4},{7,5},{8,10},{9,11},{10,... | collective-permute-start | bytes 786440 | tf_op jit(solution)/shard_map/ppermute | solution.py:25
  24.2 0.0 collective-permute-done.3
  24.2 0.1 collective-permute-start.4
  24.3 0.6 %collective-permute-start.12 = (bf16[2,2,64,512]{3,2,1,0:T(8,128)(2,1)S(1)}, bf16[2,2,64,512]{3,2,1,0:T(8,128)(2,1)S(1)}, u32[]{:S(2)}, u32[]{:S(2)}) collective-permute-start(bf16[2,2,64,512]{3,2,1,0:T(8,128)(2,1)S(1)} %pad_maximum_fusion.3), channel_id=1, source_target_pairs={{0,8},{1,9},{2,10},{3,11},{4,12},{5,13},{6,14},{7,15},{8,0},{9,1},... | collective-permute-start | bytes 786440 | tf_op jit(solution)/shard_map/ppermute | solution.py:25
  24.9 5.1 %collective-permute-done.9 = bf16[2,2,64,512]{3,2,1,0:T(8,128)(2,1)S(1)} collective-permute-done((bf16[2,2,64,512]{3,2,1,0:T(8,128)(2,1)S(1)}, bf16[2,2,64,512]{3,2,1,0:T(8,128)(2,1)S(1)}, u32[]{:S(2)}, u32[]{:S(2)}) %collective-permute-start.9) | collective-permute-done | bytes 262176 | tf_op jit(solution)/shard_map/ppermute | solution.py:25
  30.0 0.0 collective-permute-start.10
  30.0 0.0 collective-permute-done.4
  30.1 1.5 %collective-permute-done.10 = bf16[2,2,64,512]{3,2,1,0:T(8,128)(2,1)S(1)} collective-permute-done((bf16[2,2,64,512]{3,2,1,0:T(8,128)(2,1)S(1)}, bf16[2,2,64,512]{3,2,1,0:T(8,128)(2,1)S(1)}, u32[]{:S(2)}, u32[]{:S(2)}) %collective-permute-start.10) | collective-permute-done | bytes 262176 | tf_op jit(solution)/shard_map/ppermute | solution.py:25
  31.5 0.2 collective-permute-start.11
  31.7 0.0 collective-permute-done.12
  31.8 0.1 broadcast_select_fusion.1
  31.9 0.0 copy-start.2
  31.9 0.1 pad_maximum_fusion
  32.0 0.9 %collective-permute-done.11 = bf16[16,1536]{1,0:T(8,128)(2,1)S(1)} collective-permute-done((bf16[16,1536]{1,0:T(8,128)(2,1)S(1)}, bf16[16,1536]{1,0:T(8,128)(2,1)S(1)}, u32[]{:S(2)}, u32[]{:S(2)}) %collective-permute-start.11) | collective-permute-done | bytes 49184 | tf_op jit(solution)/shard_map/ppermute | solution.py:25
  32.9 0.2 fusion.41
  33.0 1.3 %collective-permute-start.13 = (bf16[16,256]{1,0:T(8,128)(2,1)S(1)}, bf16[16,256]{1,0:T(8,128)(2,1)S(1)}, u32[]{:S(2)}, u32[]{:S(2)}) collective-permute-start(bf16[16,256]{1,0:T(8,128)(2,1)S(1)} %get-tuple-element.27), channel_id=1, source_target_pairs={{0,24},{1,25},{2,26},{3,27},{4,28},{5,29},{6,30},{7,31},{8,16},{9,... | collective-permute-start | bytes 24584 | tf_op jit(solution)/shard_map/ppermute | solution.py:25
  34.3 0.0 copy-done
  34.3 0.0 copy-done.2
  34.3 1.1 %fusion.9 = f32[16,256,16]{1,2,0:T(8,128)} fusion(bf16[16,256,256]{2,1,0:T(8,128)(2,1)S(1)} %bitcast.43, bf16[16,16,256]{2,1,0:T(8,128)(2,1)S(1)} %copy-done.2), kind=kOutput, calls=%fused_computation.29 | convolution fusion | flops 33554432 | bytes 2490368 | tf_op jit(solution)/shard_map/rlq,lqp->rlp/dot_general | solution.py:148
  35.4 0.7 %collective-permute-done.13 = bf16[16,256]{1,0:T(8,128)(2,1)S(1)} collective-permute-done((bf16[16,256]{1,0:T(8,128)(2,1)S(1)}, bf16[16,256]{1,0:T(8,128)(2,1)S(1)}, u32[]{:S(2)}, u32[]{:S(2)}) %collective-permute-start.13) | collective-permute-done | bytes 8224 | tf_op jit(solution)/shard_map/ppermute | solution.py:25
  36.1 0.2 convolution_convert_fusion.2
  36.4 0.0 copy-done.4
  36.4 0.2 convolution_convert_fusion.5
  36.6 0.5 %collective-permute-start.14 = (bf16[16,128]{1,0:T(8,128)(2,1)S(1)}, bf16[16,128]{1,0:T(8,128)(2,1)S(1)}, u32[]{:S(2)}, u32[]{:S(2)}) collective-permute-start(bf16[16,128]{1,0:T(8,128)(2,1)S(1)} %convolution_convert_fusion.5), channel_id=1, source_target_pairs={{0,1},{1,0},{2,3},{3,2},{4,5},{5,4},{6,7},{7,6},{8,9},{9,8},{10,11... | collective-permute-start | bytes 12296 | tf_op jit(solution)/shard_map/ppermute | solution.py:25
  37.1 3.1 %collective-permute-done.14 = bf16[16,128]{1,0:T(8,128)(2,1)S(1)} collective-permute-done((bf16[16,128]{1,0:T(8,128)(2,1)S(1)}, bf16[16,128]{1,0:T(8,128)(2,1)S(1)}, u32[]{:S(2)}, u32[]{:S(2)}) %collective-permute-start.14) | collective-permute-done | bytes 4128 | tf_op jit(solution)/shard_map/ppermute | solution.py:25
  40.2 1.8 %collective-permute-start.15 = (bf16[16,256]{1,0:T(8,128)(2,1)S(1)}, bf16[16,256]{1,0:T(8,128)(2,1)S(1)}, u32[]{:S(2)}, u32[]{:S(2)}) collective-permute-start(bf16[16,256]{1,0:T(8,128)(2,1)S(1)} %pad_maximum_fusion.5), channel_id=1, source_target_pairs={{0,2},{1,3},{2,0},{3,1},{4,6},{5,7},{6,4},{7,5},{8,10},{9,11},{10,... | collective-permute-start | bytes 24584 | tf_op jit(solution)/shard_map/ppermute | solution.py:25
  42.1 0.0 copy-start.6
  42.1 0.0 copy-start.9
  42.1 1.8 %collective-permute-done.15 = bf16[16,256]{1,0:T(8,128)(2,1)S(1)} collective-permute-done((bf16[16,256]{1,0:T(8,128)(2,1)S(1)}, bf16[16,256]{1,0:T(8,128)(2,1)S(1)}, u32[]{:S(2)}, u32[]{:S(2)}) %collective-permute-start.15) | collective-permute-done | bytes 8224 | tf_op jit(solution)/shard_map/ppermute | solution.py:25
  43.9 1.2 %convolution_convert_fusion.4 = bf16[16,256]{1,0:T(8,128)(2,1)S(1)} fusion(bf16[256,768]{1,0:T(8,128)(2,1)} %param.19, bf16[16,256]{1,0:T(8,128)(2,1)S(1)} %get-tuple-element.20, bf16[16,256]{1,0:T(8,128)(2,1)S(1)} %get-tuple-element.19, bf16[16,256]{1,0:T(8,128)(2,1)S(1)} %slice.30), kind=kOutput, calls=%fused_computation.6 | convolution fusion | flops 6369280 | bytes 425984 | tf_op jit(solution)/shard_map/dot_general | solution.py:10
  45.1 0.0 copy-done.1
  45.1 0.5 %convolution_convert_fusion.1 = bf16[16,1024]{1,0:T(8,128)(2,1)S(1)} fusion(bf16[1024,640]{1,0:T(8,128)(2,1)S(1)} %copy-done.1, bf16[16,256]{1,0:T(8,128)(2,1)S(1)} %convolution_convert_fusion.4, bf16[16,384]{1,0:T(8,128)(2,1)S(1)} %slice.28), kind=kOutput, calls=%fused_computation.3 | convolution fusion | flops 21028864 | bytes 1363968 | tf_op jit(solution)/shard_map/dot_general | solution.py:10
  45.6 0.0 copy-done.6
  45.6 0.0 copy-done.9
  45.6 1.1 %convolution_add_fusion = f32[16,16,256]{2,1,0:T(8,128)} fusion(bf16[1024,256]{1,0:T(8,128)(2,1)S(1)} %copy-done.9, pred[16,1024]{1,0:T(8,128)(4,1)S(1)} %iota_compare_fusion, f32[16,256,16]{1,2,0:T(8,128)S(1)} %copy-done.6, bf16[16,1024]{1,0:T(8,128)(2,1)S(1)} %convolution_convert_fusion.1), kind=kOutput, calls=%fused_computation | convolution fusion | flops 134545408 | bytes 1097728 | tf_op jit(solution)/shard_map/dot_general | solution.py:16
  (26 shorter events, 0.3 us)
Async XLA Ops:
  0.0 34.3 %copy-start = (bf16[4096,256]{1,0:T(8,128)(2,1)S(1)}, bf16[4096,256]{1,0:T(8,128)(2,1)}, u32[]{:S(2)}) copy-start(bf16[4096,256]{1,0:T(8,128)(2,1)} %param.14) | copy-start | bytes 6291460
  0.0 3.4 %copy-start.5 = (bf16[256,768]{1,0:T(8,128)(2,1)S(1)}, bf16[256,768]{1,0:T(8,128)(2,1)}, u32[]{:S(2)}) copy-start(bf16[256,768]{1,0:T(8,128)(2,1)} %param.18) | copy-start | bytes 1179652
  0.0 6.6 %copy-start.7 = (bf16[64,256]{1,0:T(8,128)(2,1)S(1)}, bf16[64,256]{1,0:T(8,128)(2,1)}, u32[]{:S(2)}) copy-start(bf16[64,256]{1,0:T(8,128)(2,1)} %param.22) | copy-start | bytes 98308
  0.0 6.6 %copy-start.8 = (bf16[64,256]{1,0:T(8,128)(2,1)S(1)}, bf16[64,256]{1,0:T(8,128)(2,1)}, u32[]{:S(2)}) copy-start(bf16[64,256]{1,0:T(8,128)(2,1)} %param.23) | copy-start | bytes 98308
  1.6 12.2 %copy-start.3 = (bf16[128,1536]{1,0:T(8,128)(2,1)S(1)}, bf16[128,1536]{1,0:T(8,128)(2,1)}, u32[]{:S(2)}) copy-start(bf16[128,1536]{1,0:T(8,128)(2,1)} %param.20) | copy-start | bytes 1179652
  3.6 5.7 %collective-permute-start = (bf16[16,768]{1,0:T(8,128)(2,1)S(1)}, bf16[16,768]{1,0:T(8,128)(2,1)S(1)}, u32[]{:S(2)}, u32[]{:S(2)}) collective-permute-start(bf16[16,768]{1,0:T(8,128)(2,1)S(1)} %get-tuple-element.23), channel_id=1, source_target_pairs={{0,1},{1,0},{2,3},{3,2},{4,5},{5,4},{6,7},{7,6},{8,9},{9,8},{10,11... | collective-permute-start | bytes 73736 | tf_op jit(solution)/shard_map/ppermute | solution.py:25
  6.7 5.6 %collective-permute-start.5 = (bf16[64,512]{1,0:T(8,128)(2,1)S(1)}, bf16[64,512]{1,0:T(8,128)(2,1)S(1)}, u32[]{:S(2)}, u32[]{:S(2)}) collective-permute-start(bf16[64,512]{1,0:T(8,128)(2,1)S(1)} %constant_dynamic-update-slice_fusion), channel_id=1, source_target_pairs={{0,4},{1,5},{2,6},{3,7},{4,0},{5,1},{6,2},{7,3},{8,12},{9,13},{10,... | collective-permute-start | bytes 196616 | tf_op jit(solution)/shard_map/ppermute | solution.py:25
  9.3 3.9 %collective-permute-start.1 = (bf16[16,768]{1,0:T(8,128)(2,1)S(1)}, bf16[16,768]{1,0:T(8,128)(2,1)S(1)}, u32[]{:S(2)}, u32[]{:S(2)}) collective-permute-start(bf16[16,768]{1,0:T(8,128)(2,1)S(1)} %fusion.17), channel_id=1, source_target_pairs={{0,2},{1,3},{2,0},{3,1},{4,6},{5,7},{6,4},{7,5},{8,10},{9,11},{10,... | collective-permute-start | bytes 73736 | tf_op jit(solution)/shard_map/ppermute | solution.py:25
  12.3 1.4 %collective-permute-start.6 = (bf16[2,64,512]{2,1,0:T(8,128)(2,1)S(1)}, bf16[2,64,512]{2,1,0:T(8,128)(2,1)S(1)}, u32[]{:S(2)}, u32[]{:S(2)}) collective-permute-start(bf16[2,64,512]{2,1,0:T(8,128)(2,1)S(1)} %pad_maximum_fusion.4), channel_id=1, source_target_pairs={{0,8},{1,9},{2,10},{3,11},{4,12},{5,13},{6,14},{7,15},{8,0},{9,1},... | collective-permute-start | bytes 393224 | tf_op jit(solution)/shard_map/ppermute | solution.py:25
  13.7 2.9 %collective-permute-start.7 = (bf16[2,64,512]{2,1,0:T(8,128)(2,1)S(1)}, bf16[2,64,512]{2,1,0:T(8,128)(2,1)S(1)}, u32[]{:S(2)}, u32[]{:S(2)}) collective-permute-start(bf16[2,64,512]{2,1,0:T(8,128)(2,1)S(1)} %collective-permute-done.6), channel_id=1, source_target_pairs={{0,8},{1,9},{2,10},{3,11},{4,12},{5,13},{6,14},{7,15},{8,0},{9,1},... | collective-permute-start | bytes 393224 | tf_op jit(solution)/shard_map/ppermute | solution.py:25
  14.0 4.5 %collective-permute-start.2 = (bf16[16,1536]{1,0:T(8,128)(2,1)S(1)}, bf16[16,1536]{1,0:T(8,128)(2,1)S(1)}, u32[]{:S(2)}, u32[]{:S(2)}) collective-permute-start(bf16[16,1536]{1,0:T(8,128)(2,1)S(1)} %get-tuple-element.25), channel_id=1, source_target_pairs={{0,12},{1,13},{2,14},{3,15},{4,8},{5,9},{6,10},{7,11},{8,4},{9,5},... | collective-permute-start | bytes 147464 | tf_op jit(solution)/shard_map/ppermute | solution.py:25
  16.6 5.6 %collective-permute-start.8 = (bf16[2,64,512]{2,1,0:T(8,128)(2,1)S(1)}, bf16[2,64,512]{2,1,0:T(8,128)(2,1)S(1)}, u32[]{:S(2)}, u32[]{:S(2)}) collective-permute-start(bf16[2,64,512]{2,1,0:T(8,128)(2,1)S(1)} %collective-permute-done.7), channel_id=1, source_target_pairs={{0,1},{1,0},{2,3},{3,2},{4,5},{5,4},{6,7},{7,6},{8,9},{9,8},{10,11... | collective-permute-start | bytes 393224 | tf_op jit(solution)/shard_map/ppermute | solution.py:25
  18.5 5.7 %collective-permute-start.3 = (bf16[16,1536]{1,0:T(8,128)(2,1)S(1)}, bf16[16,1536]{1,0:T(8,128)(2,1)S(1)}, u32[]{:S(2)}, u32[]{:S(2)}) collective-permute-start(bf16[16,1536]{1,0:T(8,128)(2,1)S(1)} %fusion.12), channel_id=1, source_target_pairs={{0,10},{1,11},{2,8},{3,9},{4,14},{5,15},{6,12},{7,13},{8,2},{9,3},... | collective-permute-start | bytes 147464 | tf_op jit(solution)/shard_map/ppermute | solution.py:25
  22.2 7.8 %collective-permute-start.9 = (bf16[2,2,64,512]{3,2,1,0:T(8,128)(2,1)S(1)}, bf16[2,2,64,512]{3,2,1,0:T(8,128)(2,1)S(1)}, u32[]{:S(2)}, u32[]{:S(2)}) collective-permute-start(bf16[2,2,64,512]{3,2,1,0:T(8,128)(2,1)S(1)} %pad_maximum_fusion.3), channel_id=1, source_target_pairs={{0,2},{1,3},{2,0},{3,1},{4,6},{5,7},{6,4},{7,5},{8,10},{9,11},{10,... | collective-permute-start | bytes 786440 | tf_op jit(solution)/shard_map/ppermute | solution.py:25
  24.2 5.8 %collective-permute-start.4 = (bf16[16,1536]{1,0:T(8,128)(2,1)S(1)}, bf16[16,1536]{1,0:T(8,128)(2,1)S(1)}, u32[]{:S(2)}, u32[]{:S(2)}) collective-permute-start(bf16[16,1536]{1,0:T(8,128)(2,1)S(1)} %fusion.16), channel_id=1, source_target_pairs={{0,9},{1,8},{2,11},{3,10},{4,13},{5,12},{6,15},{7,14},{8,1},{9,0},... | collective-permute-start | bytes 147464 | tf_op jit(solution)/shard_map/ppermute | solution.py:25
  24.3 7.4 %collective-permute-start.12 = (bf16[2,2,64,512]{3,2,1,0:T(8,128)(2,1)S(1)}, bf16[2,2,64,512]{3,2,1,0:T(8,128)(2,1)S(1)}, u32[]{:S(2)}, u32[]{:S(2)}) collective-permute-start(bf16[2,2,64,512]{3,2,1,0:T(8,128)(2,1)S(1)} %pad_maximum_fusion.3), channel_id=1, source_target_pairs={{0,8},{1,9},{2,10},{3,11},{4,12},{5,13},{6,14},{7,15},{8,0},{9,1},... | collective-permute-start | bytes 786440 | tf_op jit(solution)/shard_map/ppermute | solution.py:25
  30.0 1.5 %collective-permute-start.10 = (bf16[2,2,64,512]{3,2,1,0:T(8,128)(2,1)S(1)}, bf16[2,2,64,512]{3,2,1,0:T(8,128)(2,1)S(1)}, u32[]{:S(2)}, u32[]{:S(2)}) collective-permute-start(bf16[2,2,64,512]{3,2,1,0:T(8,128)(2,1)S(1)} %collective-permute-done.9), channel_id=1, source_target_pairs={{0,8},{1,9},{2,10},{3,11},{4,12},{5,13},{6,14},{7,15},{8,0},{9,1},... | collective-permute-start | bytes 786440 | tf_op jit(solution)/shard_map/ppermute | solution.py:25
  31.5 1.3 %collective-permute-start.11 = (bf16[16,1536]{1,0:T(8,128)(2,1)S(1)}, bf16[16,1536]{1,0:T(8,128)(2,1)S(1)}, u32[]{:S(2)}, u32[]{:S(2)}) collective-permute-start(bf16[16,1536]{1,0:T(8,128)(2,1)S(1)} %convert_element_type.86), channel_id=1, source_target_pairs={{0,8},{1,9},{2,10},{3,11},{4,12},{5,13},{6,14},{7,15},{8,0},{9,1},... | collective-permute-start | bytes 147464 | tf_op jit(solution)/shard_map/ppermute | solution.py:25
  31.9 2.4 %copy-start.2 = (bf16[16,16,256]{2,1,0:T(8,128)(2,1)S(1)}, bf16[16,16,256]{2,1,0:T(8,128)(2,1)}, u32[]{:S(2)}) copy-start(bf16[16,16,256]{2,1,0:T(8,128)(2,1)} %param.12) | copy-start | bytes 393220
  33.0 3.1 %collective-permute-start.13 = (bf16[16,256]{1,0:T(8,128)(2,1)S(1)}, bf16[16,256]{1,0:T(8,128)(2,1)S(1)}, u32[]{:S(2)}, u32[]{:S(2)}) collective-permute-start(bf16[16,256]{1,0:T(8,128)(2,1)S(1)} %get-tuple-element.27), channel_id=1, source_target_pairs={{0,24},{1,25},{2,26},{3,27},{4,28},{5,29},{6,30},{7,31},{8,16},{9,... | collective-permute-start | bytes 24584 | tf_op jit(solution)/shard_map/ppermute | solution.py:25
  34.3 2.0 %copy-start.4 = (bf16[128,1536]{1,0:T(8,128)(2,1)S(1)}, bf16[128,1536]{1,0:T(8,128)(2,1)}, u32[]{:S(2)}) copy-start(bf16[128,1536]{1,0:T(8,128)(2,1)} %param.21) | copy-start | bytes 1179652
  35.4 9.7 %copy-start.1 = (bf16[1024,640]{1,0:T(8,128)(2,1)S(1)}, bf16[1024,640]{1,0:T(8,128)(2,1)}, u32[]{:S(2)}) copy-start(bf16[1024,640]{1,0:T(8,128)(2,1)} %param.17) | copy-start | bytes 3932164
  36.6 3.6 %collective-permute-start.14 = (bf16[16,128]{1,0:T(8,128)(2,1)S(1)}, bf16[16,128]{1,0:T(8,128)(2,1)S(1)}, u32[]{:S(2)}, u32[]{:S(2)}) collective-permute-start(bf16[16,128]{1,0:T(8,128)(2,1)S(1)} %convolution_convert_fusion.5), channel_id=1, source_target_pairs={{0,1},{1,0},{2,3},{3,2},{4,5},{5,4},{6,7},{7,6},{8,9},{9,8},{10,11... | collective-permute-start | bytes 12296 | tf_op jit(solution)/shard_map/ppermute | solution.py:25
  40.2 3.7 %collective-permute-start.15 = (bf16[16,256]{1,0:T(8,128)(2,1)S(1)}, bf16[16,256]{1,0:T(8,128)(2,1)S(1)}, u32[]{:S(2)}, u32[]{:S(2)}) collective-permute-start(bf16[16,256]{1,0:T(8,128)(2,1)S(1)} %pad_maximum_fusion.5), channel_id=1, source_target_pairs={{0,2},{1,3},{2,0},{3,1},{4,6},{5,7},{6,4},{7,5},{8,10},{9,11},{10,... | collective-permute-start | bytes 24584 | tf_op jit(solution)/shard_map/ppermute | solution.py:25
  42.1 3.6 %copy-start.6 = (f32[16,256,16]{1,2,0:T(8,128)S(1)}, f32[16,256,16]{1,2,0:T(8,128)}, u32[]{:S(2)}) copy-start(f32[16,256,16]{1,2,0:T(8,128)} %fusion.9) | copy-start | bytes 786436
  42.1 3.6 %copy-start.9 = (bf16[1024,256]{1,0:T(8,128)(2,1)S(1)}, bf16[1024,256]{1,0:T(8,128)(2,1)}, u32[]{:S(2)}) copy-start(bf16[1024,256]{1,0:T(8,128)(2,1)} %param.15) | copy-start | bytes 1572868

commit v17 on v13

--- a/solution.py
+++ b/solution.py
@@ -91,13 +91,11 @@
 
     far = pair // 2
 
-    flux = jnp.einsum(
-        "rlq,leq->rle",
-        source,
-        leaf_flux.reshape(leaves, edge_count, points),
-        preferred_element_type=jnp.float32,
-    )
-    flux = rounded(flux).reshape(rhs_count, leaves * edge_count)
+    every = contract(source.reshape(-1, points), leaf_flux)
+    every = every.reshape(rhs_count, leaves, leaves * edge_count)
+    owner = jnp.arange(leaves * edge_count) // edge_count
+    own = owner == jnp.arange(leaves)[:, None]
+    flux = rounded(jnp.sum(jnp.where(own, every, 0.0), axis=1))
     box_state = rounded(contract(flux, box_up))
     first_sum = product(box_state[:, inner_dev:], up_one)
 

time: 46 us -> 44.8 us (0.974)
  matrix products: 8.02 us -> 6.9 us
    dot_general x1 -> x0, matrix products: 1.44 us -> none  [per_device(): jnp.einsum('rlq,leq->rle', source, leaf_flux.reshape(leaves, edge_count,...]
    dot_general x5 -> x6, matrix products: 3.88 us -> 4.21 us  [contract(): lax.dot_general(left, right, (((1,), (1,)), ((), ())), preferred_element_...]
where the time goes in v17:
time: 44.8 us; the launch traced here: 44.6 us
  starting transfers between devices  19 us (42%)
  waiting for transfers between devices  18 us (40%)
  matrix products  6.9 us (15%)
  other arithmetic  0.49 us (1%)
    ppermute x14, starting transfers between devices, swap(): return lax.ppermute(value, AXES, [(i, i ^ mask) for i in range(count)])  19 us
    ppermute x14, waiting for transfers between devices, swap(): return lax.ppermute(value, AXES, [(i, i ^ mask) for i in range(count)])  18 us
    dot_general x6, matrix products, contract(): lax.dot_general(left, right, (((1,), (1,)), ((), ())), preferred_element_...  4.21 us
    dot_general x4, matrix products, product(): return jnp.dot(left, right, preferred_element_type=jnp.float32)  1.6 us
    dot_general x1, matrix products, per_device(): jnp.einsum('rlq,lqp->rlp', source, leaf_particular.reshape(leaves, points...  1.09 us
  transfers between devices with their start and end apart: 14, of which 10 were waited for; matrix products, arithmetic and copies ran while one was open for 4% of the time, Pallas kernels for 0%

profile of v17, /device:TPU:0, one launch (start us, length us, event | category | flops | bytes accessed | tf_op | source)
XLA Modules:
  0.0 44.6 jit_solution(13764649346162029883)
XLA Ops:
  0.0 0.0 copy-start
  0.0 0.0 copy-start.1
  0.0 0.0 copy-start.5
  0.0 0.0 copy-start.8
  0.1 1.6 %fusion = bf16[16,1024]{1,0:T(8,128)(2,1)S(1)} fusion(bf16[16,16,256]{2,1,0:T(8,128)(2,1)} %param.12, bf16[1024,256]{1,0:T(8,128)(2,1)} %param.13, pred[16,1024]{1,0:T(8,128)(4,1)S(1)} %iota_compare_fusion), kind=kOutput, calls=%fused_computation.1 | convolution fusion | flops 134725632 | bytes 704512 | tf_op jit(solution)/shard_map/dot_general | solution.py:10
  1.7 0.0 copy-done.1
  1.7 0.0 copy-start.9
  1.7 0.0 copy-start.3
  1.7 0.4 convolution_convert_fusion.2
  2.2 0.0 copy-done.5
  2.2 0.2 fusion.40
  2.4 3.0 %collective-permute-start = (bf16[16,768]{1,0:T(8,128)(2,1)S(1)}, bf16[16,768]{1,0:T(8,128)(2,1)S(1)}, u32[]{:S(2)}, u32[]{:S(2)}) collective-permute-start(bf16[16,768]{1,0:T(8,128)(2,1)S(1)} %get-tuple-element.23), channel_id=1, source_target_pairs={{0,1},{1,0},{2,3},{3,2},{4,5},{5,4},{6,7},{7,6},{8,9},{9,8},{10,11... | collective-permute-start | bytes 73736 | tf_op jit(solution)/shard_map/ppermute | solution.py:25
  5.4 0.0 copy-done.8
  5.4 1.8 %collective-permute-done = bf16[16,768]{1,0:T(8,128)(2,1)S(1)} collective-permute-done((bf16[16,768]{1,0:T(8,128)(2,1)S(1)}, bf16[16,768]{1,0:T(8,128)(2,1)S(1)}, u32[]{:S(2)}, u32[]{:S(2)}) %collective-permute-start) | collective-permute-done | bytes 24608 | tf_op jit(solution)/shard_map/ppermute | solution.py:25
  7.2 2.1 %collective-permute-start.1 = (bf16[16,768]{1,0:T(8,128)(2,1)S(1)}, bf16[16,768]{1,0:T(8,128)(2,1)S(1)}, u32[]{:S(2)}, u32[]{:S(2)}) collective-permute-start(bf16[16,768]{1,0:T(8,128)(2,1)S(1)} %fusion.17), channel_id=1, source_target_pairs={{0,2},{1,3},{2,0},{3,1},{4,6},{5,7},{6,4},{7,5},{8,10},{9,11},{10,... | collective-permute-start | bytes 73736 | tf_op jit(solution)/shard_map/ppermute | solution.py:25
  9.3 0.0 copy-done.9
  9.4 2.6 %collective-permute-start.5 = (bf16[64,512]{1,0:T(8,128)(2,1)S(1)}, bf16[64,512]{1,0:T(8,128)(2,1)S(1)}, u32[]{:S(2)}, u32[]{:S(2)}) collective-permute-start(bf16[64,512]{1,0:T(8,128)(2,1)S(1)} %constant_dynamic-update-slice_fusion), channel_id=1, source_target_pairs={{0,4},{1,5},{2,6},{3,7},{4,0},{5,1},{6,2},{7,3},{8,12},{9,13},{10,... | collective-permute-start | bytes 196616 | tf_op jit(solution)/shard_map/ppermute | solution.py:25
  11.9 0.0 collective-permute-done.1
  12.0 0.0 copy-done.3
  12.0 0.2 fusion.41
  12.1 0.1 collective-permute-start.2
  12.2 2.8 %collective-permute-done.5 = bf16[64,512]{1,0:T(8,128)(2,1)S(1)} collective-permute-done((bf16[64,512]{1,0:T(8,128)(2,1)S(1)}, bf16[64,512]{1,0:T(8,128)(2,1)S(1)}, u32[]{:S(2)}, u32[]{:S(2)}) %collective-permute-start.5) | collective-permute-done | bytes 65568 | tf_op jit(solution)/shard_map/ppermute | solution.py:25
  15.1 1.7 %collective-permute-start.6 = (bf16[2,64,512]{2,1,0:T(8,128)(2,1)S(1)}, bf16[2,64,512]{2,1,0:T(8,128)(2,1)S(1)}, u32[]{:S(2)}, u32[]{:S(2)}) collective-permute-start(bf16[2,64,512]{2,1,0:T(8,128)(2,1)S(1)} %pad_maximum_fusion.4), channel_id=1, source_target_pairs={{0,1},{1,0},{2,3},{3,2},{4,5},{5,4},{6,7},{7,6},{8,9},{9,8},{10,11... | collective-permute-start | bytes 393224 | tf_op jit(solution)/shard_map/ppermute | solution.py:25
  16.7 0.3 collective-permute-done.2
  17.0 1.3 %collective-permute-start.3 = (bf16[16,1536]{1,0:T(8,128)(2,1)S(1)}, bf16[16,1536]{1,0:T(8,128)(2,1)S(1)}, u32[]{:S(2)}, u32[]{:S(2)}) collective-permute-start(bf16[16,1536]{1,0:T(8,128)(2,1)S(1)} %fusion.12), channel_id=1, source_target_pairs={{0,10},{1,11},{2,8},{3,9},{4,14},{5,15},{6,12},{7,13},{8,2},{9,3},... | collective-permute-start | bytes 147464 | tf_op jit(solution)/shard_map/ppermute | solution.py:25
  18.4 1.7 %collective-permute-done.6 = bf16[2,64,512]{2,1,0:T(8,128)(2,1)S(1)} collective-permute-done((bf16[2,64,512]{2,1,0:T(8,128)(2,1)S(1)}, bf16[2,64,512]{2,1,0:T(8,128)(2,1)S(1)}, u32[]{:S(2)}, u32[]{:S(2)}) %collective-permute-start.6) | collective-permute-done | bytes 131104 | tf_op jit(solution)/shard_map/ppermute | solution.py:25
  20.2 1.2 %collective-permute-start.7 = (bf16[2,2,64,512]{3,2,1,0:T(8,128)(2,1)S(1)}, bf16[2,2,64,512]{3,2,1,0:T(8,128)(2,1)S(1)}, u32[]{:S(2)}, u32[]{:S(2)}) collective-permute-start(bf16[2,2,64,512]{3,2,1,0:T(8,128)(2,1)S(1)} %pad_maximum_fusion.3), channel_id=1, source_target_pairs={{0,2},{1,3},{2,0},{3,1},{4,6},{5,7},{6,4},{7,5},{8,10},{9,11},{10,... | collective-permute-start | bytes 786440 | tf_op jit(solution)/shard_map/ppermute | solution.py:25
  21.3 0.0 collective-permute-done.3
  21.4 1.2 %collective-permute-start.4 = (bf16[16,1536]{1,0:T(8,128)(2,1)S(1)}, bf16[16,1536]{1,0:T(8,128)(2,1)S(1)}, u32[]{:S(2)}, u32[]{:S(2)}) collective-permute-start(bf16[16,1536]{1,0:T(8,128)(2,1)S(1)} %fusion.16), channel_id=1, source_target_pairs={{0,9},{1,8},{2,11},{3,10},{4,13},{5,12},{6,15},{7,14},{8,1},{9,0},... | collective-permute-start | bytes 147464 | tf_op jit(solution)/shard_map/ppermute | solution.py:25
  22.6 0.7 %collective-permute-start.10 = (bf16[2,2,64,512]{3,2,1,0:T(8,128)(2,1)S(1)}, bf16[2,2,64,512]{3,2,1,0:T(8,128)(2,1)S(1)}, u32[]{:S(2)}, u32[]{:S(2)}) collective-permute-start(bf16[2,2,64,512]{3,2,1,0:T(8,128)(2,1)S(1)} %pad_maximum_fusion.3), channel_id=1, source_target_pairs={{0,8},{1,9},{2,10},{3,11},{4,12},{5,13},{6,14},{7,15},{8,0},{9,1},... | collective-permute-start | bytes 786440 | tf_op jit(solution)/shard_map/ppermute | solution.py:25
  23.2 4.7 %collective-permute-done.7 = bf16[2,2,64,512]{3,2,1,0:T(8,128)(2,1)S(1)} collective-permute-done((bf16[2,2,64,512]{3,2,1,0:T(8,128)(2,1)S(1)}, bf16[2,2,64,512]{3,2,1,0:T(8,128)(2,1)S(1)}, u32[]{:S(2)}, u32[]{:S(2)}) %collective-permute-start.7) | collective-permute-done | bytes 262176 | tf_op jit(solution)/shard_map/ppermute | solution.py:25
  27.9 0.0 collective-permute-start.8
  27.9 0.0 collective-permute-done.4
  28.0 1.5 %collective-permute-done.8 = bf16[2,2,64,512]{3,2,1,0:T(8,128)(2,1)S(1)} collective-permute-done((bf16[2,2,64,512]{3,2,1,0:T(8,128)(2,1)S(1)}, bf16[2,2,64,512]{3,2,1,0:T(8,128)(2,1)S(1)}, u32[]{:S(2)}, u32[]{:S(2)}) %collective-permute-start.8) | collective-permute-done | bytes 262176 | tf_op jit(solution)/shard_map/ppermute | solution.py:25
  29.5 0.2 collective-permute-start.9
  29.6 0.0 collective-permute-done.10
  29.7 0.1 broadcast_select_fusion.1
  29.8 0.0 copy-start.4
  29.8 0.1 pad_maximum_fusion
  29.9 0.0 copy-start.7
  29.9 0.8 %collective-permute-done.9 = bf16[16,1536]{1,0:T(8,128)(2,1)S(1)} collective-permute-done((bf16[16,1536]{1,0:T(8,128)(2,1)S(1)}, bf16[16,1536]{1,0:T(8,128)(2,1)S(1)}, u32[]{:S(2)}, u32[]{:S(2)}) %collective-permute-start.9) | collective-permute-done | bytes 49184 | tf_op jit(solution)/shard_map/ppermute | solution.py:25
  30.8 0.2 fusion.42
  31.0 1.4 %collective-permute-start.11 = (bf16[16,256]{1,0:T(8,128)(2,1)S(1)}, bf16[16,256]{1,0:T(8,128)(2,1)S(1)}, u32[]{:S(2)}, u32[]{:S(2)}) collective-permute-start(bf16[16,256]{1,0:T(8,128)(2,1)S(1)} %get-tuple-element.27), channel_id=1, source_target_pairs={{0,24},{1,25},{2,26},{3,27},{4,28},{5,29},{6,30},{7,31},{8,16},{9,... | collective-permute-start | bytes 24584 | tf_op jit(solution)/shard_map/ppermute | solution.py:25
  32.4 1.6 %collective-permute-done.11 = bf16[16,256]{1,0:T(8,128)(2,1)S(1)} collective-permute-done((bf16[16,256]{1,0:T(8,128)(2,1)S(1)}, bf16[16,256]{1,0:T(8,128)(2,1)S(1)}, u32[]{:S(2)}, u32[]{:S(2)}) %collective-permute-start.11) | collective-permute-done | bytes 8224 | tf_op jit(solution)/shard_map/ppermute | solution.py:25
  34.0 0.2 convolution_convert_fusion.1
  34.3 0.0 copy-done.4
  34.3 0.2 convolution_convert_fusion.4
  34.5 1.7 %collective-permute-start.12 = (bf16[16,128]{1,0:T(8,128)(2,1)S(1)}, bf16[16,128]{1,0:T(8,128)(2,1)S(1)}, u32[]{:S(2)}, u32[]{:S(2)}) collective-permute-start(bf16[16,128]{1,0:T(8,128)(2,1)S(1)} %convolution_convert_fusion.4), channel_id=1, source_target_pairs={{0,1},{1,0},{2,3},{3,2},{4,5},{5,4},{6,7},{7,6},{8,9},{9,8},{10,11... | collective-permute-start | bytes 12296 | tf_op jit(solution)/shard_map/ppermute | solution.py:25
  36.2 1.9 %collective-permute-done.12 = bf16[16,128]{1,0:T(8,128)(2,1)S(1)} collective-permute-done((bf16[16,128]{1,0:T(8,128)(2,1)S(1)}, bf16[16,128]{1,0:T(8,128)(2,1)S(1)}, u32[]{:S(2)}, u32[]{:S(2)}) %collective-permute-start.12) | collective-permute-done | bytes 4128 | tf_op jit(solution)/shard_map/ppermute | solution.py:25
  38.1 1.8 %collective-permute-start.13 = (bf16[16,256]{1,0:T(8,128)(2,1)S(1)}, bf16[16,256]{1,0:T(8,128)(2,1)S(1)}, u32[]{:S(2)}, u32[]{:S(2)}) collective-permute-start(bf16[16,256]{1,0:T(8,128)(2,1)S(1)} %pad_maximum_fusion.5), channel_id=1, source_target_pairs={{0,2},{1,3},{2,0},{3,1},{4,6},{5,7},{6,4},{7,5},{8,10},{9,11},{10,... | collective-permute-start | bytes 24584 | tf_op jit(solution)/shard_map/ppermute | solution.py:25
  39.9 0.0 copy-done
  39.9 0.0 copy-done.7
  39.9 0.0 copy-start.2
  40.0 1.1 %fusion.10 = f32[16,256,16]{1,2,0:T(8,128)} fusion(bf16[16,256,256]{2,1,0:T(8,128)(2,1)S(1)} %bitcast.43, bf16[16,16,256]{2,1,0:T(8,128)(2,1)S(1)} %copy-done.7), kind=kOutput, calls=%fused_computation.28 | convolution fusion | flops 33554432 | bytes 2490368 | tf_op jit(solution)/shard_map/rlq,lqp->rlp/dot_general | solution.py:145
  41.0 0.0 copy-start.6
  41.0 0.0 copy-start.10
  41.1 0.8 %collective-permute-done.13 = bf16[16,256]{1,0:T(8,128)(2,1)S(1)} collective-permute-done((bf16[16,256]{1,0:T(8,128)(2,1)S(1)}, bf16[16,256]{1,0:T(8,128)(2,1)S(1)}, u32[]{:S(2)}, u32[]{:S(2)}) %collective-permute-start.13) | collective-permute-done | bytes 8224 | tf_op jit(solution)/shard_map/ppermute | solution.py:25
  41.9 1.2 %convolution_convert_fusion.3 = bf16[16,256]{1,0:T(8,128)(2,1)S(1)} fusion(bf16[256,768]{1,0:T(8,128)(2,1)} %param.19, bf16[16,256]{1,0:T(8,128)(2,1)S(1)} %get-tuple-element.20, bf16[16,256]{1,0:T(8,128)(2,1)S(1)} %get-tuple-element.19, bf16[16,256]{1,0:T(8,128)(2,1)S(1)} %slice.30), kind=kOutput, calls=%fused_computation.6 | convolution fusion | flops 6369280 | bytes 425984 | tf_op jit(solution)/shard_map/dot_general | solution.py:10
  43.0 0.0 copy-done.2
  43.0 0.5 %convolution_convert_fusion = bf16[16,1024]{1,0:T(8,128)(2,1)S(1)} fusion(bf16[1024,640]{1,0:T(8,128)(2,1)S(1)} %copy-done.2, bf16[16,256]{1,0:T(8,128)(2,1)S(1)} %convolution_convert_fusion.3, bf16[16,384]{1,0:T(8,128)(2,1)S(1)} %slice.28), kind=kOutput, calls=%fused_computation.3 | convolution fusion | flops 21028864 | bytes 1363968 | tf_op jit(solution)/shard_map/dot_general | solution.py:10
  43.5 0.0 copy-done.6
  43.6 0.0 copy-done.10
  43.6 1.1 %convolution_add_fusion = f32[16,16,256]{2,1,0:T(8,128)} fusion(bf16[1024,256]{1,0:T(8,128)(2,1)S(1)} %copy-done.10, pred[16,1024]{1,0:T(8,128)(4,1)S(1)} %iota_compare_fusion, f32[16,256,16]{1,2,0:T(8,128)S(1)} %copy-done.6, bf16[16,1024]{1,0:T(8,128)(2,1)S(1)} %convolution_convert_fusion), kind=kOutput, calls=%fused_computation.2 | convolution fusion | flops 134545408 | bytes 1097728 | tf_op jit(solution)/shard_map/dot_general | solution.py:16
  (23 shorter events, 0.3 us)
Async XLA Ops:
  0.0 39.9 %copy-start = (bf16[4096,256]{1,0:T(8,128)(2,1)S(1)}, bf16[4096,256]{1,0:T(8,128)(2,1)}, u32[]{:S(2)}) copy-start(bf16[4096,256]{1,0:T(8,128)(2,1)} %param.14) | copy-start | bytes 6291460
  0.0 1.7 %copy-start.1 = (bf16[640,1024]{1,0:T(8,128)(2,1)S(1)}, bf16[640,1024]{1,0:T(8,128)(2,1)}, u32[]{:S(2)}) copy-start(bf16[640,1024]{1,0:T(8,128)(2,1)} %param.16) | copy-start | bytes 3932164
  0.0 2.2 %copy-start.5 = (bf16[256,768]{1,0:T(8,128)(2,1)S(1)}, bf16[256,768]{1,0:T(8,128)(2,1)}, u32[]{:S(2)}) copy-start(bf16[256,768]{1,0:T(8,128)(2,1)} %param.18) | copy-start | bytes 1179652
  0.0 5.3 %copy-start.8 = (bf16[64,256]{1,0:T(8,128)(2,1)S(1)}, bf16[64,256]{1,0:T(8,128)(2,1)}, u32[]{:S(2)}) copy-start(bf16[64,256]{1,0:T(8,128)(2,1)} %param.22) | copy-start | bytes 98308
  1.7 7.6 %copy-start.9 = (bf16[64,256]{1,0:T(8,128)(2,1)S(1)}, bf16[64,256]{1,0:T(8,128)(2,1)}, u32[]{:S(2)}) copy-start(bf16[64,256]{1,0:T(8,128)(2,1)} %param.23) | copy-start | bytes 98308
  1.7 10.2 %copy-start.3 = (bf16[128,1536]{1,0:T(8,128)(2,1)S(1)}, bf16[128,1536]{1,0:T(8,128)(2,1)}, u32[]{:S(2)}) copy-start(bf16[128,1536]{1,0:T(8,128)(2,1)} %param.20) | copy-start | bytes 1179652
  2.4 4.8 %collective-permute-start = (bf16[16,768]{1,0:T(8,128)(2,1)S(1)}, bf16[16,768]{1,0:T(8,128)(2,1)S(1)}, u32[]{:S(2)}, u32[]{:S(2)}) collective-permute-start(bf16[16,768]{1,0:T(8,128)(2,1)S(1)} %get-tuple-element.23), channel_id=1, source_target_pairs={{0,1},{1,0},{2,3},{3,2},{4,5},{5,4},{6,7},{7,6},{8,9},{9,8},{10,11... | collective-permute-start | bytes 73736 | tf_op jit(solution)/shard_map/ppermute | solution.py:25
  7.2 4.7 %collective-permute-start.1 = (bf16[16,768]{1,0:T(8,128)(2,1)S(1)}, bf16[16,768]{1,0:T(8,128)(2,1)S(1)}, u32[]{:S(2)}, u32[]{:S(2)}) collective-permute-start(bf16[16,768]{1,0:T(8,128)(2,1)S(1)} %fusion.17), channel_id=1, source_target_pairs={{0,2},{1,3},{2,0},{3,1},{4,6},{5,7},{6,4},{7,5},{8,10},{9,11},{10,... | collective-permute-start | bytes 73736 | tf_op jit(solution)/shard_map/ppermute | solution.py:25
  9.4 5.7 %collective-permute-start.5 = (bf16[64,512]{1,0:T(8,128)(2,1)S(1)}, bf16[64,512]{1,0:T(8,128)(2,1)S(1)}, u32[]{:S(2)}, u32[]{:S(2)}) collective-permute-start(bf16[64,512]{1,0:T(8,128)(2,1)S(1)} %constant_dynamic-update-slice_fusion), channel_id=1, source_target_pairs={{0,4},{1,5},{2,6},{3,7},{4,0},{5,1},{6,2},{7,3},{8,12},{9,13},{10,... | collective-permute-start | bytes 196616 | tf_op jit(solution)/shard_map/ppermute | solution.py:25
  12.1 4.9 %collective-permute-start.2 = (bf16[16,1536]{1,0:T(8,128)(2,1)S(1)}, bf16[16,1536]{1,0:T(8,128)(2,1)S(1)}, u32[]{:S(2)}, u32[]{:S(2)}) collective-permute-start(bf16[16,1536]{1,0:T(8,128)(2,1)S(1)} %get-tuple-element.25), channel_id=1, source_target_pairs={{0,12},{1,13},{2,14},{3,15},{4,8},{5,9},{6,10},{7,11},{8,4},{9,5},... | collective-permute-start | bytes 147464 | tf_op jit(solution)/shard_map/ppermute | solution.py:25
  15.1 5.0 %collective-permute-start.6 = (bf16[2,64,512]{2,1,0:T(8,128)(2,1)S(1)}, bf16[2,64,512]{2,1,0:T(8,128)(2,1)S(1)}, u32[]{:S(2)}, u32[]{:S(2)}) collective-permute-start(bf16[2,64,512]{2,1,0:T(8,128)(2,1)S(1)} %pad_maximum_fusion.4), channel_id=1, source_target_pairs={{0,1},{1,0},{2,3},{3,2},{4,5},{5,4},{6,7},{7,6},{8,9},{9,8},{10,11... | collective-permute-start | bytes 393224 | tf_op jit(solution)/shard_map/ppermute | solution.py:25
  17.0 4.3 %collective-permute-start.3 = (bf16[16,1536]{1,0:T(8,128)(2,1)S(1)}, bf16[16,1536]{1,0:T(8,128)(2,1)S(1)}, u32[]{:S(2)}, u32[]{:S(2)}) collective-permute-start(bf16[16,1536]{1,0:T(8,128)(2,1)S(1)} %fusion.12), channel_id=1, source_target_pairs={{0,10},{1,11},{2,8},{3,9},{4,14},{5,15},{6,12},{7,13},{8,2},{9,3},... | collective-permute-start | bytes 147464 | tf_op jit(solution)/shard_map/ppermute | solution.py:25
  20.2 7.8 %collective-permute-start.7 = (bf16[2,2,64,512]{3,2,1,0:T(8,128)(2,1)S(1)}, bf16[2,2,64,512]{3,2,1,0:T(8,128)(2,1)S(1)}, u32[]{:S(2)}, u32[]{:S(2)}) collective-permute-start(bf16[2,2,64,512]{3,2,1,0:T(8,128)(2,1)S(1)} %pad_maximum_fusion.3), channel_id=1, source_target_pairs={{0,2},{1,3},{2,0},{3,1},{4,6},{5,7},{6,4},{7,5},{8,10},{9,11},{10,... | collective-permute-start | bytes 786440 | tf_op jit(solution)/shard_map/ppermute | solution.py:25
  21.4 6.6 %collective-permute-start.4 = (bf16[16,1536]{1,0:T(8,128)(2,1)S(1)}, bf16[16,1536]{1,0:T(8,128)(2,1)S(1)}, u32[]{:S(2)}, u32[]{:S(2)}) collective-permute-start(bf16[16,1536]{1,0:T(8,128)(2,1)S(1)} %fusion.16), channel_id=1, source_target_pairs={{0,9},{1,8},{2,11},{3,10},{4,13},{5,12},{6,15},{7,14},{8,1},{9,0},... | collective-permute-start | bytes 147464 | tf_op jit(solution)/shard_map/ppermute | solution.py:25
  22.6 7.1 %collective-permute-start.10 = (bf16[2,2,64,512]{3,2,1,0:T(8,128)(2,1)S(1)}, bf16[2,2,64,512]{3,2,1,0:T(8,128)(2,1)S(1)}, u32[]{:S(2)}, u32[]{:S(2)}) collective-permute-start(bf16[2,2,64,512]{3,2,1,0:T(8,128)(2,1)S(1)} %pad_maximum_fusion.3), channel_id=1, source_target_pairs={{0,8},{1,9},{2,10},{3,11},{4,12},{5,13},{6,14},{7,15},{8,0},{9,1},... | collective-permute-start | bytes 786440 | tf_op jit(solution)/shard_map/ppermute | solution.py:25
  27.9 1.5 %collective-permute-start.8 = (bf16[2,2,64,512]{3,2,1,0:T(8,128)(2,1)S(1)}, bf16[2,2,64,512]{3,2,1,0:T(8,128)(2,1)S(1)}, u32[]{:S(2)}, u32[]{:S(2)}) collective-permute-start(bf16[2,2,64,512]{3,2,1,0:T(8,128)(2,1)S(1)} %collective-permute-done.7), channel_id=1, source_target_pairs={{0,8},{1,9},{2,10},{3,11},{4,12},{5,13},{6,14},{7,15},{8,0},{9,1},... | collective-permute-start | bytes 786440 | tf_op jit(solution)/shard_map/ppermute | solution.py:25
  29.5 1.3 %collective-permute-start.9 = (bf16[16,1536]{1,0:T(8,128)(2,1)S(1)}, bf16[16,1536]{1,0:T(8,128)(2,1)S(1)}, u32[]{:S(2)}, u32[]{:S(2)}) collective-permute-start(bf16[16,1536]{1,0:T(8,128)(2,1)S(1)} %convert_element_type.82), channel_id=1, source_target_pairs={{0,8},{1,9},{2,10},{3,11},{4,12},{5,13},{6,14},{7,15},{8,0},{9,1},... | collective-permute-start | bytes 147464 | tf_op jit(solution)/shard_map/ppermute | solution.py:25
  29.8 4.5 %copy-start.4 = (bf16[128,1536]{1,0:T(8,128)(2,1)S(1)}, bf16[128,1536]{1,0:T(8,128)(2,1)}, u32[]{:S(2)}) copy-start(bf16[128,1536]{1,0:T(8,128)(2,1)} %param.21) | copy-start | bytes 1179652
  29.9 10.0 %copy-start.7 = (bf16[16,16,256]{2,1,0:T(8,128)(2,1)S(1)}, bf16[16,16,256]{2,1,0:T(8,128)(2,1)}, u32[]{:S(2)}) copy-start(bf16[16,16,256]{2,1,0:T(8,128)(2,1)} %param.12) | copy-start | bytes 393220
  31.0 3.1 %collective-permute-start.11 = (bf16[16,256]{1,0:T(8,128)(2,1)S(1)}, bf16[16,256]{1,0:T(8,128)(2,1)S(1)}, u32[]{:S(2)}, u32[]{:S(2)}) collective-permute-start(bf16[16,256]{1,0:T(8,128)(2,1)S(1)} %get-tuple-element.27), channel_id=1, source_target_pairs={{0,24},{1,25},{2,26},{3,27},{4,28},{5,29},{6,30},{7,31},{8,16},{9,... | collective-permute-start | bytes 24584 | tf_op jit(solution)/shard_map/ppermute | solution.py:25
  34.5 3.6 %collective-permute-start.12 = (bf16[16,128]{1,0:T(8,128)(2,1)S(1)}, bf16[16,128]{1,0:T(8,128)(2,1)S(1)}, u32[]{:S(2)}, u32[]{:S(2)}) collective-permute-start(bf16[16,128]{1,0:T(8,128)(2,1)S(1)} %convolution_convert_fusion.4), channel_id=1, source_target_pairs={{0,1},{1,0},{2,3},{3,2},{4,5},{5,4},{6,7},{7,6},{8,9},{9,8},{10,11... | collective-permute-start | bytes 12296 | tf_op jit(solution)/shard_map/ppermute | solution.py:25
  38.1 3.7 %collective-permute-start.13 = (bf16[16,256]{1,0:T(8,128)(2,1)S(1)}, bf16[16,256]{1,0:T(8,128)(2,1)S(1)}, u32[]{:S(2)}, u32[]{:S(2)}) collective-permute-start(bf16[16,256]{1,0:T(8,128)(2,1)S(1)} %pad_maximum_fusion.5), channel_id=1, source_target_pairs={{0,2},{1,3},{2,0},{3,1},{4,6},{5,7},{6,4},{7,5},{8,10},{9,11},{10,... | collective-permute-start | bytes 24584 | tf_op jit(solution)/shard_map/ppermute | solution.py:25
  39.9 3.1 %copy-start.2 = (bf16[1024,640]{1,0:T(8,128)(2,1)S(1)}, bf16[1024,640]{1,0:T(8,128)(2,1)}, u32[]{:S(2)}) copy-start(bf16[1024,640]{1,0:T(8,128)(2,1)} %param.17) | copy-start | bytes 3932164
  41.0 2.5 %copy-start.6 = (f32[16,256,16]{1,2,0:T(8,128)S(1)}, f32[16,256,16]{1,2,0:T(8,128)}, u32[]{:S(2)}) copy-start(f32[16,256,16]{1,2,0:T(8,128)} %fusion.10) | copy-start | bytes 786436
  41.0 2.5 %copy-start.10 = (bf16[1024,256]{1,0:T(8,128)(2,1)S(1)}, bf16[1024,256]{1,0:T(8,128)(2,1)}, u32[]{:S(2)}) copy-start(bf16[1024,256]{1,0:T(8,128)(2,1)} %param.15) | copy-start | bytes 1572868
